TPU v7x, 128 devices: a whole 4x4x4 slice. The times are simulated.
128 devices in a mesh: grp: 4 (over z), seq: 32 (over x, y, core).
Axes of the slice: x: 4, y: 4, z: 4, core: 2. Of those that a mesh axis runs over, the one named last changes fastest.
Arguments:
- tokens: bfloat16 [65536, 1024], P(('grp', 'seq')), may hold values from -6 to 6
- fine_query: bfloat16 [1024, 1024], replicated, may hold values from -4 to 4, as said below
- fine_key: bfloat16 [1024, 1024], replicated, may hold values from -4 to 4, as said below
- fine_value: bfloat16 [1024, 1024], replicated, may hold values from -0.1875 to 0.1875
- fine_out: bfloat16 [1024, 1024], replicated, may hold values from -0.1875 to 0.1875
- short_weight: bfloat16 [8192, 1024], P('seq'), may hold values from -0.0625 to 0.0625
- coarse_query: bfloat16 [1024, 1024], replicated, may hold values from -4 to 4, as said below
- coarse_key: bfloat16 [1024, 1024], replicated, may hold values from -4 to 4, as said below
- coarse_value: bfloat16 [1024, 1024], replicated, may hold values from -0.1875 to 0.1875
- coarse_out: bfloat16 [1024, 1024], replicated, may hold values from -0.375 to 0.375
Outputs:
- upsampled: bfloat16 [65536, 1024], P(('grp', 'seq'))
Inputs may be any that keep to these rules, and one draw needn't show every extreme that they name: `fine_query`: entries of order 1024 ** -0.5 or a few times that. `fine_key`: entries of order 1024 ** -0.5 or a few times that. `coarse_query`: entries of order 1024 ** -0.5 or a few times that. `coarse_key`: entries of order 1024 ** -0.5 or a few times that.
All inputs are finite; a program needn't handle non-finite values.
Results may differ from a plain program's by a relative error of at most 0.02.
Values may be sent and summed in bfloat16 or wider, within the bound.
No kernel may reach another device: no remote copies, remote signals or barrier semaphores. Data moves between devices by JAX's collectives and lax.ppermute only.
A program may use at most 256 MiB of HBM per device.

v0:
```python
import math

import jax
import jax.numpy as jnp
from jax import lax
from jax.sharding import PartitionSpec as P

HEAD_DIM = 64
SHORT = 8
WIN = 1024


def from_behind(block, axis, distance):
    devices = range(lax.axis_size(axis))
    route = [(i - distance, i) for i in devices if i - distance in devices]
    return lax.ppermute(block, axis, route)


def normed(rows):
    values = rows.astype(jnp.float32)
    scale = lax.rsqrt(jnp.mean(values * values, axis=-1, keepdims=True) + 1e-06)
    return (values * scale).astype(jnp.bfloat16)


def project(rows, weight):
    return jnp.dot(rows, weight, preferred_element_type=jnp.float32).astype(jnp.bfloat16)


def window_attend(query, keys, values, keep):
    count, width = query.shape
    heads = width // HEAD_DIM
    span = keys.shape[0]
    query_heads = query.reshape(count, heads, HEAD_DIM)
    key_heads = keys.reshape(span, heads, HEAD_DIM)
    value_heads = values.reshape(span, heads, HEAD_DIM)
    scores = jnp.einsum(
        "qhd,khd->hqk", query_heads, key_heads, preferred_element_type=jnp.float32
    ) * (1.0 / math.sqrt(HEAD_DIM))
    scores = jnp.where(keep[None], scores, -1e30)
    top = jnp.max(scores, axis=-1, keepdims=True)
    weights = jnp.where(keep[None], jnp.exp(scores - top), 0.0)
    total = jnp.sum(weights, axis=-1)
    mixed = jnp.einsum(
        "hqk,khd->hqd",
        weights.astype(jnp.bfloat16),
        value_heads,
        preferred_element_type=jnp.float32,
    )
    mixed = mixed / total[..., None]
    return jnp.transpose(mixed, (1, 0, 2)).reshape(count, width).astype(jnp.bfloat16)


def body(
    tokens,
    fine_query,
    fine_key,
    fine_value,
    fine_out,
    short_weight,
    coarse_query,
    coarse_key,
    coarse_value,
    coarse_out,
):
    count, width = tokens.shape
    heads = width // HEAD_DIM
    place = lax.axis_index(("grp", "seq"))
    fine_normed = normed(tokens)
    query = project(fine_normed, fine_query)
    key_value = jnp.stack([project(fine_normed, fine_key), project(fine_normed, fine_value)])
    reach = WIN // count
    blocks = []
    for distance in range(reach, 0, -1):
        blocks.append(from_behind(key_value, ("grp", "seq"), distance))
    earlier = jnp.concatenate(blocks, axis=1)
    window = jnp.concatenate([earlier, key_value], axis=1)
    first = place * count
    query_pos = first + jnp.arange(count, dtype=jnp.int32)
    key_pos = first - WIN + jnp.arange(WIN + count, dtype=jnp.int32)
    keep = (
        (key_pos[None, :] <= query_pos[:, None])
        & (key_pos[None, :] > query_pos[:, None] - WIN)
        & (key_pos[None, :] >= 0)
    )
    fine_mixed = window_attend(query, window[0], window[1], keep)
    hidden = (
        tokens.astype(jnp.float32)
        + jnp.dot(fine_mixed, fine_out, preferred_element_type=jnp.float32)
    ).astype(jnp.bfloat16)
    tail = from_behind(hidden[count - (SHORT - 1) :], ("grp", "seq"), 1)
    delayed = jnp.concatenate([tail, hidden[: count - (SHORT - 1)]], axis=0)
    rows = count // SHORT
    grouped = delayed.reshape(rows, SHORT * width)
    summed = jnp.dot(
        grouped,
        lax.all_gather(short_weight, "seq", axis=0, tiled=True),
        preferred_element_type=jnp.float32,
    )
    shortened = summed.astype(jnp.bfloat16)
    coarse_normed = normed(shortened)
    coarse_q = project(coarse_normed, coarse_query).reshape(rows, heads, HEAD_DIM)
    coarse_k = project(coarse_normed, coarse_key)
    coarse_v = project(coarse_normed, coarse_value)
    own_pos = place * rows + jnp.arange(rows, dtype=jnp.int32)
    last_pos = place * rows + rows - 1
    initial = (
        jnp.full((heads, rows), -1e30, jnp.float32),
        jnp.zeros((heads, rows), jnp.float32),
        jnp.zeros((heads, rows, HEAD_DIM), jnp.float32),
    )
    keys_piece = lax.all_gather(coarse_k, ("grp", "seq"), axis=0, tiled=True)
    values_piece = lax.all_gather(coarse_v, ("grp", "seq"), axis=0, tiled=True)
    number = keys_piece.shape[0]

    def work(state):
        top, total, gathered = state
        piece_pos = jnp.arange(number, dtype=jnp.int32)
        keep_piece = piece_pos[None, :] <= own_pos[:, None]
        scores = jnp.einsum(
            "qhd,khd->hqk",
            coarse_q,
            keys_piece.reshape(number, heads, HEAD_DIM),
            preferred_element_type=jnp.float32,
        ) * (1.0 / math.sqrt(HEAD_DIM))
        scores = jnp.where(keep_piece[None], scores, -1e30)
        new_top = jnp.maximum(top, jnp.max(scores, axis=-1))
        weights = jnp.where(keep_piece[None], jnp.exp(scores - new_top[..., None]), 0.0)
        new_total = jnp.sum(weights, axis=-1)
        update = jnp.einsum(
            "hqk,khd->hqd",
            weights.astype(jnp.bfloat16),
            values_piece.reshape(number, heads, HEAD_DIM),
            preferred_element_type=jnp.float32,
        )
        return (new_top, new_total, update)

    def skip(state):
        return state

    top, total, gathered = lax.cond(jnp.int32(0) > last_pos, skip, work, initial)
    coarse_mixed = gathered / total[..., None]
    coarse_mixed = jnp.transpose(coarse_mixed, (1, 0, 2)).reshape(rows, width).astype(jnp.bfloat16)
    refined = shortened.astype(jnp.float32) + jnp.dot(
        coarse_mixed, coarse_out, preferred_element_type=jnp.float32
    )
    return (hidden.astype(jnp.float32) + jnp.repeat(refined, SHORT, axis=0)).astype(jnp.bfloat16)


def solution(mesh):
    return jax.shard_map(
        body,
        mesh=mesh,
        in_specs=(P(("grp", "seq"), None), P(), P(), P(), P(), P("seq", None), P(), P(), P(), P()),
        out_specs=P(("grp", "seq"), None),
        check_vma=False,
    )
```

profile of v0, /device:TPU:1, one launch (start us, length us, event | category | flops | bytes accessed | tf_op | source)
XLA Modules:
  0.0 483.2 jit_solution(6185480731886697648)
XLA Ops:
  8.9 2.7 fusion.27
  14.4 5.4 %collective-permute-start = (bf16[2,512,1024]{2,1,0:T(8,128)(2,1)}, bf16[2,512,1024]{2,1,0:T(8,128)(2,1)}, u32[]{:S(2)}, u32[]{:S(2)}) collective-permute-start(bf16[2,512,1024]{2,1,0:T(8,128)(2,1)} %pad_maximum_fusion), channel_id=1, source_target_pairs={{0,2},{1,3},{2,4},{3,5},{4,6},{5,7},{6,8},{7,9},{8,10},{9,11},{10,... | collective-permute-start | bytes 6291464 | tf_op jit(solution)/shard_map/ppermute | solution.py:16
  19.7 2.9 collective-permute-start.1
  22.7 4.0 convolution_convert_fusion.2
  30.6 60.4 %collective-permute-done = bf16[2,512,1024]{2,1,0:T(8,128)(2,1)} collective-permute-done((bf16[2,512,1024]{2,1,0:T(8,128)(2,1)}, bf16[2,512,1024]{2,1,0:T(8,128)(2,1)}, u32[]{:S(2)}, u32[]{:S(2)}) %collective-permute-start) | collective-permute-done | bytes 2097184 | tf_op jit(solution)/shard_map/ppermute | solution.py:16
  91.0 37.8 %collective-permute-done.1 = bf16[2,512,1024]{2,1,0:T(8,128)(2,1)} collective-permute-done((bf16[2,512,1024]{2,1,0:T(8,128)(2,1)}, bf16[2,512,1024]{2,1,0:T(8,128)(2,1)}, u32[]{:S(2)}, u32[]{:S(2)}) %collective-permute-start.1) | collective-permute-done | bytes 2097184 | tf_op jit(solution)/shard_map/ppermute | solution.py:16
  128.7 3.4 maximum_maximum_fusion
  132.1 3.3 fusion.36
  135.4 4.6 copy.19
  140.0 4.8 copy.20
  144.9 25.7 %fusion.37 = (f32[16,512]{1,0:T(8,128)S(1)}, bf16[16,512,1536]{2,1,0:T(8,128)(2,1)}) fusion(pred[512,1536]{1,0:T(8,128)(4,1)S(1)} %copy-done.6, bf16[512,16,64]{0,2,1:T(8,128)(2,1)S(1)} %bitcast.50, bf16[1536,16,64]{0,2,1:T(8,128)(2,1)} %bitcast.48), kind=kOutput, calls=%fused_computation.63 | convolution fusion | flops 1686111744 | bytes 30179328 | tf_op jit(solution)/shard_map/sub | solution.py:41
  170.5 13.3 %fusion.24 = bf16[512,16,64]{0,2,1:T(8,128)(2,1)S(1)} fusion(bf16[1536,16,64]{0,2,1:T(8,128)(2,1)} %bitcast.49, bf16[16,512,1536]{2,1,0:T(8,128)(2,1)} %get-tuple-element.42, f32[512,16]{0,1:T(8,128)S(1)} %bitcast.52), kind=kOutput, calls=%fused_computation.37 | convolution fusion | flops 1611661312 | bytes 29392896 | tf_op jit(solution)/shard_map/hqk,khd->hqd/dot_general | solution.py:43
  183.8 2.9 fusion.22
  186.7 4.6 collective-permute-start.2
  192.8 9.0 %multiply_reduce_fusion = (f32[64]{0:T(128)S(1)}, f32[64,1024]{1,0:T(8,128)S(1)}) fusion(bf16[64,8192]{1,0:T(8,128)(2,1)S(1)} %reshape.150, bf16[8192,1024]{1,0:T(8,128)(2,1)} %all-gather.4.cloned.1.call-done), kind=kOutput, calls=%fused_computation.52 | convolution fusion | flops 1074003968 | bytes 18088192 | tf_op jit(solution)/shard_map/dot_general | solution.py:94
  203.2 2.7 convolution_convert_fusion.3
  208.0 82.2 %all-gather.6.cloned.1.call-done = bf16[8192,1024]{1,0:T(8,128)(2,1)} async-done(((bf16[64,1024]{1,0:T(8,128)(2,1)}), bf16[8192,1024]{1,0:T(8,128)(2,1)}) %all-gather.6.cloned.1.call-update) | async-done | bytes 16777232 | tf_op jit(solution)/shard_map/all_gather | solution.py:111
  290.2 83.0 %all-gather.8.cloned.1.call-done = bf16[8192,1024]{1,0:T(8,128)(2,1)} async-done(((bf16[64,1024]{1,0:T(8,128)(2,1)}), bf16[8192,1024]{1,0:T(8,128)(2,1)}) %all-gather.8.cloned.1.call-update) | async-done | bytes 16777232 | tf_op jit(solution)/shard_map/all_gather | solution.py:112
  373.2 95.9 %conditional.1 = (f32[16,64]{1,0:T(8,128)S(1)}, f32[16,64,64]{2,1,0:T(8,128)S(1)}) conditional(s32[]{:T(128)} %convert_element_type.80, (s32[]{:T(128)}, s32[64]{0:T(128)S(1)}, bf16[64,1024]{1,0:T(8,128)(2,1)S(1)}, bf16[8192,1024]{1,0:T(8,128)(2,1)}, bf16[8192,1024]{1,0:T(8,128)(2,1)}) %tuple.13, () %tuple.14), branch_computations={%region_4.7_spmd, %region_7.8_spmd} | conditional | flops 2257058816 | bytes 204104464 | solution.py:140
  373.5 21.3 %copy.21 = bf16[8192,1024]{0,1:T(8,128)(2,1)} copy(bf16[8192,1024]{1,0:T(8,128)(2,1)} %get-tuple-element.35) | data formatting | bytes 33554432 | tf_op jit(solution)/shard_map
  395.1 17.4 %fusion = (f32[16,64]{1,0:T(8,128)S(1)}, f32[16,64,8192]{2,1,0:T(8,128)}) fusion(pred[64,8192]{1,0:T(8,128)(4,1)S(1)} %iota_compare_fusion, bf16[8192,16,64]{0,2,1:T(8,128)(2,1)} %bitcast.45, bf16[64,16,64]{2,1,0:T(8,128)(2,1)S(1)} %reshape.143), kind=kOutput, calls=%fused_computation.2 | convolution fusion | flops 1098906624 | bytes 50991104 | tf_op jit(solution)/shard_map/cond/branch_0_fun/qhd,khd->hqk/dot_general | solution.py:119
  412.5 21.3 %copy.22 = bf16[8192,1024]{0,1:T(8,128)(2,1)} copy(bf16[8192,1024]{1,0:T(8,128)(2,1)} %get-tuple-element.36) | data formatting | bytes 33554432 | tf_op jit(solution)/shard_map
  433.8 19.3 %fusion.3 = f32[16,64,64]{2,1,0:T(8,128)S(1)} fusion(bf16[8192,16,64]{0,2,1:T(8,128)(2,1)} %bitcast.46, f32[16,64,8192]{2,1,0:T(8,128)} %get-tuple-element.38, f32[16,64]{1,0:T(8,128)S(1)} %broadcast_maximum_fusion, pred[64,8192]{1,0:T(8,128)(4,1)S(1)} %iota_compare_fusion), kind=kOutput, calls=%fused_computation.5 | convolution fusion | flops 1115684864 | bytes 51122176 | tf_op jit(solution)/shard_map/cond/branch_0_fun/hqk,khd->hqd/dot_general | solution.py:129
  453.0 16.0 %fusion.2 = f32[16,64]{1,0:T(8,128)S(1)} fusion(f32[16,64,8192]{2,1,0:T(8,128)} %get-tuple-element.38, f32[16,64]{1,0:T(8,128)S(1)} %broadcast_maximum_fusion, pred[64,8192]{1,0:T(8,128)(4,1)S(1)} %iota_compare_fusion), kind=kLoop, calls=%fused_computation.4 | loop fusion | flops 41942016 | bytes 34086912 | tf_op jit(solution)/shard_map/cond/branch_0_fun/reduce_sum | solution.py:128
  (52 shorter events, 22.0 us)
Async XLA Ops:
  6.5 2.3 copy-start
  6.5 186.2 %all-gather.4.cloned.1.call-start = ((), (), s32[]{:S(2)}) async-start(), calls=%async_computation | async-start | bytes 17301504 | tf_op jit(solution)/shard_map/all_gather | solution.py:96
  7.3 282.9 %all-gather.6.cloned.1.call-start = ((), (), s32[]{:S(2)}) async-start(), calls=%async_computation.1 | async-start | bytes 16908288 | tf_op jit(solution)/shard_map/all_gather | solution.py:111
  8.8 2.7 copy-start.3
  8.8 2.7 copy-start.8
  12.8 9.8 %copy-start.4 = (bf16[512,1024]{1,0:T(8,128)(2,1)S(1)}, bf16[512,1024]{1,0:T(8,128)(2,1)}, u32[]{:S(2)}) copy-start(bf16[512,1024]{1,0:T(8,128)(2,1)} %param.12) | copy-start | bytes 3145732
  14.4 76.6 %collective-permute-start = (bf16[2,512,1024]{2,1,0:T(8,128)(2,1)}, bf16[2,512,1024]{2,1,0:T(8,128)(2,1)}, u32[]{:S(2)}, u32[]{:S(2)}) collective-permute-start(bf16[2,512,1024]{2,1,0:T(8,128)(2,1)} %pad_maximum_fusion), channel_id=1, source_target_pairs={{0,2},{1,3},{2,4},{3,5},{4,6},{5,7},{6,8},{7,9},{8,10},{9,11},{10,... | collective-permute-start | bytes 6291464 | tf_op jit(solution)/shard_map/ppermute | solution.py:16
  19.7 109.0 %collective-permute-start.1 = (bf16[2,512,1024]{2,1,0:T(8,128)(2,1)}, bf16[2,512,1024]{2,1,0:T(8,128)(2,1)}, u32[]{:S(2)}, u32[]{:S(2)}) collective-permute-start(bf16[2,512,1024]{2,1,0:T(8,128)(2,1)} %pad_maximum_fusion), channel_id=1, source_target_pairs={{0,1},{1,2},{2,3},{3,4},{4,5},{5,6},{6,7},{7,8},{8,9},{9,10},{10,1... | collective-permute-start | bytes 6291464 | tf_op jit(solution)/shard_map/ppermute | solution.py:16
  140.0 4.8 copy-start.5
  140.0 4.8 copy-start.6
  186.7 5.3 %collective-permute-start.2 = (bf16[7,1024]{1,0:T(8,128)(2,1)S(1)}, bf16[7,1024]{1,0:T(8,128)(2,1)S(1)}, u32[]{:S(2)}, u32[]{:S(2)}) collective-permute-start(bf16[7,1024]{1,0:T(8,128)(2,1)S(1)} %slice.18), channel_id=1, source_target_pairs={{0,1},{1,2},{2,3},{3,4},{4,5},{5,6},{6,7},{7,8},{8,9},{9,10},{10,1... | collective-permute-start | bytes 43016 | tf_op jit(solution)/shard_map/ppermute | solution.py:16
  192.8 9.2 %copy-start.2 = (bf16[1024,1024]{1,0:T(8,128)(2,1)S(1)}, bf16[1024,1024]{1,0:T(8,128)(2,1)}, u32[]{:S(2)}) copy-start(bf16[1024,1024]{1,0:T(8,128)(2,1)} %param.19) | copy-start | bytes 6291460
  203.1 170.0 %all-gather.8.cloned.1.call-start = ((), (), s32[]{:S(2)}) async-start(), calls=%async_computation.2 | async-start | bytes 16908288 | tf_op jit(solution)/shard_map/all_gather | solution.py:112
  469.1 0.8 copy-start.7
  469.9 6.8 %copy-start.1 = (bf16[1024,1024]{1,0:T(8,128)(2,1)S(1)}, bf16[1024,1024]{1,0:T(8,128)(2,1)}, u32[]{:S(2)}) copy-start(bf16[1024,1024]{1,0:T(8,128)(2,1)} %param.14) | copy-start | bytes 6291460
Sparse Core Ops, SparseCore 0:
  9.6 111.5 all-gather.3
  203.2 86.8 all-gather.5
  293.3 79.7 all-gather.7
where the time goes:
time: 485 us; the launch traced here: 483 us
  waiting for transfers between devices  265 us (55%)
  matrix products  103 us (21%)
  local copies, waits for them, and re-layouts  61.2 us (13%)
  other arithmetic  27.5 us (6%)
  between operations  13.3 us (3%)
  starting transfers between devices  13 us (3%)
    ppermute x3, waiting for transfers between devices, from_behind(): return lax.ppermute(block, axis, route)  98.8 us
    all_gather x1, waiting for transfers between devices, body(): values_piece = lax.all_gather(coarse_v, ('grp', 'seq'), axis=0, tiled=True)  83 us
    all_gather x1, waiting for transfers between devices, body(): keys_piece = lax.all_gather(coarse_k, ('grp', 'seq'), axis=0, tiled=True)  82.2 us
    another operation x2, local copies, waits for them, and re-layouts  42.7 us
    sub x1, matrix products, window_attend(): weights = jnp.where(keep[None], jnp.exp(scores - top), 0.0)  25.7 us
    dot_general x1, matrix products, work(): jnp.einsum('hqk,khd->hqd', weights.astype(jnp.bfloat16), values_piece.res...  19.3 us
    dot_general x1, matrix products, work(): jnp.einsum('qhd,khd->hqk', coarse_q, keys_piece.reshape(number, heads, HE...  17.4 us
    reduce_sum x1, other arithmetic, work(): new_total = jnp.sum(weights, axis=-1)  16 us
  transfers between devices with their start and end apart: 6, of which 5 were waited for; matrix products, arithmetic and copies ran while one was open for 16% of the time, Pallas kernels for 0%

commit v1 on v0

v1 whole, which is shorter than its diff:
```python
import functools
import math

import jax
import jax.numpy as jnp
from jax import lax
from jax.experimental import pallas as pl
from jax.experimental.pallas import tpu as pltpu
from jax.sharding import Mesh, PartitionSpec as P

HEAD_DIM = 64
HEADS = 16
SHORT = 8
WIN = 1024
SCALE = math.log2(math.e) / math.sqrt(HEAD_DIM)
ALL = ("z", "x", "y", "c")
QB = 128
PAIR = 2 * HEAD_DIM
NEG = -1e30


def from_behind(block, distance):
    devices = range(128)
    route = [(i - distance, i) for i in devices if i - distance in devices]
    return lax.ppermute(block, ALL, route)


def normed(rows):
    values = rows.astype(jnp.float32)
    scale = lax.rsqrt(jnp.mean(values * values, axis=-1, keepdims=True) + 1e-06)
    return (values * scale).astype(jnp.bfloat16)


def dot(a, b, contract):
    return lax.dot_general(a, b, (contract, ((), ())), preferred_element_type=jnp.float32)


def fine_kernel(place_ref, q_ref, k_ref, v_ref, out_ref, s_ref, p_ref):
    count = q_ref.shape[0]
    span = WIN + QB
    lane = lax.broadcasted_iota(jnp.int32, (QB, PAIR), 1)
    row = lax.broadcasted_iota(jnp.int32, (QB, 2 * QB), 0)
    col = lax.broadcasted_iota(jnp.int32, (QB, 2 * QB), 1) % QB
    last = row <= col
    ones = jnp.ones((16, span), jnp.bfloat16)

    def units(masked):
        for b in range(count // QB):
            q = q_ref[b * QB : (b + 1) * QB, :]
            zero = jnp.zeros_like(q)
            both = jnp.concatenate(
                [jnp.where(lane < HEAD_DIM, q, zero), jnp.where(lane < HEAD_DIM, zero, q)], axis=0
            )
            s = dot(k_ref[b * QB : b * QB + span, :], both, ((1,), (1,)))
            if masked:
                key = lax.broadcasted_iota(jnp.int32, s.shape, 0) + b * QB
                s = jnp.where(key >= WIN - place_ref[0] * count, s, NEG)
            s_ref[b] = s
            edge = jnp.where(last, s_ref[b, WIN:span, :], s_ref[b, 0:QB, :])
            top = jnp.maximum(
                jnp.max(edge, axis=0, keepdims=True),
                jnp.max(s_ref[b, QB:WIN, :], axis=0, keepdims=True),
            )
            edge = jnp.exp2(edge - top)
            p_ref[b, 0:QB, :] = jnp.where(last, 0.0, edge).astype(jnp.bfloat16)
            p_ref[b, WIN:span, :] = jnp.where(last, edge, 0.0).astype(jnp.bfloat16)
            p_ref[b, QB:WIN, :] = jnp.exp2(s_ref[b, QB:WIN, :] - top).astype(jnp.bfloat16)
            v = jnp.concatenate([v_ref[:, b * QB : b * QB + span], ones], axis=0)
            o = dot(v, p_ref[b], ((1,), (0,)))
            o = o[:PAIR] * (1.0 / o[PAIR : PAIR + 1])
            mixed = jnp.concatenate([o[:HEAD_DIM, :QB], o[HEAD_DIM:PAIR, QB:]], axis=0)
            out_ref[b * QB : (b + 1) * QB, :] = mixed.T.astype(jnp.bfloat16)

    @pl.when(place_ref[0] * count >= WIN)
    def _():
        units(False)

    @pl.when(place_ref[0] * count < WIN)
    def _():
        units(True)


def fine_attend(place, q, k, v):
    count, width = q.shape
    span = WIN + count
    blocks = count // QB
    return pl.pallas_call(
        fine_kernel,
        grid=(width // PAIR,),
        in_specs=[
            pl.BlockSpec(memory_space=pltpu.SMEM),
            pl.BlockSpec((count, PAIR), lambda i: (0, i)),
            pl.BlockSpec((span, PAIR), lambda i: (0, i)),
            pl.BlockSpec((PAIR, span), lambda i: (i, 0)),
        ],
        out_specs=pl.BlockSpec((count, PAIR), lambda i: (0, i)),
        out_shape=jax.ShapeDtypeStruct((count, width), jnp.bfloat16),
        scratch_shapes=[
            pltpu.VMEM((blocks, WIN + QB, 2 * QB), jnp.float32),
            pltpu.VMEM((blocks, WIN + QB, 2 * QB), jnp.bfloat16),
        ],
        compiler_params=pltpu.CompilerParams(vmem_limit_bytes=40 * 2**20),
        cost_estimate=pl.CostEstimate(flops=10 * 2**30, bytes_accessed=8 * 2**20, transcendentals=8 * 2**20),
    )(place.reshape(1), q, k, v)


def coarse_kernel(group_ref, q_ref, kv_ref, out_ref):
    parts, blocks, rows, _ = kv_ref.shape
    keys = parts * rows
    tile = 4 * rows
    tiles = q_ref.shape[0] // tile
    lane = lax.broadcasted_iota(jnp.int32, (1, tile), 1)
    row = lax.broadcasted_iota(jnp.int32, (keys, tile), 0)
    limit = (lane // rows) * keys + group_ref[0] * rows + lane % rows
    ones = jnp.ones((16, keys), jnp.bfloat16)
    queries = []
    for t in range(tiles):
        q = q_ref[t * tile : (t + 1) * tile, :]
        queries.append(jnp.concatenate([q, jnp.zeros_like(q)], axis=1))
    tops = [jnp.full((1, tile), NEG, jnp.float32)] * tiles
    accs = [jnp.zeros((16 + rows, tile), jnp.float32)] * tiles
    for g in range(blocks):
        kv = kv_ref[:, g].reshape(keys, 2 * HEAD_DIM)
        v = jnp.concatenate([ones, kv.T[HEAD_DIM:, :]], axis=0)
        for t in range(g // 4, tiles):
            s = dot(kv, queries[t], ((1,), (1,)))
            if t == g // 4:
                s = jnp.where(row <= limit - (g - 4 * t) * keys, s, NEG)
            top = jnp.maximum(tops[t], jnp.max(s, axis=0, keepdims=True))
            p = jnp.exp2(s - top).astype(jnp.bfloat16)
            accs[t] = accs[t] * jnp.exp2(tops[t] - top) + dot(v, p, ((1,), (0,)))
            tops[t] = top
    for t in range(tiles):
        o = accs[t][16:] * (1.0 / accs[t][0:1])
        out_ref[t * tile : (t + 1) * tile, :] = o.T.astype(jnp.bfloat16)


def coarse_attend(group, q, kv):
    return pl.pallas_call(
        coarse_kernel,
        in_specs=[
            pl.BlockSpec(memory_space=pltpu.SMEM),
            pl.BlockSpec(memory_space=pltpu.VMEM),
            pl.BlockSpec(memory_space=pltpu.VMEM),
        ],
        out_specs=pl.BlockSpec(memory_space=pltpu.VMEM),
        out_shape=jax.ShapeDtypeStruct(q.shape, jnp.bfloat16),
        compiler_params=pltpu.CompilerParams(vmem_limit_bytes=40 * 2**20),
        cost_estimate=pl.CostEstimate(flops=4 * 2**30, bytes_accessed=3 * 2**20, transcendentals=5 * 2**20),
    )(group.reshape(1), q, kv)


def body(
    tokens,
    fine_query,
    fine_key,
    fine_value,
    fine_out,
    short_weight,
    coarse_query,
    coarse_key,
    coarse_value,
    coarse_out,
):
    count, width = tokens.shape
    bf = jnp.bfloat16
    place = lax.axis_index(ALL).astype(jnp.int32)
    far = from_behind(tokens, 2)
    near = from_behind(tokens, 1)
    weight = lax.all_gather(short_weight, ("x", "c"), axis=0, tiled=True)

    window = jnp.concatenate([far, near, tokens], axis=0)
    fine_normed = normed(window)
    own = normed(tokens)
    query = (dot(own, fine_query, ((1,), (0,))) * SCALE).astype(bf)
    keys = dot(fine_normed, fine_key, ((1,), (0,))).astype(bf)
    values = dot(fine_value, fine_normed, ((0,), (1,))).astype(bf)
    fine_mixed = fine_attend(place, query, keys, values)
    hidden = (tokens.astype(jnp.float32) + dot(fine_mixed, fine_out, ((1,), (0,)))).astype(bf)
    tail = from_behind(hidden[count - (SHORT - 1) :], 1)
    delayed = jnp.concatenate([tail, hidden[: count - (SHORT - 1)]], axis=0)
    rows = count // SHORT
    grouped = delayed.reshape(rows, 4, 4, 2 * width // 4)
    grouped = jnp.transpose(grouped, (2, 0, 1, 3)).reshape(4, rows, 2 * width)
    grouped = lax.all_to_all(grouped, "y", 0, 0).reshape(4 * rows, 2 * width)
    partial = dot(grouped, weight, ((1,), (0,))).astype(bf).reshape(4, rows, width)
    partial = lax.all_to_all(partial, "y", 0, 0)
    shortened = jnp.sum(partial.astype(jnp.float32), axis=0).astype(bf)
    coarse_normed = normed(shortened)

    def heads(weights, scale=1.0):
        out = (dot(coarse_normed, weights, ((1,), (0,))) * scale).astype(bf)
        return out.reshape(rows, HEADS, HEAD_DIM)

    qkv = jnp.concatenate(
        [heads(coarse_query, SCALE), heads(coarse_key), heads(coarse_value)], axis=2
    )
    qkv = lax.all_to_all(jnp.transpose(qkv, (1, 0, 2)), ("z", "x"), 0, 0)
    q = qkv[:, :, :HEAD_DIM].reshape(HEADS * rows, HEAD_DIM)
    kv = lax.all_gather(qkv[:, :, HEAD_DIM:], ("y", "c"), axis=0)
    mixed = coarse_attend(lax.axis_index(("y", "c")).astype(jnp.int32), q, kv)
    mixed = lax.all_to_all(mixed.reshape(HEADS, rows, HEAD_DIM), ("z", "x"), 0, 0)
    coarse_mixed = jnp.transpose(mixed, (1, 0, 2)).reshape(rows, width)
    refined = shortened.astype(jnp.float32) + dot(coarse_mixed, coarse_out, ((1,), (0,)))
    return (hidden.astype(jnp.float32) + jnp.repeat(refined, SHORT, axis=0)).astype(bf)


def solution(mesh):
    fine = Mesh(mesh.devices.reshape(4, 4, 4, 2), ALL)
    return jax.shard_map(
        body,
        mesh=fine,
        in_specs=(P(ALL, None), P(), P(), P(), P(), P(("x", "y", "c"), None), P(), P(), P(), P()),
        out_specs=P(ALL, None),
        check_vma=False,
    )
```

time: 485 us -> 247 us (0.51)
  waiting for transfers between devices: 265 us -> 52 us
  blocking collectives: 0 us -> 78.4 us
  matrix products: 103 us -> 26.2 us
  local copies, waits for them, and re-layouts: 61.2 us -> 11.4 us
  Pallas kernels: 0 us -> 45.5 us
  other arithmetic: 27.5 us -> 5.41 us
    all_gather x3 -> x2, waiting for transfers between devices: 165 us -> 24.9 us  [the longest x1 24.9 us: body(): kv = lax.all_gather(qkv[:, :, HEAD_DIM:], ('y', 'c'), axis=0)]
    all_to_all x0 -> x4, blocking collectives: none -> 78.4 us  [the longest x1 34.5 us: body(): grouped = lax.all_to_all(grouped, 'y', 0, 0).reshape(4 * rows, 2 * width)]
    ppermute x3, waiting for transfers between devices: 98.8 us -> 26.4 us  [from_behind(): return lax.ppermute(block, ALL, route)]
    dot_general x12 -> x9, matrix products: 77.7 us -> 26.2 us  [dot(): lax.dot_general(a, b, (contract, ((), ())), preferred_element_type=jnp.fl...]
    pallas_call x0 -> x2, Pallas kernels: none -> 45.5 us  [the longest x1 28.8 us: fine_attend(): pl.pallas_call(fine_kernel, grid=(width // PAIR,), in_specs=[pl.BlockSpec...]
    another operation x2 -> x0, local copies, waits for them, and re-layouts: 42.7 us -> none
    sub x1 -> x0, matrix products: 25.7 us -> none  [window_attend(): weights = jnp.where(keep[None], jnp.exp(scores - top), 0.0)]
    reduce_sum x1, other arithmetic: 16 us -> 0.08 us  [body(): shortened = jnp.sum(partial.astype(jnp.float32), axis=0).astype(bf)]
  transfers between devices with their start and end apart: 6 -> 5, of which waited for: 5 -> 4; matrix products, arithmetic and copies ran while one was open for 16% -> 9% of each run, Pallas kernels for 0% -> 12%
where the time goes in v1:
time: 247 us; the launch traced here: 246 us
  blocking collectives  78.4 us (32%)
  waiting for transfers between devices  52 us (21%)
  Pallas kernels  45.5 us (18%)
  matrix products  26.2 us (11%)
  between operations  13.7 us (6%)
  starting transfers between devices  12.9 us (5%)
  local copies, waits for them, and re-layouts  11.4 us (5%)
  other arithmetic  5.41 us (2%)
    all_to_all x1, blocking collectives, body(): grouped = lax.all_to_all(grouped, 'y', 0, 0).reshape(4 * rows, 2 * width)  34.5 us
    pallas_call x1, Pallas kernels, fine_attend(): pl.pallas_call(fine_kernel, grid=(width // PAIR,), in_specs=[pl.BlockSpec...  28.8 us
    ppermute x3, waiting for transfers between devices, from_behind(): return lax.ppermute(block, ALL, route)  26.4 us
    dot_general x9, matrix products, dot(): lax.dot_general(a, b, (contract, ((), ())), preferred_element_type=jnp.fl...  26.2 us
    all_gather x1, waiting for transfers between devices, body(): kv = lax.all_gather(qkv[:, :, HEAD_DIM:], ('y', 'c'), axis=0)  24.9 us
    all_to_all x1, blocking collectives, body(): qkv = lax.all_to_all(jnp.transpose(qkv, (1, 0, 2)), ('z', 'x'), 0, 0)  20.5 us
    pallas_call x1, Pallas kernels, coarse_attend(): pl.pallas_call(coarse_kernel, in_specs=[pl.BlockSpec(memory_space=pltpu.S...  16.7 us
    all_to_all x1, blocking collectives, body(): lax.all_to_all(mixed.reshape(HEADS, rows, HEAD_DIM), ('z', 'x'), 0, 0)  13.5 us
  transfers between devices with their start and end apart: 5, of which 4 were waited for; matrix products, arithmetic and copies ran while one was open for 9% of the time, Pallas kernels for 12%

profile of v1, /device:TPU:1, one launch (start us, length us, event | category | flops | bytes accessed | tf_op | source)
XLA Modules:
  0.0 245.6 jit_solution(10687756945172305190)
XLA Ops:
  7.3 4.1 %collective-permute-start = (bf16[512,1024]{1,0:T(8,128)(2,1)}, bf16[512,1024]{1,0:T(8,128)(2,1)S(1)}, u32[]{:S(2)}, u32[]{:S(2)}) collective-permute-start(bf16[512,1024]{1,0:T(8,128)(2,1)} %param.10), channel_id=1, source_target_pairs={{0,2},{1,3},{2,4},{3,5},{4,6},{5,7},{6,8},{7,9},{8,10},{9,11},{10,... | collective-permute-start | bytes 3145736 | tf_op jit(solution)/shard_map/ppermute | solution.py:25
  11.4 4.0 %collective-permute-start.1 = (bf16[512,1024]{1,0:T(8,128)(2,1)}, bf16[512,1024]{1,0:T(8,128)(2,1)}, u32[]{:S(2)}, u32[]{:S(2)}) collective-permute-start(bf16[512,1024]{1,0:T(8,128)(2,1)} %param.10), channel_id=1, source_target_pairs={{0,1},{1,2},{2,3},{3,4},{4,5},{5,6},{6,7},{7,8},{8,9},{9,10},{10,1... | collective-permute-start | bytes 3145736 | tf_op jit(solution)/shard_map/ppermute | solution.py:25
  17.0 3.3 %multiply_convert_fusion.q_ref = bf16[512,1024]{1,0:T(8,128)(2,1)S(1)} fusion(bf16[1024,1024]{1,0:T(8,128)(2,1)} %param.11, bf16[512,1024]{1,0:T(8,128)(2,1)} %param.10, f32[512]{0:T(512)S(1)} %add_rsqrt_fusion.1), kind=kOutput, calls=%fused_computation.16 | convolution fusion | flops 1076363264 | bytes 4196352 | tf_op jit(solution)/shard_map/dot_general | solution.py:35
  20.3 13.2 %collective-permute-done = bf16[512,1024]{1,0:T(8,128)(2,1)S(1)} collective-permute-done((bf16[512,1024]{1,0:T(8,128)(2,1)}, bf16[512,1024]{1,0:T(8,128)(2,1)S(1)}, u32[]{:S(2)}, u32[]{:S(2)}) %collective-permute-start) | collective-permute-done | bytes 1048608 | tf_op jit(solution)/shard_map/ppermute | solution.py:25
  33.5 12.4 %collective-permute-done.1 = bf16[512,1024]{1,0:T(8,128)(2,1)} collective-permute-done((bf16[512,1024]{1,0:T(8,128)(2,1)}, bf16[512,1024]{1,0:T(8,128)(2,1)}, u32[]{:S(2)}, u32[]{:S(2)}) %collective-permute-start.1) | collective-permute-done | bytes 1048608 | tf_op jit(solution)/shard_map/ppermute | solution.py:25
  45.9 1.8 fusion
  47.7 5.1 %fusion.2.v_ref = bf16[1024,1536]{1,0:T(8,128)(2,1)S(1)} fusion(bf16[1024,1024]{1,0:T(8,128)(2,1)S(1)} %copy-done, f32[1536]{0:T(1024)S(1)} %add_rsqrt_fusion, bf16[512,1024]{1,0:T(8,128)(2,1)S(1)} %copy-done.4, bf16[512,1024]{1,0:T(8,128)(2,1)} %collective-permute-done.1, bf16[512,1024]{1,0:T(8,128)(2,1)S(1)} %collective-permute-done), kind=kOutput, calls=%fused_computation.6 | convolution fusion | flops 3235381248 | bytes 8394752 | tf_op jit(solution)/shard_map/dot_general | solution.py:35
  52.8 4.7 %convolution_convert_fusion.1.k_ref = bf16[1536,1024]{1,0:T(8,128)(2,1)S(1)} fusion(bf16[1024,1024]{1,0:T(8,128)(2,1)S(1)} %copy-done.5, f32[1536]{0:T(1024)S(1)} %add_rsqrt_fusion, bf16[512,1024]{1,0:T(8,128)(2,1)S(1)} %copy-done.4, bf16[512,1024]{1,0:T(8,128)(2,1)} %collective-permute-done.1, bf16[512,1024]{1,0:T(8,128)(2,1)S(1)} %collective-permute-done), kind=kOutput, calls=%fused_computation.5 | convolution fusion | flops 3235381248 | bytes 8394752 | tf_op jit(solution)/shard_map/dot_general | solution.py:35
  57.6 28.8 %shard_map.100 = bf16[512,1024]{1,0:T(8,128)(2,1)S(1)} custom-call(s32[1]{0:T(128)} %bitcast.place_ref, bf16[512,1024]{1,0:T(8,128)(2,1)S(1)} %multiply_convert_fusion.q_ref, bf16[1536,1024]{1,0:T(8,128)(2,1)S(1)} %convolution_convert_fusion.1.k_ref, bf16[1024,1536]{1,0:T(8,128)(2,1)S(1)} %fusion.2.v_ref), custom_call_target="tpu_custom_call" | custom-call | flops 10737418240 | bytes 8388608 | tf_op jit(solution)/shard_map/pallas_call | solution.py:87
  87.7 4.8 %collective-permute-start.2 = (bf16[7,1024]{1,0:T(8,128)(2,1)S(1)}, bf16[7,1024]{1,0:T(8,128)(2,1)S(1)}, u32[]{:S(2)}, u32[]{:S(2)}) collective-permute-start(bf16[7,1024]{1,0:T(8,128)(2,1)S(1)} %slice.16), channel_id=1, source_target_pairs={{0,1},{1,2},{2,3},{3,4},{4,5},{5,6},{6,7},{7,8},{8,9},{9,10},{10,1... | collective-permute-start | bytes 43016 | tf_op jit(solution)/shard_map/ppermute | solution.py:25
  95.2 1.6 copy.27
  96.8 1.6 reshape.65
  98.4 34.5 %all_to_all.20 = bf16[4,64,2048]{2,1,0:T(8,128)(2,1)S(1)} all-to-all(bf16[4,64,2048]{2,1,0:T(8,128)(2,1)} %reshape.65), channel_id=1, replica_groups=mesh['z'=4,'x'=4,'y'=4,'c'=2] {'y'}, dimensions={0} | all-to-all | bytes 2097152 | tf_op jit(solution)/shard_map/all_to_all | solution.py:185
  133.0 3.4 %convolution_convert_fusion.2 = bf16[256,1024]{1,0:T(8,128)(2,1)S(1)} fusion(bf16[256,2048]{1,0:T(8,128)(2,1)S(1)} %bitcast.37, bf16[2048,1024]{1,0:T(8,128)(2,1)} %all-gather.4.cloned.1.call-done), kind=kOutput, calls=%fused_computation.17 | convolution fusion | flops 1074003968 | bytes 5767168 | tf_op jit(solution)/shard_map/dot_general | solution.py:35
  136.4 9.9 %all_to_all.21 = bf16[4,64,1024]{2,1,0:T(8,128)(2,1)S(1)} all-to-all(bf16[4,64,1024]{2,1,0:T(8,128)(2,1)S(1)} %bitcast.39), channel_id=1, replica_groups=mesh['z'=4,'x'=4,'y'=4,'c'=2] {'y'}, dimensions={0} | all-to-all | bytes 1048576 | tf_op jit(solution)/shard_map/all_to_all | solution.py:187
  146.5 2.1 fusion.7
  148.9 2.1 convolution_convert_fusion.4
  151.3 2.1 convolution_convert_fusion.3
  153.9 20.5 %all_to_all.22 = bf16[16,64,192]{2,1,0:T(8,128)(2,1)S(1)} all-to-all(bf16[16,64,192]{2,1,0:T(8,128)(2,1)S(1)} %maximum_bitcast_fusion), channel_id=1, replica_groups=mesh['z'=4,'x'=4,'y'=4,'c'=2] {'z','x'}, dimensions={0} | all-to-all | bytes 786432 | tf_op jit(solution)/shard_map/all_to_all | solution.py:198
  175.3 24.9 %all-gather.6.cloned.1.call-done = bf16[128,64,128]{2,1,0:T(8,128)(2,1)} async-done(((bf16[16,64,128]{2,1,0:T(8,128)(2,1)}), bf16[128,64,128]{2,1,0:T(8,128)(2,1)}) %all-gather.6.cloned.1.call-update) | async-done | bytes 2097168 | tf_op jit(solution)/shard_map/all_gather | solution.py:200
  200.2 1.6 copy-done.1
  201.8 16.7 %shard_map.101 = bf16[1024,64]{1,0:T(8,128)(2,1)S(1)} custom-call(s32[1]{0:T(128)} %bitcast.5.group_ref, bf16[1024,64]{1,0:T(8,128)(2,1)S(1)} %bitcast.33, bf16[8,16,64,128]{3,2,1,0:T(8,128)(2,1)S(1)} %bitcast.34), custom_call_target="tpu_custom_call" | custom-call | flops 4294967296 | bytes 3145728 | tf_op jit(solution)/shard_map/pallas_call | solution.py:139
  218.7 13.5 %all_to_all.23 = bf16[16,2,2048]{2,1,0:T(2,128)(2,1)} all-to-all(bf16[16,2,2048]{2,1,0:T(2,128)(2,1)S(1)} %reshape.77), channel_id=1, replica_groups=mesh['z'=4,'x'=4,'y'=4,'c'=2] {'z','x'}, dimensions={0} | all-to-all | bytes 262144 | tf_op jit(solution)/shard_map/all_to_all | solution.py:202
  235.4 2.1 convolution_add_fusion
  (43 shorter events, 13.0 us)
Async XLA Ops:
  6.5 41.2 %copy-start = (bf16[1024,1024]{1,0:T(8,128)(2,1)S(1)}, bf16[1024,1024]{1,0:T(8,128)(2,1)}, u32[]{:S(2)}) copy-start(bf16[1024,1024]{1,0:T(8,128)(2,1)} %param.13) | copy-start | bytes 6291460
  6.5 126.4 %all-gather.4.cloned.1.call-start = ((), (), s32[]{:S(2)}) async-start(), calls=%async_computation.4 | async-start | bytes 4718592 | tf_op jit(solution)/shard_map/all_gather | solution.py:170
  7.3 192.9 %all-gather.6.cloned.1.call-start = ((), (), s32[]{:S(2)}) async-start(), calls=%async_computation.5 | async-start | bytes 2359296 | tf_op jit(solution)/shard_map/all_gather | solution.py:200
  7.3 26.2 %collective-permute-start = (bf16[512,1024]{1,0:T(8,128)(2,1)}, bf16[512,1024]{1,0:T(8,128)(2,1)S(1)}, u32[]{:S(2)}, u32[]{:S(2)}) collective-permute-start(bf16[512,1024]{1,0:T(8,128)(2,1)} %param.10), channel_id=1, source_target_pairs={{0,2},{1,3},{2,4},{3,5},{4,6},{5,7},{6,8},{7,9},{8,10},{9,11},{10,... | collective-permute-start | bytes 3145736 | tf_op jit(solution)/shard_map/ppermute | solution.py:25
  11.4 34.4 %collective-permute-start.1 = (bf16[512,1024]{1,0:T(8,128)(2,1)}, bf16[512,1024]{1,0:T(8,128)(2,1)}, u32[]{:S(2)}, u32[]{:S(2)}) collective-permute-start(bf16[512,1024]{1,0:T(8,128)(2,1)} %param.10), channel_id=1, source_target_pairs={{0,1},{1,2},{2,3},{3,4},{4,5},{5,6},{6,7},{7,8},{8,9},{9,10},{10,1... | collective-permute-start | bytes 3145736 | tf_op jit(solution)/shard_map/ppermute | solution.py:25
  17.0 28.9 %copy-start.4 = (bf16[512,1024]{1,0:T(8,128)(2,1)S(1)}, bf16[512,1024]{1,0:T(8,128)(2,1)}, u32[]{:S(2)}) copy-start(bf16[512,1024]{1,0:T(8,128)(2,1)} %param.10) | copy-start | bytes 3145732
  47.7 5.1 %copy-start.5 = (bf16[1024,1024]{1,0:T(8,128)(2,1)S(1)}, bf16[1024,1024]{1,0:T(8,128)(2,1)}, u32[]{:S(2)}) copy-start(bf16[1024,1024]{1,0:T(8,128)(2,1)} %param.12) | copy-start | bytes 6291460
  57.5 28.9 %copy-start.6 = (bf16[1024,1024]{1,0:T(8,128)(2,1)S(1)}, bf16[1024,1024]{1,0:T(8,128)(2,1)}, u32[]{:S(2)}) copy-start(bf16[1024,1024]{1,0:T(8,128)(2,1)} %param.14) | copy-start | bytes 6291460
  87.7 5.7 %copy-start.2 = (bf16[512,1024]{1,0:T(8,128)(2,1)}, bf16[512,1024]{1,0:T(8,128)(2,1)S(1)}, u32[]{:S(2)}) copy-start(bf16[512,1024]{1,0:T(8,128)(2,1)S(1)} %fusion.5) | copy-start | bytes 3145732
  87.7 5.7 %collective-permute-start.2 = (bf16[7,1024]{1,0:T(8,128)(2,1)S(1)}, bf16[7,1024]{1,0:T(8,128)(2,1)S(1)}, u32[]{:S(2)}, u32[]{:S(2)}) collective-permute-start(bf16[7,1024]{1,0:T(8,128)(2,1)S(1)} %slice.16), channel_id=1, source_target_pairs={{0,1},{1,2},{2,3},{3,4},{4,5},{5,6},{6,7},{7,8},{8,9},{9,10},{10,1... | collective-permute-start | bytes 43016 | tf_op jit(solution)/shard_map/ppermute | solution.py:25
  200.2 1.6 copy-start.1
  218.7 18.8 %copy-start.3 = (bf16[512,1024]{1,0:T(8,128)(2,1)S(1)}, bf16[512,1024]{1,0:T(8,128)(2,1)}, u32[]{:S(2)}) copy-start(bf16[512,1024]{1,0:T(8,128)(2,1)} %copy-done.2) | copy-start | bytes 3145732
Sparse Core Ops, SparseCore 0:
  9.1 35.6 all-gather.3
  175.4 24.7 all-gather.5

commit v2 on v1

v2 whole, which is shorter than its diff:
```python
import functools
import math

import jax
import jax.numpy as jnp
from jax import lax
from jax.experimental import pallas as pl
from jax.experimental.pallas import tpu as pltpu
from jax.sharding import Mesh, PartitionSpec as P

HEAD_DIM = 64
HEADS = 16
SHORT = 8
WIN = 1024
SCALE = math.log2(math.e) / math.sqrt(HEAD_DIM)
ALL = ("z", "x", "y", "c")
QB = 128
PAIR = 2 * HEAD_DIM
NEG = -1e30


def from_behind(block, distance):
    devices = range(128)
    route = [(i - distance, i) for i in devices if i - distance in devices]
    return lax.ppermute(block, ALL, route)


def normed(rows):
    values = rows.astype(jnp.float32)
    scale = lax.rsqrt(jnp.mean(values * values, axis=-1, keepdims=True) + 1e-06)
    return (values * scale).astype(jnp.bfloat16)


def dot(a, b, contract):
    return lax.dot_general(a, b, (contract, ((), ())), preferred_element_type=jnp.float32)


def params():
    return pltpu.CompilerParams(vmem_limit_bytes=48 * 2**20)


def fine_kernel(place_ref, q_ref, kp_ref, ko_ref, vp_ref, vo_ref, out_ref, s_ref, p_ref):
    count = q_ref.shape[0]
    span = WIN + QB
    blocks = count // QB
    groups = QB // SHORT
    lane = lax.broadcasted_iota(jnp.int32, (QB, PAIR), 1)
    row = lax.broadcasted_iota(jnp.int32, (QB, 2 * QB), 0)
    col = lax.broadcasted_iota(jnp.int32, (QB, 2 * QB), 1) % QB
    last = row <= (col % groups) * SHORT + col // groups
    ones = jnp.ones((16, span), jnp.bfloat16)

    def scores(b, masked):
        q = q_ref[b * QB : (b + 1) * QB, :]
        zero = jnp.zeros_like(q)
        both = jnp.concatenate(
            [jnp.where(lane < HEAD_DIM, q, zero), jnp.where(lane < HEAD_DIM, zero, q)], axis=0
        )
        split = WIN - b * QB
        s = dot(kp_ref[b * QB :, :], both, ((1,), (1,)))
        if masked:
            key = lax.broadcasted_iota(jnp.int32, s.shape, 0) + b * QB
            s = jnp.where(key >= WIN - place_ref[0] * count, s, NEG)
        s_ref[b, :split, :] = s
        s_ref[b, split:, :] = dot(ko_ref[: (b + 1) * QB, :], both, ((1,), (1,)))

    def weights(b):
        edge = jnp.where(last, s_ref[b, WIN:span, :], s_ref[b, 0:QB, :])
        top = jnp.maximum(
            jnp.max(edge, axis=0, keepdims=True),
            jnp.max(s_ref[b, QB:WIN, :], axis=0, keepdims=True),
        )
        edge = jnp.exp2(edge - top).astype(jnp.bfloat16)
        zero = jnp.zeros_like(edge)
        p_ref[b, 0:QB, :] = jnp.where(last, zero, edge)
        p_ref[b, WIN:span, :] = jnp.where(last, edge, zero)
        p_ref[b, QB:WIN, :] = jnp.exp2(s_ref[b, QB:WIN, :] - top).astype(jnp.bfloat16)

    def mix(b):
        v = jnp.concatenate([vp_ref[:, b * QB :], vo_ref[:, : (b + 1) * QB]], axis=1)
        v = jnp.concatenate([v, ones], axis=0)
        o = dot(v, p_ref[b], ((1,), (0,)))
        o = o[:PAIR] * (1.0 / o[PAIR : PAIR + 1])
        mixed = jnp.concatenate([o[:HEAD_DIM, :QB], o[HEAD_DIM:PAIR, QB:]], axis=0)
        out_ref[b * QB : (b + 1) * QB, :] = mixed.T.astype(jnp.bfloat16)

    def units(masked):
        for b in range(blocks):
            scores(b, masked)
        for b in range(blocks):
            weights(b)
        for b in range(blocks):
            mix(b)

    @pl.when(place_ref[0] * count >= WIN)
    def _():
        units(False)

    @pl.when(place_ref[0] * count < WIN)
    def _():
        units(True)


def fine_attend(place, q, keys, values):
    count, width = q.shape
    blocks = count // QB
    return pl.pallas_call(
        fine_kernel,
        name="fine_attend",
        grid=(width // PAIR,),
        in_specs=[
            pl.BlockSpec(memory_space=pltpu.SMEM),
            pl.BlockSpec((count, PAIR), lambda i: (0, i)),
            pl.BlockSpec((WIN, PAIR), lambda i: (0, i)),
            pl.BlockSpec((count, PAIR), lambda i: (0, i)),
            pl.BlockSpec((PAIR, WIN), lambda i: (i, 0)),
            pl.BlockSpec((PAIR, count), lambda i: (i, 0)),
        ],
        out_specs=pl.BlockSpec((count, PAIR), lambda i: (0, i)),
        out_shape=jax.ShapeDtypeStruct((count, width), jnp.bfloat16),
        scratch_shapes=[
            pltpu.VMEM((blocks, WIN + QB, 2 * QB), jnp.float32),
            pltpu.VMEM((blocks, WIN + QB, 2 * QB), jnp.bfloat16),
        ],
        compiler_params=params(),
        cost_estimate=pl.CostEstimate(flops=10 * 2**30, bytes_accessed=8 * 2**20, transcendentals=8 * 2**20),
    )(place.reshape(1), q, *keys, *values)


def pack_kernel(hidden_ref, tail_ref, out_ref):
    blocks, places, groups, width = hidden_ref.shape
    rows = blocks * groups
    half = width // 2
    for j in range(SHORT):
        p = (j + 1) % SHORT
        part = hidden_ref[:, p].reshape(rows, width)
        if p > 0:
            wide = part.astype(jnp.float32)
            tail = tail_ref[p : p + 1, :].astype(jnp.float32)
            first = lax.broadcasted_iota(jnp.int32, wide.shape, 0) == 0
            wide = jnp.where(first, tail, pltpu.roll(wide, 1, 0))
            part = wide.astype(jnp.bfloat16)
        for f in range(2):
            out_ref[(j % 2) * 2 + f, j // 2] = part[:, f * half : (f + 1) * half]


def pack(hidden, tail):
    count, width = hidden.shape
    groups = QB // SHORT
    blocks = count // QB
    return pl.pallas_call(
        pack_kernel,
        name="pack",
        out_shape=jax.ShapeDtypeStruct((4, 4, count // SHORT, width // 2), jnp.bfloat16),
        compiler_params=params(),
    )(hidden.reshape(blocks, SHORT, groups, width), tail)


def shorten_kernel(grouped_ref, weight_ref, out_ref):
    owners, parts, rows, depth = grouped_ref.shape
    total = None
    for j in range(parts):
        part = grouped_ref[:, j].reshape(owners * rows, depth)
        term = dot(part, weight_ref[j], ((1,), (0,)))
        total = term if total is None else total + term
    out_ref[...] = total.reshape(owners, rows, -1).astype(jnp.bfloat16)


def shorten(grouped, weight):
    owners, parts, rows, depth = grouped.shape
    width = weight.shape[1]
    tile = width // 4
    return pl.pallas_call(
        shorten_kernel,
        name="shorten",
        grid=(4,),
        in_specs=[
            pl.BlockSpec(grouped.shape, lambda i: (0, 0, 0, 0)),
            pl.BlockSpec((parts, depth, tile), lambda i: (0, 0, i)),
        ],
        out_specs=pl.BlockSpec((owners, rows, tile), lambda i: (0, 0, i)),
        out_shape=jax.ShapeDtypeStruct((owners, rows, width), jnp.bfloat16),
        compiler_params=params(),
    )(grouped, weight.reshape(parts, depth, width))


def coarse_project_kernel(part_ref, q_ref, k_ref, v_ref, short_ref, qkv_ref, norm_ref):
    @pl.when(pl.program_id(0) == 0)
    def _():
        short = jnp.sum(part_ref[...].astype(jnp.float32), axis=0).astype(jnp.bfloat16)
        short_ref[...] = short
        norm_ref[...] = normed(short)

    rows = norm_ref[...]
    for i, (ref, scale) in enumerate(((q_ref, SCALE), (k_ref, None), (v_ref, None))):
        out = dot(rows, ref[...], ((1,), (0,)))
        if scale is not None:
            out = out * scale
        out = out.astype(jnp.bfloat16)
        for h in range(qkv_ref.shape[0]):
            qkv_ref[h, :, i * HEAD_DIM : (i + 1) * HEAD_DIM] = out[:, h * HEAD_DIM : (h + 1) * HEAD_DIM]


def coarse_project(partial, query, key, value):
    owners, rows, width = partial.shape
    tile = 4 * HEAD_DIM
    spec = pl.BlockSpec((width, tile), lambda i: (0, i))
    return pl.pallas_call(
        coarse_project_kernel,
        name="coarse_project",
        grid=(width // tile,),
        in_specs=[pl.BlockSpec(partial.shape, lambda i: (0, 0, 0)), spec, spec, spec],
        out_specs=[
            pl.BlockSpec((rows, width), lambda i: (0, 0)),
            pl.BlockSpec((4, rows, 3 * HEAD_DIM), lambda i: (i, 0, 0)),
        ],
        out_shape=[
            jax.ShapeDtypeStruct((rows, width), jnp.bfloat16),
            jax.ShapeDtypeStruct((HEADS, rows, 3 * HEAD_DIM), jnp.bfloat16),
        ],
        scratch_shapes=[pltpu.VMEM((rows, width), jnp.bfloat16)],
        compiler_params=params(),
    )(partial, query, key, value)


def finish_kernel(mixed_ref, out_weight_ref, short_ref, hidden_ref, out_ref):
    heads, rows, _ = mixed_ref.shape
    mixed = jnp.concatenate([mixed_ref[h] for h in range(heads)], axis=1)
    refined = short_ref[...].astype(jnp.float32) + dot(mixed, out_weight_ref[...], ((1,), (0,)))
    tile = refined.shape[1]
    spread = jnp.broadcast_to(refined[:, None, :], (rows, SHORT, tile)).reshape(rows * SHORT, tile)
    out_ref[...] = (hidden_ref[...].astype(jnp.float32) + spread).astype(jnp.bfloat16)


def finish(mixed, out_weight, short, hidden):
    count, width = hidden.shape
    heads, rows, _ = mixed.shape
    tile = width // 4
    return pl.pallas_call(
        finish_kernel,
        name="finish",
        grid=(4,),
        in_specs=[
            pl.BlockSpec(mixed.shape, lambda i: (0, 0, 0)),
            pl.BlockSpec((width, tile), lambda i: (0, i)),
            pl.BlockSpec((rows, tile), lambda i: (0, i)),
            pl.BlockSpec((count, tile), lambda i: (0, i)),
        ],
        out_specs=pl.BlockSpec((count, tile), lambda i: (0, i)),
        out_shape=jax.ShapeDtypeStruct((count, width), jnp.bfloat16),
        compiler_params=params(),
    )(mixed, out_weight, short, hidden)


def coarse_kernel(group_ref, q_ref, kv_ref, out_ref):
    parts, blocks, rows, _ = kv_ref.shape
    keys = parts * rows
    tile = 4 * rows
    tiles = q_ref.shape[0] // tile
    lane = lax.broadcasted_iota(jnp.int32, (1, tile), 1)
    row = lax.broadcasted_iota(jnp.int32, (keys, tile), 0)
    limit = (lane // rows) * keys + group_ref[0] * rows + lane % rows
    ones = jnp.ones((16, keys), jnp.bfloat16)
    queries = []
    for t in range(tiles):
        q = q_ref[t * tile : (t + 1) * tile, :]
        queries.append(jnp.concatenate([q, jnp.zeros_like(q)], axis=1))
    tops = [jnp.full((1, tile), NEG, jnp.float32)] * tiles
    accs = [jnp.zeros((16 + rows, tile), jnp.float32)] * tiles
    for g in range(blocks):
        kv = kv_ref[:, g].reshape(keys, 2 * HEAD_DIM)
        v = jnp.concatenate([ones, kv.T[HEAD_DIM:, :]], axis=0)
        live = range(g // 4, tiles)
        scores = [dot(kv, queries[t], ((1,), (1,))) for t in live]
        scores[0] = jnp.where(row <= limit - (g % 4) * keys, scores[0], NEG)
        news = [jnp.maximum(tops[t], jnp.max(s, axis=0, keepdims=True)) for t, s in zip(live, scores)]
        ps = [jnp.exp2(s - top).astype(jnp.bfloat16) for s, top in zip(scores, news)]
        for t, top, p in zip(live, news, ps):
            accs[t] = accs[t] * jnp.exp2(tops[t] - top) + dot(v, p, ((1,), (0,)))
            tops[t] = top
    for t in range(tiles):
        o = accs[t][16:] * (1.0 / accs[t][0:1])
        out_ref[t * tile : (t + 1) * tile, :] = o.T.astype(jnp.bfloat16)


def coarse_attend(group, q, kv):
    return pl.pallas_call(
        coarse_kernel,
        in_specs=[
            pl.BlockSpec(memory_space=pltpu.SMEM),
            pl.BlockSpec(memory_space=pltpu.VMEM),
            pl.BlockSpec(memory_space=pltpu.VMEM),
        ],
        out_specs=pl.BlockSpec(memory_space=pltpu.VMEM),
        out_shape=jax.ShapeDtypeStruct(q.shape, jnp.bfloat16),
        name="coarse_attend",
        compiler_params=params(),
        cost_estimate=pl.CostEstimate(flops=4 * 2**30, bytes_accessed=3 * 2**20, transcendentals=5 * 2**20),
    )(group.reshape(1), q, kv)


def body(
    tokens,
    fine_query,
    fine_key,
    fine_value,
    fine_out,
    short_weight,
    coarse_query,
    coarse_key,
    coarse_value,
    coarse_out,
):
    count, width = tokens.shape
    bf = jnp.bfloat16
    place = lax.axis_index(ALL).astype(jnp.int32)
    groups = QB // SHORT
    blocks = count // QB
    first_core = lax.axis_index("c") == 0
    far = from_behind(tokens, 2)
    mate = lax.ppermute(tokens, "c", [(0, 1)])
    weight = lax.all_gather(short_weight, ("x", "c"), axis=0, tiled=True)

    shuffled = tokens.reshape(blocks, groups, SHORT, width)
    shuffled = jnp.transpose(shuffled, (0, 2, 1, 3)).reshape(count, width)
    query = (dot(normed(shuffled), fine_query, ((1,), (0,))) * SCALE).astype(bf)
    own = normed(tokens)
    own_keys = dot(own, fine_key, ((1,), (0,))).astype(bf)
    own_values = dot(fine_value, own, ((0,), (1,))).astype(bf)
    far, own_keys, own_values, query = lax.optimization_barrier((far, own_keys, own_values, query))
    near = jnp.where(first_core, lax.ppermute(far, "c", [(1, 0)]), mate)
    before = normed(jnp.concatenate([far, near], axis=0))
    keys = dot(before, fine_key, ((1,), (0,))).astype(bf)
    values = dot(fine_value, before, ((0,), (1,))).astype(bf)
    fine_mixed = fine_attend(place, query, (keys, own_keys), (values, own_values))
    hidden = (shuffled.astype(jnp.float32) + dot(fine_mixed, fine_out, ((1,), (0,)))).astype(bf)
    tail = from_behind(hidden.reshape(blocks, SHORT, groups, width)[-1, :, -1], 1)
    rows = count // SHORT
    grouped = lax.all_to_all(pack(hidden, tail), "y", 0, 0)
    partial = lax.all_to_all(shorten(grouped, weight), "y", 0, 0)
    shortened, qkv = coarse_project(partial, coarse_query, coarse_key, coarse_value)
    natural = jnp.transpose(hidden.reshape(blocks, SHORT, groups, width), (0, 2, 1, 3)).reshape(count, width)
    qkv = lax.all_to_all(qkv, ("z", "x"), 0, 0)
    q = qkv[:, :, :HEAD_DIM].reshape(HEADS * rows, HEAD_DIM)
    kv = lax.all_gather(qkv[:, :, HEAD_DIM:], ("y", "c"), axis=0)
    mixed = coarse_attend(lax.axis_index(("y", "c")).astype(jnp.int32), q, kv)
    mixed = lax.all_to_all(mixed.reshape(HEADS, rows, HEAD_DIM), ("z", "x"), 0, 0)
    return finish(mixed, coarse_out, shortened, natural)


def solution(mesh):
    fine = Mesh(mesh.devices.reshape(4, 4, 4, 2), ALL)
    return jax.shard_map(
        body,
        mesh=fine,
        in_specs=(P(ALL, None), P(), P(), P(), P(), P(("x", "y", "c"), None), P(), P(), P(), P()),
        out_specs=P(ALL, None),
        check_vma=False,
    )
```

time: 247 us -> 215 us (0.87)
  blocking collectives: 78.4 us -> 62.8 us
  waiting for transfers between devices: 52 us -> 39.8 us
  Pallas kernels: 45.5 us -> 35 us
  starting transfers between devices: 12.9 us -> 22.6 us
  matrix products: 26.2 us -> 17.7 us
  local copies, waits for them, and re-layouts: 11.4 us -> 17.8 us
    ppermute x3 -> x2, waiting for transfers between devices: 26.4 us -> 10 us  [from_behind(): return lax.ppermute(block, ALL, route)]
    all_to_all x4 -> x3, blocking collectives: 78.4 us -> 62.8 us  [the longest x1 32.2 us: body(): grouped = lax.all_to_all(pack(hidden, tail), 'y', 0, 0)]
    unnamed x16 -> x43, local copies, waits for them, and re-layouts: 2.98 us -> 12.9 us
    dot_general x9 -> x6, matrix products: 26.2 us -> 17.7 us  [dot(): lax.dot_general(a, b, (contract, ((), ())), preferred_element_type=jnp.fl...]
    pallas_call x1, Pallas kernels: 16.7 us -> 8.63 us  [coarse_attend(): pl.pallas_call(coarse_kernel, in_specs=[pl.BlockSpec(memory_space=pltpu.S...]
    all_to_all x0 -> x1, starting transfers between devices: none -> 6.66 us  [body(): lax.all_to_all(mixed.reshape(HEADS, rows, HEAD_DIM), ('z', 'x'), 0, 0)]
    reshape x10 -> x0, local copies, waits for them, and re-layouts: 6.64 us -> none  [the longest x2 3.14 us: body(): grouped = delayed.reshape(rows, 4, 4, 2 * width // 4)]
    ppermute x0 -> x2, starting transfers between devices: none -> 5.8 us  [the longest x1 4.52 us: body(): near = jnp.where(first_core, lax.ppermute(far, 'c', [(1, 0)]), mate)]
  transfers between devices with their start and end apart: 5 -> 7, of which waited for: 4 -> 5; matrix products, arithmetic and copies ran while one was open for 9% -> 12% of each run, Pallas kernels for 12% -> 8%
where the time goes in v2:
time: 215 us; the launch traced here: 214 us
  blocking collectives  62.8 us (29%)
  waiting for transfers between devices  39.8 us (19%)
  Pallas kernels  35 us (16%)
  starting transfers between devices  22.6 us (11%)
  local copies, waits for them, and re-layouts  17.8 us (8%)
  matrix products  17.7 us (8%)
  between operations  13.6 us (6%)
  other arithmetic  4.73 us (2%)
    all_to_all x1, blocking collectives, body(): grouped = lax.all_to_all(pack(hidden, tail), 'y', 0, 0)  32.2 us
    all_gather x1, waiting for transfers between devices, body(): kv = lax.all_gather(qkv[:, :, HEAD_DIM:], ('y', 'c'), axis=0)  22.2 us
    all_to_all x1, blocking collectives, body(): qkv = lax.all_to_all(qkv, ('z', 'x'), 0, 0)  18.2 us
    dot_general x6, matrix products, dot(): lax.dot_general(a, b, (contract, ((), ())), preferred_element_type=jnp.fl...  17.7 us
    pallas_call x1, Pallas kernels, fine_attend(): pl.pallas_call(fine_kernel, name='fine_attend', grid=(width // PAIR,), in...  16.9 us
    unnamed x43, local copies, waits for them, and re-layouts  12.9 us
    all_to_all x1, blocking collectives, body(): partial = lax.all_to_all(shorten(grouped, weight), 'y', 0, 0)  12.4 us
    ppermute x2, starting transfers between devices, from_behind(): return lax.ppermute(block, ALL, route)  10.1 us
  transfers between devices with their start and end apart: 7, of which 5 were waited for; matrix products, arithmetic and copies ran while one was open for 12% of the time, Pallas kernels for 8%

profile of v2, /device:TPU:1, one launch (start us, length us, event | category | flops | bytes accessed | tf_op | source)
XLA Modules:
  0.0 214.2 jit_solution(14889430869000164440)
XLA Ops:
  7.3 5.1 %collective-permute-start = (bf16[512,1024]{1,0:T(8,128)(2,1)}, bf16[512,1024]{1,0:T(8,128)(2,1)}, u32[]{:S(2)}, u32[]{:S(2)}) collective-permute-start(bf16[512,1024]{1,0:T(8,128)(2,1)} %param.10), channel_id=1, source_target_pairs={{0,2},{1,3},{2,4},{3,5},{4,6},{5,7},{6,8},{7,9},{8,10},{9,11},{10,... | collective-permute-start | bytes 3145736 | tf_op jit(solution)/shard_map/ppermute | solution.py:25
  16.3 2.2 %copy-done.16 = bf16[1024,1024]{1,0:T(8,128)(2,1)S(1)} copy-done((bf16[1024,1024]{1,0:T(8,128)(2,1)S(1)}, bf16[1024,1024]{1,0:T(8,128)(2,1)}, u32[]{:S(2)}) %copy-start.16) | copy-done | bytes 2097176
  18.5 2.2 %multiply_convert_fusion.q_ref = bf16[512,1024]{1,0:T(8,128)(2,1)} fusion(bf16[512,1024]{1,0:T(8,128)(2,1)S(1)} %fusion.2, bf16[1024,1024]{1,0:T(8,128)(2,1)S(1)} %copy-done.16), kind=kOutput, calls=%fused_computation.10 | convolution fusion | flops 1074790400 | bytes 4194304 | tf_op jit(solution)/shard_map/dot_general | solution.py:35
  20.7 2.3 %convolution_convert_fusion.2.ko_ref = bf16[512,1024]{1,0:T(8,128)(2,1)} fusion(bf16[1024,1024]{1,0:T(8,128)(2,1)S(1)} %copy-done.17, bf16[512,1024]{1,0:T(8,128)(2,1)S(1)} %copy-done.13, f32[512]{0:T(512)S(1)} %add_rsqrt_fusion.1), kind=kOutput, calls=%fused_computation.15 | convolution fusion | flops 1075838976 | bytes 4196352 | tf_op jit(solution)/shard_map/dot_general | solution.py:35
  24.4 9.2 %collective-permute-done = bf16[512,1024]{1,0:T(8,128)(2,1)} collective-permute-done((bf16[512,1024]{1,0:T(8,128)(2,1)}, bf16[512,1024]{1,0:T(8,128)(2,1)}, u32[]{:S(2)}, u32[]{:S(2)}) %collective-permute-start) | collective-permute-done | bytes 1048608 | tf_op jit(solution)/shard_map/ppermute | solution.py:25
  33.6 4.5 %collective-permute-start.1 = (bf16[512,1024]{1,0:T(8,128)(2,1)}, bf16[512,1024]{1,0:T(8,128)(2,1)}, u32[]{:S(2)}, u32[]{:S(2)}) collective-permute-start(bf16[512,1024]{1,0:T(8,128)(2,1)} %collective-permute-done), channel_id=1, source_target_pairs={{1,0},{3,2},{5,4},{7,6},{9,8},{11,10},{13,12},{15,14},{17,16},{19,... | collective-permute-start | bytes 3145736 | tf_op jit(solution)/shard_map/ppermute | solution.py:331
  41.0 1.7 fusion
  42.7 5.4 %convert_bitcast_fusion.vp_ref = bf16[1024,1024]{1,0:T(8,128)(2,1)} fusion(bf16[1024,1024]{1,0:T(8,128)(2,1)S(1)} %copy-done, f32[1024]{0:T(1024)S(1)} %add_rsqrt_fusion, bf16[512,1024]{1,0:T(8,128)(2,1)S(1)} %broadcast_select_fusion, bf16[512,1024]{1,0:T(8,128)(2,1)} %collective-permute-done), kind=kOutput, calls=%fused_computation.9 | convolution fusion | flops 2154823680 | bytes 6295552 | tf_op jit(solution)/shard_map/dot_general | solution.py:35
  48.1 5.2 %convolution_convert_fusion.kp_ref = bf16[1024,1024]{1,0:T(8,128)(2,1)} fusion(bf16[1024,1024]{1,0:T(8,128)(2,1)S(1)} %copy-done.18, f32[1024]{0:T(1024)S(1)} %add_rsqrt_fusion, bf16[512,1024]{1,0:T(8,128)(2,1)S(1)} %broadcast_select_fusion, bf16[512,1024]{1,0:T(8,128)(2,1)} %collective-permute-done), kind=kOutput, calls=%fused_computation.13 | convolution fusion | flops 2154823680 | bytes 6295552 | tf_op jit(solution)/shard_map/dot_general | solution.py:35
  53.3 16.9 %fine_attend.1 = bf16[512,1024]{1,0:T(8,128)(2,1)S(1)} custom-call(s32[1]{0:T(128)} %bitcast.4.place_ref, bf16[512,1024]{1,0:T(8,128)(2,1)S(1)} %copy-done.9, bf16[1024,1024]{1,0:T(8,128)(2,1)} %convolution_convert_fusion.kp_ref, bf16[512,1024]{1,0:T(8,128)(2,1)S(1)} %copy-done.10, bf16[1024,1024]{1,0:T(8,128)(2,1)} %convert_bitcast_fusion.vp_ref, ...), custom_call_target="tpu_custom_call" | custom-call | flops 10737418240 | bytes 8388608 | tf_op jit(solution)/shard_map/fine_attend/pallas_call | solution.py:107
  71.6 5.0 %collective-permute-start.3 = (bf16[8,1024]{1,0:T(8,128)(2,1)S(1)}, bf16[8,1024]{1,0:T(8,128)(2,1)S(1)}, u32[]{:S(2)}, u32[]{:S(2)}) collective-permute-start(bf16[8,1024]{1,0:T(8,128)(2,1)S(1)} %bitcast.47), channel_id=1, source_target_pairs={{0,1},{1,2},{2,3},{3,4},{4,5},{5,6},{6,7},{7,8},{8,9},{9,10},{10,1... | collective-permute-start | bytes 49160 | tf_op jit(solution)/shard_map/ppermute | solution.py:25
  77.6 32.2 %all_to_all.20.grouped_ref = bf16[4,4,64,512]{3,2,1,0:T(8,128)(2,1)} all-to-all(bf16[4,4,64,512]{3,2,1,0:T(8,128)(2,1)S(1)} %pack.1), channel_id=1, replica_groups=mesh['z'=4,'x'=4,'y'=4,'c'=2] {'y'}, dimensions={0} | all-to-all | bytes 2097152 | tf_op jit(solution)/shard_map/all_to_all | solution.py:339
  109.9 2.2 %copy-done.1 = bf16[2048,1024]{1,0:T(8,128)(2,1)S(1)} copy-done((bf16[2048,1024]{1,0:T(8,128)(2,1)S(1)}, bf16[2048,1024]{1,0:T(8,128)(2,1)}, u32[]{:S(2)}) %copy-start.1) | copy-done | bytes 4194328
  113.3 2.4 %shorten.1 = bf16[4,64,1024]{2,1,0:T(8,128)(2,1)S(1)} custom-call(bf16[4,4,64,512]{3,2,1,0:T(8,128)(2,1)S(1)} %copy-done.3, bf16[4,512,1024]{2,1,0:T(8,128)(2,1)S(1)} %bitcast.40), custom_call_target="tpu_custom_call" | custom-call | tf_op jit(solution)/shard_map/shorten/pallas_call | solution.py:173
  115.7 12.4 %all_to_all.21.part_ref = bf16[4,64,1024]{2,1,0:T(8,128)(2,1)S(1)} all-to-all(bf16[4,64,1024]{2,1,0:T(8,128)(2,1)S(1)} %shorten.1), channel_id=1, replica_groups=mesh['z'=4,'x'=4,'y'=4,'c'=2] {'y'}, dimensions={0} | all-to-all | bytes 1048576 | tf_op jit(solution)/shard_map/all_to_all | solution.py:340
  128.1 4.2 %coarse_project.1 = (bf16[64,1024]{1,0:T(8,128)(2,1)S(1)}, bf16[16,64,192]{2,1,0:T(8,128)(2,1)S(1)}) custom-call(bf16[4,64,1024]{2,1,0:T(8,128)(2,1)S(1)} %all_to_all.21.part_ref, bf16[1024,1024]{1,0:T(8,128)(2,1)S(1)} %copy-done.4, bf16[1024,1024]{1,0:T(8,128)(2,1)S(1)} %copy-done.5, bf16[1024,1024]{1,0:T(8,128)(2,1)} %v_ref.1), custom_call_target="tpu_custom_call" | custom-call | tf_op jit(solution)/shard_map/coarse_project/pallas_call | solution.py:208
  132.3 18.2 %all_to_all.22 = bf16[16,64,192]{2,1,0:T(8,128)(2,1)S(1)} all-to-all(bf16[16,64,192]{2,1,0:T(8,128)(2,1)S(1)} %get-tuple-element.15), channel_id=1, replica_groups=mesh['z'=4,'x'=4,'y'=4,'c'=2] {'z','x'}, dimensions={0} | all-to-all | bytes 786432 | tf_op jit(solution)/shard_map/all_to_all | solution.py:343
  152.2 1.7 slice.13
  153.8 22.2 %all-gather.6.cloned.1.call-done = bf16[128,64,128]{2,1,0:T(8,128)(2,1)} async-done(((bf16[16,64,128]{2,1,0:T(8,128)(2,1)}), bf16[128,64,128]{2,1,0:T(8,128)(2,1)}) %all-gather.6.cloned.1.call-update) | async-done | bytes 2097168 | tf_op jit(solution)/shard_map/all_gather | solution.py:345
  177.0 1.6 copy-done.8
  178.6 8.6 %coarse_attend.1 = bf16[1024,64]{1,0:T(8,128)(2,1)S(1)} custom-call(s32[1]{0:T(128)} %bitcast.group_ref, bf16[1024,64]{1,0:T(8,128)(2,1)S(1)} %bitcast.43, bf16[8,16,64,128]{3,2,1,0:T(8,128)(2,1)S(1)} %bitcast.44), custom_call_target="tpu_custom_call" | custom-call | flops 4294967296 | bytes 3145728 | tf_op jit(solution)/shard_map/coarse_attend/pallas_call | solution.py:287
  188.1 6.7 %all-to-all-start.3 = ((bf16[16,2,2048]{2,1,0:T(2,128)(2,1)}), bf16[16,2,2048]{2,1,0:T(2,128)(2,1)S(1)}, u32[]{:S(2)}, u32[]{:S(2)}) async-start(bf16[16,2,2048]{2,1,0:T(2,128)(2,1)} %reshape.80), calls=%async_computation.3 | async-start | bytes 262144 | tf_op jit(solution)/shard_map/all_to_all | solution.py:347
  196.4 5.3 %all-to-all-done.3 = bf16[16,2,2048]{2,1,0:T(2,128)(2,1)S(1)} async-done(((bf16[16,2,2048]{2,1,0:T(2,128)(2,1)}), bf16[16,2,2048]{2,1,0:T(2,128)(2,1)S(1)}, u32[]{:S(2)}, u32[]{:S(2)}) %all-to-all-start.3) | async-done | bytes 131104 | tf_op jit(solution)/shard_map/all_to_all | solution.py:347
  204.7 2.7 %finish.1 = bf16[512,1024]{1,0:T(8,128)(2,1)} custom-call(bf16[16,64,64]{2,1,0:T(8,128)(2,1)S(1)} %reshape.81.mixed_ref, bf16[1024,1024]{1,0:T(8,128)(2,1)S(1)} %copy-done.6, bf16[64,1024]{1,0:T(8,128)(2,1)S(1)} %get-tuple-element.16.short_ref, bf16[512,1024]{1,0:T(8,128)(2,1)S(1)} %bitcast.41), custom_call_target="tpu_custom_call" | custom-call | tf_op jit(solution)/shard_map/finish/pallas_call | solution.py:239
  (64 shorter events, 20.6 us)
Async XLA Ops:
  6.5 16.5 %copy-start = (bf16[1024,1024]{1,0:T(8,128)(2,1)S(1)}, bf16[1024,1024]{1,0:T(8,128)(2,1)}, u32[]{:S(2)}) copy-start(bf16[1024,1024]{1,0:T(8,128)(2,1)} %param.13) | copy-start | bytes 6291460
  6.5 9.0 %copy-start.13 = (bf16[512,1024]{1,0:T(8,128)(2,1)S(1)}, bf16[512,1024]{1,0:T(8,128)(2,1)}, u32[]{:S(2)}) copy-start(bf16[512,1024]{1,0:T(8,128)(2,1)} %param.10) | copy-start | bytes 3145732
  6.5 103.3 %all-gather.4.cloned.1.call-start = ((), (), s32[]{:S(2)}) async-start(), calls=%async_computation.4 | async-start | bytes 4718592 | tf_op jit(solution)/shard_map/all_gather | solution.py:322
  7.3 168.8 %all-gather.6.cloned.1.call-start = ((), (), s32[]{:S(2)}) async-start(), calls=%async_computation.5 | async-start | bytes 2359296 | tf_op jit(solution)/shard_map/all_gather | solution.py:345
  7.3 26.3 %collective-permute-start = (bf16[512,1024]{1,0:T(8,128)(2,1)}, bf16[512,1024]{1,0:T(8,128)(2,1)}, u32[]{:S(2)}, u32[]{:S(2)}) collective-permute-start(bf16[512,1024]{1,0:T(8,128)(2,1)} %param.10), channel_id=1, source_target_pairs={{0,2},{1,3},{2,4},{3,5},{4,6},{5,7},{6,8},{7,9},{8,10},{9,11},{10,... | collective-permute-start | bytes 3145736 | tf_op jit(solution)/shard_map/ppermute | solution.py:25
  12.5 25.7 %collective-permute-start.2 = (bf16[512,1024]{1,0:T(8,128)(2,1)}, bf16[512,1024]{1,0:T(8,128)(2,1)}, u32[]{:S(2)}, u32[]{:S(2)}) collective-permute-start(bf16[512,1024]{1,0:T(8,128)(2,1)} %param.10), channel_id=1, source_target_pairs={{0,1},{2,3},{4,5},{6,7},{8,9},{10,11},{12,13},{14,15},{16,17},{18,... | collective-permute-start | bytes 3145736 | tf_op jit(solution)/shard_map/ppermute | solution.py:321
  16.1 4.6 %copy-start.11 = (f32[4,16,8,1024]{3,1,2,0:T(8,128)}, f32[4,16,8,1024]{3,1,2,0:T(8,128)S(1)}, u32[]{:S(2)}) copy-start(f32[4,16,8,1024]{3,1,2,0:T(8,128)S(1)} %copy.19) | copy-start | bytes 6291460
  16.1 2.4 %copy-start.16 = (bf16[1024,1024]{1,0:T(8,128)(2,1)S(1)}, bf16[1024,1024]{1,0:T(8,128)(2,1)}, u32[]{:S(2)}) copy-start(bf16[1024,1024]{1,0:T(8,128)(2,1)} %param.11) | copy-start | bytes 6291460
  18.5 2.2 %copy-start.17 = (bf16[1024,1024]{1,0:T(8,128)(2,1)S(1)}, bf16[1024,1024]{1,0:T(8,128)(2,1)}, u32[]{:S(2)}) copy-start(bf16[1024,1024]{1,0:T(8,128)(2,1)} %param.12) | copy-start | bytes 6291460
  20.7 2.3 %copy-start.14 = (bf16[512,1024]{1,0:T(8,128)(2,1)S(1)}, bf16[512,1024]{1,0:T(8,128)(2,1)}, u32[]{:S(2)}) copy-start(bf16[512,1024]{1,0:T(8,128)(2,1)} %param.10) | copy-start | bytes 3145732
  33.6 6.1 %collective-permute-start.1 = (bf16[512,1024]{1,0:T(8,128)(2,1)}, bf16[512,1024]{1,0:T(8,128)(2,1)}, u32[]{:S(2)}, u32[]{:S(2)}) collective-permute-start(bf16[512,1024]{1,0:T(8,128)(2,1)} %collective-permute-done), channel_id=1, source_target_pairs={{1,0},{3,2},{5,4},{7,6},{9,8},{11,10},{13,12},{15,14},{17,16},{19,... | collective-permute-start | bytes 3145736 | tf_op jit(solution)/shard_map/ppermute | solution.py:331
  42.7 5.4 %copy-start.18 = (bf16[1024,1024]{1,0:T(8,128)(2,1)S(1)}, bf16[1024,1024]{1,0:T(8,128)(2,1)}, u32[]{:S(2)}) copy-start(bf16[1024,1024]{1,0:T(8,128)(2,1)} %param.12) | copy-start | bytes 6291460
  48.1 5.2 %copy-start.9 = (bf16[512,1024]{1,0:T(8,128)(2,1)S(1)}, bf16[512,1024]{1,0:T(8,128)(2,1)}, u32[]{:S(2)}) copy-start(bf16[512,1024]{1,0:T(8,128)(2,1)} %multiply_convert_fusion.q_ref) | copy-start | bytes 3145732
  48.1 5.2 %copy-start.10 = (bf16[512,1024]{1,0:T(8,128)(2,1)S(1)}, bf16[512,1024]{1,0:T(8,128)(2,1)}, u32[]{:S(2)}) copy-start(bf16[512,1024]{1,0:T(8,128)(2,1)} %convolution_convert_fusion.2.ko_ref) | copy-start | bytes 3145732
  53.3 16.9 %copy-start.12 = (f32[4,16,8,1024]{3,1,2,0:T(8,128)S(1)}, f32[4,16,8,1024]{3,1,2,0:T(8,128)}, u32[]{:S(2)}) copy-start(f32[4,16,8,1024]{3,1,2,0:T(8,128)} %copy-done.11) | copy-start | bytes 6291460
  53.3 16.9 %copy-start.19 = (bf16[1024,1024]{1,0:T(8,128)(2,1)S(1)}, bf16[1024,1024]{1,0:T(8,128)(2,1)}, u32[]{:S(2)}) copy-start(bf16[1024,1024]{1,0:T(8,128)(2,1)} %param.14) | copy-start | bytes 6291460
  71.6 5.8 %collective-permute-start.3 = (bf16[8,1024]{1,0:T(8,128)(2,1)S(1)}, bf16[8,1024]{1,0:T(8,128)(2,1)S(1)}, u32[]{:S(2)}, u32[]{:S(2)}) collective-permute-start(bf16[8,1024]{1,0:T(8,128)(2,1)S(1)} %bitcast.47), channel_id=1, source_target_pairs={{0,1},{1,2},{2,3},{3,4},{4,5},{5,6},{6,7},{7,8},{8,9},{9,10},{10,1... | collective-permute-start | bytes 49160 | tf_op jit(solution)/shard_map/ppermute | solution.py:25
  109.9 2.2 %copy-start.1 = (bf16[2048,1024]{1,0:T(8,128)(2,1)S(1)}, bf16[2048,1024]{1,0:T(8,128)(2,1)}, u32[]{:S(2)}) copy-start(bf16[2048,1024]{1,0:T(8,128)(2,1)} %all-gather.4.cloned.1.call-done) | copy-start | bytes 12582916
  113.3 14.8 %copy-start.4 = (bf16[1024,1024]{1,0:T(8,128)(2,1)S(1)}, bf16[1024,1024]{1,0:T(8,128)(2,1)}, u32[]{:S(2)}) copy-start(bf16[1024,1024]{1,0:T(8,128)(2,1)} %q_ref.1) | copy-start | bytes 6291460
  113.3 14.8 %copy-start.5 = (bf16[1024,1024]{1,0:T(8,128)(2,1)S(1)}, bf16[1024,1024]{1,0:T(8,128)(2,1)}, u32[]{:S(2)}) copy-start(bf16[1024,1024]{1,0:T(8,128)(2,1)} %k_ref.1) | copy-start | bytes 6291460
  177.0 1.6 copy-start.8
  188.1 13.5 %all-to-all-start.3 = ((bf16[16,2,2048]{2,1,0:T(2,128)(2,1)}), bf16[16,2,2048]{2,1,0:T(2,128)(2,1)S(1)}, u32[]{:S(2)}, u32[]{:S(2)}) async-start(bf16[16,2,2048]{2,1,0:T(2,128)(2,1)} %reshape.80), calls=%async_computation.3 | async-start | bytes 262144 | tf_op jit(solution)/shard_map/all_to_all | solution.py:347
  201.9 1.2 copy-start.2
  203.1 1.6 copy-start.6
  (3 other events, 3.0 us)
Sparse Core Ops, SparseCore 0:
  9.1 35.6 all-gather.3
  152.3 23.7 all-gather.5

commit v3 on v2

--- a/solution.py
+++ b/solution.py
@@ -39,7 +39,7 @@
     return pltpu.CompilerParams(vmem_limit_bytes=48 * 2**20)
 
 
-def fine_kernel(place_ref, q_ref, kp_ref, ko_ref, vp_ref, vo_ref, out_ref, s_ref, p_ref):
+def fine_kernel(place_ref, q_ref, kf_ref, kn_ref, ko_ref, vf_ref, vn_ref, vo_ref, out_ref, s_ref, p_ref):
     count = q_ref.shape[0]
     span = WIN + QB
     blocks = count // QB
@@ -56,13 +56,13 @@
         both = jnp.concatenate(
             [jnp.where(lane < HEAD_DIM, q, zero), jnp.where(lane < HEAD_DIM, zero, q)], axis=0
         )
-        split = WIN - b * QB
-        s = dot(kp_ref[b * QB :, :], both, ((1,), (1,)))
-        if masked:
-            key = lax.broadcasted_iota(jnp.int32, s.shape, 0) + b * QB
-            s = jnp.where(key >= WIN - place_ref[0] * count, s, NEG)
-        s_ref[b, :split, :] = s
-        s_ref[b, split:, :] = dot(ko_ref[: (b + 1) * QB, :], both, ((1,), (1,)))
+        start = 0
+        for i, part in enumerate((kf_ref[b * QB :, :], kn_ref[...], ko_ref[: (b + 1) * QB, :])):
+            s = dot(part, both, ((1,), (1,)))
+            if masked and i < 2:
+                s = jnp.where(place_ref[0] + i >= 2, s, NEG)
+            s_ref[b, start : start + part.shape[0], :] = s
+            start += part.shape[0]
 
     def weights(b):
         edge = jnp.where(last, s_ref[b, WIN:span, :], s_ref[b, 0:QB, :])
@@ -77,7 +77,7 @@
         p_ref[b, QB:WIN, :] = jnp.exp2(s_ref[b, QB:WIN, :] - top).astype(jnp.bfloat16)
 
     def mix(b):
-        v = jnp.concatenate([vp_ref[:, b * QB :], vo_ref[:, : (b + 1) * QB]], axis=1)
+        v = jnp.concatenate([vf_ref[:, b * QB :], vn_ref[...], vo_ref[:, : (b + 1) * QB]], axis=1)
         v = jnp.concatenate([v, ones], axis=0)
         o = dot(v, p_ref[b], ((1,), (0,)))
         o = o[:PAIR] * (1.0 / o[PAIR : PAIR + 1])
@@ -111,11 +111,9 @@
         in_specs=[
             pl.BlockSpec(memory_space=pltpu.SMEM),
             pl.BlockSpec((count, PAIR), lambda i: (0, i)),
-            pl.BlockSpec((WIN, PAIR), lambda i: (0, i)),
-            pl.BlockSpec((count, PAIR), lambda i: (0, i)),
-            pl.BlockSpec((PAIR, WIN), lambda i: (i, 0)),
-            pl.BlockSpec((PAIR, count), lambda i: (i, 0)),
-        ],
+        ]
+        + [pl.BlockSpec((count, PAIR), lambda i: (0, i))] * 3
+        + [pl.BlockSpec((PAIR, count), lambda i: (i, 0))] * 3,
         out_specs=pl.BlockSpec((count, PAIR), lambda i: (0, i)),
         out_shape=jax.ShapeDtypeStruct((count, width), jnp.bfloat16),
         scratch_shapes=[
@@ -192,7 +190,7 @@
         norm_ref[...] = normed(short)
 
     rows = norm_ref[...]
-    for i, (ref, scale) in enumerate(((q_ref, SCALE), (k_ref, None), (v_ref, None))):
+    for i, (ref, scale) in enumerate(((k_ref, None), (v_ref, None), (q_ref, SCALE))):
         out = dot(rows, ref[...], ((1,), (0,)))
         if scale is not None:
             out = out * scale
@@ -256,14 +254,14 @@
     parts, blocks, rows, _ = kv_ref.shape
     keys = parts * rows
     tile = 4 * rows
-    tiles = q_ref.shape[0] // tile
+    tiles = blocks // 4
     lane = lax.broadcasted_iota(jnp.int32, (1, tile), 1)
     row = lax.broadcasted_iota(jnp.int32, (keys, tile), 0)
     limit = (lane // rows) * keys + group_ref[0] * rows + lane % rows
     ones = jnp.ones((16, keys), jnp.bfloat16)
     queries = []
     for t in range(tiles):
-        q = q_ref[t * tile : (t + 1) * tile, :]
+        q = q_ref[4 * t : 4 * t + 4, :, 2 * HEAD_DIM :].reshape(tile, HEAD_DIM)
         queries.append(jnp.concatenate([q, jnp.zeros_like(q)], axis=1))
     tops = [jnp.full((1, tile), NEG, jnp.float32)] * tiles
     accs = [jnp.zeros((16 + rows, tile), jnp.float32)] * tiles
@@ -280,7 +278,7 @@
             tops[t] = top
     for t in range(tiles):
         o = accs[t][16:] * (1.0 / accs[t][0:1])
-        out_ref[t * tile : (t + 1) * tile, :] = o.T.astype(jnp.bfloat16)
+        out_ref[4 * t : 4 * t + 4] = o.T.astype(jnp.bfloat16).reshape(4, rows, HEAD_DIM)
 
 
 def coarse_attend(group, q, kv):
@@ -292,7 +290,7 @@
             pl.BlockSpec(memory_space=pltpu.VMEM),
         ],
         out_specs=pl.BlockSpec(memory_space=pltpu.VMEM),
-        out_shape=jax.ShapeDtypeStruct(q.shape, jnp.bfloat16),
+        out_shape=jax.ShapeDtypeStruct((*q.shape[:2], HEAD_DIM), jnp.bfloat16),
         name="coarse_attend",
         compiler_params=params(),
         cost_estimate=pl.CostEstimate(flops=4 * 2**30, bytes_accessed=3 * 2**20, transcendentals=5 * 2**20),
@@ -319,20 +317,21 @@
     first_core = lax.axis_index("c") == 0
     far = from_behind(tokens, 2)
     mate = lax.ppermute(tokens, "c", [(0, 1)])
-    weight = lax.all_gather(short_weight, ("x", "c"), axis=0, tiled=True)
-
     shuffled = tokens.reshape(blocks, groups, SHORT, width)
     shuffled = jnp.transpose(shuffled, (0, 2, 1, 3)).reshape(count, width)
     query = (dot(normed(shuffled), fine_query, ((1,), (0,))) * SCALE).astype(bf)
-    own = normed(tokens)
-    own_keys = dot(own, fine_key, ((1,), (0,))).astype(bf)
-    own_values = dot(fine_value, own, ((0,), (1,))).astype(bf)
-    far, own_keys, own_values, query = lax.optimization_barrier((far, own_keys, own_values, query))
+
+    def keys_values(rows):
+        rows = normed(rows)
+        keys = dot(rows, fine_key, ((1,), (0,))).astype(bf)
+        return keys, dot(fine_value, rows, ((0,), (1,))).astype(bf)
+
+    own = keys_values(tokens)
+    far, own, query, short_weight = lax.optimization_barrier((far, own, query, short_weight))
     near = jnp.where(first_core, lax.ppermute(far, "c", [(1, 0)]), mate)
-    before = normed(jnp.concatenate([far, near], axis=0))
-    keys = dot(before, fine_key, ((1,), (0,))).astype(bf)
-    values = dot(fine_value, before, ((0,), (1,))).astype(bf)
-    fine_mixed = fine_attend(place, query, (keys, own_keys), (values, own_values))
+    weight = lax.all_gather(short_weight, ("x", "c"), axis=0, tiled=True)
+    kinds = zip(keys_values(far), keys_values(near), own)
+    fine_mixed = fine_attend(place, query, *kinds)
     hidden = (shuffled.astype(jnp.float32) + dot(fine_mixed, fine_out, ((1,), (0,)))).astype(bf)
     tail = from_behind(hidden.reshape(blocks, SHORT, groups, width)[-1, :, -1], 1)
     rows = count // SHORT
@@ -341,10 +340,9 @@
     shortened, qkv = coarse_project(partial, coarse_query, coarse_key, coarse_value)
     natural = jnp.transpose(hidden.reshape(blocks, SHORT, groups, width), (0, 2, 1, 3)).reshape(count, width)
     qkv = lax.all_to_all(qkv, ("z", "x"), 0, 0)
-    q = qkv[:, :, :HEAD_DIM].reshape(HEADS * rows, HEAD_DIM)
-    kv = lax.all_gather(qkv[:, :, HEAD_DIM:], ("y", "c"), axis=0)
-    mixed = coarse_attend(lax.axis_index(("y", "c")).astype(jnp.int32), q, kv)
-    mixed = lax.all_to_all(mixed.reshape(HEADS, rows, HEAD_DIM), ("z", "x"), 0, 0)
+    kv = lax.all_gather(qkv[:, :, : 2 * HEAD_DIM], ("y", "c"), axis=0)
+    mixed = coarse_attend(lax.axis_index(("y", "c")).astype(jnp.int32), qkv, kv)
+    mixed = lax.all_to_all(mixed, ("z", "x"), 0, 0)
     return finish(mixed, coarse_out, shortened, natural)
 
 

time: 215 us -> 199 us (0.926)
  blocking collectives: 62.8 us -> 47.9 us
    all_to_all x1, blocking collectives: 32.2 us -> 19.9 us  [body(): grouped = lax.all_to_all(pack(hidden, tail), 'y', 0, 0)]
    all_gather x1, waiting for transfers between devices: 22.2 us -> 25 us  [body(): kv = lax.all_gather(qkv[:, :, :2 * HEAD_DIM], ('y', 'c'), axis=0)]
    all_to_all x1, blocking collectives: 12.4 us -> 10 us  [body(): partial = lax.all_to_all(shorten(grouped, weight), 'y', 0, 0)]
    ppermute x2, starting transfers between devices: 10.1 us -> 7.91 us  [from_behind(): return lax.ppermute(block, ALL, route)]
    reduce_sum x2 -> x3, other arithmetic: 3.21 us -> 4.73 us  [normed(): scale = lax.rsqrt(jnp.mean(values * values, axis=-1, keepdims=True) + 1e-06)]
    unnamed x43 -> x39, local copies, waits for them, and re-layouts: 12.9 us -> 13.6 us
    dot_general x6 -> x8, matrix products: 17.7 us -> 17.3 us  [dot(): lax.dot_general(a, b, (contract, ((), ())), preferred_element_type=jnp.fl...]
  transfers between devices with their start and end apart: 7 -> 7, of which waited for: 5 -> 4; matrix products, arithmetic and copies ran while one was open for 12% -> 13% of each run, Pallas kernels for 8% -> 9%
where the time goes in v3:
time: 199 us; the launch traced here: 197 us
  blocking collectives  47.9 us (24%)
  waiting for transfers between devices  39.7 us (20%)
  Pallas kernels  35.3 us (18%)
  starting transfers between devices  20.6 us (10%)
  local copies, waits for them, and re-layouts  18 us (9%)
  matrix products  17.3 us (9%)
  between operations  13.7 us (7%)
  other arithmetic  4.93 us (2%)
    all_gather x1, waiting for transfers between devices, body(): kv = lax.all_gather(qkv[:, :, :2 * HEAD_DIM], ('y', 'c'), axis=0)  25 us
    all_to_all x1, blocking collectives, body(): grouped = lax.all_to_all(pack(hidden, tail), 'y', 0, 0)  19.9 us
    all_to_all x1, blocking collectives, body(): qkv = lax.all_to_all(qkv, ('z', 'x'), 0, 0)  18 us
    dot_general x8, matrix products, dot(): lax.dot_general(a, b, (contract, ((), ())), preferred_element_type=jnp.fl...  17.3 us
    pallas_call x1, Pallas kernels, fine_attend(): pl.pallas_call(fine_kernel, name='fine_attend', grid=(width // PAIR,), in...  17.1 us
    unnamed x39, local copies, waits for them, and re-layouts  13.6 us
    all_to_all x1, blocking collectives, body(): partial = lax.all_to_all(shorten(grouped, weight), 'y', 0, 0)  10 us
    ppermute x2, waiting for transfers between devices, from_behind(): return lax.ppermute(block, ALL, route)  9.4 us
  transfers between devices with their start and end apart: 7, of which 4 were waited for; matrix products, arithmetic and copies ran while one was open for 13% of the time, Pallas kernels for 9%

profile of v3, /device:TPU:1, one launch (start us, length us, event | category | flops | bytes accessed | tf_op | source)
XLA Modules:
  0.0 197.4 jit_solution(8251710127566017950)
XLA Ops:
  6.5 5.2 %collective-permute-start = (bf16[512,1024]{1,0:T(8,128)(2,1)}, bf16[512,1024]{1,0:T(8,128)(2,1)}, u32[]{:S(2)}, u32[]{:S(2)}) collective-permute-start(bf16[512,1024]{1,0:T(8,128)(2,1)} %param.10), channel_id=1, source_target_pairs={{0,2},{1,3},{2,4},{3,5},{4,6},{5,7},{6,8},{7,9},{8,10},{9,11},{10,... | collective-permute-start | bytes 3145736 | tf_op jit(solution)/shard_map/ppermute | solution.py:25
  13.5 1.8 copy.19
  15.6 2.2 %copy-done.14 = bf16[1024,1024]{1,0:T(8,128)(2,1)S(1)} copy-done((bf16[1024,1024]{1,0:T(8,128)(2,1)S(1)}, bf16[1024,1024]{1,0:T(8,128)(2,1)}, u32[]{:S(2)}) %copy-start.14) | copy-done | bytes 2097176
  19.7 2.3 %convolution_convert_fusion.5.ko_ref = bf16[512,1024]{1,0:T(8,128)(2,1)} fusion(bf16[1024,1024]{1,0:T(8,128)(2,1)S(1)} %copy-done.15, bf16[512,1024]{1,0:T(8,128)(2,1)S(1)} %copy-done.13, f32[512]{0:T(512)S(1)} %add_rsqrt_fusion.2), kind=kOutput, calls=%fused_computation.20 | convolution fusion | flops 1075838976 | bytes 4196352 | tf_op jit(solution)/shard_map/dot_general | solution.py:35
  21.9 2.4 %fusion.6.vo_ref = bf16[1024,512]{1,0:T(8,128)(2,1)} fusion(bf16[1024,1024]{1,0:T(8,128)(2,1)S(1)} %copy-done, bf16[512,1024]{1,0:T(8,128)(2,1)S(1)} %copy-done.13, f32[512]{0:T(512)S(1)} %add_rsqrt_fusion.2), kind=kOutput, calls=%fused_computation.21 | convolution fusion | flops 1075838976 | bytes 4196352 | tf_op jit(solution)/shard_map/dot_general | solution.py:35
  24.3 8.6 %collective-permute-done = bf16[512,1024]{1,0:T(8,128)(2,1)} collective-permute-done((bf16[512,1024]{1,0:T(8,128)(2,1)}, bf16[512,1024]{1,0:T(8,128)(2,1)}, u32[]{:S(2)}, u32[]{:S(2)}) %collective-permute-start) | collective-permute-done | bytes 1048608 | tf_op jit(solution)/shard_map/ppermute | solution.py:25
  34.2 4.7 %collective-permute-start.1 = (bf16[512,1024]{1,0:T(8,128)(2,1)}, bf16[512,1024]{1,0:T(8,128)(2,1)S(1)}, u32[]{:S(2)}, u32[]{:S(2)}) collective-permute-start(bf16[512,1024]{1,0:T(8,128)(2,1)} %collective-permute-done), channel_id=1, source_target_pairs={{1,0},{3,2},{5,4},{7,6},{9,8},{11,10},{13,12},{15,14},{17,16},{19,... | collective-permute-start | bytes 3145736 | tf_op jit(solution)/shard_map/ppermute | solution.py:331
  40.4 3.8 %fusion.7.vf_ref = bf16[1024,512]{1,0:T(8,128)(2,1)} fusion(bf16[1024,1024]{1,0:T(8,128)(2,1)S(1)} %copy-done, bf16[512,1024]{1,0:T(8,128)(2,1)} %collective-permute-done, f32[512]{0:T(512)S(1)} %add_rsqrt_fusion.1), kind=kOutput, calls=%fused_computation.22 | convolution fusion | flops 1075838976 | bytes 4196352 | tf_op jit(solution)/shard_map/dot_general | solution.py:35
  44.2 2.5 %convolution_convert_fusion.3.kf_ref = bf16[512,1024]{1,0:T(8,128)(2,1)S(1)} fusion(bf16[1024,1024]{1,0:T(8,128)(2,1)S(1)} %copy-done.16, bf16[512,1024]{1,0:T(8,128)(2,1)} %collective-permute-done, f32[512]{0:T(512)S(1)} %add_rsqrt_fusion.1), kind=kOutput, calls=%fused_computation.18 | convolution fusion | flops 1075838976 | bytes 4196352 | tf_op jit(solution)/shard_map/dot_general | solution.py:35
  46.8 1.7 fusion.2
  48.5 2.4 %fusion.8.vn_ref = bf16[1024,512]{1,0:T(8,128)(2,1)} fusion(bf16[1024,1024]{1,0:T(8,128)(2,1)S(1)} %copy-done, bf16[512,1024]{1,0:T(8,128)(2,1)S(1)} %get-tuple-element.20, f32[512]{0:T(512)S(1)} %add_rsqrt_fusion), kind=kOutput, calls=%fused_computation.23 | convolution fusion | flops 1075838976 | bytes 4196352 | tf_op jit(solution)/shard_map/dot_general | solution.py:35
  52.3 17.1 %fine_attend.1 = bf16[512,1024]{1,0:T(8,128)(2,1)S(1)} custom-call(s32[1]{0:T(128)} %bitcast.4.place_ref, bf16[512,1024]{1,0:T(8,128)(2,1)S(1)} %multiply_convert_fusion.q_ref, bf16[512,1024]{1,0:T(8,128)(2,1)S(1)} %convolution_convert_fusion.3.kf_ref, bf16[512,1024]{1,0:T(8,128)(2,1)S(1)} %convolution_convert_fusion.2.kn_ref, ...), custom_call_target="tpu_custom_call" | custom-call | flops 10737418240 | bytes 8388608 | tf_op jit(solution)/shard_map/fine_attend/pallas_call | solution.py:107
  70.8 2.7 %collective-permute-start.3 = (bf16[8,1024]{1,0:T(8,128)(2,1)S(1)}, bf16[8,1024]{1,0:T(8,128)(2,1)S(1)}, u32[]{:S(2)}, u32[]{:S(2)}) collective-permute-start(bf16[8,1024]{1,0:T(8,128)(2,1)S(1)} %bitcast.47), channel_id=1, source_target_pairs={{0,1},{1,2},{2,3},{3,4},{4,5},{5,6},{6,7},{7,8},{8,9},{9,10},{10,1... | collective-permute-start | bytes 49160 | tf_op jit(solution)/shard_map/ppermute | solution.py:25
  74.6 19.9 %all_to_all.20.grouped_ref = bf16[4,4,64,512]{3,2,1,0:T(8,128)(2,1)} all-to-all(bf16[4,4,64,512]{3,2,1,0:T(8,128)(2,1)S(1)} %pack.1), channel_id=1, replica_groups=mesh['z'=4,'x'=4,'y'=4,'c'=2] {'y'}, dimensions={0} | all-to-all | bytes 2097152 | tf_op jit(solution)/shard_map/all_to_all | solution.py:338
  94.5 2.2 %copy-done.1 = bf16[2048,1024]{1,0:T(8,128)(2,1)S(1)} copy-done((bf16[2048,1024]{1,0:T(8,128)(2,1)S(1)}, bf16[2048,1024]{1,0:T(8,128)(2,1)}, u32[]{:S(2)}) %copy-start.1) | copy-done | bytes 4194328
  97.9 2.4 %shorten.1 = bf16[4,64,1024]{2,1,0:T(8,128)(2,1)S(1)} custom-call(bf16[4,4,64,512]{3,2,1,0:T(8,128)(2,1)S(1)} %copy-done.3, bf16[4,512,1024]{2,1,0:T(8,128)(2,1)S(1)} %bitcast.42), custom_call_target="tpu_custom_call" | custom-call | tf_op jit(solution)/shard_map/shorten/pallas_call | solution.py:171
  100.3 10.0 %all_to_all.21.part_ref = bf16[4,64,1024]{2,1,0:T(8,128)(2,1)S(1)} all-to-all(bf16[4,64,1024]{2,1,0:T(8,128)(2,1)S(1)} %shorten.1), channel_id=1, replica_groups=mesh['z'=4,'x'=4,'y'=4,'c'=2] {'y'}, dimensions={0} | all-to-all | bytes 1048576 | tf_op jit(solution)/shard_map/all_to_all | solution.py:339
  110.4 4.2 %coarse_project.1 = (bf16[64,1024]{1,0:T(8,128)(2,1)S(1)}, bf16[16,64,192]{2,1,0:T(8,128)(2,1)S(1)}) custom-call(bf16[4,64,1024]{2,1,0:T(8,128)(2,1)S(1)} %all_to_all.21.part_ref, bf16[1024,1024]{1,0:T(8,128)(2,1)S(1)} %copy-done.4, bf16[1024,1024]{1,0:T(8,128)(2,1)S(1)} %copy-done.5, bf16[1024,1024]{1,0:T(8,128)(2,1)} %v_ref.1), custom_call_target="tpu_custom_call" | custom-call | tf_op jit(solution)/shard_map/coarse_project/pallas_call | solution.py:206
  114.5 18.0 %all_to_all.22.q_ref = bf16[16,64,192]{2,1,0:T(8,128)(2,1)S(1)} all-to-all(bf16[16,64,192]{2,1,0:T(8,128)(2,1)S(1)} %get-tuple-element.17), channel_id=1, replica_groups=mesh['z'=4,'x'=4,'y'=4,'c'=2] {'z','x'}, dimensions={0} | all-to-all | bytes 786432 | tf_op jit(solution)/shard_map/all_to_all | solution.py:342
  134.1 25.0 %all-gather.6.cloned.1.call-done = bf16[128,64,128]{2,1,0:T(8,128)(2,1)} async-done(((bf16[16,64,128]{2,1,0:T(8,128)(2,1)}), bf16[128,64,128]{2,1,0:T(8,128)(2,1)}) %all-gather.6.cloned.1.call-update) | async-done | bytes 2097168 | tf_op jit(solution)/shard_map/all_gather | solution.py:343
  161.7 8.6 %coarse_attend.1 = bf16[16,64,64]{2,1,0:T(8,128)(2,1)S(1)} custom-call(s32[1]{0:T(128)} %bitcast.group_ref, bf16[16,64,192]{2,1,0:T(8,128)(2,1)S(1)} %copy-done.8, bf16[8,16,64,128]{3,2,1,0:T(8,128)(2,1)S(1)} %bitcast.44), custom_call_target="tpu_custom_call" | custom-call | flops 4294967296 | bytes 3145728 | tf_op jit(solution)/shard_map/coarse_attend/pallas_call | solution.py:285
  171.3 6.7 %all-to-all-start.3 = ((bf16[16,2,2048]{2,1,0:T(2,128)(2,1)}), bf16[16,2,2048]{2,1,0:T(2,128)(2,1)S(1)}, u32[]{:S(2)}, u32[]{:S(2)}) async-start(bf16[16,2,2048]{2,1,0:T(2,128)(2,1)} %reshape.80), calls=%async_computation.3 | async-start | bytes 262144 | tf_op jit(solution)/shard_map/all_to_all | solution.py:345
  179.5 5.3 %all-to-all-done.3 = bf16[16,2,2048]{2,1,0:T(2,128)(2,1)S(1)} async-done(((bf16[16,2,2048]{2,1,0:T(2,128)(2,1)}), bf16[16,2,2048]{2,1,0:T(2,128)(2,1)S(1)}, u32[]{:S(2)}, u32[]{:S(2)}) %all-to-all-start.3) | async-done | bytes 131104 | tf_op jit(solution)/shard_map/all_to_all | solution.py:345
  187.8 2.7 %finish.1 = bf16[512,1024]{1,0:T(8,128)(2,1)} custom-call(bf16[16,64,64]{2,1,0:T(8,128)(2,1)S(1)} %reshape.81.mixed_ref, bf16[1024,1024]{1,0:T(8,128)(2,1)S(1)} %copy-done.6, bf16[64,1024]{1,0:T(8,128)(2,1)S(1)} %get-tuple-element.18.short_ref, bf16[512,1024]{1,0:T(8,128)(2,1)S(1)} %bitcast.43), custom_call_target="tpu_custom_call" | custom-call | tf_op jit(solution)/shard_map/finish/pallas_call | solution.py:237
  (62 shorter events, 21.4 us)
Async XLA Ops:
  6.5 15.4 %copy-start = (bf16[1024,1024]{1,0:T(8,128)(2,1)S(1)}, bf16[1024,1024]{1,0:T(8,128)(2,1)}, u32[]{:S(2)}) copy-start(bf16[1024,1024]{1,0:T(8,128)(2,1)} %param.13) | copy-start | bytes 6291460
  6.5 87.9 %all-gather.4.cloned.1.call-start = ((), (), s32[]{:S(2)}) async-start(), calls=%async_computation.4 | async-start | bytes 4718592 | tf_op jit(solution)/shard_map/all_gather | solution.py:332
  6.5 26.3 %collective-permute-start = (bf16[512,1024]{1,0:T(8,128)(2,1)}, bf16[512,1024]{1,0:T(8,128)(2,1)}, u32[]{:S(2)}, u32[]{:S(2)}) collective-permute-start(bf16[512,1024]{1,0:T(8,128)(2,1)} %param.10), channel_id=1, source_target_pairs={{0,2},{1,3},{2,4},{3,5},{4,6},{5,7},{6,8},{7,9},{8,10},{9,11},{10,... | collective-permute-start | bytes 3145736 | tf_op jit(solution)/shard_map/ppermute | solution.py:25
  15.4 3.6 %copy-start.11 = (f32[4,16,8,1024]{3,1,2,0:T(8,128)}, f32[4,16,8,1024]{3,1,2,0:T(8,128)S(1)}, u32[]{:S(2)}) copy-start(f32[4,16,8,1024]{3,1,2,0:T(8,128)S(1)} %copy.19) | copy-start | bytes 6291460
  15.4 2.4 %copy-start.14 = (bf16[1024,1024]{1,0:T(8,128)(2,1)S(1)}, bf16[1024,1024]{1,0:T(8,128)(2,1)}, u32[]{:S(2)}) copy-start(bf16[1024,1024]{1,0:T(8,128)(2,1)} %param.11) | copy-start | bytes 6291460
  17.7 1.3 copy-start.13
  17.7 1.9 copy-start.15
  32.9 126.2 %all-gather.6.cloned.1.call-start = ((), (), s32[]{:S(2)}) async-start(), calls=%async_computation.5 | async-start | bytes 2359296 | tf_op jit(solution)/shard_map/all_gather | solution.py:343
  32.9 13.9 %collective-permute-start.2 = (bf16[512,1024]{1,0:T(8,128)(2,1)}, bf16[512,1024]{1,0:T(8,128)(2,1)}, u32[]{:S(2)}, u32[]{:S(2)}) collective-permute-start(bf16[512,1024]{1,0:T(8,128)(2,1)} %param.10), channel_id=1, source_target_pairs={{0,1},{2,3},{4,5},{6,7},{8,9},{10,11},{12,13},{14,15},{16,17},{18,... | collective-permute-start | bytes 3145736 | tf_op jit(solution)/shard_map/ppermute | solution.py:319
  34.2 12.6 %collective-permute-start.1 = (bf16[512,1024]{1,0:T(8,128)(2,1)}, bf16[512,1024]{1,0:T(8,128)(2,1)S(1)}, u32[]{:S(2)}, u32[]{:S(2)}) collective-permute-start(bf16[512,1024]{1,0:T(8,128)(2,1)} %collective-permute-done), channel_id=1, source_target_pairs={{1,0},{3,2},{5,4},{7,6},{9,8},{11,10},{13,12},{15,14},{17,16},{19,... | collective-permute-start | bytes 3145736 | tf_op jit(solution)/shard_map/ppermute | solution.py:331
  40.4 3.8 %copy-start.16 = (bf16[1024,1024]{1,0:T(8,128)(2,1)S(1)}, bf16[1024,1024]{1,0:T(8,128)(2,1)}, u32[]{:S(2)}) copy-start(bf16[1024,1024]{1,0:T(8,128)(2,1)} %param.12) | copy-start | bytes 6291460
  51.0 1.3 copy-start.10
  52.3 17.1 %copy-start.12 = (f32[4,16,8,1024]{3,1,2,0:T(8,128)S(1)}, f32[4,16,8,1024]{3,1,2,0:T(8,128)}, u32[]{:S(2)}) copy-start(f32[4,16,8,1024]{3,1,2,0:T(8,128)} %copy-done.11) | copy-start | bytes 6291460
  52.3 17.1 %copy-start.17 = (bf16[1024,1024]{1,0:T(8,128)(2,1)S(1)}, bf16[1024,1024]{1,0:T(8,128)(2,1)}, u32[]{:S(2)}) copy-start(bf16[1024,1024]{1,0:T(8,128)(2,1)} %param.14) | copy-start | bytes 6291460
  70.8 3.5 %collective-permute-start.3 = (bf16[8,1024]{1,0:T(8,128)(2,1)S(1)}, bf16[8,1024]{1,0:T(8,128)(2,1)S(1)}, u32[]{:S(2)}, u32[]{:S(2)}) collective-permute-start(bf16[8,1024]{1,0:T(8,128)(2,1)S(1)} %bitcast.47), channel_id=1, source_target_pairs={{0,1},{1,2},{2,3},{3,4},{4,5},{5,6},{6,7},{7,8},{8,9},{9,10},{10,1... | collective-permute-start | bytes 49160 | tf_op jit(solution)/shard_map/ppermute | solution.py:25
  94.5 2.2 %copy-start.1 = (bf16[2048,1024]{1,0:T(8,128)(2,1)S(1)}, bf16[2048,1024]{1,0:T(8,128)(2,1)}, u32[]{:S(2)}) copy-start(bf16[2048,1024]{1,0:T(8,128)(2,1)} %all-gather.4.cloned.1.call-done) | copy-start | bytes 12582916
  96.7 1.2 copy-start.3
  97.9 12.5 %copy-start.4 = (bf16[1024,1024]{1,0:T(8,128)(2,1)S(1)}, bf16[1024,1024]{1,0:T(8,128)(2,1)}, u32[]{:S(2)}) copy-start(bf16[1024,1024]{1,0:T(8,128)(2,1)} %q_ref.1) | copy-start | bytes 6291460
  97.9 12.5 %copy-start.5 = (bf16[1024,1024]{1,0:T(8,128)(2,1)S(1)}, bf16[1024,1024]{1,0:T(8,128)(2,1)}, u32[]{:S(2)}) copy-start(bf16[1024,1024]{1,0:T(8,128)(2,1)} %k_ref.1) | copy-start | bytes 6291460
  159.1 1.0 copy-start.8
  160.1 1.6 copy-start.9
  171.3 13.5 %all-to-all-start.3 = ((bf16[16,2,2048]{2,1,0:T(2,128)(2,1)}), bf16[16,2,2048]{2,1,0:T(2,128)(2,1)S(1)}, u32[]{:S(2)}, u32[]{:S(2)}) async-start(bf16[16,2,2048]{2,1,0:T(2,128)(2,1)} %reshape.80), calls=%async_computation.3 | async-start | bytes 262144 | tf_op jit(solution)/shard_map/all_to_all | solution.py:345
  185.0 1.2 copy-start.2
  186.2 1.6 copy-start.6
  (1 other events, 0.8 us)
Sparse Core Ops, SparseCore 0:
  33.0 36.6 all-gather.3
  134.2 24.7 all-gather.5

commit v4 on v3

--- a/solution.py
+++ b/solution.py
@@ -250,51 +250,76 @@
     )(mixed, out_weight, short, hidden)
 
 
-def coarse_kernel(group_ref, q_ref, kv_ref, out_ref):
-    parts, blocks, rows, _ = kv_ref.shape
-    keys = parts * rows
+def coarse_kernel(number, first, final, where_ref, q_ref, *refs):
+    parts = refs[:number]
+    old = None if first else refs[number : number + 2]
+    outs = refs[number if first else number + 2 :]
+    blocks, rows, _ = parts[0].shape
     tile = 4 * rows
     tiles = blocks // 4
     lane = lax.broadcasted_iota(jnp.int32, (1, tile), 1)
-    row = lax.broadcasted_iota(jnp.int32, (keys, tile), 0)
-    limit = (lane // rows) * keys + group_ref[0] * rows + lane % rows
-    ones = jnp.ones((16, keys), jnp.bfloat16)
+    row = lax.broadcasted_iota(jnp.int32, (tile, tile), 0)
+    stride = 8 * rows
+    place = (row // rows) * stride + row % rows
+    limit = (lane // rows) * stride + where_ref[0] * rows + lane % rows
+    ones = jnp.ones((16, number * tile), jnp.bfloat16)
     queries = []
     for t in range(tiles):
         q = q_ref[4 * t : 4 * t + 4, :, 2 * HEAD_DIM :].reshape(tile, HEAD_DIM)
         queries.append(jnp.concatenate([q, jnp.zeros_like(q)], axis=1))
-    tops = [jnp.full((1, tile), NEG, jnp.float32)] * tiles
-    accs = [jnp.zeros((16 + rows, tile), jnp.float32)] * tiles
-    for g in range(blocks):
-        kv = kv_ref[:, g].reshape(keys, 2 * HEAD_DIM)
+    if first:
+        tops = [jnp.full((1, tile), NEG, jnp.float32)] * tiles
+        accs = [jnp.zeros((16 + HEAD_DIM, tile), jnp.float32)] * tiles
+    else:
+        tops = [old[0][t, 0:1, :] for t in range(tiles)]
+        accs = [old[1][t] for t in range(tiles)]
+    for g in range(tiles):
+        kv = jnp.concatenate([part[4 * g : 4 * g + 4].reshape(tile, PAIR) for part in parts], axis=0)
         v = jnp.concatenate([ones, kv.T[HEAD_DIM:, :]], axis=0)
-        live = range(g // 4, tiles)
+        live = range(g, tiles)
         scores = [dot(kv, queries[t], ((1,), (1,))) for t in live]
-        scores[0] = jnp.where(row <= limit - (g % 4) * keys, scores[0], NEG)
+        keep = jnp.concatenate(
+            [place <= limit - where_ref[1 + i] * rows for i in range(number)], axis=0
+        )
+        scores[0] = jnp.where(keep, scores[0], NEG)
         news = [jnp.maximum(tops[t], jnp.max(s, axis=0, keepdims=True)) for t, s in zip(live, scores)]
         ps = [jnp.exp2(s - top).astype(jnp.bfloat16) for s, top in zip(scores, news)]
         for t, top, p in zip(live, news, ps):
             accs[t] = accs[t] * jnp.exp2(tops[t] - top) + dot(v, p, ((1,), (0,)))
             tops[t] = top
     for t in range(tiles):
-        o = accs[t][16:] * (1.0 / accs[t][0:1])
-        out_ref[4 * t : 4 * t + 4] = o.T.astype(jnp.bfloat16).reshape(4, rows, HEAD_DIM)
-
-
-def coarse_attend(group, q, kv):
-    return pl.pallas_call(
-        coarse_kernel,
-        in_specs=[
-            pl.BlockSpec(memory_space=pltpu.SMEM),
-            pl.BlockSpec(memory_space=pltpu.VMEM),
-            pl.BlockSpec(memory_space=pltpu.VMEM),
-        ],
-        out_specs=pl.BlockSpec(memory_space=pltpu.VMEM),
-        out_shape=jax.ShapeDtypeStruct((*q.shape[:2], HEAD_DIM), jnp.bfloat16),
+        if final:
+            o = accs[t][16:] * (1.0 / accs[t][0:1])
+            outs[0][4 * t : 4 * t + 4] = o.T.astype(jnp.bfloat16).reshape(4, rows, HEAD_DIM)
+        else:
+            outs[0][t] = jnp.broadcast_to(tops[t], (8, tile))
+            outs[1][t] = accs[t]
+
+
+def coarse_attend(places, q, parts, state, final):
+    heads, rows, _ = q.shape
+    tile = 4 * rows
+    if final:
+        out_shape = jax.ShapeDtypeStruct((heads, rows, HEAD_DIM), jnp.bfloat16)
+    else:
+        out_shape = [
+            jax.ShapeDtypeStruct((heads // 4, 8, tile), jnp.float32),
+            jax.ShapeDtypeStruct((heads // 4, 16 + HEAD_DIM, tile), jnp.float32),
+        ]
+    first = state is None
+    arrays = [q, *parts] + ([] if first else list(state))
+    share = len(parts) / 8
+    return pl.pallas_call(
+        functools.partial(coarse_kernel, len(parts), first, final),
+        in_specs=[pl.BlockSpec(memory_space=pltpu.SMEM)]
+        + [pl.BlockSpec(memory_space=pltpu.VMEM)] * len(arrays),
+        out_shape=out_shape,
         name="coarse_attend",
         compiler_params=params(),
-        cost_estimate=pl.CostEstimate(flops=4 * 2**30, bytes_accessed=3 * 2**20, transcendentals=5 * 2**20),
-    )(group.reshape(1), q, kv)
+        cost_estimate=pl.CostEstimate(
+            flops=int(share * 6 * 2**30), bytes_accessed=2 * 2**20, transcendentals=int(share * 5 * 2**20)
+        ),
+    )(jnp.stack(places).astype(jnp.int32), *arrays)
 
 
 def body(
@@ -340,8 +365,28 @@
     shortened, qkv = coarse_project(partial, coarse_query, coarse_key, coarse_value)
     natural = jnp.transpose(hidden.reshape(blocks, SHORT, groups, width), (0, 2, 1, 3)).reshape(count, width)
     qkv = lax.all_to_all(qkv, ("z", "x"), 0, 0)
-    kv = lax.all_gather(qkv[:, :, : 2 * HEAD_DIM], ("y", "c"), axis=0)
-    mixed = coarse_attend(lax.axis_index(("y", "c")).astype(jnp.int32), qkv, kv)
+    kv = qkv[:, :, : 2 * HEAD_DIM]
+    y, c = lax.axis_index("y"), lax.axis_index("c")
+    mine = y * 2 + c
+
+    def around(block, distance):
+        return lax.ppermute(block, "y", [(i, (i + distance) % 4) for i in range(4)])
+
+    def across(block):
+        return lax.ppermute(block, "c", [(0, 1), (1, 0)])
+
+    def spot(distance, other=0):
+        return ((y + distance) % 4) * 2 + (1 - c if other else c)
+
+    mate_kv = across(kv)
+    below, above, beyond = around(kv, 1), around(kv, 3), around(kv, 2)
+    state = coarse_attend((mine, mine, spot(0, 1)), qkv, (kv, mate_kv), None, False)
+    others = (below, above, beyond)
+    state, *others = lax.optimization_barrier((state, *others))
+    swapped = [across(block) for block in others]
+    state = coarse_attend((mine, spot(3), spot(1), spot(2)), qkv, others, state, False)
+    state, *swapped = lax.optimization_barrier((state, *swapped))
+    mixed = coarse_attend((mine, spot(3, 1), spot(1, 1), spot(2, 1)), qkv, swapped, state, True)
     mixed = lax.all_to_all(mixed, ("z", "x"), 0, 0)
     return finish(mixed, coarse_out, shortened, natural)
 

time: 199 us -> 186 us (0.935)
  waiting for transfers between devices: 39.7 us -> 22.9 us
  starting transfers between devices: 20.6 us -> 25.7 us
  local copies, waits for them, and re-layouts: 18 us -> 15.7 us
    all_gather x1 -> x0, waiting for transfers between devices: 25 us -> none  [body(): kv = lax.all_gather(qkv[:, :, :2 * HEAD_DIM], ('y', 'c'), axis=0)]
    ppermute x0 -> x7, starting transfers between devices: none -> 8.25 us  [the longest x4 5.57 us: across(): return lax.ppermute(block, 'c', [(0, 1), (1, 0)])]
    ppermute x0 -> x7, waiting for transfers between devices: none -> 7.72 us  [the longest x3 7.71 us: around(): return lax.ppermute(block, 'y', [(i, (i + distance) % 4) for i in range(4)])]
    all_to_all x1, starting transfers between devices: 6.67 us -> 3.51 us  [body(): mixed = lax.all_to_all(mixed, ('z', 'x'), 0, 0)]
    pallas_call x1 -> x3, Pallas kernels: 8.64 us -> 10.6 us  [coarse_attend(): pl.pallas_call(functools.partial(coarse_kernel, len(parts), first, final)...]
  transfers between devices with their start and end apart: 7 -> 13, of which waited for: 4 -> 4; matrix products, arithmetic and copies ran while one was open for 13% -> 14% of each run, Pallas kernels for 9% -> 13%
where the time goes in v4:
time: 186 us; the launch traced here: 185 us
  blocking collectives  47.9 us (26%)
  Pallas kernels  37.2 us (20%)
  starting transfers between devices  25.7 us (14%)
  waiting for transfers between devices  22.9 us (12%)
  matrix products  17.2 us (9%)
  local copies, waits for them, and re-layouts  15.7 us (8%)
  between operations  13.7 us (7%)
  other arithmetic  5.12 us (3%)
    all_to_all x1, blocking collectives, body(): grouped = lax.all_to_all(pack(hidden, tail), 'y', 0, 0)  19.8 us
    all_to_all x1, blocking collectives, body(): qkv = lax.all_to_all(qkv, ('z', 'x'), 0, 0)  18 us
    dot_general x8, matrix products, dot(): lax.dot_general(a, b, (contract, ((), ())), preferred_element_type=jnp.fl...  17.2 us
    pallas_call x1, Pallas kernels, fine_attend(): pl.pallas_call(fine_kernel, name='fine_attend', grid=(width // PAIR,), in...  17.1 us
    unnamed x39, local copies, waits for them, and re-layouts  12 us
    pallas_call x3, Pallas kernels, coarse_attend(): pl.pallas_call(functools.partial(coarse_kernel, len(parts), first, final)...  10.6 us
    all_to_all x1, blocking collectives, body(): partial = lax.all_to_all(shorten(grouped, weight), 'y', 0, 0)  10 us
    ppermute x2, waiting for transfers between devices, from_behind(): return lax.ppermute(block, ALL, route)  9.39 us
  transfers between devices with their start and end apart: 13, of which 4 were waited for; matrix products, arithmetic and copies ran while one was open for 14% of the time, Pallas kernels for 13%

profile of v4, /device:TPU:1, one launch (start us, length us, event | category | flops | bytes accessed | tf_op | source)
XLA Modules:
  0.0 185.5 jit_solution(2741227702114483078)
XLA Ops:
  6.5 5.2 %collective-permute-start = (bf16[512,1024]{1,0:T(8,128)(2,1)}, bf16[512,1024]{1,0:T(8,128)(2,1)}, u32[]{:S(2)}, u32[]{:S(2)}) collective-permute-start(bf16[512,1024]{1,0:T(8,128)(2,1)} %param.10), channel_id=1, source_target_pairs={{0,2},{1,3},{2,4},{3,5},{4,6},{5,7},{6,8},{7,9},{8,10},{9,11},{10,... | collective-permute-start | bytes 3145736 | tf_op jit(solution)/shard_map/ppermute | solution.py:25
  19.7 2.3 %convolution_convert_fusion.5.ko_ref = bf16[512,1024]{1,0:T(8,128)(2,1)} fusion(bf16[1024,1024]{1,0:T(8,128)(2,1)S(1)} %copy-done.15, bf16[512,1024]{1,0:T(8,128)(2,1)S(1)} %copy-done.13, f32[512]{0:T(512)S(1)} %add_rsqrt_fusion.2), kind=kOutput, calls=%fused_computation.20 | convolution fusion | flops 1075838976 | bytes 4196352 | tf_op jit(solution)/shard_map/dot_general | solution.py:35
  21.9 2.3 %fusion.6.vo_ref = bf16[1024,512]{1,0:T(8,128)(2,1)} fusion(bf16[1024,1024]{1,0:T(8,128)(2,1)S(1)} %copy-done, bf16[512,1024]{1,0:T(8,128)(2,1)S(1)} %copy-done.13, f32[512]{0:T(512)S(1)} %add_rsqrt_fusion.2), kind=kOutput, calls=%fused_computation.21 | convolution fusion | flops 1075838976 | bytes 4196352 | tf_op jit(solution)/shard_map/dot_general | solution.py:35
  24.3 8.5 %collective-permute-done = bf16[512,1024]{1,0:T(8,128)(2,1)} collective-permute-done((bf16[512,1024]{1,0:T(8,128)(2,1)}, bf16[512,1024]{1,0:T(8,128)(2,1)}, u32[]{:S(2)}, u32[]{:S(2)}) %collective-permute-start) | collective-permute-done | bytes 1048608 | tf_op jit(solution)/shard_map/ppermute | solution.py:25
  34.2 4.7 %collective-permute-start.1 = (bf16[512,1024]{1,0:T(8,128)(2,1)}, bf16[512,1024]{1,0:T(8,128)(2,1)S(1)}, u32[]{:S(2)}, u32[]{:S(2)}) collective-permute-start(bf16[512,1024]{1,0:T(8,128)(2,1)} %collective-permute-done), channel_id=1, source_target_pairs={{1,0},{3,2},{5,4},{7,6},{9,8},{11,10},{13,12},{15,14},{17,16},{19,... | collective-permute-start | bytes 3145736 | tf_op jit(solution)/shard_map/ppermute | solution.py:356
  40.4 3.8 %fusion.7.vf_ref = bf16[1024,512]{1,0:T(8,128)(2,1)} fusion(bf16[1024,1024]{1,0:T(8,128)(2,1)S(1)} %copy-done, bf16[512,1024]{1,0:T(8,128)(2,1)} %collective-permute-done, f32[512]{0:T(512)S(1)} %add_rsqrt_fusion.1), kind=kOutput, calls=%fused_computation.22 | convolution fusion | flops 1075838976 | bytes 4196352 | tf_op jit(solution)/shard_map/dot_general | solution.py:35
  44.2 2.5 %convolution_convert_fusion.3.kf_ref = bf16[512,1024]{1,0:T(8,128)(2,1)S(1)} fusion(bf16[1024,1024]{1,0:T(8,128)(2,1)S(1)} %copy-done.16, bf16[512,1024]{1,0:T(8,128)(2,1)} %collective-permute-done, f32[512]{0:T(512)S(1)} %add_rsqrt_fusion.1), kind=kOutput, calls=%fused_computation.18 | convolution fusion | flops 1075838976 | bytes 4196352 | tf_op jit(solution)/shard_map/dot_general | solution.py:35
  48.5 2.5 %fusion.8.vn_ref = bf16[1024,512]{1,0:T(8,128)(2,1)} fusion(bf16[1024,1024]{1,0:T(8,128)(2,1)S(1)} %copy-done, bf16[512,1024]{1,0:T(8,128)(2,1)S(1)} %get-tuple-element.48, f32[512]{0:T(512)S(1)} %add_rsqrt_fusion), kind=kOutput, calls=%fused_computation.23 | convolution fusion | flops 1075838976 | bytes 4196352 | tf_op jit(solution)/shard_map/dot_general | solution.py:35
  52.3 17.1 %fine_attend.1 = bf16[512,1024]{1,0:T(8,128)(2,1)S(1)} custom-call(s32[1]{0:T(128)} %bitcast.7.place_ref, bf16[512,1024]{1,0:T(8,128)(2,1)S(1)} %multiply_convert_fusion.q_ref, bf16[512,1024]{1,0:T(8,128)(2,1)S(1)} %convolution_convert_fusion.3.kf_ref, bf16[512,1024]{1,0:T(8,128)(2,1)S(1)} %convolution_convert_fusion.2.kn_ref, ...), custom_call_target="tpu_custom_call" | custom-call | flops 10737418240 | bytes 8388608 | tf_op jit(solution)/shard_map/fine_attend/pallas_call | solution.py:107
  70.7 2.7 %collective-permute-start.3 = (bf16[8,1024]{1,0:T(8,128)(2,1)S(1)}, bf16[8,1024]{1,0:T(8,128)(2,1)S(1)}, u32[]{:S(2)}, u32[]{:S(2)}) collective-permute-start(bf16[8,1024]{1,0:T(8,128)(2,1)S(1)} %bitcast.52), channel_id=1, source_target_pairs={{0,1},{1,2},{2,3},{3,4},{4,5},{5,6},{6,7},{7,8},{8,9},{9,10},{10,1... | collective-permute-start | bytes 49160 | tf_op jit(solution)/shard_map/ppermute | solution.py:25
  74.5 19.8 %all_to_all.20.grouped_ref = bf16[4,4,64,512]{3,2,1,0:T(8,128)(2,1)} all-to-all(bf16[4,4,64,512]{3,2,1,0:T(8,128)(2,1)S(1)} %pack.1), channel_id=1, replica_groups=mesh['z'=4,'x'=4,'y'=4,'c'=2] {'y'}, dimensions={0} | all-to-all | bytes 2097152 | tf_op jit(solution)/shard_map/all_to_all | solution.py:363
  97.8 2.4 %shorten.1 = bf16[4,64,1024]{2,1,0:T(8,128)(2,1)S(1)} custom-call(bf16[4,4,64,512]{3,2,1,0:T(8,128)(2,1)S(1)} %copy-done.3, bf16[4,512,1024]{2,1,0:T(8,128)(2,1)S(1)} %bitcast.48), custom_call_target="tpu_custom_call" | custom-call | tf_op jit(solution)/shard_map/shorten/pallas_call | solution.py:171
  100.2 10.0 %all_to_all.21.part_ref = bf16[4,64,1024]{2,1,0:T(8,128)(2,1)S(1)} all-to-all(bf16[4,64,1024]{2,1,0:T(8,128)(2,1)S(1)} %shorten.1), channel_id=1, replica_groups=mesh['z'=4,'x'=4,'y'=4,'c'=2] {'y'}, dimensions={0} | all-to-all | bytes 1048576 | tf_op jit(solution)/shard_map/all_to_all | solution.py:364
  110.3 4.2 %coarse_project.1 = (bf16[64,1024]{1,0:T(8,128)(2,1)S(1)}, bf16[16,64,192]{2,1,0:T(8,128)(2,1)S(1)}) custom-call(bf16[4,64,1024]{2,1,0:T(8,128)(2,1)S(1)} %all_to_all.21.part_ref, bf16[1024,1024]{1,0:T(8,128)(2,1)S(1)} %copy-done.4, bf16[1024,1024]{1,0:T(8,128)(2,1)S(1)} %copy-done.5, bf16[1024,1024]{1,0:T(8,128)(2,1)} %v_ref.1), custom_call_target="tpu_custom_call" | custom-call | tf_op jit(solution)/shard_map/coarse_project/pallas_call | solution.py:206
  114.5 18.0 %all_to_all.22.q_ref = bf16[16,64,192]{2,1,0:T(8,128)(2,1)S(1)} all-to-all(bf16[16,64,192]{2,1,0:T(8,128)(2,1)S(1)} %get-tuple-element.31), channel_id=1, replica_groups=mesh['z'=4,'x'=4,'y'=4,'c'=2] {'z','x'}, dimensions={0} | all-to-all | bytes 786432 | tf_op jit(solution)/shard_map/all_to_all | solution.py:367
  133.3 4.3 %collective-permute-start.4 = (bf16[16,64,128]{2,1,0:T(8,128)(2,1)S(1)}, bf16[16,64,128]{2,1,0:T(8,128)(2,1)}, u32[]{:S(2)}, u32[]{:S(2)}) collective-permute-start(bf16[16,64,128]{2,1,0:T(8,128)(2,1)S(1)} %slice.9.refs_0_), channel_id=1, source_target_pairs={{0,1},{1,0},{2,3},{3,2},{4,5},{5,4},{6,7},{7,6},{8,9},{9,8},{10,11... | collective-permute-start | bytes 786440 | tf_op jit(solution)/shard_map/ppermute | solution.py:376
  137.9 2.4 %collective-permute-start.6 = (bf16[16,64,128]{2,1,0:T(8,128)(2,1)S(1)}, bf16[16,64,128]{2,1,0:T(8,128)(2,1)S(1)}, u32[]{:S(2)}, u32[]{:S(2)}) collective-permute-start(bf16[16,64,128]{2,1,0:T(8,128)(2,1)S(1)} %slice.9.refs_0_), channel_id=1, source_target_pairs={{0,6},{2,0},{4,2},{6,4},{1,7},{3,1},{5,3},{7,5},{8,14},{10,8},{12,... | collective-permute-start | bytes 786440 | tf_op jit(solution)/shard_map/ppermute | solution.py:373
  141.4 3.2 %coarse_attend.3 = (f32[4,8,256]{2,1,0:T(8,128)S(1)}, f32[4,80,256]{2,1,0:T(8,128)S(1)}) custom-call(s32[3]{0:T(128)S(1)} %pad_add_fusion.2.where_ref, bf16[16,64,192]{2,1,0:T(8,128)(2,1)S(1)} %copy-done.8, bf16[16,64,128]{2,1,0:T(8,128)(2,1)S(1)} %slice.9.refs_0_, bf16[16,64,128]{2,1,0:T(8,128)(2,1)} %collective-permute-done.4.refs_1_), custom_call_target="tpu_custom_call" | custom-call | flops 1610612736 | bytes 2097152 | tf_op jit(solution)/shard_map/coarse_attend/pallas_call | solution.py:312
  144.7 7.7 %collective-permute-done.5.refs_0_ = bf16[16,64,128]{2,1,0:T(8,128)(2,1)S(1)} collective-permute-done((bf16[16,64,128]{2,1,0:T(8,128)(2,1)S(1)}, bf16[16,64,128]{2,1,0:T(8,128)(2,1)S(1)}, u32[]{:S(2)}, u32[]{:S(2)}) %collective-permute-start.5) | collective-permute-done | bytes 262176 | tf_op jit(solution)/shard_map/ppermute | solution.py:373
  153.8 3.6 %coarse_attend.4 = (f32[4,8,256]{2,1,0:T(8,128)S(1)}, f32[4,80,256]{2,1,0:T(8,128)S(1)}) custom-call(s32[4]{0:T(128)S(1)} %get-tuple-element.50.where_ref, bf16[16,64,192]{2,1,0:T(8,128)(2,1)S(1)} %copy-done.9, bf16[16,64,128]{2,1,0:T(8,128)(2,1)S(1)} %collective-permute-done.5.refs_0_, bf16[16,64,128]{2,1,0:T(8,128)(2,1)S(1)} %collective-permute-done.6.refs_1_, ...), custom_call_target="tpu_custom_call" | custom-call | flops 2415919104 | bytes 2097152 | tf_op jit(solution)/shard_map/coarse_attend/pallas_call | solution.py:312
  157.4 3.7 %coarse_attend.5 = bf16[16,64,64]{2,1,0:T(8,128)(2,1)S(1)} custom-call(s32[4]{0:T(128)S(1)} %get-tuple-element.49.where_ref, bf16[16,64,192]{2,1,0:T(8,128)(2,1)S(1)} %copy-done.9, bf16[16,64,128]{2,1,0:T(8,128)(2,1)S(1)} %collective-permute-done.8.refs_0_, bf16[16,64,128]{2,1,0:T(8,128)(2,1)S(1)} %collective-permute-done.9.refs_1_, ...), custom_call_target="tpu_custom_call" | custom-call | flops 2415919104 | bytes 2097152 | tf_op jit(solution)/shard_map/coarse_attend/pallas_call | solution.py:312
  162.0 3.5 %all-to-all-start.3 = ((bf16[16,2,2048]{2,1,0:T(2,128)(2,1)}), bf16[16,2,2048]{2,1,0:T(2,128)(2,1)S(1)}, u32[]{:S(2)}, u32[]{:S(2)}) async-start(bf16[16,2,2048]{2,1,0:T(2,128)(2,1)} %reshape.75), calls=%async_computation.3 | async-start | bytes 262144 | tf_op jit(solution)/shard_map/all_to_all | solution.py:390
  167.1 5.8 %all-to-all-done.3 = bf16[16,2,2048]{2,1,0:T(2,128)(2,1)S(1)} async-done(((bf16[16,2,2048]{2,1,0:T(2,128)(2,1)}), bf16[16,2,2048]{2,1,0:T(2,128)(2,1)S(1)}, u32[]{:S(2)}, u32[]{:S(2)}) %all-to-all-start.3) | async-done | bytes 131104 | tf_op jit(solution)/shard_map/all_to_all | solution.py:390
  175.9 2.7 %finish.1 = bf16[512,1024]{1,0:T(8,128)(2,1)} custom-call(bf16[16,64,64]{2,1,0:T(8,128)(2,1)S(1)} %reshape.76.mixed_ref, bf16[1024,1024]{1,0:T(8,128)(2,1)S(1)} %copy-done.6, bf16[64,1024]{1,0:T(8,128)(2,1)S(1)} %get-tuple-element.46.short_ref, bf16[512,1024]{1,0:T(8,128)(2,1)S(1)} %bitcast.49), custom_call_target="tpu_custom_call" | custom-call | tf_op jit(solution)/shard_map/finish/pallas_call | solution.py:237
  (77 shorter events, 28.7 us)
Async XLA Ops:
  6.5 15.4 %copy-start = (bf16[1024,1024]{1,0:T(8,128)(2,1)S(1)}, bf16[1024,1024]{1,0:T(8,128)(2,1)}, u32[]{:S(2)}) copy-start(bf16[1024,1024]{1,0:T(8,128)(2,1)} %param.13) | copy-start | bytes 6291460
  6.5 87.8 %all-gather.2.cloned.1.call-start = ((), (), s32[]{:S(2)}) async-start(), calls=%async_computation.4 | async-start | bytes 4718592 | tf_op jit(solution)/shard_map/all_gather | solution.py:357
  6.5 26.3 %collective-permute-start = (bf16[512,1024]{1,0:T(8,128)(2,1)}, bf16[512,1024]{1,0:T(8,128)(2,1)}, u32[]{:S(2)}, u32[]{:S(2)}) collective-permute-start(bf16[512,1024]{1,0:T(8,128)(2,1)} %param.10), channel_id=1, source_target_pairs={{0,2},{1,3},{2,4},{3,5},{4,6},{5,7},{6,8},{7,9},{8,10},{9,11},{10,... | collective-permute-start | bytes 3145736 | tf_op jit(solution)/shard_map/ppermute | solution.py:25
  15.4 3.6 %copy-start.11 = (f32[4,16,8,1024]{3,1,2,0:T(8,128)}, f32[4,16,8,1024]{3,1,2,0:T(8,128)S(1)}, u32[]{:S(2)}) copy-start(f32[4,16,8,1024]{3,1,2,0:T(8,128)S(1)} %copy.14) | copy-start | bytes 6291460
  15.4 2.4 %copy-start.14 = (bf16[1024,1024]{1,0:T(8,128)(2,1)S(1)}, bf16[1024,1024]{1,0:T(8,128)(2,1)}, u32[]{:S(2)}) copy-start(bf16[1024,1024]{1,0:T(8,128)(2,1)} %param.11) | copy-start | bytes 6291460
  17.8 1.9 %copy-start.15 = (bf16[1024,1024]{1,0:T(8,128)(2,1)S(1)}, bf16[1024,1024]{1,0:T(8,128)(2,1)}, u32[]{:S(2)}) copy-start(bf16[1024,1024]{1,0:T(8,128)(2,1)} %param.12) | copy-start | bytes 6291460
  32.9 13.9 %collective-permute-start.2 = (bf16[512,1024]{1,0:T(8,128)(2,1)}, bf16[512,1024]{1,0:T(8,128)(2,1)}, u32[]{:S(2)}, u32[]{:S(2)}) collective-permute-start(bf16[512,1024]{1,0:T(8,128)(2,1)} %param.10), channel_id=1, source_target_pairs={{0,1},{2,3},{4,5},{6,7},{8,9},{10,11},{12,13},{14,15},{16,17},{18,... | collective-permute-start | bytes 3145736 | tf_op jit(solution)/shard_map/ppermute | solution.py:344
  34.2 12.5 %collective-permute-start.1 = (bf16[512,1024]{1,0:T(8,128)(2,1)}, bf16[512,1024]{1,0:T(8,128)(2,1)S(1)}, u32[]{:S(2)}, u32[]{:S(2)}) collective-permute-start(bf16[512,1024]{1,0:T(8,128)(2,1)} %collective-permute-done), channel_id=1, source_target_pairs={{1,0},{3,2},{5,4},{7,6},{9,8},{11,10},{13,12},{15,14},{17,16},{19,... | collective-permute-start | bytes 3145736 | tf_op jit(solution)/shard_map/ppermute | solution.py:356
  40.4 3.8 %copy-start.16 = (bf16[1024,1024]{1,0:T(8,128)(2,1)S(1)}, bf16[1024,1024]{1,0:T(8,128)(2,1)}, u32[]{:S(2)}) copy-start(bf16[1024,1024]{1,0:T(8,128)(2,1)} %param.12) | copy-start | bytes 6291460
  52.3 17.1 %copy-start.12 = (f32[4,16,8,1024]{3,1,2,0:T(8,128)S(1)}, f32[4,16,8,1024]{3,1,2,0:T(8,128)}, u32[]{:S(2)}) copy-start(f32[4,16,8,1024]{3,1,2,0:T(8,128)} %copy-done.11) | copy-start | bytes 6291460
  52.3 17.1 %copy-start.17 = (bf16[1024,1024]{1,0:T(8,128)(2,1)S(1)}, bf16[1024,1024]{1,0:T(8,128)(2,1)}, u32[]{:S(2)}) copy-start(bf16[1024,1024]{1,0:T(8,128)(2,1)} %param.14) | copy-start | bytes 6291460
  70.7 3.6 %collective-permute-start.3 = (bf16[8,1024]{1,0:T(8,128)(2,1)S(1)}, bf16[8,1024]{1,0:T(8,128)(2,1)S(1)}, u32[]{:S(2)}, u32[]{:S(2)}) collective-permute-start(bf16[8,1024]{1,0:T(8,128)(2,1)S(1)} %bitcast.52), channel_id=1, source_target_pairs={{0,1},{1,2},{2,3},{3,4},{4,5},{5,6},{6,7},{7,8},{8,9},{9,10},{10,1... | collective-permute-start | bytes 49160 | tf_op jit(solution)/shard_map/ppermute | solution.py:25
  94.4 2.2 %copy-start.1 = (bf16[2048,1024]{1,0:T(8,128)(2,1)S(1)}, bf16[2048,1024]{1,0:T(8,128)(2,1)}, u32[]{:S(2)}) copy-start(bf16[2048,1024]{1,0:T(8,128)(2,1)} %all-gather.2.cloned.1.call-done) | copy-start | bytes 12582916
  97.8 12.5 %copy-start.4 = (bf16[1024,1024]{1,0:T(8,128)(2,1)S(1)}, bf16[1024,1024]{1,0:T(8,128)(2,1)}, u32[]{:S(2)}) copy-start(bf16[1024,1024]{1,0:T(8,128)(2,1)} %q_ref.1) | copy-start | bytes 6291460
  97.8 12.5 %copy-start.5 = (bf16[1024,1024]{1,0:T(8,128)(2,1)S(1)}, bf16[1024,1024]{1,0:T(8,128)(2,1)}, u32[]{:S(2)}) copy-start(bf16[1024,1024]{1,0:T(8,128)(2,1)} %k_ref.1) | copy-start | bytes 6291460
  133.3 7.0 %collective-permute-start.4 = (bf16[16,64,128]{2,1,0:T(8,128)(2,1)S(1)}, bf16[16,64,128]{2,1,0:T(8,128)(2,1)}, u32[]{:S(2)}, u32[]{:S(2)}) collective-permute-start(bf16[16,64,128]{2,1,0:T(8,128)(2,1)S(1)} %slice.9.refs_0_), channel_id=1, source_target_pairs={{0,1},{1,0},{2,3},{3,2},{4,5},{5,4},{6,7},{7,6},{8,9},{9,8},{10,11... | collective-permute-start | bytes 786440 | tf_op jit(solution)/shard_map/ppermute | solution.py:376
  137.6 14.8 %collective-permute-start.5 = (bf16[16,64,128]{2,1,0:T(8,128)(2,1)S(1)}, bf16[16,64,128]{2,1,0:T(8,128)(2,1)S(1)}, u32[]{:S(2)}, u32[]{:S(2)}) collective-permute-start(bf16[16,64,128]{2,1,0:T(8,128)(2,1)S(1)} %slice.9.refs_0_), channel_id=1, source_target_pairs={{0,2},{2,4},{4,6},{6,0},{1,3},{3,5},{5,7},{7,1},{8,10},{10,12},{12... | collective-permute-start | bytes 786440 | tf_op jit(solution)/shard_map/ppermute | solution.py:373
  137.9 14.5 %collective-permute-start.6 = (bf16[16,64,128]{2,1,0:T(8,128)(2,1)S(1)}, bf16[16,64,128]{2,1,0:T(8,128)(2,1)S(1)}, u32[]{:S(2)}, u32[]{:S(2)}) collective-permute-start(bf16[16,64,128]{2,1,0:T(8,128)(2,1)S(1)} %slice.9.refs_0_), channel_id=1, source_target_pairs={{0,6},{2,0},{4,2},{6,4},{1,7},{3,1},{5,3},{7,5},{8,14},{10,8},{12,... | collective-permute-start | bytes 786440 | tf_op jit(solution)/shard_map/ppermute | solution.py:373
  140.3 12.1 %collective-permute-start.7 = (bf16[16,64,128]{2,1,0:T(8,128)(2,1)S(1)}, bf16[16,64,128]{2,1,0:T(8,128)(2,1)S(1)}, u32[]{:S(2)}, u32[]{:S(2)}) collective-permute-start(bf16[16,64,128]{2,1,0:T(8,128)(2,1)S(1)} %slice.9.refs_0_), channel_id=1, source_target_pairs={{0,4},{2,6},{4,0},{6,2},{1,5},{3,7},{5,1},{7,3},{8,12},{10,14},{12... | collective-permute-start | bytes 786440 | tf_op jit(solution)/shard_map/ppermute | solution.py:373
  141.4 12.3 %copy-start.9 = (bf16[16,64,192]{2,1,0:T(8,128)(2,1)S(1)}, bf16[16,64,192]{2,1,0:T(8,128)(2,1)}, u32[]{:S(2)}) copy-start(bf16[16,64,192]{2,1,0:T(8,128)(2,1)} %copy-done.7) | copy-start | bytes 1179652
  152.4 5.0 %collective-permute-start.10 = (bf16[16,64,128]{2,1,0:T(8,128)(2,1)S(1)}, bf16[16,64,128]{2,1,0:T(8,128)(2,1)S(1)}, u32[]{:S(2)}, u32[]{:S(2)}) collective-permute-start(bf16[16,64,128]{2,1,0:T(8,128)(2,1)S(1)} %collective-permute-done.7.refs_2_), channel_id=1, source_target_pairs={{0,1},{1,0},{2,3},{3,2},{4,5},{5,4},{6,7},{7,6},{8,9},{9,8},{10,11... | collective-permute-start | bytes 786440 | tf_op jit(solution)/shard_map/ppermute | solution.py:376
  153.2 4.2 %collective-permute-start.8 = (bf16[16,64,128]{2,1,0:T(8,128)(2,1)S(1)}, bf16[16,64,128]{2,1,0:T(8,128)(2,1)S(1)}, u32[]{:S(2)}, u32[]{:S(2)}) collective-permute-start(bf16[16,64,128]{2,1,0:T(8,128)(2,1)S(1)} %collective-permute-done.5.refs_0_), channel_id=1, source_target_pairs={{0,1},{1,0},{2,3},{3,2},{4,5},{5,4},{6,7},{7,6},{8,9},{9,8},{10,11... | collective-permute-start | bytes 786440 | tf_op jit(solution)/shard_map/ppermute | solution.py:376
  153.3 4.2 %collective-permute-start.9 = (bf16[16,64,128]{2,1,0:T(8,128)(2,1)S(1)}, bf16[16,64,128]{2,1,0:T(8,128)(2,1)S(1)}, u32[]{:S(2)}, u32[]{:S(2)}) collective-permute-start(bf16[16,64,128]{2,1,0:T(8,128)(2,1)S(1)} %collective-permute-done.6.refs_1_), channel_id=1, source_target_pairs={{0,1},{1,0},{2,3},{3,2},{4,5},{5,4},{6,7},{7,6},{8,9},{9,8},{10,11... | collective-permute-start | bytes 786440 | tf_op jit(solution)/shard_map/ppermute | solution.py:376
  162.0 10.8 %all-to-all-start.3 = ((bf16[16,2,2048]{2,1,0:T(2,128)(2,1)}), bf16[16,2,2048]{2,1,0:T(2,128)(2,1)S(1)}, u32[]{:S(2)}, u32[]{:S(2)}) async-start(bf16[16,2,2048]{2,1,0:T(2,128)(2,1)} %reshape.75), calls=%async_computation.3 | async-start | bytes 262144 | tf_op jit(solution)/shard_map/all_to_all | solution.py:390
  (7 other events, 8.5 us)
Sparse Core Ops, SparseCore 0:
  33.0 36.6 all-gather.1

commit v5 on v4

--- a/solution.py
+++ b/solution.py
@@ -35,94 +35,156 @@
     return lax.dot_general(a, b, (contract, ((), ())), preferred_element_type=jnp.float32)
 
 
-def params():
-    return pltpu.CompilerParams(vmem_limit_bytes=48 * 2**20)
-
-
-def fine_kernel(place_ref, q_ref, kf_ref, kn_ref, ko_ref, vf_ref, vn_ref, vo_ref, out_ref, s_ref, p_ref):
-    count = q_ref.shape[0]
-    span = WIN + QB
-    blocks = count // QB
+def params(mib=48):
+    return pltpu.CompilerParams(vmem_limit_bytes=mib * 2**20)
+
+
+def spots(index):
     groups = QB // SHORT
+    return (index % groups) * SHORT + index // groups
+
+
+def two_heads(q_ref, b):
     lane = lax.broadcasted_iota(jnp.int32, (QB, PAIR), 1)
+    q = q_ref[b * QB : (b + 1) * QB, :]
+    zero = jnp.zeros_like(q)
+    return jnp.concatenate(
+        [jnp.where(lane < HEAD_DIM, q, zero), jnp.where(lane < HEAD_DIM, zero, q)], axis=0
+    )
+
+
+def with_sums(v):
+    return jnp.concatenate([v, jnp.ones((16, v.shape[1]), jnp.bfloat16)], axis=0)
+
+
+def fine_own_kernel(q_ref, k_ref, v_ref, top_ref, acc_ref, s_ref, p_ref):
+    blocks = q_ref.shape[0] // QB
     row = lax.broadcasted_iota(jnp.int32, (QB, 2 * QB), 0)
     col = lax.broadcasted_iota(jnp.int32, (QB, 2 * QB), 1) % QB
-    last = row <= (col % groups) * SHORT + col // groups
-    ones = jnp.ones((16, span), jnp.bfloat16)
-
-    def scores(b, masked):
-        q = q_ref[b * QB : (b + 1) * QB, :]
-        zero = jnp.zeros_like(q)
-        both = jnp.concatenate(
-            [jnp.where(lane < HEAD_DIM, q, zero), jnp.where(lane < HEAD_DIM, zero, q)], axis=0
-        )
-        start = 0
-        for i, part in enumerate((kf_ref[b * QB :, :], kn_ref[...], ko_ref[: (b + 1) * QB, :])):
-            s = dot(part, both, ((1,), (1,)))
-            if masked and i < 2:
-                s = jnp.where(place_ref[0] + i >= 2, s, NEG)
-            s_ref[b, start : start + part.shape[0], :] = s
-            start += part.shape[0]
-
-    def weights(b):
-        edge = jnp.where(last, s_ref[b, WIN:span, :], s_ref[b, 0:QB, :])
-        top = jnp.maximum(
-            jnp.max(edge, axis=0, keepdims=True),
-            jnp.max(s_ref[b, QB:WIN, :], axis=0, keepdims=True),
-        )
-        edge = jnp.exp2(edge - top).astype(jnp.bfloat16)
-        zero = jnp.zeros_like(edge)
-        p_ref[b, 0:QB, :] = jnp.where(last, zero, edge)
-        p_ref[b, WIN:span, :] = jnp.where(last, edge, zero)
-        p_ref[b, QB:WIN, :] = jnp.exp2(s_ref[b, QB:WIN, :] - top).astype(jnp.bfloat16)
-
-    def mix(b):
-        v = jnp.concatenate([vf_ref[:, b * QB :], vn_ref[...], vo_ref[:, : (b + 1) * QB]], axis=1)
-        v = jnp.concatenate([v, ones], axis=0)
-        o = dot(v, p_ref[b], ((1,), (0,)))
-        o = o[:PAIR] * (1.0 / o[PAIR : PAIR + 1])
-        mixed = jnp.concatenate([o[:HEAD_DIM, :QB], o[HEAD_DIM:PAIR, QB:]], axis=0)
-        out_ref[b * QB : (b + 1) * QB, :] = mixed.T.astype(jnp.bfloat16)
-
-    def units(masked):
+    keep = spots(row) <= spots(col)
+    for b in range(blocks):
+        both = two_heads(q_ref, b)
+        if b > 0:
+            s_ref[b, : b * QB, :] = dot(k_ref[: b * QB, :], both, ((1,), (1,)))
+        s = dot(k_ref[b * QB : (b + 1) * QB, :], both, ((1,), (1,)))
+        s_ref[b, b * QB : (b + 1) * QB, :] = jnp.where(keep, s, NEG)
+    for b in range(blocks):
+        end = (b + 1) * QB
+        top = jnp.max(s_ref[b, :end, :], axis=0, keepdims=True)
+        p_ref[b, :end, :] = jnp.exp2(s_ref[b, :end, :] - top).astype(jnp.bfloat16)
+        top_ref[0, b] = jnp.broadcast_to(top, (8, 2 * QB))
+    for b in range(blocks):
+        end = (b + 1) * QB
+        o = dot(with_sums(v_ref[:, :end]), p_ref[b, :end, :], ((1,), (0,)))
+        acc_ref[0, b, :16, :] = o[PAIR:]
+        acc_ref[0, b, 16:, :QB] = o[:HEAD_DIM, :QB]
+        acc_ref[0, b, 16:, QB:] = o[HEAD_DIM:PAIR, QB:]
+
+
+def fine_before_kernel(
+    where_ref, q_ref, kf_ref, kn_ref, vf_ref, vn_ref, top_ref, acc_ref, out_ref, k_ref, v_ref, s_ref, p_ref
+):
+    half = kf_ref.shape[0]
+    blocks = q_ref.shape[0] // QB
+    core = where_ref[0]
+    row = lax.broadcasted_iota(jnp.int32, (QB, 2 * QB), 0)
+    col = lax.broadcasted_iota(jnp.int32, (QB, 2 * QB), 1) % QB
+    keep = row > spots(col)
+
+    def store(b, total, o):
+        o = o * (1.0 / total)
+        mixed = jnp.concatenate([o[:, :QB], o[:, QB:]], axis=0)
+        at = b * QB // half
+        out_ref[(at + core) % 2, b * QB - at * half : (b + 1) * QB - at * half, :] = mixed.T.astype(jnp.bfloat16)
+
+    @pl.when(where_ref[1] == 0)
+    def _():
         for b in range(blocks):
-            scores(b, masked)
+            store(b, acc_ref[0, b, 0:1, :], acc_ref[0, b, 16:, :])
+
+    @pl.when(where_ref[1] > 0)
+    def _():
+        mine = pl.ds(pl.multiple_of(core * half, half), half)
+        other = pl.ds(pl.multiple_of((1 - core) * half, half), half)
+        k_ref[mine, :] = kf_ref[...]
+        k_ref[other, :] = kn_ref[...]
+        v_ref[:, mine] = vf_ref[...]
+        v_ref[:, other] = vn_ref[...]
         for b in range(blocks):
-            weights(b)
+            both = two_heads(q_ref, b)
+            s = dot(k_ref[b * QB : (b + 1) * QB, :], both, ((1,), (1,)))
+            s_ref[b, b * QB : (b + 1) * QB, :] = jnp.where(keep, s, NEG)
+            if b < blocks - 1:
+                s_ref[b, (b + 1) * QB :, :] = dot(k_ref[(b + 1) * QB :, :], both, ((1,), (1,)))
+        fades = []
         for b in range(blocks):
-            mix(b)
-
-    @pl.when(place_ref[0] * count >= WIN)
-    def _():
-        units(False)
-
-    @pl.when(place_ref[0] * count < WIN)
-    def _():
-        units(True)
-
-
-def fine_attend(place, q, keys, values):
+            old = top_ref[0, b, 0:1, :]
+            top = jnp.maximum(old, jnp.max(s_ref[b, b * QB :, :], axis=0, keepdims=True))
+            p_ref[b, b * QB :, :] = jnp.exp2(s_ref[b, b * QB :, :] - top).astype(jnp.bfloat16)
+            fades.append(jnp.exp2(old - top))
+        for b in range(blocks):
+            o = dot(with_sums(v_ref[:, b * QB :]), p_ref[b, b * QB :, :], ((1,), (0,)))
+            acc = acc_ref[0, b] * fades[b]
+            new = jnp.concatenate([o[:HEAD_DIM, :QB], o[HEAD_DIM:PAIR, QB:]], axis=1)
+            store(b, acc[0:1] + o[PAIR : PAIR + 1], acc[16:] + new)
+
+
+def fine_own(q, k, v):
     count, width = q.shape
     blocks = count // QB
-    return pl.pallas_call(
-        fine_kernel,
-        name="fine_attend",
+    pairs = width // PAIR
+    return pl.pallas_call(
+        fine_own_kernel,
+        name="fine_own",
+        grid=(pairs,),
+        in_specs=[
+            pl.BlockSpec((count, PAIR), lambda i: (0, i)),
+            pl.BlockSpec((count, PAIR), lambda i: (0, i)),
+            pl.BlockSpec((PAIR, count), lambda i: (i, 0)),
+        ],
+        out_specs=[
+            pl.BlockSpec((1, blocks, 8, 2 * QB), lambda i: (i, 0, 0, 0)),
+            pl.BlockSpec((1, blocks, 16 + HEAD_DIM, 2 * QB), lambda i: (i, 0, 0, 0)),
+        ],
+        out_shape=[
+            jax.ShapeDtypeStruct((pairs, blocks, 8, 2 * QB), jnp.float32),
+            jax.ShapeDtypeStruct((pairs, blocks, 16 + HEAD_DIM, 2 * QB), jnp.float32),
+        ],
+        scratch_shapes=[
+            pltpu.VMEM((blocks, count, 2 * QB), jnp.float32),
+            pltpu.VMEM((blocks, count, 2 * QB), jnp.bfloat16),
+        ],
+        compiler_params=params(),
+        cost_estimate=pl.CostEstimate(flops=5 * 2**30, bytes_accessed=6 * 2**20, transcendentals=5 * 2**20),
+    )(q, k, v)
+
+
+def fine_before(where, q, keys, values, state):
+    count, width = q.shape
+    blocks = count // QB
+    half = count // 2
+    return pl.pallas_call(
+        fine_before_kernel,
+        name="fine_before",
         grid=(width // PAIR,),
-        in_specs=[
-            pl.BlockSpec(memory_space=pltpu.SMEM),
-            pl.BlockSpec((count, PAIR), lambda i: (0, i)),
-        ]
-        + [pl.BlockSpec((count, PAIR), lambda i: (0, i))] * 3
-        + [pl.BlockSpec((PAIR, count), lambda i: (i, 0))] * 3,
-        out_specs=pl.BlockSpec((count, PAIR), lambda i: (0, i)),
-        out_shape=jax.ShapeDtypeStruct((count, width), jnp.bfloat16),
+        in_specs=[pl.BlockSpec(memory_space=pltpu.SMEM), pl.BlockSpec((count, PAIR), lambda i: (0, i))]
+        + [pl.BlockSpec((half, PAIR), lambda i: (0, i))] * 2
+        + [pl.BlockSpec((PAIR, half), lambda i: (i, 0))] * 2
+        + [
+            pl.BlockSpec((1, blocks, 8, 2 * QB), lambda i: (i, 0, 0, 0)),
+            pl.BlockSpec((1, blocks, 16 + HEAD_DIM, 2 * QB), lambda i: (i, 0, 0, 0)),
+        ],
+        out_specs=pl.BlockSpec((2, half, PAIR), lambda i: (0, 0, i)),
+        out_shape=jax.ShapeDtypeStruct((2, half, width), jnp.bfloat16),
         scratch_shapes=[
-            pltpu.VMEM((blocks, WIN + QB, 2 * QB), jnp.float32),
-            pltpu.VMEM((blocks, WIN + QB, 2 * QB), jnp.bfloat16),
+            pltpu.VMEM((count, PAIR), jnp.bfloat16),
+            pltpu.VMEM((PAIR, count), jnp.bfloat16),
+            pltpu.VMEM((blocks, count, 2 * QB), jnp.float32),
+            pltpu.VMEM((blocks, count, 2 * QB), jnp.bfloat16),
         ],
         compiler_params=params(),
-        cost_estimate=pl.CostEstimate(flops=10 * 2**30, bytes_accessed=8 * 2**20, transcendentals=8 * 2**20),
-    )(place.reshape(1), q, *keys, *values)
+        cost_estimate=pl.CostEstimate(flops=5 * 2**30, bytes_accessed=6 * 2**20, transcendentals=5 * 2**20),
+    )(where, q, *keys, *values, *state)
 
 
 def pack_kernel(hidden_ref, tail_ref, out_ref):
@@ -178,7 +240,7 @@
         ],
         out_specs=pl.BlockSpec((owners, rows, tile), lambda i: (0, 0, i)),
         out_shape=jax.ShapeDtypeStruct((owners, rows, width), jnp.bfloat16),
-        compiler_params=params(),
+        compiler_params=params(60),
     )(grouped, weight.reshape(parts, depth, width))
 
 
@@ -246,7 +308,7 @@
         ],
         out_specs=pl.BlockSpec((count, tile), lambda i: (0, i)),
         out_shape=jax.ShapeDtypeStruct((count, width), jnp.bfloat16),
-        compiler_params=params(),
+        compiler_params=params(60),
     )(mixed, out_weight, short, hidden)
 
 
@@ -339,25 +401,48 @@
     place = lax.axis_index(ALL).astype(jnp.int32)
     groups = QB // SHORT
     blocks = count // QB
-    first_core = lax.axis_index("c") == 0
+    core = lax.axis_index("c").astype(jnp.int32)
+
+    def across(block):
+        return lax.ppermute(block, "c", [(0, 1), (1, 0)])
+
     far = from_behind(tokens, 2)
-    mate = lax.ppermute(tokens, "c", [(0, 1)])
     shuffled = tokens.reshape(blocks, groups, SHORT, width)
     shuffled = jnp.transpose(shuffled, (0, 2, 1, 3)).reshape(count, width)
-    query = (dot(normed(shuffled), fine_query, ((1,), (0,))) * SCALE).astype(bf)
+    mate = across(shuffled)
+    half = width // 2
+
+    def own_heads(weight, axis):
+        return lax.dynamic_slice_in_dim(weight, core * half, half, axis)
+
+    query_weight, key_weight, value_weight = (
+        own_heads(weight, 1) for weight in (fine_query, fine_key, fine_value)
+    )
+    out_weight = own_heads(fine_out, 0)
+    out_weight_mate = lax.dynamic_slice_in_dim(fine_out, (1 - core) * half, half, 0)
+    chip = normed(
+        jnp.concatenate(
+            [jnp.where(core == 0, shuffled, mate), jnp.where(core == 0, mate, shuffled)], axis=0
+        )
+    )
 
     def keys_values(rows):
-        rows = normed(rows)
-        keys = dot(rows, fine_key, ((1,), (0,))).astype(bf)
-        return keys, dot(fine_value, rows, ((0,), (1,))).astype(bf)
-
-    own = keys_values(tokens)
-    far, own, query, short_weight = lax.optimization_barrier((far, own, query, short_weight))
-    near = jnp.where(first_core, lax.ppermute(far, "c", [(1, 0)]), mate)
+        keys = dot(rows, key_weight, ((1,), (0,))).astype(bf)
+        return keys, dot(value_weight, rows, ((0,), (1,))).astype(bf)
+
+    query = (dot(chip, query_weight, ((1,), (0,))) * SCALE).astype(bf)
+    state = fine_own(query, *keys_values(chip))
+    far, state, query, short_weight, out_weight, out_weight_mate = lax.optimization_barrier(
+        (far, state, query, short_weight, out_weight, out_weight_mate)
+    )
+    near = across(far)
     weight = lax.all_gather(short_weight, ("x", "c"), axis=0, tiled=True)
-    kinds = zip(keys_values(far), keys_values(near), own)
-    fine_mixed = fine_attend(place, query, *kinds)
-    hidden = (shuffled.astype(jnp.float32) + dot(fine_mixed, fine_out, ((1,), (0,)))).astype(bf)
+    keys, values = zip(keys_values(normed(far)), keys_values(normed(near)))
+    where = jnp.stack([core, (place > 1).astype(jnp.int32)])
+    fine_mixed = fine_before(where, query, keys, values, state)
+    theirs = across(fine_mixed[1])
+    hidden = shuffled.astype(jnp.float32) + dot(fine_mixed[0], out_weight, ((1,), (0,)))
+    hidden = (hidden + dot(theirs, out_weight_mate, ((1,), (0,)))).astype(bf)
     tail = from_behind(hidden.reshape(blocks, SHORT, groups, width)[-1, :, -1], 1)
     rows = count // SHORT
     grouped = lax.all_to_all(pack(hidden, tail), "y", 0, 0)
@@ -371,9 +456,6 @@
 
     def around(block, distance):
         return lax.ppermute(block, "y", [(i, (i + distance) % 4) for i in range(4)])
-
-    def across(block):
-        return lax.ppermute(block, "c", [(0, 1), (1, 0)])
 
     def spot(distance, other=0):
         return ((y + distance) % 4) * 2 + (1 - c if other else c)

time: 186 us -> 181 us (0.973)
  waiting for transfers between devices: 22.9 us -> 18.7 us
  matrix products: 17.2 us -> 13.7 us
  starting transfers between devices: 25.7 us -> 28.7 us
  Pallas kernels: 37.2 us -> 34.5 us
    pallas_call x1 -> x2, Pallas kernels: 17.1 us -> 9.97 us  [the longest x1 6.53 us: fine_own(): pl.pallas_call(fine_own_kernel, name='fine_own', grid=(pairs,), in_specs=...]
    ppermute x2 -> x0, starting transfers between devices: 5.96 us -> none  [the longest x1 4.67 us: body(): near = jnp.where(first_core, lax.ppermute(far, 'c', [(1, 0)]), mate)]
    ppermute x2, starting transfers between devices: 7.96 us -> 13.8 us  [from_behind(): return lax.ppermute(block, ALL, route)]
    ppermute x2, waiting for transfers between devices: 9.39 us -> 4.35 us  [from_behind(): return lax.ppermute(block, ALL, route)]
    dot_general x8 -> x9, matrix products: 17.2 us -> 13.7 us  [dot(): lax.dot_general(a, b, (contract, ((), ())), preferred_element_type=jnp.fl...]
    dynamic_slice x0 -> x1, local copies, waits for them, and re-layouts: none -> 3.13 us  [body(): lax.dynamic_slice_in_dim(fine_out, (1 - core) * half, half, 0)]
    ppermute x4 -> x7, starting transfers between devices: 5.57 us -> 8.64 us  [across(): return lax.ppermute(block, 'c', [(0, 1), (1, 0)])]
    pallas_call x1, Pallas kernels: 2.42 us -> 5.05 us  [shorten(): pl.pallas_call(shorten_kernel, name='shorten', grid=(4,), in_specs=[pl.Bl...]
  transfers between devices with their start and end apart: 13 -> 14, of which waited for: 4 -> 5; matrix products, arithmetic and copies ran while one was open for 14% -> 13% of each run, Pallas kernels for 13% -> 10%
where the time goes in v5:
time: 181 us; the launch traced here: 180 us
  blocking collectives  48.7 us (27%)
  Pallas kernels  34.5 us (19%)
  starting transfers between devices  28.7 us (16%)
  waiting for transfers between devices  18.7 us (10%)
  local copies, waits for them, and re-layouts  16.4 us (9%)
  matrix products  13.7 us (8%)
  between operations  13.7 us (8%)
  other arithmetic  5.25 us (3%)
    all_to_all x1, blocking collectives, body(): grouped = lax.all_to_all(pack(hidden, tail), 'y', 0, 0)  20.6 us
    all_to_all x1, blocking collectives, body(): qkv = lax.all_to_all(qkv, ('z', 'x'), 0, 0)  16.3 us
    ppermute x2, starting transfers between devices, from_behind(): return lax.ppermute(block, ALL, route)  13.8 us
    dot_general x9, matrix products, dot(): lax.dot_general(a, b, (contract, ((), ())), preferred_element_type=jnp.fl...  13.7 us
    all_to_all x1, blocking collectives, body(): partial = lax.all_to_all(shorten(grouped, weight), 'y', 0, 0)  11.9 us
    pallas_call x3, Pallas kernels, coarse_attend(): pl.pallas_call(functools.partial(coarse_kernel, len(parts), first, final)...  10.6 us
    unnamed x33, local copies, waits for them, and re-layouts  9.58 us
    ppermute x7, starting transfers between devices, across(): return lax.ppermute(block, 'c', [(0, 1), (1, 0)])  8.64 us
  transfers between devices with their start and end apart: 14, of which 5 were waited for; matrix products, arithmetic and copies ran while one was open for 13% of the time, Pallas kernels for 10%

profile of v5, /device:TPU:1, one launch (start us, length us, event | category | flops | bytes accessed | tf_op | source)
XLA Modules:
  0.0 179.6 jit_solution(4170898919882943174)
XLA Ops:
  10.0 4.3 %collective-permute-start = (bf16[512,1024]{1,0:T(8,128)(2,1)}, bf16[512,1024]{1,0:T(8,128)(2,1)}, u32[]{:S(2)}, u32[]{:S(2)}) collective-permute-start(bf16[512,1024]{1,0:T(8,128)(2,1)} %param.10), channel_id=1, source_target_pairs={{0,2},{1,3},{2,4},{3,5},{4,6},{5,7},{6,8},{7,9},{8,10},{9,11},{10,... | collective-permute-start | bytes 3145736 | tf_op jit(solution)/shard_map/ppermute | solution.py:25
  14.3 3.1 %constant_dynamic-slice_fusion = (bf16[512,1024]{1,0:T(8,128)(2,1)}, bf16[512,1024]{1,0:T(8,128)(2,1)}) fusion(bf16[1024,1024]{1,0:T(8,128)(2,1)} %param.14, s32[]{:T(128)S(6)} %select_n.53, s32[]{:T(128)S(6)} %select_n.52), kind=kLoop, calls=%fused_computation.41 | loop fusion | bytes 4194312 | tf_op jit(solution)/shard_map/dynamic_slice | solution.py:422
  24.6 6.5 %fine_own.1 = (f32[4,8,8,256]{3,2,1,0:T(8,128)S(1)}, f32[4,8,80,256]{3,2,1,0:T(8,128)S(1)}) custom-call(bf16[1024,512]{1,0:T(8,128)(2,1)S(1)} %multiply_convert_fusion.q_ref, bf16[1024,512]{1,0:T(8,128)(2,1)S(1)} %convolution_convert_fusion.1.k_ref, bf16[512,1024]{1,0:T(8,128)(2,1)S(1)} %convolution_convert_fusion.v_ref), custom_call_target="tpu_custom_call" | custom-call | flops 5368709120 | bytes 6291456 | tf_op jit(solution)/shard_map/fine_own/pallas_call | solution.py:136
  32.7 3.5 %collective-permute-done = bf16[512,1024]{1,0:T(8,128)(2,1)} collective-permute-done((bf16[512,1024]{1,0:T(8,128)(2,1)}, bf16[512,1024]{1,0:T(8,128)(2,1)}, u32[]{:S(2)}, u32[]{:S(2)}) %collective-permute-start) | collective-permute-done | bytes 1048608 | tf_op jit(solution)/shard_map/ppermute | solution.py:25
  39.0 2.1 %convolution_convert_fusion.3.vf_ref = bf16[512,512]{1,0:T(8,128)(2,1)S(1)} fusion(bf16[1024,1024]{1,0:T(8,128)(2,1)S(1)} %copy-done, s32[]{:T(128)S(6)} %select_n.52, bf16[512,1024]{1,0:T(8,128)(2,1)} %collective-permute-done, f32[512]{0:T(512)S(1)} %add_rsqrt_fusion.2), kind=kOutput, calls=%fused_computation.18 | convolution fusion | flops 538705920 | bytes 2623492 | tf_op jit(solution)/shard_map/dot_general | solution.py:35
  41.1 2.0 %convolution_convert_fusion.5.kf_ref = bf16[512,512]{1,0:T(8,128)(2,1)S(1)} fusion(bf16[1024,1024]{1,0:T(8,128)(2,1)S(1)} %copy-done.14, s32[]{:T(128)S(6)} %select_n.52, bf16[512,1024]{1,0:T(8,128)(2,1)} %collective-permute-done, f32[512]{0:T(512)S(1)} %add_rsqrt_fusion.2), kind=kOutput, calls=%fused_computation.20 | convolution fusion | flops 538705920 | bytes 2623492 | tf_op jit(solution)/shard_map/dot_general | solution.py:35
  44.6 2.1 %convolution_convert_fusion.2.vn_ref = bf16[512,512]{1,0:T(8,128)(2,1)S(1)} fusion(bf16[1024,1024]{1,0:T(8,128)(2,1)S(1)} %copy-done, s32[]{:T(128)S(6)} %select_n.52, bf16[512,1024]{1,0:T(8,128)(2,1)} %collective-permute-done.2, f32[512]{0:T(512)S(1)} %add_rsqrt_fusion.1), kind=kOutput, calls=%fused_computation.17 | convolution fusion | flops 538705920 | bytes 2623492 | tf_op jit(solution)/shard_map/dot_general | solution.py:35
  46.7 2.0 %convolution_convert_fusion.4.kn_ref = bf16[512,512]{1,0:T(8,128)(2,1)S(1)} fusion(bf16[1024,1024]{1,0:T(8,128)(2,1)S(1)} %copy-done.14, s32[]{:T(128)S(6)} %select_n.52, bf16[512,1024]{1,0:T(8,128)(2,1)} %collective-permute-done.2, f32[512]{0:T(512)S(1)} %add_rsqrt_fusion.1), kind=kOutput, calls=%fused_computation.19 | convolution fusion | flops 538705920 | bytes 2623492 | tf_op jit(solution)/shard_map/dot_general | solution.py:35
  48.7 3.4 %fine_before.1 = bf16[2,512,512]{2,1,0:T(8,128)(2,1)S(1)} custom-call(s32[2]{0:T(128)S(1)} %pad_add_fusion.1.where_ref, bf16[1024,512]{1,0:T(8,128)(2,1)S(1)} %multiply_convert_fusion.q_ref, bf16[512,512]{1,0:T(8,128)(2,1)S(1)} %convolution_convert_fusion.5.kf_ref, bf16[512,512]{1,0:T(8,128)(2,1)S(1)} %convolution_convert_fusion.4.kn_ref, ...), custom_call_target="tpu_custom_call" | custom-call | flops 5368709120 | bytes 6291456 | tf_op jit(solution)/shard_map/fine_before/pallas_call | solution.py:166
  55.1 9.6 %collective-permute-start.4 = (bf16[8,1024]{1,0:T(8,128)(2,1)S(1)}, bf16[8,1024]{1,0:T(8,128)(2,1)S(1)}, u32[]{:S(2)}, u32[]{:S(2)}) collective-permute-start(bf16[8,1024]{1,0:T(8,128)(2,1)S(1)} %bitcast.39), channel_id=1, source_target_pairs={{0,1},{1,2},{2,3},{3,4},{4,5},{5,6},{6,7},{7,8},{8,9},{9,10},{10,1... | collective-permute-start | bytes 49160 | tf_op jit(solution)/shard_map/ppermute | solution.py:25
  65.7 20.6 %all_to_all.20.grouped_ref = bf16[4,4,64,512]{3,2,1,0:T(8,128)(2,1)} all-to-all(bf16[4,4,64,512]{3,2,1,0:T(8,128)(2,1)S(1)} %pack.1), channel_id=1, replica_groups=mesh['z'=4,'x'=4,'y'=4,'c'=2] {'y'}, dimensions={0} | all-to-all | bytes 2097152 | tf_op jit(solution)/shard_map/all_to_all | solution.py:448
  86.3 5.1 %shorten.1 = bf16[4,64,1024]{2,1,0:T(8,128)(2,1)} custom-call(bf16[4,4,64,512]{3,2,1,0:T(8,128)(2,1)} %all_to_all.20.grouped_ref, bf16[4,512,1024]{2,1,0:T(8,128)(2,1)} %bitcast.37), custom_call_target="tpu_custom_call" | custom-call | tf_op jit(solution)/shard_map/shorten/pallas_call | solution.py:233
  91.4 11.9 %all_to_all.21.part_ref = bf16[4,64,1024]{2,1,0:T(8,128)(2,1)S(1)} all-to-all(bf16[4,64,1024]{2,1,0:T(8,128)(2,1)} %shorten.1), channel_id=1, replica_groups=mesh['z'=4,'x'=4,'y'=4,'c'=2] {'y'}, dimensions={0} | all-to-all | bytes 1048576 | tf_op jit(solution)/shard_map/all_to_all | solution.py:449
  106.4 4.2 %coarse_project.1 = (bf16[64,1024]{1,0:T(8,128)(2,1)S(1)}, bf16[16,64,192]{2,1,0:T(8,128)(2,1)S(1)}) custom-call(bf16[4,64,1024]{2,1,0:T(8,128)(2,1)S(1)} %all_to_all.21.part_ref, bf16[1024,1024]{1,0:T(8,128)(2,1)S(1)} %copy-done.1, bf16[1024,1024]{1,0:T(8,128)(2,1)S(1)} %copy-done.2, bf16[1024,1024]{1,0:T(8,128)(2,1)} %v_ref.1), custom_call_target="tpu_custom_call" | custom-call | tf_op jit(solution)/shard_map/coarse_project/pallas_call | solution.py:268
  110.6 16.3 %all_to_all.22.q_ref = bf16[16,64,192]{2,1,0:T(8,128)(2,1)S(1)} all-to-all(bf16[16,64,192]{2,1,0:T(8,128)(2,1)S(1)} %get-tuple-element.39), channel_id=1, replica_groups=mesh['z'=4,'x'=4,'y'=4,'c'=2] {'z','x'}, dimensions={0} | all-to-all | bytes 786432 | tf_op jit(solution)/shard_map/all_to_all | solution.py:452
  127.8 4.6 %collective-permute-start.5 = (bf16[16,64,128]{2,1,0:T(8,128)(2,1)S(1)}, bf16[16,64,128]{2,1,0:T(8,128)(2,1)}, u32[]{:S(2)}, u32[]{:S(2)}) collective-permute-start(bf16[16,64,128]{2,1,0:T(8,128)(2,1)S(1)} %slice.19.refs_0_), channel_id=1, source_target_pairs={{0,1},{1,0},{2,3},{3,2},{4,5},{5,4},{6,7},{7,6},{8,9},{9,8},{10,11... | collective-permute-start | bytes 786440 | tf_op jit(solution)/shard_map/ppermute | solution.py:407
  132.6 2.4 %collective-permute-start.7 = (bf16[16,64,128]{2,1,0:T(8,128)(2,1)S(1)}, bf16[16,64,128]{2,1,0:T(8,128)(2,1)S(1)}, u32[]{:S(2)}, u32[]{:S(2)}) collective-permute-start(bf16[16,64,128]{2,1,0:T(8,128)(2,1)S(1)} %slice.19.refs_0_), channel_id=1, source_target_pairs={{0,6},{2,0},{4,2},{6,4},{1,7},{3,1},{5,3},{7,5},{8,14},{10,8},{12,... | collective-permute-start | bytes 786440 | tf_op jit(solution)/shard_map/ppermute | solution.py:458
  136.1 3.2 %coarse_attend.3 = (f32[4,8,256]{2,1,0:T(8,128)S(1)}, f32[4,80,256]{2,1,0:T(8,128)S(1)}) custom-call(s32[3]{0:T(128)S(1)} %pad_add_fusion.3.where_ref, bf16[16,64,192]{2,1,0:T(8,128)(2,1)S(1)} %copy-done.4, bf16[16,64,128]{2,1,0:T(8,128)(2,1)S(1)} %slice.19.refs_0_, bf16[16,64,128]{2,1,0:T(8,128)(2,1)} %collective-permute-done.5.refs_1_), custom_call_target="tpu_custom_call" | custom-call | flops 1610612736 | bytes 2097152 | tf_op jit(solution)/shard_map/coarse_attend/pallas_call | solution.py:374
  139.4 7.7 %collective-permute-done.6.refs_0_ = bf16[16,64,128]{2,1,0:T(8,128)(2,1)S(1)} collective-permute-done((bf16[16,64,128]{2,1,0:T(8,128)(2,1)S(1)}, bf16[16,64,128]{2,1,0:T(8,128)(2,1)S(1)}, u32[]{:S(2)}, u32[]{:S(2)}) %collective-permute-start.6) | collective-permute-done | bytes 262176 | tf_op jit(solution)/shard_map/ppermute | solution.py:458
  148.5 3.6 %coarse_attend.4 = (f32[4,8,256]{2,1,0:T(8,128)S(1)}, f32[4,80,256]{2,1,0:T(8,128)S(1)}) custom-call(s32[4]{0:T(128)S(1)} %get-tuple-element.60.where_ref, bf16[16,64,192]{2,1,0:T(8,128)(2,1)S(1)} %copy-done.5, bf16[16,64,128]{2,1,0:T(8,128)(2,1)S(1)} %collective-permute-done.6.refs_0_, bf16[16,64,128]{2,1,0:T(8,128)(2,1)S(1)} %collective-permute-done.7.refs_1_, ...), custom_call_target="tpu_custom_call" | custom-call | flops 2415919104 | bytes 2097152 | tf_op jit(solution)/shard_map/coarse_attend/pallas_call | solution.py:374
  152.1 3.7 %coarse_attend.5 = bf16[16,64,64]{2,1,0:T(8,128)(2,1)S(1)} custom-call(s32[4]{0:T(128)S(1)} %get-tuple-element.59.where_ref, bf16[16,64,192]{2,1,0:T(8,128)(2,1)S(1)} %copy-done.5, bf16[16,64,128]{2,1,0:T(8,128)(2,1)S(1)} %collective-permute-done.9.refs_0_, bf16[16,64,128]{2,1,0:T(8,128)(2,1)S(1)} %collective-permute-done.10.refs_1_, ...), custom_call_target="tpu_custom_call" | custom-call | flops 2415919104 | bytes 2097152 | tf_op jit(solution)/shard_map/coarse_attend/pallas_call | solution.py:374
  156.8 3.5 %all-to-all-start.3 = ((bf16[16,2,2048]{2,1,0:T(2,128)(2,1)}), bf16[16,2,2048]{2,1,0:T(2,128)(2,1)S(1)}, u32[]{:S(2)}, u32[]{:S(2)}) async-start(bf16[16,2,2048]{2,1,0:T(2,128)(2,1)} %reshape.47), calls=%async_computation.3 | async-start | bytes 262144 | tf_op jit(solution)/shard_map/all_to_all | solution.py:472
  161.9 5.5 %all-to-all-done.3 = bf16[16,2,2048]{2,1,0:T(2,128)(2,1)S(1)} async-done(((bf16[16,2,2048]{2,1,0:T(2,128)(2,1)}), bf16[16,2,2048]{2,1,0:T(2,128)(2,1)S(1)}, u32[]{:S(2)}, u32[]{:S(2)}) %all-to-all-start.3) | async-done | bytes 131104 | tf_op jit(solution)/shard_map/all_to_all | solution.py:472
  168.3 4.5 %finish.1 = bf16[512,1024]{1,0:T(8,128)(2,1)} custom-call(bf16[16,64,64]{2,1,0:T(8,128)(2,1)} %reshape.48.mixed_ref, bf16[1024,1024]{1,0:T(8,128)(2,1)} %out_weight_ref.1, bf16[64,1024]{1,0:T(8,128)(2,1)} %copy-done.6, bf16[512,1024]{1,0:T(8,128)(2,1)} %bitcast.38), custom_call_target="tpu_custom_call" | custom-call | tf_op jit(solution)/shard_map/finish/pallas_call | solution.py:299
  (75 shorter events, 30.6 us)
Async XLA Ops:
  6.5 15.1 %copy-start = (bf16[1024,1024]{1,0:T(8,128)(2,1)S(1)}, bf16[1024,1024]{1,0:T(8,128)(2,1)}, u32[]{:S(2)}) copy-start(bf16[1024,1024]{1,0:T(8,128)(2,1)} %param.13) | copy-start | bytes 6291460
  6.5 79.8 %all-gather.2.cloned.1.call-start = ((), (), s32[]{:S(2)}) async-start(), calls=%async_computation.4 | async-start | bytes 4718592 | tf_op jit(solution)/shard_map/all_gather | solution.py:439
  8.5 8.9 %copy-start.8 = (bf16[4,16,8,1024]{3,1,2,0:T(8,128)(2,1)}, bf16[4,16,8,1024]{3,1,2,0:T(8,128)(2,1)S(1)}, u32[]{:S(2)}) copy-start(bf16[4,16,8,1024]{3,1,2,0:T(8,128)(2,1)S(1)} %copy.13) | copy-start | bytes 3145732
  8.5 8.9 %collective-permute-start.1 = (bf16[512,1024]{1,0:T(8,128)(2,1)S(1)}, bf16[512,1024]{1,0:T(8,128)(2,1)}, u32[]{:S(2)}, u32[]{:S(2)}) collective-permute-start(bf16[512,1024]{1,0:T(8,128)(2,1)S(1)} %bitcast.36), channel_id=1, source_target_pairs={{0,1},{1,0},{2,3},{3,2},{4,5},{5,4},{6,7},{7,6},{8,9},{9,8},{10,11... | collective-permute-start | bytes 3145736 | tf_op jit(solution)/shard_map/ppermute | solution.py:407
  10.0 26.1 %collective-permute-start = (bf16[512,1024]{1,0:T(8,128)(2,1)}, bf16[512,1024]{1,0:T(8,128)(2,1)}, u32[]{:S(2)}, u32[]{:S(2)}) collective-permute-start(bf16[512,1024]{1,0:T(8,128)(2,1)} %param.10), channel_id=1, source_target_pairs={{0,2},{1,3},{2,4},{3,5},{4,6},{5,7},{6,8},{7,9},{8,10},{9,11},{10,... | collective-permute-start | bytes 3145736 | tf_op jit(solution)/shard_map/ppermute | solution.py:25
  18.8 1.6 copy-start.13
  21.7 1.6 copy-start.12
  36.2 6.9 %collective-permute-start.2 = (bf16[512,1024]{1,0:T(8,128)(2,1)}, bf16[512,1024]{1,0:T(8,128)(2,1)}, u32[]{:S(2)}, u32[]{:S(2)}) collective-permute-start(bf16[512,1024]{1,0:T(8,128)(2,1)} %collective-permute-done), channel_id=1, source_target_pairs={{0,1},{1,0},{2,3},{3,2},{4,5},{5,4},{6,7},{7,6},{8,9},{9,8},{10,11... | collective-permute-start | bytes 3145736 | tf_op jit(solution)/shard_map/ppermute | solution.py:407
  37.3 3.8 %copy-start.14 = (bf16[1024,1024]{1,0:T(8,128)(2,1)S(1)}, bf16[1024,1024]{1,0:T(8,128)(2,1)}, u32[]{:S(2)}) copy-start(bf16[1024,1024]{1,0:T(8,128)(2,1)} %param.12) | copy-start | bytes 6291460
  48.7 3.7 %copy-start.10 = (bf16[512,1024]{1,0:T(8,128)(2,1)S(1)}, bf16[512,1024]{1,0:T(8,128)(2,1)}, u32[]{:S(2)}) copy-start(bf16[512,1024]{1,0:T(8,128)(2,1)} %get-tuple-element.36) | copy-start | bytes 3145732
  52.2 2.0 %copy-start.9 = (bf16[4,16,8,1024]{3,1,2,0:T(8,128)(2,1)S(1)}, bf16[4,16,8,1024]{3,1,2,0:T(8,128)(2,1)}, u32[]{:S(2)}) copy-start(bf16[4,16,8,1024]{3,1,2,0:T(8,128)(2,1)} %copy-done.8) | copy-start | bytes 3145732
  52.2 2.0 %copy-start.11 = (bf16[512,1024]{1,0:T(8,128)(2,1)S(1)}, bf16[512,1024]{1,0:T(8,128)(2,1)}, u32[]{:S(2)}) copy-start(bf16[512,1024]{1,0:T(8,128)(2,1)} %get-tuple-element.37) | copy-start | bytes 3145732
  52.2 2.0 %collective-permute-start.3 = (bf16[512,512]{1,0:T(8,128)(2,1)S(1)}, bf16[512,512]{1,0:T(8,128)(2,1)S(1)}, u32[]{:S(2)}, u32[]{:S(2)}) collective-permute-start(bf16[512,512]{1,0:T(8,128)(2,1)S(1)} %slice_bitcast_fusion), channel_id=1, source_target_pairs={{0,1},{1,0},{2,3},{3,2},{4,5},{5,4},{6,7},{7,6},{8,9},{9,8},{10,11... | collective-permute-start | bytes 1572872 | tf_op jit(solution)/shard_map/ppermute | solution.py:407
  55.1 10.4 %collective-permute-start.4 = (bf16[8,1024]{1,0:T(8,128)(2,1)S(1)}, bf16[8,1024]{1,0:T(8,128)(2,1)S(1)}, u32[]{:S(2)}, u32[]{:S(2)}) collective-permute-start(bf16[8,1024]{1,0:T(8,128)(2,1)S(1)} %bitcast.39), channel_id=1, source_target_pairs={{0,1},{1,2},{2,3},{3,4},{4,5},{5,6},{6,7},{7,8},{8,9},{9,10},{10,1... | collective-permute-start | bytes 49160 | tf_op jit(solution)/shard_map/ppermute | solution.py:25
  110.6 16.3 %copy-start.6 = (bf16[64,1024]{1,0:T(8,128)(2,1)}, bf16[64,1024]{1,0:T(8,128)(2,1)S(1)}, u32[]{:S(2)}) copy-start(bf16[64,1024]{1,0:T(8,128)(2,1)S(1)} %get-tuple-element.54.short_ref) | copy-start | bytes 393220
  127.8 7.3 %collective-permute-start.5 = (bf16[16,64,128]{2,1,0:T(8,128)(2,1)S(1)}, bf16[16,64,128]{2,1,0:T(8,128)(2,1)}, u32[]{:S(2)}, u32[]{:S(2)}) collective-permute-start(bf16[16,64,128]{2,1,0:T(8,128)(2,1)S(1)} %slice.19.refs_0_), channel_id=1, source_target_pairs={{0,1},{1,0},{2,3},{3,2},{4,5},{5,4},{6,7},{7,6},{8,9},{9,8},{10,11... | collective-permute-start | bytes 786440 | tf_op jit(solution)/shard_map/ppermute | solution.py:407
  132.3 14.8 %collective-permute-start.6 = (bf16[16,64,128]{2,1,0:T(8,128)(2,1)S(1)}, bf16[16,64,128]{2,1,0:T(8,128)(2,1)S(1)}, u32[]{:S(2)}, u32[]{:S(2)}) collective-permute-start(bf16[16,64,128]{2,1,0:T(8,128)(2,1)S(1)} %slice.19.refs_0_), channel_id=1, source_target_pairs={{0,2},{2,4},{4,6},{6,0},{1,3},{3,5},{5,7},{7,1},{8,10},{10,12},{12... | collective-permute-start | bytes 786440 | tf_op jit(solution)/shard_map/ppermute | solution.py:458
  132.6 14.5 %collective-permute-start.7 = (bf16[16,64,128]{2,1,0:T(8,128)(2,1)S(1)}, bf16[16,64,128]{2,1,0:T(8,128)(2,1)S(1)}, u32[]{:S(2)}, u32[]{:S(2)}) collective-permute-start(bf16[16,64,128]{2,1,0:T(8,128)(2,1)S(1)} %slice.19.refs_0_), channel_id=1, source_target_pairs={{0,6},{2,0},{4,2},{6,4},{1,7},{3,1},{5,3},{7,5},{8,14},{10,8},{12,... | collective-permute-start | bytes 786440 | tf_op jit(solution)/shard_map/ppermute | solution.py:458
  135.0 12.1 %collective-permute-start.8 = (bf16[16,64,128]{2,1,0:T(8,128)(2,1)S(1)}, bf16[16,64,128]{2,1,0:T(8,128)(2,1)S(1)}, u32[]{:S(2)}, u32[]{:S(2)}) collective-permute-start(bf16[16,64,128]{2,1,0:T(8,128)(2,1)S(1)} %slice.19.refs_0_), channel_id=1, source_target_pairs={{0,4},{2,6},{4,0},{6,2},{1,5},{3,7},{5,1},{7,3},{8,12},{10,14},{12... | collective-permute-start | bytes 786440 | tf_op jit(solution)/shard_map/ppermute | solution.py:458
  136.1 12.3 %copy-start.5 = (bf16[16,64,192]{2,1,0:T(8,128)(2,1)S(1)}, bf16[16,64,192]{2,1,0:T(8,128)(2,1)}, u32[]{:S(2)}) copy-start(bf16[16,64,192]{2,1,0:T(8,128)(2,1)} %copy-done.3) | copy-start | bytes 1179652
  147.1 5.0 %collective-permute-start.10 = (bf16[16,64,128]{2,1,0:T(8,128)(2,1)S(1)}, bf16[16,64,128]{2,1,0:T(8,128)(2,1)S(1)}, u32[]{:S(2)}, u32[]{:S(2)}) collective-permute-start(bf16[16,64,128]{2,1,0:T(8,128)(2,1)S(1)} %collective-permute-done.7.refs_1_), channel_id=1, source_target_pairs={{0,1},{1,0},{2,3},{3,2},{4,5},{5,4},{6,7},{7,6},{8,9},{9,8},{10,11... | collective-permute-start | bytes 786440 | tf_op jit(solution)/shard_map/ppermute | solution.py:407
  147.9 4.2 %collective-permute-start.11 = (bf16[16,64,128]{2,1,0:T(8,128)(2,1)S(1)}, bf16[16,64,128]{2,1,0:T(8,128)(2,1)S(1)}, u32[]{:S(2)}, u32[]{:S(2)}) collective-permute-start(bf16[16,64,128]{2,1,0:T(8,128)(2,1)S(1)} %collective-permute-done.8.refs_2_), channel_id=1, source_target_pairs={{0,1},{1,0},{2,3},{3,2},{4,5},{5,4},{6,7},{7,6},{8,9},{9,8},{10,11... | collective-permute-start | bytes 786440 | tf_op jit(solution)/shard_map/ppermute | solution.py:407
  148.2 3.9 %collective-permute-start.9 = (bf16[16,64,128]{2,1,0:T(8,128)(2,1)S(1)}, bf16[16,64,128]{2,1,0:T(8,128)(2,1)S(1)}, u32[]{:S(2)}, u32[]{:S(2)}) collective-permute-start(bf16[16,64,128]{2,1,0:T(8,128)(2,1)S(1)} %collective-permute-done.6.refs_0_), channel_id=1, source_target_pairs={{0,1},{1,0},{2,3},{3,2},{4,5},{5,4},{6,7},{7,6},{8,9},{9,8},{10,11... | collective-permute-start | bytes 786440 | tf_op jit(solution)/shard_map/ppermute | solution.py:407
  156.8 10.6 %all-to-all-start.3 = ((bf16[16,2,2048]{2,1,0:T(2,128)(2,1)}), bf16[16,2,2048]{2,1,0:T(2,128)(2,1)S(1)}, u32[]{:S(2)}, u32[]{:S(2)}) async-start(bf16[16,2,2048]{2,1,0:T(2,128)(2,1)} %reshape.47), calls=%async_computation.3 | async-start | bytes 262144 | tf_op jit(solution)/shard_map/all_to_all | solution.py:472
  (5 other events, 6.5 us)
Sparse Core Ops, SparseCore 0:
  36.3 35.8 all-gather.1

commit v6 on v5

--- a/solution.py
+++ b/solution.py
@@ -55,6 +55,90 @@
 
 def with_sums(v):
     return jnp.concatenate([v, jnp.ones((16, v.shape[1]), jnp.bfloat16)], axis=0)
+
+
+def moves(rows, take):
+    col = lax.broadcasted_iota(jnp.int32, (rows, QB), 1)
+    row = lax.broadcasted_iota(jnp.int32, (rows, QB), 0)
+    return jnp.where(take(row) == col, 1.0, 0.0).astype(jnp.bfloat16)
+
+
+def reorder(move, rows):
+    parts = [dot(move, rows[i : i + QB], ((1,), (0,))) for i in range(0, rows.shape[0], QB)]
+    return jnp.concatenate(parts, axis=0)
+
+
+def project_kernel(number, rows_ref, *refs):
+    weights, outs = refs[:number], refs[number:]
+    rows = normed(rows_ref[...])
+    if number == 3:
+        rows = reorder(moves(QB, spots), rows).astype(jnp.bfloat16)
+        outs[2][...] = (dot(rows, weights[2][...], ((1,), (0,))) * SCALE).astype(jnp.bfloat16)
+    outs[0][...] = dot(rows, weights[0][...], ((1,), (0,))).astype(jnp.bfloat16)
+    outs[1][...] = dot(weights[1][...], rows, ((1,), (1,))).astype(jnp.bfloat16)
+
+
+def project(rows, weights):
+    count, width = rows.shape
+    half = width // 2
+    tile = 512
+    by_row = pl.BlockSpec((tile, half), lambda i: (i, 0))
+    number = len(weights)
+    return pl.pallas_call(
+        functools.partial(project_kernel, number),
+        name="project",
+        grid=(count // tile,),
+        in_specs=[pl.BlockSpec((tile, width), lambda i: (i, 0))]
+        + [pl.BlockSpec(weight.shape, lambda i: (0, 0)) for weight in weights],
+        out_specs=[by_row, pl.BlockSpec((half, tile), lambda i: (0, i)), by_row][:number],
+        out_shape=[
+            jax.ShapeDtypeStruct((count, half), jnp.bfloat16),
+            jax.ShapeDtypeStruct((half, count), jnp.bfloat16),
+            jax.ShapeDtypeStruct((count, half), jnp.bfloat16),
+        ][:number],
+        compiler_params=params(20),
+        cost_estimate=pl.CostEstimate(
+            flops=2 * number * count * width * half, bytes_accessed=4 * 2**20, transcendentals=0
+        ),
+    )(rows, *weights)
+
+
+def out_project_kernel(tokens_ref, mine_ref, theirs_ref, my_ref, their_ref, hidden_ref, natural_ref, tail_ref):
+    total = reorder(moves(QB, spots), tokens_ref[...])
+    total = total + dot(mine_ref[0], my_ref[...], ((1,), (0,)))
+    total = total + dot(theirs_ref[...], their_ref[...], ((1,), (0,)))
+    hidden = total.astype(jnp.bfloat16)
+    hidden_ref[...] = hidden
+    groups = QB // SHORT
+    natural_ref[...] = reorder(moves(QB, lambda r: (r % SHORT) * groups + r // SHORT), hidden).astype(jnp.bfloat16)
+    tail = dot(moves(16, lambda r: r * groups + groups - 1), hidden[-QB:], ((1,), (0,)))
+    tail_ref[...] = tail.astype(jnp.bfloat16)
+
+
+def out_project(tokens, mixed, theirs, my_weight, their_weight):
+    count, width = tokens.shape
+    half = width // 2
+    tile = width // 2
+    by_column = pl.BlockSpec((count, tile), lambda i: (0, i))
+    return pl.pallas_call(
+        out_project_kernel,
+        name="out_project",
+        grid=(width // tile,),
+        in_specs=[
+            by_column,
+            pl.BlockSpec((1, count, half), lambda i: (0, 0, 0)),
+            pl.BlockSpec((count, half), lambda i: (0, 0)),
+            pl.BlockSpec((half, tile), lambda i: (0, i)),
+            pl.BlockSpec((half, tile), lambda i: (0, i)),
+        ],
+        out_specs=[by_column, by_column, pl.BlockSpec((16, tile), lambda i: (0, i))],
+        out_shape=[
+            jax.ShapeDtypeStruct((count, width), jnp.bfloat16),
+            jax.ShapeDtypeStruct((count, width), jnp.bfloat16),
+            jax.ShapeDtypeStruct((16, width), jnp.bfloat16),
+        ],
+        compiler_params=params(20),
+    )(tokens, mixed, theirs, my_weight, their_weight)
 
 
 def fine_own_kernel(q_ref, k_ref, v_ref, top_ref, acc_ref, s_ref, p_ref):
@@ -216,32 +300,38 @@
     )(hidden.reshape(blocks, SHORT, groups, width), tail)
 
 
-def shorten_kernel(grouped_ref, weight_ref, out_ref):
+def shorten_kernel(where_ref, grouped_ref, *refs):
+    pieces, out_ref = refs[:-1], refs[-1]
     owners, parts, rows, depth = grouped_ref.shape
+    size = depth // 2
     total = None
-    for j in range(parts):
-        part = grouped_ref[:, j].reshape(owners * rows, depth)
-        term = dot(part, weight_ref[j], ((1,), (0,)))
+    for i, piece in enumerate(pieces):
+        x = (where_ref[0] + parts - i % parts) % parts
+        core = where_ref[1] if i < parts else 1 - where_ref[1]
+        columns = pl.ds(pl.multiple_of(core * size, size), size)
+        part = grouped_ref[:, x, :, columns].reshape(owners * rows, size)
+        term = dot(part, piece[...], ((1,), (0,)))
         total = term if total is None else total + term
     out_ref[...] = total.reshape(owners, rows, -1).astype(jnp.bfloat16)
 
 
-def shorten(grouped, weight):
+def shorten(where, grouped, pieces):
     owners, parts, rows, depth = grouped.shape
-    width = weight.shape[1]
+    width = pieces[0].shape[1]
     tile = width // 4
     return pl.pallas_call(
         shorten_kernel,
         name="shorten",
         grid=(4,),
         in_specs=[
+            pl.BlockSpec(memory_space=pltpu.SMEM),
             pl.BlockSpec(grouped.shape, lambda i: (0, 0, 0, 0)),
-            pl.BlockSpec((parts, depth, tile), lambda i: (0, 0, i)),
-        ],
+        ]
+        + [pl.BlockSpec((depth // 2, tile), lambda i: (0, i))] * len(pieces),
         out_specs=pl.BlockSpec((owners, rows, tile), lambda i: (0, 0, i)),
         out_shape=jax.ShapeDtypeStruct((owners, rows, width), jnp.bfloat16),
         compiler_params=params(60),
-    )(grouped, weight.reshape(parts, depth, width))
+    )(where, grouped, *pieces)
 
 
 def coarse_project_kernel(part_ref, q_ref, k_ref, v_ref, short_ref, qkv_ref, norm_ref):
@@ -279,14 +369,23 @@
             jax.ShapeDtypeStruct((HEADS, rows, 3 * HEAD_DIM), jnp.bfloat16),
         ],
         scratch_shapes=[pltpu.VMEM((rows, width), jnp.bfloat16)],
-        compiler_params=params(),
+        compiler_params=params(60),
     )(partial, query, key, value)
 
 
-def finish_kernel(mixed_ref, out_weight_ref, short_ref, hidden_ref, out_ref):
+def finish_kernel(mixed_ref, out_weight_ref, short_ref, hidden_ref, out_ref, rows_ref):
     heads, rows, _ = mixed_ref.shape
-    mixed = jnp.concatenate([mixed_ref[h] for h in range(heads)], axis=1)
-    refined = short_ref[...].astype(jnp.float32) + dot(mixed, out_weight_ref[...], ((1,), (0,)))
+    rows = 2 * rows
+
+    @pl.when(pl.program_id(0) == 0)
+    def _():
+        for h in range(heads):
+            m = mixed_ref[h]
+            rows_ref[:, h * HEAD_DIM : (h + 1) * HEAD_DIM] = jnp.concatenate(
+                [m[:, :HEAD_DIM], m[:, HEAD_DIM:]], axis=0
+            )
+
+    refined = short_ref[...].astype(jnp.float32) + dot(rows_ref[...], out_weight_ref[...], ((1,), (0,)))
     tile = refined.shape[1]
     spread = jnp.broadcast_to(refined[:, None, :], (rows, SHORT, tile)).reshape(rows * SHORT, tile)
     out_ref[...] = (hidden_ref[...].astype(jnp.float32) + spread).astype(jnp.bfloat16)
@@ -294,7 +393,7 @@
 
 def finish(mixed, out_weight, short, hidden):
     count, width = hidden.shape
-    heads, rows, _ = mixed.shape
+    rows = count // SHORT
     tile = width // 4
     return pl.pallas_call(
         finish_kernel,
@@ -308,6 +407,7 @@
         ],
         out_specs=pl.BlockSpec((count, tile), lambda i: (0, i)),
         out_shape=jax.ShapeDtypeStruct((count, width), jnp.bfloat16),
+        scratch_shapes=[pltpu.VMEM((rows, width), jnp.bfloat16)],
         compiler_params=params(60),
     )(mixed, out_weight, short, hidden)
 
@@ -352,7 +452,10 @@
     for t in range(tiles):
         if final:
             o = accs[t][16:] * (1.0 / accs[t][0:1])
-            outs[0][4 * t : 4 * t + 4] = o.T.astype(jnp.bfloat16).reshape(4, rows, HEAD_DIM)
+            o = o.T.astype(jnp.bfloat16)
+            for i in range(0, tile, rows):
+                low, high = o[i : i + rows // 2], o[i + rows // 2 : i + rows]
+                outs[0][4 * t + i // rows] = jnp.concatenate([low, high], axis=1)
         else:
             outs[0][t] = jnp.broadcast_to(tops[t], (8, tile))
             outs[1][t] = accs[t]
@@ -362,7 +465,7 @@
     heads, rows, _ = q.shape
     tile = 4 * rows
     if final:
-        out_shape = jax.ShapeDtypeStruct((heads, rows, HEAD_DIM), jnp.bfloat16)
+        out_shape = jax.ShapeDtypeStruct((heads, rows // 2, PAIR), jnp.bfloat16)
     else:
         out_shape = [
             jax.ShapeDtypeStruct((heads // 4, 8, tile), jnp.float32),
@@ -399,17 +502,13 @@
     count, width = tokens.shape
     bf = jnp.bfloat16
     place = lax.axis_index(ALL).astype(jnp.int32)
-    groups = QB // SHORT
-    blocks = count // QB
     core = lax.axis_index("c").astype(jnp.int32)
 
     def across(block):
         return lax.ppermute(block, "c", [(0, 1), (1, 0)])
 
     far = from_behind(tokens, 2)
-    shuffled = tokens.reshape(blocks, groups, SHORT, width)
-    shuffled = jnp.transpose(shuffled, (0, 2, 1, 3)).reshape(count, width)
-    mate = across(shuffled)
+    mate = across(tokens)
     half = width // 2
 
     def own_heads(weight, axis):
@@ -418,37 +517,34 @@
     query_weight, key_weight, value_weight = (
         own_heads(weight, 1) for weight in (fine_query, fine_key, fine_value)
     )
+    weights = [key_weight, value_weight.T]
     out_weight = own_heads(fine_out, 0)
     out_weight_mate = lax.dynamic_slice_in_dim(fine_out, (1 - core) * half, half, 0)
-    chip = normed(
-        jnp.concatenate(
-            [jnp.where(core == 0, shuffled, mate), jnp.where(core == 0, mate, shuffled)], axis=0
-        )
+    chip = jnp.concatenate(
+        [jnp.where(core == 0, tokens, mate), jnp.where(core == 0, mate, tokens)], axis=0
     )
-
-    def keys_values(rows):
-        keys = dot(rows, key_weight, ((1,), (0,))).astype(bf)
-        return keys, dot(value_weight, rows, ((0,), (1,))).astype(bf)
-
-    query = (dot(chip, query_weight, ((1,), (0,))) * SCALE).astype(bf)
-    state = fine_own(query, *keys_values(chip))
-    far, state, query, short_weight, out_weight, out_weight_mate = lax.optimization_barrier(
-        (far, state, query, short_weight, out_weight, out_weight_mate)
+    keys, values, query = project(chip, [*weights, query_weight])
+    state = fine_own(query, keys, values)
+    state, short_weight = lax.optimization_barrier((state, short_weight))
+    pieces = [short_weight] + [
+        lax.ppermute(short_weight, "x", [(i, (i + d) % 4) for i in range(4)]) for d in (1, 2, 3)
+    ]
+    far, state, query, out_weight, out_weight_mate = lax.optimization_barrier(
+        (far, state, query, out_weight, out_weight_mate)
     )
     near = across(far)
-    weight = lax.all_gather(short_weight, ("x", "c"), axis=0, tiled=True)
-    keys, values = zip(keys_values(normed(far)), keys_values(normed(near)))
+    keys, values = zip(project(far, weights), project(near, weights))
     where = jnp.stack([core, (place > 1).astype(jnp.int32)])
     fine_mixed = fine_before(where, query, keys, values, state)
     theirs = across(fine_mixed[1])
-    hidden = shuffled.astype(jnp.float32) + dot(fine_mixed[0], out_weight, ((1,), (0,)))
-    hidden = (hidden + dot(theirs, out_weight_mate, ((1,), (0,)))).astype(bf)
-    tail = from_behind(hidden.reshape(blocks, SHORT, groups, width)[-1, :, -1], 1)
+    hidden, natural, tail = out_project(tokens, fine_mixed, theirs, out_weight, out_weight_mate)
+    tail = from_behind(tail, 1)
+    pieces = pieces + [across(piece) for piece in pieces]
     rows = count // SHORT
     grouped = lax.all_to_all(pack(hidden, tail), "y", 0, 0)
-    partial = lax.all_to_all(shorten(grouped, weight), "y", 0, 0)
+    where = jnp.stack([lax.axis_index("x").astype(jnp.int32), core])
+    partial = lax.all_to_all(shorten(where, grouped, pieces), "y", 0, 0)
     shortened, qkv = coarse_project(partial, coarse_query, coarse_key, coarse_value)
-    natural = jnp.transpose(hidden.reshape(blocks, SHORT, groups, width), (0, 2, 1, 3)).reshape(count, width)
     qkv = lax.all_to_all(qkv, ("z", "x"), 0, 0)
     kv = qkv[:, :, : 2 * HEAD_DIM]
     y, c = lax.axis_index("y"), lax.axis_index("c")

time: 181 us -> 174 us (0.961)
  starting transfers between devices: 28.7 us -> 49.8 us
  Pallas kernels: 34.5 us -> 49.1 us
  matrix products: 13.7 us -> 0 us
  between operations: 13.7 us -> 0.26 us
  blocking collectives: 48.7 us -> 39.4 us
  other arithmetic: 5.25 us -> 2.43 us
  waiting for transfers between devices: 18.7 us -> 16.7 us
    dot_general x9 -> x0, matrix products: 13.7 us -> none  [dot(): lax.dot_general(a, b, (contract, ((), ())), preferred_element_type=jnp.fl...]
    all_to_all x1, starting transfers between devices: 3.51 us -> 16.8 us  [body(): grouped = lax.all_to_all(pack(hidden, tail), 'y', 0, 0)]
    pallas_call x0 -> x4, Pallas kernels: none -> 12.3 us  [the longest x3 9.9 us: project(): pl.pallas_call(functools.partial(project_kernel, number), name='project',...]
    ppermute x0 -> x3, starting transfers between devices: none -> 11.9 us  [body(): lax.ppermute(short_weight, 'x', [(i, (i + d) % 4) for i in range(4)])]
    all_to_all x2, blocking collectives: 32.5 us -> 21.8 us  [the longest x1 11.1 us: body(): partial = lax.all_to_all(shorten(where, grouped, pieces), 'y', 0, 0)]
    ppermute x2, starting transfers between devices: 13.8 us -> 6.51 us  [from_behind(): return lax.ppermute(block, ALL, route)]
    reduce_sum x3 -> x0, other arithmetic: 3.64 us -> none  [normed(): scale = lax.rsqrt(jnp.mean(values * values, axis=-1, keepdims=True) + 1e-06)]
    ppermute x2, waiting for transfers between devices: 4.35 us -> 1 us  [from_behind(): return lax.ppermute(block, ALL, route)]
  transfers between devices with their start and end apart: 14 -> 20, of which waited for: 5 -> 7; matrix products, arithmetic and copies ran while one was open for 13% -> 5% of each run, Pallas kernels for 10% -> 14%
where the time goes in v6:
time: 174 us; the launch traced here: 173 us
  starting transfers between devices  49.8 us (29%)
  Pallas kernels  49.1 us (28%)
  blocking collectives  39.4 us (23%)
  waiting for transfers between devices  16.7 us (10%)
  local copies, waits for them, and re-layouts  15.7 us (9%)
  other arithmetic  2.43 us (1%)
    all_to_all x1, blocking collectives, body(): qkv = lax.all_to_all(qkv, ('z', 'x'), 0, 0)  17.7 us
    all_to_all x1, starting transfers between devices, body(): grouped = lax.all_to_all(pack(hidden, tail), 'y', 0, 0)  16.8 us
    ppermute x3, starting transfers between devices, body(): lax.ppermute(short_weight, 'x', [(i, (i + d) % 4) for i in range(4)])  11.9 us
    ppermute x11, starting transfers between devices, across(): return lax.ppermute(block, 'c', [(0, 1), (1, 0)])  11.8 us
    unnamed x37, local copies, waits for them, and re-layouts  11.4 us
    all_to_all x1, blocking collectives, body(): partial = lax.all_to_all(shorten(where, grouped, pieces), 'y', 0, 0)  11.1 us
    all_to_all x1, blocking collectives, body(): mixed = lax.all_to_all(mixed, ('z', 'x'), 0, 0)  10.6 us
    pallas_call x3, Pallas kernels, coarse_attend(): pl.pallas_call(functools.partial(coarse_kernel, len(parts), first, final)...  10.2 us
  transfers between devices with their start and end apart: 20, of which 7 were waited for; matrix products, arithmetic and copies ran while one was open for 5% of the time, Pallas kernels for 14%

profile of v6, /device:TPU:1, one launch (start us, length us, event | category | flops | bytes accessed | tf_op | source)
XLA Modules:
  0.0 173.4 jit_solution(13538561332106140215)
XLA Ops:
  1.4 4.3 %collective-permute-start = (bf16[512,1024]{1,0:T(8,128)(2,1)}, bf16[512,1024]{1,0:T(8,128)(2,1)}, u32[]{:S(2)}, u32[]{:S(2)}) collective-permute-start(bf16[512,1024]{1,0:T(8,128)(2,1)} %tokens_ref.1), channel_id=1, source_target_pairs={{0,2},{1,3},{2,4},{3,5},{4,6},{5,7},{6,8},{7,9},{8,10},{9,11},{10,... | collective-permute-start | bytes 3145736 | tf_op jit(solution)/shard_map/ppermute | solution.py:25
  5.7 2.6 %constant_dynamic-slice_fusion.2 = (bf16[1024,512]{1,0:T(8,128)(2,1)}, bf16[1024,512]{1,0:T(8,128)(2,1)S(1)}) fusion(bf16[1024,1024]{1,0:T(8,128)(2,1)} %param.11, s32[]{:T(128)S(6)} %select_n.52, bf16[1024,1024]{1,0:T(8,128)(2,1)} %param.13), kind=kLoop, calls=%fused_computation.6 | loop fusion | bytes 4194308 | tf_op jit(solution)/shard_map/dynamic_slice | solution.py:515
  16.2 4.5 %project.3 = (bf16[1024,512]{1,0:T(8,128)(2,1)S(1)}, bf16[512,1024]{1,0:T(8,128)(2,1)S(1)}, bf16[1024,512]{1,0:T(8,128)(2,1)S(1)}) custom-call(bf16[1024,1024]{1,0:T(8,128)(2,1)S(1)} %pad_maximum_fusion.rows_ref, bf16[1024,512]{1,0:T(8,128)(2,1)S(1)} %constant_dynamic-slice_fusion.4.refs_0_, bf16[512,1024]{1,0:T(8,128)(2,1)S(1)} %bitcast.15, ...), custom_call_target="tpu_custom_call" | custom-call | flops 3221225472 | bytes 4194304 | tf_op jit(solution)/shard_map/project/pallas_call | solution.py:87
  20.7 6.5 %fine_own.1 = (f32[4,8,8,256]{3,2,1,0:T(8,128)S(1)}, f32[4,8,80,256]{3,2,1,0:T(8,128)S(1)}) custom-call(bf16[1024,512]{1,0:T(8,128)(2,1)S(1)} %get-tuple-element.49.q_ref, bf16[1024,512]{1,0:T(8,128)(2,1)S(1)} %get-tuple-element.43.k_ref, bf16[512,1024]{1,0:T(8,128)(2,1)S(1)} %get-tuple-element.44.v_ref), custom_call_target="tpu_custom_call" | custom-call | flops 5368709120 | bytes 6291456 | tf_op jit(solution)/shard_map/fine_own/pallas_call | solution.py:220
  31.7 2.6 %project.4 = (bf16[512,512]{1,0:T(8,128)(2,1)S(1)}, bf16[512,512]{1,0:T(8,128)(2,1)S(1)}) custom-call(bf16[512,1024]{1,0:T(8,128)(2,1)} %collective-permute-done.rows_ref, bf16[1024,512]{1,0:T(8,128)(2,1)S(1)} %copy-done.7, bf16[512,1024]{1,0:T(8,128)(2,1)S(1)} %bitcast.16), custom_call_target="tpu_custom_call" | custom-call | flops 1073741824 | bytes 4194304 | tf_op jit(solution)/shard_map/project/pallas_call | solution.py:87
  34.4 2.7 %project.5 = (bf16[512,512]{1,0:T(8,128)(2,1)S(1)}, bf16[512,512]{1,0:T(8,128)(2,1)S(1)}) custom-call(bf16[512,1024]{1,0:T(8,128)(2,1)} %collective-permute-done.2.rows_ref, bf16[1024,512]{1,0:T(8,128)(2,1)S(1)} %copy-done.7, bf16[512,1024]{1,0:T(8,128)(2,1)S(1)} %bitcast.17), custom_call_target="tpu_custom_call" | custom-call | flops 1073741824 | bytes 4194304 | tf_op jit(solution)/shard_map/project/pallas_call | solution.py:87
  37.2 3.4 %fine_before.1.mine_ref = bf16[2,512,512]{2,1,0:T(8,128)(2,1)S(1)} custom-call(s32[2]{0:T(128)S(1)} %pad_add_fusion.2.where_ref, bf16[1024,512]{1,0:T(8,128)(2,1)S(1)} %copy-done.11, bf16[512,512]{1,0:T(8,128)(2,1)S(1)} %get-tuple-element.51.kf_ref, bf16[512,512]{1,0:T(8,128)(2,1)S(1)} %get-tuple-element.52.kn_ref, ...), custom_call_target="tpu_custom_call" | custom-call | flops 5368709120 | bytes 6291456 | tf_op jit(solution)/shard_map/fine_before/pallas_call | solution.py:250
  40.7 10.4 %collective-permute-start.6 = (bf16[256,1024]{1,0:T(8,128)(2,1)}, bf16[256,1024]{1,0:T(8,128)(2,1)}, u32[]{:S(2)}, u32[]{:S(2)}) collective-permute-start(bf16[256,1024]{1,0:T(8,128)(2,1)} %refs_0_), channel_id=1, source_target_pairs={{0,16},{8,24},{16,0},{24,8},{1,17},{9,25},{17,1},{25,9},{2,18},{10... | collective-permute-start | bytes 1572872 | tf_op jit(solution)/shard_map/ppermute | solution.py:530
  52.7 2.4 %out_project.1 = (bf16[512,1024]{1,0:T(8,128)(2,1)S(1)}, bf16[512,1024]{1,0:T(8,128)(2,1)S(1)}, bf16[16,1024]{1,0:T(8,128)(2,1)S(1)}) custom-call(bf16[512,1024]{1,0:T(8,128)(2,1)S(1)} %copy-done.1, bf16[2,512,512]{2,1,0:T(8,128)(2,1)S(1)} %fine_before.1.mine_ref, bf16[512,512]{1,0:T(8,128)(2,1)S(1)} %collective-permute-done.3.theirs_ref, ...), custom_call_target="tpu_custom_call" | custom-call | tf_op jit(solution)/shard_map/out_project/pallas_call | solution.py:123
  60.5 16.8 %all-to-all-start = ((bf16[4,4,64,512]{3,2,1,0:T(8,128)(2,1)}), bf16[4,4,64,512]{3,2,1,0:T(8,128)(2,1)S(1)}, u32[]{:S(2)}, u32[]{:S(2)}) async-start(bf16[4,4,64,512]{3,2,1,0:T(8,128)(2,1)} %pack.1), calls=%async_computation | async-start | bytes 2097152 | tf_op jit(solution)/shard_map/all_to_all | solution.py:544
  82.6 4.5 %all-to-all-done.grouped_ref = bf16[4,4,64,512]{3,2,1,0:T(8,128)(2,1)S(1)} async-done(((bf16[4,4,64,512]{3,2,1,0:T(8,128)(2,1)}), bf16[4,4,64,512]{3,2,1,0:T(8,128)(2,1)S(1)}, u32[]{:S(2)}, u32[]{:S(2)}) %all-to-all-start) | async-done | bytes 1048608 | tf_op jit(solution)/shard_map/all_to_all | solution.py:544
  88.1 5.3 %shorten.1 = bf16[4,64,1024]{2,1,0:T(8,128)(2,1)} custom-call(s32[2]{0:T(128)} %pad_add_fusion.1.where_ref, bf16[4,4,64,512]{3,2,1,0:T(8,128)(2,1)} %copy-done.13, bf16[256,1024]{1,0:T(8,128)(2,1)} %refs_0_, bf16[256,1024]{1,0:T(8,128)(2,1)} %collective-permute-done.5.refs_1_, bf16[256,1024]{1,0:T(8,128)(2,1)} %collective-permute-done.6.refs_2_, ...), custom_call_target="tpu_custom_call" | custom-call | tf_op jit(solution)/shard_map/shorten/pallas_call | solution.py:322
  93.4 11.1 %all_to_all.20.part_ref = bf16[4,64,1024]{2,1,0:T(8,128)(2,1)} all-to-all(bf16[4,64,1024]{2,1,0:T(8,128)(2,1)} %shorten.1), channel_id=1, replica_groups=mesh['z'=4,'x'=4,'y'=4,'c'=2] {'y'}, dimensions={0} | all-to-all | bytes 1048576 | tf_op jit(solution)/shard_map/all_to_all | solution.py:546
  104.5 5.6 %coarse_project.1 = (bf16[64,1024]{1,0:T(8,128)(2,1)}, bf16[16,64,192]{2,1,0:T(8,128)(2,1)}) custom-call(bf16[4,64,1024]{2,1,0:T(8,128)(2,1)} %all_to_all.20.part_ref, bf16[1024,1024]{1,0:T(8,128)(2,1)} %q_ref.1, bf16[1024,1024]{1,0:T(8,128)(2,1)} %k_ref.1, bf16[1024,1024]{1,0:T(8,128)(2,1)} %v_ref.1), custom_call_target="tpu_custom_call" | custom-call | tf_op jit(solution)/shard_map/coarse_project/pallas_call | solution.py:358
  110.1 17.7 %all_to_all.21.q_ref = bf16[16,64,192]{2,1,0:T(8,128)(2,1)S(1)} all-to-all(bf16[16,64,192]{2,1,0:T(8,128)(2,1)} %get-tuple-element.62), channel_id=1, replica_groups=mesh['z'=4,'x'=4,'y'=4,'c'=2] {'z','x'}, dimensions={0} | all-to-all | bytes 786432 | tf_op jit(solution)/shard_map/all_to_all | solution.py:548
  127.9 6.8 %collective-permute-start.12 = (bf16[16,64,128]{2,1,0:T(8,128)(2,1)S(1)}, bf16[16,64,128]{2,1,0:T(8,128)(2,1)S(1)}, u32[]{:S(2)}, u32[]{:S(2)}) collective-permute-start(bf16[16,64,128]{2,1,0:T(8,128)(2,1)S(1)} %slice.9.refs_0_), channel_id=1, source_target_pairs={{0,1},{1,0},{2,3},{3,2},{4,5},{5,4},{6,7},{7,6},{8,9},{9,8},{10,11... | collective-permute-start | bytes 786440 | tf_op jit(solution)/shard_map/ppermute | solution.py:508
  134.9 2.4 %collective-permute-start.14 = (bf16[16,64,128]{2,1,0:T(8,128)(2,1)S(1)}, bf16[16,64,128]{2,1,0:T(8,128)(2,1)S(1)}, u32[]{:S(2)}, u32[]{:S(2)}) collective-permute-start(bf16[16,64,128]{2,1,0:T(8,128)(2,1)S(1)} %slice.9.refs_0_), channel_id=1, source_target_pairs={{0,6},{2,0},{4,2},{6,4},{1,7},{3,1},{5,3},{7,5},{8,14},{10,8},{12,... | collective-permute-start | bytes 786440 | tf_op jit(solution)/shard_map/ppermute | solution.py:554
  137.4 2.8 %coarse_attend.3 = (f32[4,8,256]{2,1,0:T(8,128)S(1)}, f32[4,80,256]{2,1,0:T(8,128)S(1)}) custom-call(s32[3]{0:T(128)S(1)} %pad_add_fusion.4.where_ref, bf16[16,64,192]{2,1,0:T(8,128)(2,1)S(1)} %all_to_all.21.q_ref, bf16[16,64,128]{2,1,0:T(8,128)(2,1)S(1)} %slice.9.refs_0_, bf16[16,64,128]{2,1,0:T(8,128)(2,1)S(1)} %collective-permute-done.12.refs_1_), custom_call_target="tpu_custom_call" | custom-call | flops 1610612736 | bytes 2097152 | tf_op jit(solution)/shard_map/coarse_attend/pallas_call | solution.py:477
  140.2 4.0 %collective-permute-done.13.refs_0_ = bf16[16,64,128]{2,1,0:T(8,128)(2,1)S(1)} collective-permute-done((bf16[16,64,128]{2,1,0:T(8,128)(2,1)S(1)}, bf16[16,64,128]{2,1,0:T(8,128)(2,1)S(1)}, u32[]{:S(2)}, u32[]{:S(2)}) %collective-permute-start.13) | collective-permute-done | bytes 262176 | tf_op jit(solution)/shard_map/ppermute | solution.py:554
  144.2 4.5 %collective-permute-done.15.refs_2_ = bf16[16,64,128]{2,1,0:T(8,128)(2,1)S(1)} collective-permute-done((bf16[16,64,128]{2,1,0:T(8,128)(2,1)S(1)}, bf16[16,64,128]{2,1,0:T(8,128)(2,1)S(1)}, u32[]{:S(2)}, u32[]{:S(2)}) %collective-permute-start.15) | collective-permute-done | bytes 262176 | tf_op jit(solution)/shard_map/ppermute | solution.py:554
  150.8 3.6 %coarse_attend.4 = (f32[4,8,256]{2,1,0:T(8,128)S(1)}, f32[4,80,256]{2,1,0:T(8,128)S(1)}) custom-call(s32[4]{0:T(128)S(1)} %get-tuple-element.84.where_ref, bf16[16,64,192]{2,1,0:T(8,128)(2,1)S(1)} %all_to_all.21.q_ref, bf16[16,64,128]{2,1,0:T(8,128)(2,1)S(1)} %collective-permute-done.13.refs_0_, bf16[16,64,128]{2,1,0:T(8,128)(2,1)S(1)} %collective-permute-done.14.refs_1_, ...), custom_call_target="tpu_custom_call" | custom-call | flops 2415919104 | bytes 2097152 | tf_op jit(solution)/shard_map/coarse_attend/pallas_call | solution.py:477
  154.5 3.8 %coarse_attend.5 = bf16[16,32,128]{2,1,0:T(8,128)(2,1)S(1)} custom-call(s32[4]{0:T(128)S(1)} %get-tuple-element.83.where_ref, bf16[16,64,192]{2,1,0:T(8,128)(2,1)S(1)} %all_to_all.21.q_ref, bf16[16,64,128]{2,1,0:T(8,128)(2,1)S(1)} %collective-permute-done.16.refs_0_, bf16[16,64,128]{2,1,0:T(8,128)(2,1)S(1)} %collective-permute-done.17.refs_1_, ...), custom_call_target="tpu_custom_call" | custom-call | flops 2415919104 | bytes 2097152 | tf_op jit(solution)/shard_map/coarse_attend/pallas_call | solution.py:477
  158.3 10.6 %all_to_all.22.mixed_ref = bf16[16,32,128]{2,1,0:T(8,128)(2,1)} all-to-all(bf16[16,32,128]{2,1,0:T(8,128)(2,1)S(1)} %coarse_attend.5), channel_id=1, replica_groups=mesh['z'=4,'x'=4,'y'=4,'c'=2] {'z','x'}, dimensions={0} | all-to-all | bytes 262144 | tf_op jit(solution)/shard_map/all_to_all | solution.py:568
  168.9 4.5 %finish.1 = bf16[512,1024]{1,0:T(8,128)(2,1)} custom-call(bf16[16,32,128]{2,1,0:T(8,128)(2,1)} %all_to_all.22.mixed_ref, bf16[1024,1024]{1,0:T(8,128)(2,1)} %out_weight_ref.1, bf16[64,1024]{1,0:T(8,128)(2,1)} %get-tuple-element.77.short_ref, bf16[512,1024]{1,0:T(8,128)(2,1)} %copy-done.4), custom_call_target="tpu_custom_call" | custom-call | tf_op jit(solution)/shard_map/finish/pallas_call | solution.py:398
  (80 shorter events, 29.5 us)
Async XLA Ops:
  0.0 9.7 %copy-start = (bf16[1024,1024]{1,0:T(8,128)(2,1)S(1)}, bf16[1024,1024]{1,0:T(8,128)(2,1)}, u32[]{:S(2)}) copy-start(bf16[1024,1024]{1,0:T(8,128)(2,1)} %param.12) | copy-start | bytes 6291460
  0.0 12.8 %collective-permute-start.1 = (bf16[512,1024]{1,0:T(8,128)(2,1)}, bf16[512,1024]{1,0:T(8,128)(2,1)}, u32[]{:S(2)}, u32[]{:S(2)}) collective-permute-start(bf16[512,1024]{1,0:T(8,128)(2,1)} %tokens_ref.1), channel_id=1, source_target_pairs={{0,1},{1,0},{2,3},{3,2},{4,5},{5,4},{6,7},{7,6},{8,9},{9,8},{10,11... | collective-permute-start | bytes 3145736 | tf_op jit(solution)/shard_map/ppermute | solution.py:508
  1.4 27.3 %collective-permute-start = (bf16[512,1024]{1,0:T(8,128)(2,1)}, bf16[512,1024]{1,0:T(8,128)(2,1)}, u32[]{:S(2)}, u32[]{:S(2)}) collective-permute-start(bf16[512,1024]{1,0:T(8,128)(2,1)} %tokens_ref.1), channel_id=1, source_target_pairs={{0,2},{1,3},{2,4},{3,5},{4,6},{5,7},{6,8},{7,9},{8,10},{9,11},{10,... | collective-permute-start | bytes 3145736 | tf_op jit(solution)/shard_map/ppermute | solution.py:25
  20.7 6.5 %copy-start.10 = (bf16[1024,512]{1,0:T(8,128)(2,1)}, bf16[1024,512]{1,0:T(8,128)(2,1)S(1)}, u32[]{:S(2)}) copy-start(bf16[1024,512]{1,0:T(8,128)(2,1)S(1)} %get-tuple-element.49.q_ref) | copy-start | bytes 3145732
  28.8 5.6 %collective-permute-start.2 = (bf16[512,1024]{1,0:T(8,128)(2,1)}, bf16[512,1024]{1,0:T(8,128)(2,1)}, u32[]{:S(2)}, u32[]{:S(2)}) collective-permute-start(bf16[512,1024]{1,0:T(8,128)(2,1)} %collective-permute-done.rows_ref), channel_id=1, source_target_pairs={{0,1},{1,0},{2,3},{3,2},{4,5},{5,4},{6,7},{7,6},{8,9},{9,8},{10,11... | collective-permute-start | bytes 3145736 | tf_op jit(solution)/shard_map/ppermute | solution.py:508
  37.1 15.5 %copy-start.2 = (bf16[512,1024]{1,0:T(8,128)(2,1)S(1)}, bf16[512,1024]{1,0:T(8,128)(2,1)}, u32[]{:S(2)}) copy-start(bf16[512,1024]{1,0:T(8,128)(2,1)} %get-tuple-element.58.their_ref) | copy-start | bytes 3145732
  37.2 15.5 %copy-start.3 = (bf16[512,1024]{1,0:T(8,128)(2,1)S(1)}, bf16[512,1024]{1,0:T(8,128)(2,1)}, u32[]{:S(2)}) copy-start(bf16[512,1024]{1,0:T(8,128)(2,1)} %get-tuple-element.57.my_ref) | copy-start | bytes 3145732
  40.6 12.0 %collective-permute-start.3 = (bf16[512,512]{1,0:T(8,128)(2,1)S(1)}, bf16[512,512]{1,0:T(8,128)(2,1)S(1)}, u32[]{:S(2)}, u32[]{:S(2)}) collective-permute-start(bf16[512,512]{1,0:T(8,128)(2,1)S(1)} %slice_bitcast_fusion), channel_id=1, source_target_pairs={{0,1},{1,0},{2,3},{3,2},{4,5},{5,4},{6,7},{7,6},{8,9},{9,8},{10,11... | collective-permute-start | bytes 1572872 | tf_op jit(solution)/shard_map/ppermute | solution.py:508
  40.7 36.6 %collective-permute-start.6 = (bf16[256,1024]{1,0:T(8,128)(2,1)}, bf16[256,1024]{1,0:T(8,128)(2,1)}, u32[]{:S(2)}, u32[]{:S(2)}) collective-permute-start(bf16[256,1024]{1,0:T(8,128)(2,1)} %refs_0_), channel_id=1, source_target_pairs={{0,16},{8,24},{16,0},{24,8},{1,17},{9,25},{17,1},{25,9},{2,18},{10... | collective-permute-start | bytes 1572872 | tf_op jit(solution)/shard_map/ppermute | solution.py:530
  51.2 26.7 %collective-permute-start.7 = (bf16[256,1024]{1,0:T(8,128)(2,1)}, bf16[256,1024]{1,0:T(8,128)(2,1)}, u32[]{:S(2)}, u32[]{:S(2)}) collective-permute-start(bf16[256,1024]{1,0:T(8,128)(2,1)} %refs_0_), channel_id=1, source_target_pairs={{0,24},{8,0},{16,8},{24,16},{1,25},{9,1},{17,9},{25,17},{2,26},{10... | collective-permute-start | bytes 1572872 | tf_op jit(solution)/shard_map/ppermute | solution.py:530
  52.0 25.9 %collective-permute-start.5 = (bf16[256,1024]{1,0:T(8,128)(2,1)}, bf16[256,1024]{1,0:T(8,128)(2,1)}, u32[]{:S(2)}, u32[]{:S(2)}) collective-permute-start(bf16[256,1024]{1,0:T(8,128)(2,1)} %refs_0_), channel_id=1, source_target_pairs={{0,8},{8,16},{16,24},{24,0},{1,9},{9,17},{17,25},{25,1},{2,10},{10... | collective-permute-start | bytes 1572872 | tf_op jit(solution)/shard_map/ppermute | solution.py:530
  56.1 3.2 %collective-permute-start.4 = (bf16[16,1024]{1,0:T(8,128)(2,1)S(1)}, bf16[16,1024]{1,0:T(8,128)(2,1)S(1)}, u32[]{:S(2)}, u32[]{:S(2)}) collective-permute-start(bf16[16,1024]{1,0:T(8,128)(2,1)S(1)} %get-tuple-element.60), channel_id=1, source_target_pairs={{0,1},{1,2},{2,3},{3,4},{4,5},{5,6},{6,7},{7,8},{8,9},{9,10},{10,1... | collective-permute-start | bytes 98312 | tf_op jit(solution)/shard_map/ppermute | solution.py:25
  60.5 26.6 %all-to-all-start = ((bf16[4,4,64,512]{3,2,1,0:T(8,128)(2,1)}), bf16[4,4,64,512]{3,2,1,0:T(8,128)(2,1)S(1)}, u32[]{:S(2)}, u32[]{:S(2)}) async-start(bf16[4,4,64,512]{3,2,1,0:T(8,128)(2,1)} %pack.1), calls=%async_computation | async-start | bytes 2097152 | tf_op jit(solution)/shard_map/all_to_all | solution.py:544
  77.3 2.1 %collective-permute-start.8 = (bf16[256,1024]{1,0:T(8,128)(2,1)}, bf16[256,1024]{1,0:T(8,128)(2,1)S(1)}, u32[]{:S(2)}, u32[]{:S(2)}) collective-permute-start(bf16[256,1024]{1,0:T(8,128)(2,1)} %refs_0_), channel_id=1, source_target_pairs={{0,1},{1,0},{2,3},{3,2},{4,5},{5,4},{6,7},{7,6},{8,9},{9,8},{10,11... | collective-permute-start | bytes 1572872 | tf_op jit(solution)/shard_map/ppermute | solution.py:508
  77.4 3.6 %collective-permute-start.10 = (bf16[256,1024]{1,0:T(8,128)(2,1)}, bf16[256,1024]{1,0:T(8,128)(2,1)S(1)}, u32[]{:S(2)}, u32[]{:S(2)}) collective-permute-start(bf16[256,1024]{1,0:T(8,128)(2,1)} %collective-permute-done.6.refs_2_), channel_id=1, source_target_pairs={{0,1},{1,0},{2,3},{3,2},{4,5},{5,4},{6,7},{7,6},{8,9},{9,8},{10,11... | collective-permute-start | bytes 1572872 | tf_op jit(solution)/shard_map/ppermute | solution.py:508
  77.9 3.9 %collective-permute-start.11 = (bf16[256,1024]{1,0:T(8,128)(2,1)}, bf16[256,1024]{1,0:T(8,128)(2,1)S(1)}, u32[]{:S(2)}, u32[]{:S(2)}) collective-permute-start(bf16[256,1024]{1,0:T(8,128)(2,1)} %collective-permute-done.7.refs_3_), channel_id=1, source_target_pairs={{0,1},{1,0},{2,3},{3,2},{4,5},{5,4},{6,7},{7,6},{8,9},{9,8},{10,11... | collective-permute-start | bytes 1572872 | tf_op jit(solution)/shard_map/ppermute | solution.py:508
  78.0 4.7 %collective-permute-start.9 = (bf16[256,1024]{1,0:T(8,128)(2,1)}, bf16[256,1024]{1,0:T(8,128)(2,1)}, u32[]{:S(2)}, u32[]{:S(2)}) collective-permute-start(bf16[256,1024]{1,0:T(8,128)(2,1)} %collective-permute-done.5.refs_1_), channel_id=1, source_target_pairs={{0,1},{1,0},{2,3},{3,2},{4,5},{5,4},{6,7},{7,6},{8,9},{9,8},{10,11... | collective-permute-start | bytes 1572872 | tf_op jit(solution)/shard_map/ppermute | solution.py:508
  127.9 9.5 %collective-permute-start.12 = (bf16[16,64,128]{2,1,0:T(8,128)(2,1)S(1)}, bf16[16,64,128]{2,1,0:T(8,128)(2,1)S(1)}, u32[]{:S(2)}, u32[]{:S(2)}) collective-permute-start(bf16[16,64,128]{2,1,0:T(8,128)(2,1)S(1)} %slice.9.refs_0_), channel_id=1, source_target_pairs={{0,1},{1,0},{2,3},{3,2},{4,5},{5,4},{6,7},{7,6},{8,9},{9,8},{10,11... | collective-permute-start | bytes 786440 | tf_op jit(solution)/shard_map/ppermute | solution.py:508
  134.7 9.5 %collective-permute-start.13 = (bf16[16,64,128]{2,1,0:T(8,128)(2,1)S(1)}, bf16[16,64,128]{2,1,0:T(8,128)(2,1)S(1)}, u32[]{:S(2)}, u32[]{:S(2)}) collective-permute-start(bf16[16,64,128]{2,1,0:T(8,128)(2,1)S(1)} %slice.9.refs_0_), channel_id=1, source_target_pairs={{0,2},{2,4},{4,6},{6,0},{1,3},{3,5},{5,7},{7,1},{8,10},{10,12},{12... | collective-permute-start | bytes 786440 | tf_op jit(solution)/shard_map/ppermute | solution.py:554
  134.9 9.3 %collective-permute-start.14 = (bf16[16,64,128]{2,1,0:T(8,128)(2,1)S(1)}, bf16[16,64,128]{2,1,0:T(8,128)(2,1)S(1)}, u32[]{:S(2)}, u32[]{:S(2)}) collective-permute-start(bf16[16,64,128]{2,1,0:T(8,128)(2,1)S(1)} %slice.9.refs_0_), channel_id=1, source_target_pairs={{0,6},{2,0},{4,2},{6,4},{1,7},{3,1},{5,3},{7,5},{8,14},{10,8},{12,... | collective-permute-start | bytes 786440 | tf_op jit(solution)/shard_map/ppermute | solution.py:554
  137.3 11.4 %collective-permute-start.15 = (bf16[16,64,128]{2,1,0:T(8,128)(2,1)S(1)}, bf16[16,64,128]{2,1,0:T(8,128)(2,1)S(1)}, u32[]{:S(2)}, u32[]{:S(2)}) collective-permute-start(bf16[16,64,128]{2,1,0:T(8,128)(2,1)S(1)} %slice.9.refs_0_), channel_id=1, source_target_pairs={{0,4},{2,6},{4,0},{6,2},{1,5},{3,7},{5,1},{7,3},{8,12},{10,14},{12... | collective-permute-start | bytes 786440 | tf_op jit(solution)/shard_map/ppermute | solution.py:554
  148.7 5.7 %collective-permute-start.16 = (bf16[16,64,128]{2,1,0:T(8,128)(2,1)S(1)}, bf16[16,64,128]{2,1,0:T(8,128)(2,1)S(1)}, u32[]{:S(2)}, u32[]{:S(2)}) collective-permute-start(bf16[16,64,128]{2,1,0:T(8,128)(2,1)S(1)} %collective-permute-done.13.refs_0_), channel_id=1, source_target_pairs={{0,1},{1,0},{2,3},{3,2},{4,5},{5,4},{6,7},{7,6},{8,9},{9,8},{10,11... | collective-permute-start | bytes 786440 | tf_op jit(solution)/shard_map/ppermute | solution.py:508
  150.2 4.2 %collective-permute-start.17 = (bf16[16,64,128]{2,1,0:T(8,128)(2,1)S(1)}, bf16[16,64,128]{2,1,0:T(8,128)(2,1)S(1)}, u32[]{:S(2)}, u32[]{:S(2)}) collective-permute-start(bf16[16,64,128]{2,1,0:T(8,128)(2,1)S(1)} %collective-permute-done.14.refs_1_), channel_id=1, source_target_pairs={{0,1},{1,0},{2,3},{3,2},{4,5},{5,4},{6,7},{7,6},{8,9},{9,8},{10,11... | collective-permute-start | bytes 786440 | tf_op jit(solution)/shard_map/ppermute | solution.py:508
  150.3 4.2 %collective-permute-start.18 = (bf16[16,64,128]{2,1,0:T(8,128)(2,1)S(1)}, bf16[16,64,128]{2,1,0:T(8,128)(2,1)S(1)}, u32[]{:S(2)}, u32[]{:S(2)}) collective-permute-start(bf16[16,64,128]{2,1,0:T(8,128)(2,1)S(1)} %collective-permute-done.15.refs_2_), channel_id=1, source_target_pairs={{0,1},{1,0},{2,3},{3,2},{4,5},{5,4},{6,7},{7,6},{8,9},{9,8},{10,11... | collective-permute-start | bytes 786440 | tf_op jit(solution)/shard_map/ppermute | solution.py:508
  (14 other events, 22.4 us)

commit v7 on v6

--- a/solution.py
+++ b/solution.py
@@ -35,7 +35,7 @@
     return lax.dot_general(a, b, (contract, ((), ())), preferred_element_type=jnp.float32)
 
 
-def params(mib=48):
+def params(mib=24):
     return pltpu.CompilerParams(vmem_limit_bytes=mib * 2**20)
 
 
@@ -97,9 +97,7 @@
             jax.ShapeDtypeStruct((count, half), jnp.bfloat16),
         ][:number],
         compiler_params=params(20),
-        cost_estimate=pl.CostEstimate(
-            flops=2 * number * count * width * half, bytes_accessed=4 * 2**20, transcendentals=0
-        ),
+        cost_estimate=pl.CostEstimate(flops=1, bytes_accessed=1, transcendentals=0)
     )(rows, *weights)
 
 
@@ -166,7 +164,7 @@
 
 
 def fine_before_kernel(
-    where_ref, q_ref, kf_ref, kn_ref, vf_ref, vn_ref, top_ref, acc_ref, out_ref, k_ref, v_ref, s_ref, p_ref
+    where_ref, q_ref, kf_ref, kn_ref, vf_ref, vn_ref, top_ref, acc_ref, out_ref, s_ref, p_ref
 ):
     half = kf_ref.shape[0]
     blocks = q_ref.shape[0] // QB
@@ -186,20 +184,23 @@
         for b in range(blocks):
             store(b, acc_ref[0, b, 0:1, :], acc_ref[0, b, 16:, :])
 
-    @pl.when(where_ref[1] > 0)
-    def _():
-        mine = pl.ds(pl.multiple_of(core * half, half), half)
-        other = pl.ds(pl.multiple_of((1 - core) * half, half), half)
-        k_ref[mine, :] = kf_ref[...]
-        k_ref[other, :] = kn_ref[...]
-        v_ref[:, mine] = vf_ref[...]
-        v_ref[:, other] = vn_ref[...]
+    def units(low, high):
+        def spans(b):
+            if b * QB < half:
+                return [(low, b * QB, half - b * QB), (high, 0, half)]
+            return [(high, b * QB - half, 2 * half - b * QB)]
+
         for b in range(blocks):
             both = two_heads(q_ref, b)
-            s = dot(k_ref[b * QB : (b + 1) * QB, :], both, ((1,), (1,)))
-            s_ref[b, b * QB : (b + 1) * QB, :] = jnp.where(keep, s, NEG)
-            if b < blocks - 1:
-                s_ref[b, (b + 1) * QB :, :] = dot(k_ref[(b + 1) * QB :, :], both, ((1,), (1,)))
+            at = b * QB
+            for (k_ref, _), first, size in spans(b):
+                if at == b * QB:
+                    s = dot(k_ref[first : first + QB, :], both, ((1,), (1,)))
+                    s_ref[b, at : at + QB, :] = jnp.where(keep, s, NEG)
+                    at, first, size = at + QB, first + QB, size - QB
+                if size > 0:
+                    s_ref[b, at : at + size, :] = dot(k_ref[first : first + size, :], both, ((1,), (1,)))
+                at += size
         fades = []
         for b in range(blocks):
             old = top_ref[0, b, 0:1, :]
@@ -207,10 +208,19 @@
             p_ref[b, b * QB :, :] = jnp.exp2(s_ref[b, b * QB :, :] - top).astype(jnp.bfloat16)
             fades.append(jnp.exp2(old - top))
         for b in range(blocks):
-            o = dot(with_sums(v_ref[:, b * QB :]), p_ref[b, b * QB :, :], ((1,), (0,)))
+            v = [v_ref[:, first : first + size] for (_, v_ref), first, size in spans(b)]
+            o = dot(with_sums(jnp.concatenate(v, axis=1)), p_ref[b, b * QB :, :], ((1,), (0,)))
             acc = acc_ref[0, b] * fades[b]
             new = jnp.concatenate([o[:HEAD_DIM, :QB], o[HEAD_DIM:PAIR, QB:]], axis=1)
             store(b, acc[0:1] + o[PAIR : PAIR + 1], acc[16:] + new)
+
+    @pl.when((where_ref[1] > 0) & (core == 0))
+    def _():
+        units((kf_ref, vf_ref), (kn_ref, vn_ref))
+
+    @pl.when((where_ref[1] > 0) & (core == 1))
+    def _():
+        units((kn_ref, vn_ref), (kf_ref, vf_ref))
 
 
 def fine_own(q, k, v):
@@ -261,13 +271,11 @@
         out_specs=pl.BlockSpec((2, half, PAIR), lambda i: (0, 0, i)),
         out_shape=jax.ShapeDtypeStruct((2, half, width), jnp.bfloat16),
         scratch_shapes=[
-            pltpu.VMEM((count, PAIR), jnp.bfloat16),
-            pltpu.VMEM((PAIR, count), jnp.bfloat16),
             pltpu.VMEM((blocks, count, 2 * QB), jnp.float32),
             pltpu.VMEM((blocks, count, 2 * QB), jnp.bfloat16),
         ],
         compiler_params=params(),
-        cost_estimate=pl.CostEstimate(flops=5 * 2**30, bytes_accessed=6 * 2**20, transcendentals=5 * 2**20),
+        cost_estimate=pl.CostEstimate(flops=1, bytes_accessed=1, transcendentals=0),
     )(where, q, *keys, *values, *state)
 
 
@@ -300,34 +308,34 @@
     )(hidden.reshape(blocks, SHORT, groups, width), tail)
 
 
-def shorten_kernel(where_ref, grouped_ref, *refs):
+def shorten_kernel(spots_of, where_ref, grouped_ref, *refs):
     pieces, out_ref = refs[:-1], refs[-1]
     owners, parts, rows, depth = grouped_ref.shape
-    size = depth // 2
     total = None
-    for i, piece in enumerate(pieces):
-        x = (where_ref[0] + parts - i % parts) % parts
-        core = where_ref[1] if i < parts else 1 - where_ref[1]
-        columns = pl.ds(pl.multiple_of(core * size, size), size)
+    for (distance, other, first), piece in zip(spots_of, pieces):
+        size = piece.shape[0]
+        x = (where_ref[0] + parts - distance) % parts
+        core = 1 - where_ref[1] if other else where_ref[1]
+        columns = pl.ds(pl.multiple_of(core * (depth // 2) + first, 128), size)
         part = grouped_ref[:, x, :, columns].reshape(owners * rows, size)
         term = dot(part, piece[...], ((1,), (0,)))
         total = term if total is None else total + term
     out_ref[...] = total.reshape(owners, rows, -1).astype(jnp.bfloat16)
 
 
-def shorten(where, grouped, pieces):
+def shorten(where, grouped, pieces, spots_of):
     owners, parts, rows, depth = grouped.shape
     width = pieces[0].shape[1]
     tile = width // 4
     return pl.pallas_call(
-        shorten_kernel,
+        functools.partial(shorten_kernel, spots_of),
         name="shorten",
         grid=(4,),
         in_specs=[
             pl.BlockSpec(memory_space=pltpu.SMEM),
             pl.BlockSpec(grouped.shape, lambda i: (0, 0, 0, 0)),
         ]
-        + [pl.BlockSpec((depth // 2, tile), lambda i: (0, i))] * len(pieces),
+        + [pl.BlockSpec((piece.shape[0], tile), lambda i: (0, i)) for piece in pieces],
         out_specs=pl.BlockSpec((owners, rows, tile), lambda i: (0, 0, i)),
         out_shape=jax.ShapeDtypeStruct((owners, rows, width), jnp.bfloat16),
         compiler_params=params(60),
@@ -526,9 +534,10 @@
     keys, values, query = project(chip, [*weights, query_weight])
     state = fine_own(query, keys, values)
     state, short_weight = lax.optimization_barrier((state, short_weight))
-    pieces = [short_weight] + [
-        lax.ppermute(short_weight, "x", [(i, (i + d) % 4) for i in range(4)]) for d in (1, 2, 3)
-    ]
+    def along_x(block, distance):
+        return lax.ppermute(block, "x", [(i, (i + distance) % 4) for i in range(4)])
+
+    behind, ahead = along_x(short_weight, 1), along_x(short_weight, 3)
     far, state, query, out_weight, out_weight_mate = lax.optimization_barrier(
         (far, state, query, out_weight, out_weight_mate)
     )
@@ -536,14 +545,20 @@
     keys, values = zip(project(far, weights), project(near, weights))
     where = jnp.stack([core, (place > 1).astype(jnp.int32)])
     fine_mixed = fine_before(where, query, keys, values, state)
+    fine_mixed, behind, ahead = lax.optimization_barrier((fine_mixed, behind, ahead))
+    part = short_weight.shape[0] // 2
+    halves = along_x(behind[:part], 1), along_x(ahead[part:], 3)
     theirs = across(fine_mixed[1])
     hidden, natural, tail = out_project(tokens, fine_mixed, theirs, out_weight, out_weight_mate)
+    tail, halves = lax.optimization_barrier((tail, halves))
     tail = from_behind(tail, 1)
+    pieces = [short_weight, behind, ahead, *halves]
     pieces = pieces + [across(piece) for piece in pieces]
+    spots_of = [(d, other, at) for other in (0, 1) for d, at in ((0, 0), (1, 0), (3, 0), (2, 0), (2, part))]
     rows = count // SHORT
     grouped = lax.all_to_all(pack(hidden, tail), "y", 0, 0)
     where = jnp.stack([lax.axis_index("x").astype(jnp.int32), core])
-    partial = lax.all_to_all(shorten(where, grouped, pieces), "y", 0, 0)
+    partial = lax.all_to_all(shorten(where, grouped, pieces, spots_of), "y", 0, 0)
     shortened, qkv = coarse_project(partial, coarse_query, coarse_key, coarse_value)
     qkv = lax.all_to_all(qkv, ("z", "x"), 0, 0)
     kv = qkv[:, :, : 2 * HEAD_DIM]

time: 174 us -> 172 us (0.989)
  starting transfers between devices: 49.8 us -> 35.6 us
  waiting for transfers between devices: 16.7 us -> 27.6 us
    all_to_all x1, starting transfers between devices: 16.8 us -> 5.21 us  [body(): grouped = lax.all_to_all(pack(hidden, tail), 'y', 0, 0)]
    ppermute x3 -> x4, waiting for transfers between devices: 0.01 us -> 6.78 us  [along_x(): return lax.ppermute(block, 'x', [(i, (i + distance) % 4) for i in range(4)])]
    all_to_all x1, waiting for transfers between devices: 4.48 us -> 8.95 us  [body(): grouped = lax.all_to_all(pack(hidden, tail), 'y', 0, 0)]
    ppermute x3 -> x4, starting transfers between devices: 11.9 us -> 9.38 us  [along_x(): return lax.ppermute(block, 'x', [(i, (i + distance) % 4) for i in range(4)])]
    slice x0 -> x2, local copies, waits for them, and re-layouts: none -> 1.93 us  [body(): halves = (along_x(behind[:part], 1), along_x(ahead[part:], 3))]
    unnamed x37 -> x41, local copies, waits for them, and re-layouts: 11.4 us -> 9.84 us
    ppermute x11 -> x12, starting transfers between devices: 11.8 us -> 11.5 us  [across(): return lax.ppermute(block, 'c', [(0, 1), (1, 0)])]
  transfers between devices with their start and end apart: 20 -> 22, of which waited for: 7 -> 10; matrix products, arithmetic and copies ran while one was open for 5% -> 7% of each run, Pallas kernels for 14% -> 16%
where the time goes in v7:
time: 172 us; the launch traced here: 171 us
  Pallas kernels  47.9 us (28%)
  blocking collectives  40.2 us (23%)
  starting transfers between devices  35.6 us (21%)
  waiting for transfers between devices  27.6 us (16%)
  local copies, waits for them, and re-layouts  16.6 us (10%)
  other arithmetic  2.69 us (2%)
    all_to_all x1, blocking collectives, body(): qkv = lax.all_to_all(qkv, ('z', 'x'), 0, 0)  17.1 us
    all_to_all x1, blocking collectives, body(): lax.all_to_all(shorten(where, grouped, pieces, spots_of), 'y', 0, 0)  12.5 us
    ppermute x12, starting transfers between devices, across(): return lax.ppermute(block, 'c', [(0, 1), (1, 0)])  11.5 us
    all_to_all x1, blocking collectives, body(): mixed = lax.all_to_all(mixed, ('z', 'x'), 0, 0)  10.6 us
    pallas_call x3, Pallas kernels, coarse_attend(): pl.pallas_call(functools.partial(coarse_kernel, len(parts), first, final)...  10.2 us
    pallas_call x3, Pallas kernels, project(): pl.pallas_call(functools.partial(project_kernel, number), name='project',...  10 us
    unnamed x41, local copies, waits for them, and re-layouts  9.84 us
    ppermute x4, starting transfers between devices, along_x(): return lax.ppermute(block, 'x', [(i, (i + distance) % 4) for i in range(4)])  9.38 us
  transfers between devices with their start and end apart: 22, of which 10 were waited for; matrix products, arithmetic and copies ran while one was open for 7% of the time, Pallas kernels for 16%

profile of v7, /device:TPU:1, one launch (start us, length us, event | category | flops | bytes accessed | tf_op | source)
XLA Modules:
  0.0 170.9 jit_solution(10024009481865649862)
XLA Ops:
  1.4 4.3 %collective-permute-start = (bf16[512,1024]{1,0:T(8,128)(2,1)}, bf16[512,1024]{1,0:T(8,128)(2,1)}, u32[]{:S(2)}, u32[]{:S(2)}) collective-permute-start(bf16[512,1024]{1,0:T(8,128)(2,1)} %tokens_ref.1), channel_id=1, source_target_pairs={{0,2},{1,3},{2,4},{3,5},{4,6},{5,7},{6,8},{7,9},{8,10},{9,11},{10,... | collective-permute-start | bytes 3145736 | tf_op jit(solution)/shard_map/ppermute | solution.py:25
  5.7 3.1 %constant_dynamic-slice_fusion.2 = (bf16[1024,512]{1,0:T(8,128)(2,1)}, bf16[1024,512]{1,0:T(8,128)(2,1)}) fusion(bf16[1024,1024]{1,0:T(8,128)(2,1)} %param.11, s32[]{:T(128)S(6)} %select_n.52, bf16[1024,1024]{1,0:T(8,128)(2,1)} %param.13), kind=kLoop, calls=%fused_computation.6 | loop fusion | bytes 4194308 | tf_op jit(solution)/shard_map/dynamic_slice | solution.py:523
  16.0 4.5 %project.3 = (bf16[1024,512]{1,0:T(8,128)(2,1)S(1)}, bf16[512,1024]{1,0:T(8,128)(2,1)S(1)}, bf16[1024,512]{1,0:T(8,128)(2,1)S(1)}) custom-call(bf16[1024,1024]{1,0:T(8,128)(2,1)S(1)} %pad_maximum_fusion.rows_ref, bf16[1024,512]{1,0:T(8,128)(2,1)S(1)} %constant_dynamic-slice_fusion.4.refs_0_, bf16[512,1024]{1,0:T(8,128)(2,1)S(1)} %bitcast.15, ...), custom_call_target="tpu_custom_call" | custom-call | flops 1 | bytes 1 | tf_op jit(solution)/shard_map/project/pallas_call | solution.py:87
  20.5 6.5 %fine_own.1 = (f32[4,8,8,256]{3,2,1,0:T(8,128)S(1)}, f32[4,8,80,256]{3,2,1,0:T(8,128)S(1)}) custom-call(bf16[1024,512]{1,0:T(8,128)(2,1)S(1)} %get-tuple-element.55.q_ref, bf16[1024,512]{1,0:T(8,128)(2,1)S(1)} %get-tuple-element.49.k_ref, bf16[512,1024]{1,0:T(8,128)(2,1)S(1)} %get-tuple-element.50.v_ref), custom_call_target="tpu_custom_call" | custom-call | flops 5368709120 | bytes 6291456 | tf_op jit(solution)/shard_map/fine_own/pallas_call | solution.py:230
  29.0 3.6 %collective-permute-start.3 = (bf16[256,1024]{1,0:T(8,128)(2,1)}, bf16[256,1024]{1,0:T(8,128)(2,1)}, u32[]{:S(2)}, u32[]{:S(2)}) collective-permute-start(bf16[256,1024]{1,0:T(8,128)(2,1)} %refs_0_), channel_id=1, source_target_pairs={{0,8},{8,16},{16,24},{24,0},{1,9},{9,17},{17,25},{25,1},{2,10},{10... | collective-permute-start | bytes 1572872 | tf_op jit(solution)/shard_map/ppermute | solution.py:538
  35.2 2.7 %project.4 = (bf16[512,512]{1,0:T(8,128)(2,1)S(1)}, bf16[512,512]{1,0:T(8,128)(2,1)S(1)}) custom-call(bf16[512,1024]{1,0:T(8,128)(2,1)} %collective-permute-done.rows_ref, bf16[1024,512]{1,0:T(8,128)(2,1)S(1)} %constant_dynamic-slice_fusion.4.refs_0_, bf16[512,1024]{1,0:T(8,128)(2,1)S(1)} %bitcast.16), custom_call_target="tpu_custom_call" | custom-call | flops 1 | bytes 1 | tf_op jit(solution)/shard_map/project/pallas_call | solution.py:87
  37.9 2.8 %project.5 = (bf16[512,512]{1,0:T(8,128)(2,1)S(1)}, bf16[512,512]{1,0:T(8,128)(2,1)S(1)}) custom-call(bf16[512,1024]{1,0:T(8,128)(2,1)} %collective-permute-done.2.rows_ref, bf16[1024,512]{1,0:T(8,128)(2,1)S(1)} %constant_dynamic-slice_fusion.4.refs_0_, bf16[512,1024]{1,0:T(8,128)(2,1)S(1)} %bitcast.17), custom_call_target="tpu_custom_call" | custom-call | flops 1 | bytes 1 | tf_op jit(solution)/shard_map/project/pallas_call | solution.py:87
  42.6 3.9 %collective-permute-done.3.refs_1_ = bf16[256,1024]{1,0:T(8,128)(2,1)} collective-permute-done((bf16[256,1024]{1,0:T(8,128)(2,1)}, bf16[256,1024]{1,0:T(8,128)(2,1)}, u32[]{:S(2)}, u32[]{:S(2)}) %collective-permute-start.3) | collective-permute-done | bytes 524320 | tf_op jit(solution)/shard_map/ppermute | solution.py:538
  48.5 3.2 %collective-permute-start.6 = (bf16[128,1024]{1,0:T(8,128)(2,1)S(1)}, bf16[128,1024]{1,0:T(8,128)(2,1)S(1)}, u32[]{:S(2)}, u32[]{:S(2)}) collective-permute-start(bf16[128,1024]{1,0:T(8,128)(2,1)S(1)} %slice.13), channel_id=1, source_target_pairs={{0,8},{8,16},{16,24},{24,0},{1,9},{9,17},{17,25},{25,1},{2,10},{10... | collective-permute-start | bytes 786440 | tf_op jit(solution)/shard_map/ppermute | solution.py:538
  60.3 2.5 %collective-permute-start.8 = (bf16[16,1024]{1,0:T(8,128)(2,1)S(1)}, bf16[16,1024]{1,0:T(8,128)(2,1)S(1)}, u32[]{:S(2)}, u32[]{:S(2)}) collective-permute-start(bf16[16,1024]{1,0:T(8,128)(2,1)S(1)} %get-tuple-element.71), channel_id=1, source_target_pairs={{0,1},{1,2},{2,3},{3,4},{4,5},{5,6},{6,7},{7,8},{8,9},{9,10},{10,1... | collective-permute-start | bytes 98312 | tf_op jit(solution)/shard_map/ppermute | solution.py:25
  65.1 5.2 %all-to-all-start = ((bf16[4,4,64,512]{3,2,1,0:T(8,128)(2,1)}), bf16[4,4,64,512]{3,2,1,0:T(8,128)(2,1)S(1)}, u32[]{:S(2)}, u32[]{:S(2)}) async-start(bf16[4,4,64,512]{3,2,1,0:T(8,128)(2,1)} %pack.1), calls=%async_computation | async-start | bytes 2097152 | tf_op jit(solution)/shard_map/all_to_all | solution.py:559
  76.2 8.9 %all-to-all-done.grouped_ref = bf16[4,4,64,512]{3,2,1,0:T(8,128)(2,1)S(1)} async-done(((bf16[4,4,64,512]{3,2,1,0:T(8,128)(2,1)}), bf16[4,4,64,512]{3,2,1,0:T(8,128)(2,1)S(1)}, u32[]{:S(2)}, u32[]{:S(2)}) %all-to-all-start) | async-done | bytes 1048608 | tf_op jit(solution)/shard_map/all_to_all | solution.py:559
  86.1 5.5 %shorten.1 = bf16[4,64,1024]{2,1,0:T(8,128)(2,1)} custom-call(s32[2]{0:T(128)} %pad_add_fusion.1.where_ref, bf16[4,4,64,512]{3,2,1,0:T(8,128)(2,1)} %copy-done.12, bf16[256,1024]{1,0:T(8,128)(2,1)} %refs_0_, bf16[256,1024]{1,0:T(8,128)(2,1)} %collective-permute-done.3.refs_1_, bf16[256,1024]{1,0:T(8,128)(2,1)} %collective-permute-done.4.refs_2_, ...), custom_call_target="tpu_custom_call" | custom-call | tf_op jit(solution)/shard_map/shorten/pallas_call | solution.py:330
  91.6 12.5 %all_to_all.20.part_ref = bf16[4,64,1024]{2,1,0:T(8,128)(2,1)} all-to-all(bf16[4,64,1024]{2,1,0:T(8,128)(2,1)} %shorten.1), channel_id=1, replica_groups=mesh['z'=4,'x'=4,'y'=4,'c'=2] {'y'}, dimensions={0} | all-to-all | bytes 1048576 | tf_op jit(solution)/shard_map/all_to_all | solution.py:561
  104.1 5.6 %coarse_project.1 = (bf16[64,1024]{1,0:T(8,128)(2,1)}, bf16[16,64,192]{2,1,0:T(8,128)(2,1)}) custom-call(bf16[4,64,1024]{2,1,0:T(8,128)(2,1)} %all_to_all.20.part_ref, bf16[1024,1024]{1,0:T(8,128)(2,1)} %q_ref.1, bf16[1024,1024]{1,0:T(8,128)(2,1)} %k_ref.1, bf16[1024,1024]{1,0:T(8,128)(2,1)} %v_ref.1), custom_call_target="tpu_custom_call" | custom-call | tf_op jit(solution)/shard_map/coarse_project/pallas_call | solution.py:366
  109.7 17.1 %all_to_all.21.q_ref = bf16[16,64,192]{2,1,0:T(8,128)(2,1)S(1)} all-to-all(bf16[16,64,192]{2,1,0:T(8,128)(2,1)} %get-tuple-element.74), channel_id=1, replica_groups=mesh['z'=4,'x'=4,'y'=4,'c'=2] {'z','x'}, dimensions={0} | all-to-all | bytes 786432 | tf_op jit(solution)/shard_map/all_to_all | solution.py:563
  126.9 5.2 %collective-permute-start.14 = (bf16[16,64,128]{2,1,0:T(8,128)(2,1)S(1)}, bf16[16,64,128]{2,1,0:T(8,128)(2,1)S(1)}, u32[]{:S(2)}, u32[]{:S(2)}) collective-permute-start(bf16[16,64,128]{2,1,0:T(8,128)(2,1)S(1)} %slice.16.refs_0_), channel_id=1, source_target_pairs={{0,1},{1,0},{2,3},{3,2},{4,5},{5,4},{6,7},{7,6},{8,9},{9,8},{10,11... | collective-permute-start | bytes 786440 | tf_op jit(solution)/shard_map/ppermute | solution.py:516
  134.9 2.8 %coarse_attend.3 = (f32[4,8,256]{2,1,0:T(8,128)S(1)}, f32[4,80,256]{2,1,0:T(8,128)S(1)}) custom-call(s32[3]{0:T(128)S(1)} %pad_add_fusion.4.where_ref, bf16[16,64,192]{2,1,0:T(8,128)(2,1)S(1)} %all_to_all.21.q_ref, bf16[16,64,128]{2,1,0:T(8,128)(2,1)S(1)} %slice.16.refs_0_, bf16[16,64,128]{2,1,0:T(8,128)(2,1)S(1)} %collective-permute-done.14.refs_1_), custom_call_target="tpu_custom_call" | custom-call | flops 1610612736 | bytes 2097152 | tf_op jit(solution)/shard_map/coarse_attend/pallas_call | solution.py:485
  137.6 4.0 %collective-permute-done.15.refs_0_ = bf16[16,64,128]{2,1,0:T(8,128)(2,1)S(1)} collective-permute-done((bf16[16,64,128]{2,1,0:T(8,128)(2,1)S(1)}, bf16[16,64,128]{2,1,0:T(8,128)(2,1)S(1)}, u32[]{:S(2)}, u32[]{:S(2)}) %collective-permute-start.15) | collective-permute-done | bytes 262176 | tf_op jit(solution)/shard_map/ppermute | solution.py:569
  141.7 4.5 %collective-permute-done.17.refs_2_ = bf16[16,64,128]{2,1,0:T(8,128)(2,1)S(1)} collective-permute-done((bf16[16,64,128]{2,1,0:T(8,128)(2,1)S(1)}, bf16[16,64,128]{2,1,0:T(8,128)(2,1)S(1)}, u32[]{:S(2)}, u32[]{:S(2)}) %collective-permute-start.17) | collective-permute-done | bytes 262176 | tf_op jit(solution)/shard_map/ppermute | solution.py:569
  148.3 3.6 %coarse_attend.4 = (f32[4,8,256]{2,1,0:T(8,128)S(1)}, f32[4,80,256]{2,1,0:T(8,128)S(1)}) custom-call(s32[4]{0:T(128)S(1)} %get-tuple-element.96.where_ref, bf16[16,64,192]{2,1,0:T(8,128)(2,1)S(1)} %all_to_all.21.q_ref, bf16[16,64,128]{2,1,0:T(8,128)(2,1)S(1)} %collective-permute-done.15.refs_0_, bf16[16,64,128]{2,1,0:T(8,128)(2,1)S(1)} %collective-permute-done.16.refs_1_, ...), custom_call_target="tpu_custom_call" | custom-call | flops 2415919104 | bytes 2097152 | tf_op jit(solution)/shard_map/coarse_attend/pallas_call | solution.py:485
  151.9 3.8 %coarse_attend.5 = bf16[16,32,128]{2,1,0:T(8,128)(2,1)S(1)} custom-call(s32[4]{0:T(128)S(1)} %get-tuple-element.95.where_ref, bf16[16,64,192]{2,1,0:T(8,128)(2,1)S(1)} %all_to_all.21.q_ref, bf16[16,64,128]{2,1,0:T(8,128)(2,1)S(1)} %collective-permute-done.18.refs_0_, bf16[16,64,128]{2,1,0:T(8,128)(2,1)S(1)} %collective-permute-done.19.refs_1_, ...), custom_call_target="tpu_custom_call" | custom-call | flops 2415919104 | bytes 2097152 | tf_op jit(solution)/shard_map/coarse_attend/pallas_call | solution.py:485
  155.7 10.6 %all_to_all.22.mixed_ref = bf16[16,32,128]{2,1,0:T(8,128)(2,1)} all-to-all(bf16[16,32,128]{2,1,0:T(8,128)(2,1)S(1)} %coarse_attend.5), channel_id=1, replica_groups=mesh['z'=4,'x'=4,'y'=4,'c'=2] {'z','x'}, dimensions={0} | all-to-all | bytes 262144 | tf_op jit(solution)/shard_map/all_to_all | solution.py:583
  166.3 4.5 %finish.1 = bf16[512,1024]{1,0:T(8,128)(2,1)} custom-call(bf16[16,32,128]{2,1,0:T(8,128)(2,1)} %all_to_all.22.mixed_ref, bf16[1024,1024]{1,0:T(8,128)(2,1)} %out_weight_ref.1, bf16[64,1024]{1,0:T(8,128)(2,1)} %get-tuple-element.89.short_ref, bf16[512,1024]{1,0:T(8,128)(2,1)} %copy-done.9), custom_call_target="tpu_custom_call" | custom-call | tf_op jit(solution)/shard_map/finish/pallas_call | solution.py:406
  (90 shorter events, 39.5 us)
Async XLA Ops:
  0.0 12.7 %collective-permute-start.1 = (bf16[512,1024]{1,0:T(8,128)(2,1)}, bf16[512,1024]{1,0:T(8,128)(2,1)}, u32[]{:S(2)}, u32[]{:S(2)}) collective-permute-start(bf16[512,1024]{1,0:T(8,128)(2,1)} %tokens_ref.1), channel_id=1, source_target_pairs={{0,1},{1,0},{2,3},{3,2},{4,5},{5,4},{6,7},{7,6},{8,9},{9,8},{10,11... | collective-permute-start | bytes 3145736 | tf_op jit(solution)/shard_map/ppermute | solution.py:516
  1.4 27.1 %collective-permute-start = (bf16[512,1024]{1,0:T(8,128)(2,1)}, bf16[512,1024]{1,0:T(8,128)(2,1)}, u32[]{:S(2)}, u32[]{:S(2)}) collective-permute-start(bf16[512,1024]{1,0:T(8,128)(2,1)} %tokens_ref.1), channel_id=1, source_target_pairs={{0,2},{1,3},{2,4},{3,5},{4,6},{5,7},{6,8},{7,9},{8,10},{9,11},{10,... | collective-permute-start | bytes 3145736 | tf_op jit(solution)/shard_map/ppermute | solution.py:25
  28.5 9.4 %collective-permute-start.2 = (bf16[512,1024]{1,0:T(8,128)(2,1)}, bf16[512,1024]{1,0:T(8,128)(2,1)}, u32[]{:S(2)}, u32[]{:S(2)}) collective-permute-start(bf16[512,1024]{1,0:T(8,128)(2,1)} %collective-permute-done.rows_ref), channel_id=1, source_target_pairs={{0,1},{1,0},{2,3},{3,2},{4,5},{5,4},{6,7},{7,6},{8,9},{9,8},{10,11... | collective-permute-start | bytes 3145736 | tf_op jit(solution)/shard_map/ppermute | solution.py:516
  29.0 17.5 %collective-permute-start.3 = (bf16[256,1024]{1,0:T(8,128)(2,1)}, bf16[256,1024]{1,0:T(8,128)(2,1)}, u32[]{:S(2)}, u32[]{:S(2)}) collective-permute-start(bf16[256,1024]{1,0:T(8,128)(2,1)} %refs_0_), channel_id=1, source_target_pairs={{0,8},{8,16},{16,24},{24,0},{1,9},{9,17},{17,25},{25,1},{2,10},{10... | collective-permute-start | bytes 1572872 | tf_op jit(solution)/shard_map/ppermute | solution.py:538
  32.6 13.9 %collective-permute-start.4 = (bf16[256,1024]{1,0:T(8,128)(2,1)}, bf16[256,1024]{1,0:T(8,128)(2,1)}, u32[]{:S(2)}, u32[]{:S(2)}) collective-permute-start(bf16[256,1024]{1,0:T(8,128)(2,1)} %refs_0_), channel_id=1, source_target_pairs={{0,24},{8,0},{16,8},{24,16},{1,25},{9,1},{17,9},{25,17},{2,26},{10... | collective-permute-start | bytes 1572872 | tf_op jit(solution)/shard_map/ppermute | solution.py:538
  40.7 13.3 %copy-start.5 = (bf16[512,1024]{1,0:T(8,128)(2,1)S(1)}, bf16[512,1024]{1,0:T(8,128)(2,1)}, u32[]{:S(2)}) copy-start(bf16[512,1024]{1,0:T(8,128)(2,1)} %get-tuple-element.66.their_ref) | copy-start | bytes 3145732
  40.7 13.3 %copy-start.6 = (bf16[512,1024]{1,0:T(8,128)(2,1)S(1)}, bf16[512,1024]{1,0:T(8,128)(2,1)}, u32[]{:S(2)}) copy-start(bf16[512,1024]{1,0:T(8,128)(2,1)} %get-tuple-element.65.my_ref) | copy-start | bytes 3145732
  46.5 7.5 %collective-permute-start.5 = (bf16[512,512]{1,0:T(8,128)(2,1)S(1)}, bf16[512,512]{1,0:T(8,128)(2,1)S(1)}, u32[]{:S(2)}, u32[]{:S(2)}) collective-permute-start(bf16[512,512]{1,0:T(8,128)(2,1)S(1)} %slice_bitcast_fusion), channel_id=1, source_target_pairs={{0,1},{1,0},{2,3},{3,2},{4,5},{5,4},{6,7},{7,6},{8,9},{9,8},{10,11... | collective-permute-start | bytes 1572872 | tf_op jit(solution)/shard_map/ppermute | solution.py:516
  48.5 11.1 %collective-permute-start.6 = (bf16[128,1024]{1,0:T(8,128)(2,1)S(1)}, bf16[128,1024]{1,0:T(8,128)(2,1)S(1)}, u32[]{:S(2)}, u32[]{:S(2)}) collective-permute-start(bf16[128,1024]{1,0:T(8,128)(2,1)S(1)} %slice.13), channel_id=1, source_target_pairs={{0,8},{8,16},{16,24},{24,0},{1,9},{9,17},{17,25},{25,1},{2,10},{10... | collective-permute-start | bytes 786440 | tf_op jit(solution)/shard_map/ppermute | solution.py:538
  52.7 7.7 %collective-permute-start.7 = (bf16[128,1024]{1,0:T(8,128)(2,1)S(1)}, bf16[128,1024]{1,0:T(8,128)(2,1)S(1)}, u32[]{:S(2)}, u32[]{:S(2)}) collective-permute-start(bf16[128,1024]{1,0:T(8,128)(2,1)S(1)} %slice.14), channel_id=1, source_target_pairs={{0,24},{8,0},{16,8},{24,16},{1,25},{9,1},{17,9},{25,17},{2,26},{10... | collective-permute-start | bytes 786440 | tf_op jit(solution)/shard_map/ppermute | solution.py:538
  60.3 3.6 %collective-permute-start.8 = (bf16[16,1024]{1,0:T(8,128)(2,1)S(1)}, bf16[16,1024]{1,0:T(8,128)(2,1)S(1)}, u32[]{:S(2)}, u32[]{:S(2)}) collective-permute-start(bf16[16,1024]{1,0:T(8,128)(2,1)S(1)} %get-tuple-element.71), channel_id=1, source_target_pairs={{0,1},{1,2},{2,3},{3,4},{4,5},{5,6},{6,7},{7,8},{8,9},{9,10},{10,1... | collective-permute-start | bytes 98312 | tf_op jit(solution)/shard_map/ppermute | solution.py:25
  65.1 20.0 %all-to-all-start = ((bf16[4,4,64,512]{3,2,1,0:T(8,128)(2,1)}), bf16[4,4,64,512]{3,2,1,0:T(8,128)(2,1)S(1)}, u32[]{:S(2)}, u32[]{:S(2)}) async-start(bf16[4,4,64,512]{3,2,1,0:T(8,128)(2,1)} %pack.1), calls=%async_computation | async-start | bytes 2097152 | tf_op jit(solution)/shard_map/all_to_all | solution.py:559
  70.3 2.1 %collective-permute-start.9 = (bf16[256,1024]{1,0:T(8,128)(2,1)}, bf16[256,1024]{1,0:T(8,128)(2,1)S(1)}, u32[]{:S(2)}, u32[]{:S(2)}) collective-permute-start(bf16[256,1024]{1,0:T(8,128)(2,1)} %refs_0_), channel_id=1, source_target_pairs={{0,1},{1,0},{2,3},{3,2},{4,5},{5,4},{6,7},{7,6},{8,9},{9,8},{10,11... | collective-permute-start | bytes 1572872 | tf_op jit(solution)/shard_map/ppermute | solution.py:516
  70.7 3.2 %collective-permute-start.10 = (bf16[256,1024]{1,0:T(8,128)(2,1)}, bf16[256,1024]{1,0:T(8,128)(2,1)S(1)}, u32[]{:S(2)}, u32[]{:S(2)}) collective-permute-start(bf16[256,1024]{1,0:T(8,128)(2,1)} %collective-permute-done.3.refs_1_), channel_id=1, source_target_pairs={{0,1},{1,0},{2,3},{3,2},{4,5},{5,4},{6,7},{7,6},{8,9},{9,8},{10,11... | collective-permute-start | bytes 1572872 | tf_op jit(solution)/shard_map/ppermute | solution.py:516
  70.8 3.9 %collective-permute-start.11 = (bf16[256,1024]{1,0:T(8,128)(2,1)}, bf16[256,1024]{1,0:T(8,128)(2,1)S(1)}, u32[]{:S(2)}, u32[]{:S(2)}) collective-permute-start(bf16[256,1024]{1,0:T(8,128)(2,1)} %collective-permute-done.4.refs_2_), channel_id=1, source_target_pairs={{0,1},{1,0},{2,3},{3,2},{4,5},{5,4},{6,7},{7,6},{8,9},{9,8},{10,11... | collective-permute-start | bytes 1572872 | tf_op jit(solution)/shard_map/ppermute | solution.py:516
  71.2 3.5 %collective-permute-start.12 = (bf16[128,1024]{1,0:T(8,128)(2,1)S(1)}, bf16[128,1024]{1,0:T(8,128)(2,1)S(1)}, u32[]{:S(2)}, u32[]{:S(2)}) collective-permute-start(bf16[128,1024]{1,0:T(8,128)(2,1)S(1)} %collective-permute-done.6.refs_3_), channel_id=1, source_target_pairs={{0,1},{1,0},{2,3},{3,2},{4,5},{5,4},{6,7},{7,6},{8,9},{9,8},{10,11... | collective-permute-start | bytes 786440 | tf_op jit(solution)/shard_map/ppermute | solution.py:516
  71.3 4.9 %collective-permute-start.13 = (bf16[128,1024]{1,0:T(8,128)(2,1)}, bf16[128,1024]{1,0:T(8,128)(2,1)}, u32[]{:S(2)}, u32[]{:S(2)}) collective-permute-start(bf16[128,1024]{1,0:T(8,128)(2,1)} %copy-done.18), channel_id=1, source_target_pairs={{0,1},{1,0},{2,3},{3,2},{4,5},{5,4},{6,7},{7,6},{8,9},{9,8},{10,11... | collective-permute-start | bytes 786440 | tf_op jit(solution)/shard_map/ppermute | solution.py:516
  126.9 8.0 %collective-permute-start.14 = (bf16[16,64,128]{2,1,0:T(8,128)(2,1)S(1)}, bf16[16,64,128]{2,1,0:T(8,128)(2,1)S(1)}, u32[]{:S(2)}, u32[]{:S(2)}) collective-permute-start(bf16[16,64,128]{2,1,0:T(8,128)(2,1)S(1)} %slice.16.refs_0_), channel_id=1, source_target_pairs={{0,1},{1,0},{2,3},{3,2},{4,5},{5,4},{6,7},{7,6},{8,9},{9,8},{10,11... | collective-permute-start | bytes 786440 | tf_op jit(solution)/shard_map/ppermute | solution.py:516
  132.1 9.5 %collective-permute-start.15 = (bf16[16,64,128]{2,1,0:T(8,128)(2,1)S(1)}, bf16[16,64,128]{2,1,0:T(8,128)(2,1)S(1)}, u32[]{:S(2)}, u32[]{:S(2)}) collective-permute-start(bf16[16,64,128]{2,1,0:T(8,128)(2,1)S(1)} %slice.16.refs_0_), channel_id=1, source_target_pairs={{0,2},{2,4},{4,6},{6,0},{1,3},{3,5},{5,7},{7,1},{8,10},{10,12},{12... | collective-permute-start | bytes 786440 | tf_op jit(solution)/shard_map/ppermute | solution.py:569
  132.4 9.3 %collective-permute-start.16 = (bf16[16,64,128]{2,1,0:T(8,128)(2,1)S(1)}, bf16[16,64,128]{2,1,0:T(8,128)(2,1)S(1)}, u32[]{:S(2)}, u32[]{:S(2)}) collective-permute-start(bf16[16,64,128]{2,1,0:T(8,128)(2,1)S(1)} %slice.16.refs_0_), channel_id=1, source_target_pairs={{0,6},{2,0},{4,2},{6,4},{1,7},{3,1},{5,3},{7,5},{8,14},{10,8},{12,... | collective-permute-start | bytes 786440 | tf_op jit(solution)/shard_map/ppermute | solution.py:569
  134.8 11.4 %collective-permute-start.17 = (bf16[16,64,128]{2,1,0:T(8,128)(2,1)S(1)}, bf16[16,64,128]{2,1,0:T(8,128)(2,1)S(1)}, u32[]{:S(2)}, u32[]{:S(2)}) collective-permute-start(bf16[16,64,128]{2,1,0:T(8,128)(2,1)S(1)} %slice.16.refs_0_), channel_id=1, source_target_pairs={{0,4},{2,6},{4,0},{6,2},{1,5},{3,7},{5,1},{7,3},{8,12},{10,14},{12... | collective-permute-start | bytes 786440 | tf_op jit(solution)/shard_map/ppermute | solution.py:569
  146.1 5.7 %collective-permute-start.18 = (bf16[16,64,128]{2,1,0:T(8,128)(2,1)S(1)}, bf16[16,64,128]{2,1,0:T(8,128)(2,1)S(1)}, u32[]{:S(2)}, u32[]{:S(2)}) collective-permute-start(bf16[16,64,128]{2,1,0:T(8,128)(2,1)S(1)} %collective-permute-done.15.refs_0_), channel_id=1, source_target_pairs={{0,1},{1,0},{2,3},{3,2},{4,5},{5,4},{6,7},{7,6},{8,9},{9,8},{10,11... | collective-permute-start | bytes 786440 | tf_op jit(solution)/shard_map/ppermute | solution.py:516
  147.7 4.2 %collective-permute-start.19 = (bf16[16,64,128]{2,1,0:T(8,128)(2,1)S(1)}, bf16[16,64,128]{2,1,0:T(8,128)(2,1)S(1)}, u32[]{:S(2)}, u32[]{:S(2)}) collective-permute-start(bf16[16,64,128]{2,1,0:T(8,128)(2,1)S(1)} %collective-permute-done.16.refs_1_), channel_id=1, source_target_pairs={{0,1},{1,0},{2,3},{3,2},{4,5},{5,4},{6,7},{7,6},{8,9},{9,8},{10,11... | collective-permute-start | bytes 786440 | tf_op jit(solution)/shard_map/ppermute | solution.py:516
  147.8 4.2 %collective-permute-start.20 = (bf16[16,64,128]{2,1,0:T(8,128)(2,1)S(1)}, bf16[16,64,128]{2,1,0:T(8,128)(2,1)S(1)}, u32[]{:S(2)}, u32[]{:S(2)}) collective-permute-start(bf16[16,64,128]{2,1,0:T(8,128)(2,1)S(1)} %collective-permute-done.17.refs_2_), channel_id=1, source_target_pairs={{0,1},{1,0},{2,3},{3,2},{4,5},{5,4},{6,7},{7,6},{8,9},{9,8},{10,11... | collective-permute-start | bytes 786440 | tf_op jit(solution)/shard_map/ppermute | solution.py:516
  (18 other events, 66.9 us)

commit v8 on v7

--- a/solution.py
+++ b/solution.py
@@ -68,7 +68,7 @@
     return jnp.concatenate(parts, axis=0)
 
 
-def project_kernel(number, rows_ref, *refs):
+def project_kernel(number, core_ref, rows_ref, *refs):
     weights, outs = refs[:number], refs[number:]
     rows = normed(rows_ref[...])
     if number == 3:
@@ -78,65 +78,113 @@
     outs[1][...] = dot(weights[1][...], rows, ((1,), (1,))).astype(jnp.bfloat16)
 
 
-def project(rows, weights):
+def project(core, rows, weights):
     count, width = rows.shape
     half = width // 2
     tile = 512
-    by_row = pl.BlockSpec((tile, half), lambda i: (i, 0))
+    by_row = pl.BlockSpec((tile, half), lambda i, c: (i, 0))
+    columns = pl.BlockSpec((width, half), lambda i, c: (0, c[0]))
     number = len(weights)
     return pl.pallas_call(
         functools.partial(project_kernel, number),
         name="project",
-        grid=(count // tile,),
-        in_specs=[pl.BlockSpec((tile, width), lambda i: (i, 0))]
-        + [pl.BlockSpec(weight.shape, lambda i: (0, 0)) for weight in weights],
-        out_specs=[by_row, pl.BlockSpec((half, tile), lambda i: (0, i)), by_row][:number],
+        grid_spec=pltpu.PrefetchScalarGridSpec(
+            num_scalar_prefetch=1,
+            grid=(count // tile,),
+            in_specs=[pl.BlockSpec((tile, width), lambda i, c: (i, 0))]
+            + [columns, pl.BlockSpec((half, width), lambda i, c: (c[0], 0)), columns][:number],
+            out_specs=[by_row, pl.BlockSpec((half, tile), lambda i, c: (0, i)), by_row][:number],
+        ),
         out_shape=[
             jax.ShapeDtypeStruct((count, half), jnp.bfloat16),
             jax.ShapeDtypeStruct((half, count), jnp.bfloat16),
             jax.ShapeDtypeStruct((count, half), jnp.bfloat16),
         ][:number],
         compiler_params=params(20),
-        cost_estimate=pl.CostEstimate(flops=1, bytes_accessed=1, transcendentals=0)
-    )(rows, *weights)
-
-
-def out_project_kernel(tokens_ref, mine_ref, theirs_ref, my_ref, their_ref, hidden_ref, natural_ref, tail_ref):
+        cost_estimate=pl.CostEstimate(flops=1, bytes_accessed=1, transcendentals=0),
+    )(core.reshape(1), *[rows, *weights])
+
+
+def out_project_kernel(
+    core_ref, tokens_ref, mine_ref, theirs_ref, my_ref, their_ref, natural_ref, grouped_ref, tail_ref
+):
     total = reorder(moves(QB, spots), tokens_ref[...])
     total = total + dot(mine_ref[0], my_ref[...], ((1,), (0,)))
     total = total + dot(theirs_ref[...], their_ref[...], ((1,), (0,)))
     hidden = total.astype(jnp.bfloat16)
-    hidden_ref[...] = hidden
     groups = QB // SHORT
     natural_ref[...] = reorder(moves(QB, lambda r: (r % SHORT) * groups + r // SHORT), hidden).astype(jnp.bfloat16)
     tail = dot(moves(16, lambda r: r * groups + groups - 1), hidden[-QB:], ((1,), (0,)))
     tail_ref[...] = tail.astype(jnp.bfloat16)
-
-
-def out_project(tokens, mixed, theirs, my_weight, their_weight):
+    count, tile = hidden.shape
+    rows = count // SHORT
+    blocks = hidden.reshape(count // QB, SHORT, groups, tile)
+    for j in range(SHORT):
+        p = (j + 1) % SHORT
+        part = blocks[:, p].reshape(rows, tile)
+        if p > 0:
+            part = pltpu.roll(part.astype(jnp.float32), 1, 0).astype(jnp.bfloat16)
+        grouped_ref[j % 2, 0, j // 2] = part
+
+
+def out_project(core, tokens, mixed, theirs, weight):
     count, width = tokens.shape
     half = width // 2
-    tile = width // 2
-    by_column = pl.BlockSpec((count, tile), lambda i: (0, i))
+    rows = count // SHORT
+    by_column = pl.BlockSpec((count, half), lambda i, c: (0, i))
     return pl.pallas_call(
         out_project_kernel,
         name="out_project",
-        grid=(width // tile,),
-        in_specs=[
-            by_column,
-            pl.BlockSpec((1, count, half), lambda i: (0, 0, 0)),
-            pl.BlockSpec((count, half), lambda i: (0, 0)),
-            pl.BlockSpec((half, tile), lambda i: (0, i)),
-            pl.BlockSpec((half, tile), lambda i: (0, i)),
-        ],
-        out_specs=[by_column, by_column, pl.BlockSpec((16, tile), lambda i: (0, i))],
+        grid_spec=pltpu.PrefetchScalarGridSpec(
+            num_scalar_prefetch=1,
+            grid=(2,),
+            in_specs=[
+                by_column,
+                pl.BlockSpec((1, count, half), lambda i, c: (0, 0, 0)),
+                pl.BlockSpec((count, half), lambda i, c: (0, 0)),
+                pl.BlockSpec((half, half), lambda i, c: (c[0], i)),
+                pl.BlockSpec((half, half), lambda i, c: (1 - c[0], i)),
+            ],
+            out_specs=[
+                by_column,
+                pl.BlockSpec((2, 1, 4, rows, half), lambda i, c: (0, i, 0, 0, 0)),
+                pl.BlockSpec((16, half), lambda i, c: (0, i)),
+            ],
+        ),
         out_shape=[
             jax.ShapeDtypeStruct((count, width), jnp.bfloat16),
-            jax.ShapeDtypeStruct((count, width), jnp.bfloat16),
+            jax.ShapeDtypeStruct((2, 2, 4, rows, half), jnp.bfloat16),
             jax.ShapeDtypeStruct((16, width), jnp.bfloat16),
         ],
         compiler_params=params(20),
-    )(tokens, mixed, theirs, my_weight, their_weight)
+    )(core.reshape(1), tokens, mixed, theirs, weight, weight)
+
+
+def fix_first_kernel(grouped_ref, tail_ref, out_ref):
+    half = grouped_ref.shape[-1]
+    for j in range(SHORT):
+        for f in range(2):
+            old = grouped_ref[j % 2, f, j // 2].astype(jnp.float32)
+            if j < SHORT - 1:
+                row = tail_ref[j + 1 : j + 2, f * half : (f + 1) * half].astype(jnp.float32)
+                first = lax.broadcasted_iota(jnp.int32, old.shape, 0) == 0
+                old = jnp.where(first, row, old)
+            out_ref[j % 2, f, j // 2] = old.astype(jnp.bfloat16)
+
+
+def fix_first(grouped, tail):
+    block = (*grouped.shape[:3], 16, grouped.shape[4])
+    spec = pl.BlockSpec(block, lambda i: (0, 0, 0, 0, 0))
+    return pl.pallas_call(
+        fix_first_kernel,
+        name="fix_first",
+        grid=(1,),
+        in_specs=[spec, pl.BlockSpec(tail.shape, lambda i: (0, 0))],
+        out_specs=spec,
+        out_shape=jax.ShapeDtypeStruct(grouped.shape, jnp.bfloat16),
+        input_output_aliases={0: 0},
+        compiler_params=params(20),
+    )(grouped, tail)
 
 
 def fine_own_kernel(q_ref, k_ref, v_ref, top_ref, acc_ref, s_ref, p_ref):
@@ -249,7 +297,7 @@
             pltpu.VMEM((blocks, count, 2 * QB), jnp.bfloat16),
         ],
         compiler_params=params(),
-        cost_estimate=pl.CostEstimate(flops=5 * 2**30, bytes_accessed=6 * 2**20, transcendentals=5 * 2**20),
+        cost_estimate=pl.CostEstimate(flops=1, bytes_accessed=1, transcendentals=0),
     )(q, k, v)
 
 
@@ -277,35 +325,6 @@
         compiler_params=params(),
         cost_estimate=pl.CostEstimate(flops=1, bytes_accessed=1, transcendentals=0),
     )(where, q, *keys, *values, *state)
-
-
-def pack_kernel(hidden_ref, tail_ref, out_ref):
-    blocks, places, groups, width = hidden_ref.shape
-    rows = blocks * groups
-    half = width // 2
-    for j in range(SHORT):
-        p = (j + 1) % SHORT
-        part = hidden_ref[:, p].reshape(rows, width)
-        if p > 0:
-            wide = part.astype(jnp.float32)
-            tail = tail_ref[p : p + 1, :].astype(jnp.float32)
-            first = lax.broadcasted_iota(jnp.int32, wide.shape, 0) == 0
-            wide = jnp.where(first, tail, pltpu.roll(wide, 1, 0))
-            part = wide.astype(jnp.bfloat16)
-        for f in range(2):
-            out_ref[(j % 2) * 2 + f, j // 2] = part[:, f * half : (f + 1) * half]
-
-
-def pack(hidden, tail):
-    count, width = hidden.shape
-    groups = QB // SHORT
-    blocks = count // QB
-    return pl.pallas_call(
-        pack_kernel,
-        name="pack",
-        out_shape=jax.ShapeDtypeStruct((4, 4, count // SHORT, width // 2), jnp.bfloat16),
-        compiler_params=params(),
-    )(hidden.reshape(blocks, SHORT, groups, width), tail)
 
 
 def shorten_kernel(spots_of, where_ref, grouped_ref, *refs):
@@ -326,11 +345,11 @@
 def shorten(where, grouped, pieces, spots_of):
     owners, parts, rows, depth = grouped.shape
     width = pieces[0].shape[1]
-    tile = width // 4
+    tile = width // 2
     return pl.pallas_call(
         functools.partial(shorten_kernel, spots_of),
         name="shorten",
-        grid=(4,),
+        grid=(2,),
         in_specs=[
             pl.BlockSpec(memory_space=pltpu.SMEM),
             pl.BlockSpec(grouped.shape, lambda i: (0, 0, 0, 0)),
@@ -517,46 +536,35 @@
 
     far = from_behind(tokens, 2)
     mate = across(tokens)
-    half = width // 2
-
-    def own_heads(weight, axis):
-        return lax.dynamic_slice_in_dim(weight, core * half, half, axis)
-
-    query_weight, key_weight, value_weight = (
-        own_heads(weight, 1) for weight in (fine_query, fine_key, fine_value)
-    )
-    weights = [key_weight, value_weight.T]
-    out_weight = own_heads(fine_out, 0)
-    out_weight_mate = lax.dynamic_slice_in_dim(fine_out, (1 - core) * half, half, 0)
+    weights = [fine_key, fine_value.T]
     chip = jnp.concatenate(
         [jnp.where(core == 0, tokens, mate), jnp.where(core == 0, mate, tokens)], axis=0
     )
-    keys, values, query = project(chip, [*weights, query_weight])
+
+    def from_ahead(block):
+        return lax.ppermute(block, "x", [(i, (i + 3) % 4) for i in range(4)])
+
+    together = lax.optimization_barrier
+    pieces = [short_weight, from_ahead(short_weight)]
+    keys, values, query = project(core, chip, [*weights, fine_query])
+    keys, pieces[1] = together((keys, pieces[1]))
+    pieces.append(from_ahead(pieces[1]))
     state = fine_own(query, keys, values)
-    state, short_weight = lax.optimization_barrier((state, short_weight))
-    def along_x(block, distance):
-        return lax.ppermute(block, "x", [(i, (i + distance) % 4) for i in range(4)])
-
-    behind, ahead = along_x(short_weight, 1), along_x(short_weight, 3)
-    far, state, query, out_weight, out_weight_mate = lax.optimization_barrier(
-        (far, state, query, out_weight, out_weight_mate)
-    )
+    far, state, query, pieces[2] = together((far, state, query, pieces[2]))
+    pieces.append(from_ahead(pieces[2]))
     near = across(far)
-    keys, values = zip(project(far, weights), project(near, weights))
+    far_keys, far_values = project(core, far, weights)
+    near_keys, near_values = project(core, near, weights)
     where = jnp.stack([core, (place > 1).astype(jnp.int32)])
-    fine_mixed = fine_before(where, query, keys, values, state)
-    fine_mixed, behind, ahead = lax.optimization_barrier((fine_mixed, behind, ahead))
-    part = short_weight.shape[0] // 2
-    halves = along_x(behind[:part], 1), along_x(ahead[part:], 3)
+    fine_mixed = fine_before(where, query, (far_keys, near_keys), (far_values, near_values), state)
+    fine_mixed, pieces[3] = together((fine_mixed, pieces[3]))
     theirs = across(fine_mixed[1])
-    hidden, natural, tail = out_project(tokens, fine_mixed, theirs, out_weight, out_weight_mate)
-    tail, halves = lax.optimization_barrier((tail, halves))
+    natural, grouped, tail = out_project(core, tokens, fine_mixed, theirs, fine_out)
     tail = from_behind(tail, 1)
-    pieces = [short_weight, behind, ahead, *halves]
+    grouped = fix_first(grouped, tail).reshape(4, 4, count // SHORT, width // 2)
+    grouped = lax.all_to_all(grouped, "y", 0, 0)
     pieces = pieces + [across(piece) for piece in pieces]
-    spots_of = [(d, other, at) for other in (0, 1) for d, at in ((0, 0), (1, 0), (3, 0), (2, 0), (2, part))]
-    rows = count // SHORT
-    grouped = lax.all_to_all(pack(hidden, tail), "y", 0, 0)
+    spots_of = [(-d % 4, other, 0) for other in (0, 1) for d in range(4)]
     where = jnp.stack([lax.axis_index("x").astype(jnp.int32), core])
     partial = lax.all_to_all(shorten(where, grouped, pieces, spots_of), "y", 0, 0)
     shortened, qkv = coarse_project(partial, coarse_query, coarse_key, coarse_value)

time: 172 us -> 166 us (0.965)
  local copies, waits for them, and re-layouts: 16.6 us -> 10.1 us
  waiting for transfers between devices: 27.6 us -> 30.7 us
  starting transfers between devices: 35.6 us -> 33.6 us
    ppermute x4 -> x3, starting transfers between devices: 9.38 us -> 3.85 us  [from_ahead(): return lax.ppermute(block, 'x', [(i, (i + 3) % 4) for i in range(4)])]
    dynamic_slice x3 -> x0, local copies, waits for them, and re-layouts: 4.76 us -> none  [the longest x2 3.25 us: own_heads(): return lax.dynamic_slice_in_dim(weight, core * half, half, axis)]
    ppermute x2, starting transfers between devices: 6.8 us -> 10 us  [from_behind(): return lax.ppermute(block, ALL, route)]
    ppermute x2, waiting for transfers between devices: 1 us -> 3.22 us  [from_behind(): return lax.ppermute(block, ALL, route)]
    slice x2 -> x0, local copies, waits for them, and re-layouts: 1.93 us -> none  [body(): halves = (along_x(behind[:part], 1), along_x(ahead[part:], 3))]
    ppermute x12 -> x11, waiting for transfers between devices: 2.38 us -> 4.28 us  [across(): return lax.ppermute(block, 'c', [(0, 1), (1, 0)])]
    ppermute x12 -> x11, starting transfers between devices: 11.5 us -> 11.3 us  [across(): return lax.ppermute(block, 'c', [(0, 1), (1, 0)])]
    unnamed x41 -> x29, local copies, waits for them, and re-layouts: 9.84 us -> 10 us
  transfers between devices with their start and end apart: 22 -> 20, of which waited for: 10 -> 11; matrix products, arithmetic and copies ran while one was open for 7% -> 3% of each run, Pallas kernels for 16% -> 15%
where the time goes in v8:
time: 166 us; the launch traced here: 165 us
  Pallas kernels  48.1 us (29%)
  blocking collectives  39.6 us (24%)
  starting transfers between devices  33.6 us (20%)
  waiting for transfers between devices  30.7 us (18%)
  local copies, waits for them, and re-layouts  10.1 us (6%)
  other arithmetic  2.43 us (1%)
    all_to_all x1, blocking collectives, body(): qkv = lax.all_to_all(qkv, ('z', 'x'), 0, 0)  17.8 us
    ppermute x11, starting transfers between devices, across(): return lax.ppermute(block, 'c', [(0, 1), (1, 0)])  11.3 us
    all_to_all x1, blocking collectives, body(): lax.all_to_all(shorten(where, grouped, pieces, spots_of), 'y', 0, 0)  11.1 us
    all_to_all x1, blocking collectives, body(): mixed = lax.all_to_all(mixed, ('z', 'x'), 0, 0)  10.6 us
    pallas_call x3, Pallas kernels, coarse_attend(): pl.pallas_call(functools.partial(coarse_kernel, len(parts), first, final)...  10.2 us
    pallas_call x3, Pallas kernels, project(): pl.pallas_call(functools.partial(project_kernel, number), name='project',...  10.1 us
    ppermute x2, starting transfers between devices, from_behind(): return lax.ppermute(block, ALL, route)  10 us
    unnamed x29, local copies, waits for them, and re-layouts  10 us
  transfers between devices with their start and end apart: 20, of which 11 were waited for; matrix products, arithmetic and copies ran while one was open for 3% of the time, Pallas kernels for 15%

profile of v8, /device:TPU:1, one launch (start us, length us, event | category | flops | bytes accessed | tf_op | source)
XLA Modules:
  0.0 164.8 jit_solution(18363688450527812214)
XLA Ops:
  4.0 4.2 %collective-permute-start = (bf16[512,1024]{1,0:T(8,128)(2,1)}, bf16[512,1024]{1,0:T(8,128)(2,1)}, u32[]{:S(2)}, u32[]{:S(2)}) collective-permute-start(bf16[512,1024]{1,0:T(8,128)(2,1)} %tokens_ref.1), channel_id=1, source_target_pairs={{0,2},{1,3},{2,4},{3,5},{4,6},{5,7},{6,8},{7,9},{8,10},{9,11},{10,... | collective-permute-start | bytes 3145736 | tf_op jit(solution)/shard_map/ppermute | solution.py:25
  8.2 2.9 %copy.12 = bf16[1024,1024]{0,1:T(8,128)(2,1)S(1)} copy(bf16[1024,1024]{1,0:T(8,128)(2,1)} %param.13) | data formatting | bytes 4194304 | tf_op args[3]
  14.8 4.7 %project.3 = (bf16[1024,512]{1,0:T(8,128)(2,1)S(1)}, bf16[512,1024]{1,0:T(8,128)(2,1)S(1)}, bf16[1024,512]{1,0:T(8,128)(2,1)S(1)}) custom-call(s32[1]{0:T(128)} %bitcast.5.core_ref, bf16[1024,1024]{1,0:T(8,128)(2,1)S(1)} %pad_maximum_fusion.rows_ref, bf16[1024,1024]{1,0:T(8,128)(2,1)S(1)} %copy-done, bf16[1024,1024]{1,0:T(8,128)(2,1)S(1)} %bitcast.15, ...), custom_call_target="tpu_custom_call" | custom-call | flops 1 | bytes 1 | tf_op jit(solution)/shard_map/project/pallas_call | solution.py:88
  19.5 6.5 %fine_own.1 = (f32[4,8,8,256]{3,2,1,0:T(8,128)S(1)}, f32[4,8,80,256]{3,2,1,0:T(8,128)S(1)}) custom-call(bf16[1024,512]{1,0:T(8,128)(2,1)S(1)} %get-tuple-element.49.q_ref, bf16[1024,512]{1,0:T(8,128)(2,1)S(1)} %get-tuple-element.44.k_ref, bf16[512,1024]{1,0:T(8,128)(2,1)S(1)} %get-tuple-element.45.v_ref), custom_call_target="tpu_custom_call" | custom-call | flops 1 | bytes 1 | tf_op jit(solution)/shard_map/fine_own/pallas_call | solution.py:278
  29.8 3.0 %collective-permute-done.3.refs_2_ = bf16[256,1024]{1,0:T(8,128)(2,1)} collective-permute-done((bf16[256,1024]{1,0:T(8,128)(2,1)}, bf16[256,1024]{1,0:T(8,128)(2,1)}, u32[]{:S(2)}, u32[]{:S(2)}) %collective-permute-start.3) | collective-permute-done | bytes 524320 | tf_op jit(solution)/shard_map/ppermute | solution.py:545
  37.1 2.6 %project.4 = (bf16[512,512]{1,0:T(8,128)(2,1)S(1)}, bf16[512,512]{1,0:T(8,128)(2,1)S(1)}) custom-call(s32[1]{0:T(128)} %bitcast.5.core_ref, bf16[512,1024]{1,0:T(8,128)(2,1)} %collective-permute-done.rows_ref, bf16[1024,1024]{1,0:T(8,128)(2,1)S(1)} %copy-done.1, bf16[1024,1024]{1,0:T(8,128)(2,1)S(1)} %bitcast.16), custom_call_target="tpu_custom_call" | custom-call | flops 1 | bytes 1 | tf_op jit(solution)/shard_map/project/pallas_call | solution.py:88
  39.7 2.8 %project.5 = (bf16[512,512]{1,0:T(8,128)(2,1)S(1)}, bf16[512,512]{1,0:T(8,128)(2,1)S(1)}) custom-call(s32[1]{0:T(128)} %bitcast.5.core_ref, bf16[512,1024]{1,0:T(8,128)(2,1)} %collective-permute-done.4.rows_ref, bf16[1024,1024]{1,0:T(8,128)(2,1)S(1)} %copy-done.1, bf16[1024,1024]{1,0:T(8,128)(2,1)S(1)} %bitcast.17), custom_call_target="tpu_custom_call" | custom-call | flops 1 | bytes 1 | tf_op jit(solution)/shard_map/project/pallas_call | solution.py:88
  44.4 3.6 %collective-permute-done.5.refs_3_ = bf16[256,1024]{1,0:T(8,128)(2,1)} collective-permute-done((bf16[256,1024]{1,0:T(8,128)(2,1)}, bf16[256,1024]{1,0:T(8,128)(2,1)}, u32[]{:S(2)}, u32[]{:S(2)}) %collective-permute-start.5) | collective-permute-done | bytes 524320 | tf_op jit(solution)/shard_map/ppermute | solution.py:545
  50.7 3.1 %out_project.1 = (bf16[512,1024]{1,0:T(8,128)(2,1)S(1)}, bf16[2,2,4,64,512]{4,3,2,1,0:T(8,128)(2,1)}, bf16[16,1024]{1,0:T(8,128)(2,1)S(1)}) custom-call(s32[1]{0:T(128)} %bitcast.5.core_ref, bf16[512,1024]{1,0:T(8,128)(2,1)S(1)} %copy-done.4, bf16[2,512,512]{2,1,0:T(8,128)(2,1)S(1)} %fine_before.1.mine_ref, ...), custom_call_target="tpu_custom_call" | custom-call | tf_op jit(solution)/shard_map/out_project/pallas_call | solution.py:135
  54.8 5.8 %collective-permute-start.7 = (bf16[16,1024]{1,0:T(8,128)(2,1)S(1)}, bf16[16,1024]{1,0:T(8,128)(2,1)S(1)}, u32[]{:S(2)}, u32[]{:S(2)}) collective-permute-start(bf16[16,1024]{1,0:T(8,128)(2,1)S(1)} %get-tuple-element.60), channel_id=1, source_target_pairs={{0,1},{1,2},{2,3},{3,4},{4,5},{5,6},{6,7},{7,8},{8,9},{9,10},{10,1... | collective-permute-start | bytes 98312 | tf_op jit(solution)/shard_map/ppermute | solution.py:25
  63.4 5.7 %all-to-all-start = ((bf16[4,4,64,512]{3,2,1,0:T(8,128)(2,1)}), bf16[4,4,64,512]{3,2,1,0:T(8,128)(2,1)S(1)}, u32[]{:S(2)}, u32[]{:S(2)}) async-start(bf16[4,4,64,512]{3,2,1,0:T(8,128)(2,1)} %bitcast.9), calls=%async_computation | async-start | bytes 2097152 | tf_op jit(solution)/shard_map/all_to_all | solution.py:565
  74.6 8.1 %all-to-all-done.grouped_ref = bf16[4,4,64,512]{3,2,1,0:T(8,128)(2,1)S(1)} async-done(((bf16[4,4,64,512]{3,2,1,0:T(8,128)(2,1)}), bf16[4,4,64,512]{3,2,1,0:T(8,128)(2,1)S(1)}, u32[]{:S(2)}, u32[]{:S(2)}) %all-to-all-start) | async-done | bytes 1048608 | tf_op jit(solution)/shard_map/all_to_all | solution.py:565
  83.7 4.4 %shorten.1 = bf16[4,64,1024]{2,1,0:T(8,128)(2,1)} custom-call(s32[2]{0:T(128)} %pad_add_fusion.1.where_ref, bf16[4,4,64,512]{3,2,1,0:T(8,128)(2,1)} %copy-done.9, bf16[256,1024]{1,0:T(8,128)(2,1)} %refs_0_.7, bf16[256,1024]{1,0:T(8,128)(2,1)} %collective-permute-done.2.refs_1_, bf16[256,1024]{1,0:T(8,128)(2,1)} %collective-permute-done.3.refs_2_, ...), custom_call_target="tpu_custom_call" | custom-call | tf_op jit(solution)/shard_map/shorten/pallas_call | solution.py:349
  88.1 11.1 %all_to_all.20.part_ref = bf16[4,64,1024]{2,1,0:T(8,128)(2,1)} all-to-all(bf16[4,64,1024]{2,1,0:T(8,128)(2,1)} %shorten.1), channel_id=1, replica_groups=mesh['z'=4,'x'=4,'y'=4,'c'=2] {'y'}, dimensions={0} | all-to-all | bytes 1048576 | tf_op jit(solution)/shard_map/all_to_all | solution.py:569
  99.2 5.6 %coarse_project.1 = (bf16[64,1024]{1,0:T(8,128)(2,1)}, bf16[16,64,192]{2,1,0:T(8,128)(2,1)}) custom-call(bf16[4,64,1024]{2,1,0:T(8,128)(2,1)} %all_to_all.20.part_ref, bf16[1024,1024]{1,0:T(8,128)(2,1)} %q_ref.1, bf16[1024,1024]{1,0:T(8,128)(2,1)} %k_ref.1, bf16[1024,1024]{1,0:T(8,128)(2,1)} %v_ref.1), custom_call_target="tpu_custom_call" | custom-call | tf_op jit(solution)/shard_map/coarse_project/pallas_call | solution.py:385
  104.9 17.8 %all_to_all.21.q_ref = bf16[16,64,192]{2,1,0:T(8,128)(2,1)S(1)} all-to-all(bf16[16,64,192]{2,1,0:T(8,128)(2,1)} %get-tuple-element.62), channel_id=1, replica_groups=mesh['z'=4,'x'=4,'y'=4,'c'=2] {'z','x'}, dimensions={0} | all-to-all | bytes 786432 | tf_op jit(solution)/shard_map/all_to_all | solution.py:571
  122.8 3.3 %collective-permute-start.12 = (bf16[16,64,128]{2,1,0:T(8,128)(2,1)S(1)}, bf16[16,64,128]{2,1,0:T(8,128)(2,1)S(1)}, u32[]{:S(2)}, u32[]{:S(2)}) collective-permute-start(bf16[16,64,128]{2,1,0:T(8,128)(2,1)S(1)} %slice.8.refs_0_), channel_id=1, source_target_pairs={{0,1},{1,0},{2,3},{3,2},{4,5},{5,4},{6,7},{7,6},{8,9},{9,8},{10,11... | collective-permute-start | bytes 786440 | tf_op jit(solution)/shard_map/ppermute | solution.py:535
  128.8 2.8 %coarse_attend.3 = (f32[4,8,256]{2,1,0:T(8,128)S(1)}, f32[4,80,256]{2,1,0:T(8,128)S(1)}) custom-call(s32[3]{0:T(128)S(1)} %pad_add_fusion.4.where_ref, bf16[16,64,192]{2,1,0:T(8,128)(2,1)S(1)} %all_to_all.21.q_ref, bf16[16,64,128]{2,1,0:T(8,128)(2,1)S(1)} %slice.8.refs_0_, bf16[16,64,128]{2,1,0:T(8,128)(2,1)S(1)} %collective-permute-done.12.refs_1_), custom_call_target="tpu_custom_call" | custom-call | flops 1610612736 | bytes 2097152 | tf_op jit(solution)/shard_map/coarse_attend/pallas_call | solution.py:504
  131.6 4.0 %collective-permute-done.13.refs_0_ = bf16[16,64,128]{2,1,0:T(8,128)(2,1)S(1)} collective-permute-done((bf16[16,64,128]{2,1,0:T(8,128)(2,1)S(1)}, bf16[16,64,128]{2,1,0:T(8,128)(2,1)S(1)}, u32[]{:S(2)}, u32[]{:S(2)}) %collective-permute-start.13) | collective-permute-done | bytes 262176 | tf_op jit(solution)/shard_map/ppermute | solution.py:577
  135.6 4.5 %collective-permute-done.15.refs_2_ = bf16[16,64,128]{2,1,0:T(8,128)(2,1)S(1)} collective-permute-done((bf16[16,64,128]{2,1,0:T(8,128)(2,1)S(1)}, bf16[16,64,128]{2,1,0:T(8,128)(2,1)S(1)}, u32[]{:S(2)}, u32[]{:S(2)}) %collective-permute-start.15) | collective-permute-done | bytes 262176 | tf_op jit(solution)/shard_map/ppermute | solution.py:577
  142.2 3.6 %coarse_attend.4 = (f32[4,8,256]{2,1,0:T(8,128)S(1)}, f32[4,80,256]{2,1,0:T(8,128)S(1)}) custom-call(s32[4]{0:T(128)S(1)} %get-tuple-element.82.where_ref, bf16[16,64,192]{2,1,0:T(8,128)(2,1)S(1)} %all_to_all.21.q_ref, bf16[16,64,128]{2,1,0:T(8,128)(2,1)S(1)} %collective-permute-done.13.refs_0_, bf16[16,64,128]{2,1,0:T(8,128)(2,1)S(1)} %collective-permute-done.14.refs_1_, ...), custom_call_target="tpu_custom_call" | custom-call | flops 2415919104 | bytes 2097152 | tf_op jit(solution)/shard_map/coarse_attend/pallas_call | solution.py:504
  145.9 3.8 %coarse_attend.5 = bf16[16,32,128]{2,1,0:T(8,128)(2,1)S(1)} custom-call(s32[4]{0:T(128)S(1)} %get-tuple-element.81.where_ref, bf16[16,64,192]{2,1,0:T(8,128)(2,1)S(1)} %all_to_all.21.q_ref, bf16[16,64,128]{2,1,0:T(8,128)(2,1)S(1)} %collective-permute-done.16.refs_0_, bf16[16,64,128]{2,1,0:T(8,128)(2,1)S(1)} %collective-permute-done.17.refs_1_, ...), custom_call_target="tpu_custom_call" | custom-call | flops 2415919104 | bytes 2097152 | tf_op jit(solution)/shard_map/coarse_attend/pallas_call | solution.py:504
  149.7 10.6 %all_to_all.22.mixed_ref = bf16[16,32,128]{2,1,0:T(8,128)(2,1)} all-to-all(bf16[16,32,128]{2,1,0:T(8,128)(2,1)S(1)} %coarse_attend.5), channel_id=1, replica_groups=mesh['z'=4,'x'=4,'y'=4,'c'=2] {'z','x'}, dimensions={0} | all-to-all | bytes 262144 | tf_op jit(solution)/shard_map/all_to_all | solution.py:591
  160.3 4.5 %finish.1 = bf16[512,1024]{1,0:T(8,128)(2,1)} custom-call(bf16[16,32,128]{2,1,0:T(8,128)(2,1)} %all_to_all.22.mixed_ref, bf16[1024,1024]{1,0:T(8,128)(2,1)} %out_weight_ref.1, bf16[64,1024]{1,0:T(8,128)(2,1)} %get-tuple-element.77.short_ref, bf16[512,1024]{1,0:T(8,128)(2,1)} %copy-done.8), custom_call_target="tpu_custom_call" | custom-call | tf_op jit(solution)/shard_map/finish/pallas_call | solution.py:425
  (69 shorter events, 35.3 us)
Async XLA Ops:
  0.0 11.1 %collective-permute-start.1 = (bf16[512,1024]{1,0:T(8,128)(2,1)}, bf16[512,1024]{1,0:T(8,128)(2,1)}, u32[]{:S(2)}, u32[]{:S(2)}) collective-permute-start(bf16[512,1024]{1,0:T(8,128)(2,1)} %tokens_ref.1), channel_id=1, source_target_pairs={{0,1},{1,0},{2,3},{3,2},{4,5},{5,4},{6,7},{7,6},{8,9},{9,8},{10,11... | collective-permute-start | bytes 3145736 | tf_op jit(solution)/shard_map/ppermute | solution.py:535
  1.4 18.0 %collective-permute-start.2 = (bf16[256,1024]{1,0:T(8,128)(2,1)}, bf16[256,1024]{1,0:T(8,128)(2,1)}, u32[]{:S(2)}, u32[]{:S(2)}) collective-permute-start(bf16[256,1024]{1,0:T(8,128)(2,1)} %refs_0_.7), channel_id=1, source_target_pairs={{0,24},{8,0},{16,8},{24,16},{1,25},{9,1},{17,9},{25,17},{2,26},{10... | collective-permute-start | bytes 1572872 | tf_op jit(solution)/shard_map/ppermute | solution.py:545
  4.0 25.8 %collective-permute-start = (bf16[512,1024]{1,0:T(8,128)(2,1)}, bf16[512,1024]{1,0:T(8,128)(2,1)}, u32[]{:S(2)}, u32[]{:S(2)}) collective-permute-start(bf16[512,1024]{1,0:T(8,128)(2,1)} %tokens_ref.1), channel_id=1, source_target_pairs={{0,2},{1,3},{2,4},{3,5},{4,6},{5,7},{6,8},{7,9},{8,10},{9,11},{10,... | collective-permute-start | bytes 3145736 | tf_op jit(solution)/shard_map/ppermute | solution.py:25
  19.5 13.3 %collective-permute-start.3 = (bf16[256,1024]{1,0:T(8,128)(2,1)}, bf16[256,1024]{1,0:T(8,128)(2,1)}, u32[]{:S(2)}, u32[]{:S(2)}) collective-permute-start(bf16[256,1024]{1,0:T(8,128)(2,1)} %collective-permute-done.2.refs_1_), channel_id=1, source_target_pairs={{0,24},{8,0},{16,8},{24,16},{1,25},{9,1},{17,9},{25,17},{2,26},{10... | collective-permute-start | bytes 1572872 | tf_op jit(solution)/shard_map/ppermute | solution.py:545
  32.8 7.0 %collective-permute-start.4 = (bf16[512,1024]{1,0:T(8,128)(2,1)}, bf16[512,1024]{1,0:T(8,128)(2,1)}, u32[]{:S(2)}, u32[]{:S(2)}) collective-permute-start(bf16[512,1024]{1,0:T(8,128)(2,1)} %collective-permute-done.rows_ref), channel_id=1, source_target_pairs={{0,1},{1,0},{2,3},{3,2},{4,5},{5,4},{6,7},{7,6},{8,9},{9,8},{10,11... | collective-permute-start | bytes 3145736 | tf_op jit(solution)/shard_map/ppermute | solution.py:535
  34.2 13.9 %collective-permute-start.5 = (bf16[256,1024]{1,0:T(8,128)(2,1)}, bf16[256,1024]{1,0:T(8,128)(2,1)}, u32[]{:S(2)}, u32[]{:S(2)}) collective-permute-start(bf16[256,1024]{1,0:T(8,128)(2,1)} %collective-permute-done.3.refs_2_), channel_id=1, source_target_pairs={{0,24},{8,0},{16,8},{24,16},{1,25},{9,1},{17,9},{25,17},{2,26},{10... | collective-permute-start | bytes 1572872 | tf_op jit(solution)/shard_map/ppermute | solution.py:545
  42.5 8.1 %copy-start.2 = (bf16[1024,1024]{1,0:T(8,128)(2,1)S(1)}, bf16[1024,1024]{1,0:T(8,128)(2,1)}, u32[]{:S(2)}) copy-start(bf16[1024,1024]{1,0:T(8,128)(2,1)} %their_ref.1) | copy-start | bytes 6291460
  42.6 8.1 %copy-start.4 = (bf16[512,1024]{1,0:T(8,128)(2,1)S(1)}, bf16[512,1024]{1,0:T(8,128)(2,1)}, u32[]{:S(2)}) copy-start(bf16[512,1024]{1,0:T(8,128)(2,1)} %tokens_ref.1) | copy-start | bytes 3145732
  48.1 2.6 %collective-permute-start.6 = (bf16[512,512]{1,0:T(8,128)(2,1)S(1)}, bf16[512,512]{1,0:T(8,128)(2,1)S(1)}, u32[]{:S(2)}, u32[]{:S(2)}) collective-permute-start(bf16[512,512]{1,0:T(8,128)(2,1)S(1)} %slice_bitcast_fusion), channel_id=1, source_target_pairs={{0,1},{1,0},{2,3},{3,2},{4,5},{5,4},{6,7},{7,6},{8,9},{9,8},{10,11... | collective-permute-start | bytes 1572872 | tf_op jit(solution)/shard_map/ppermute | solution.py:535
  54.8 6.9 %collective-permute-start.7 = (bf16[16,1024]{1,0:T(8,128)(2,1)S(1)}, bf16[16,1024]{1,0:T(8,128)(2,1)S(1)}, u32[]{:S(2)}, u32[]{:S(2)}) collective-permute-start(bf16[16,1024]{1,0:T(8,128)(2,1)S(1)} %get-tuple-element.60), channel_id=1, source_target_pairs={{0,1},{1,2},{2,3},{3,4},{4,5},{5,6},{6,7},{7,8},{8,9},{9,10},{10,1... | collective-permute-start | bytes 98312 | tf_op jit(solution)/shard_map/ppermute | solution.py:25
  63.4 19.3 %all-to-all-start = ((bf16[4,4,64,512]{3,2,1,0:T(8,128)(2,1)}), bf16[4,4,64,512]{3,2,1,0:T(8,128)(2,1)S(1)}, u32[]{:S(2)}, u32[]{:S(2)}) async-start(bf16[4,4,64,512]{3,2,1,0:T(8,128)(2,1)} %bitcast.9), calls=%async_computation | async-start | bytes 2097152 | tf_op jit(solution)/shard_map/all_to_all | solution.py:565
  69.1 3.1 %collective-permute-start.8 = (bf16[256,1024]{1,0:T(8,128)(2,1)S(1)}, bf16[256,1024]{1,0:T(8,128)(2,1)S(1)}, u32[]{:S(2)}, u32[]{:S(2)}) collective-permute-start(bf16[256,1024]{1,0:T(8,128)(2,1)S(1)} %copy-done.10), channel_id=1, source_target_pairs={{0,1},{1,0},{2,3},{3,2},{4,5},{5,4},{6,7},{7,6},{8,9},{9,8},{10,11... | collective-permute-start | bytes 1572872 | tf_op jit(solution)/shard_map/ppermute | solution.py:535
  70.6 3.2 %collective-permute-start.9 = (bf16[256,1024]{1,0:T(8,128)(2,1)}, bf16[256,1024]{1,0:T(8,128)(2,1)S(1)}, u32[]{:S(2)}, u32[]{:S(2)}) collective-permute-start(bf16[256,1024]{1,0:T(8,128)(2,1)} %collective-permute-done.2.refs_1_), channel_id=1, source_target_pairs={{0,1},{1,0},{2,3},{3,2},{4,5},{5,4},{6,7},{7,6},{8,9},{9,8},{10,11... | collective-permute-start | bytes 1572872 | tf_op jit(solution)/shard_map/ppermute | solution.py:535
  70.7 3.9 %collective-permute-start.10 = (bf16[256,1024]{1,0:T(8,128)(2,1)}, bf16[256,1024]{1,0:T(8,128)(2,1)S(1)}, u32[]{:S(2)}, u32[]{:S(2)}) collective-permute-start(bf16[256,1024]{1,0:T(8,128)(2,1)} %collective-permute-done.3.refs_2_), channel_id=1, source_target_pairs={{0,1},{1,0},{2,3},{3,2},{4,5},{5,4},{6,7},{7,6},{8,9},{9,8},{10,11... | collective-permute-start | bytes 1572872 | tf_op jit(solution)/shard_map/ppermute | solution.py:535
  71.2 3.5 %collective-permute-start.11 = (bf16[256,1024]{1,0:T(8,128)(2,1)}, bf16[256,1024]{1,0:T(8,128)(2,1)}, u32[]{:S(2)}, u32[]{:S(2)}) collective-permute-start(bf16[256,1024]{1,0:T(8,128)(2,1)} %collective-permute-done.5.refs_3_), channel_id=1, source_target_pairs={{0,1},{1,0},{2,3},{3,2},{4,5},{5,4},{6,7},{7,6},{8,9},{9,8},{10,11... | collective-permute-start | bytes 1572872 | tf_op jit(solution)/shard_map/ppermute | solution.py:535
  72.2 10.5 %copy-start.11 = (bf16[256,1024]{1,0:T(8,128)(2,1)}, bf16[256,1024]{1,0:T(8,128)(2,1)S(1)}, u32[]{:S(2)}) copy-start(bf16[256,1024]{1,0:T(8,128)(2,1)S(1)} %collective-permute-done.8.refs_4_) | copy-start | bytes 1572868
  73.9 8.8 %copy-start.12 = (bf16[256,1024]{1,0:T(8,128)(2,1)}, bf16[256,1024]{1,0:T(8,128)(2,1)S(1)}, u32[]{:S(2)}) copy-start(bf16[256,1024]{1,0:T(8,128)(2,1)S(1)} %collective-permute-done.9.refs_5_) | copy-start | bytes 1572868
  122.8 6.0 %collective-permute-start.12 = (bf16[16,64,128]{2,1,0:T(8,128)(2,1)S(1)}, bf16[16,64,128]{2,1,0:T(8,128)(2,1)S(1)}, u32[]{:S(2)}, u32[]{:S(2)}) collective-permute-start(bf16[16,64,128]{2,1,0:T(8,128)(2,1)S(1)} %slice.8.refs_0_), channel_id=1, source_target_pairs={{0,1},{1,0},{2,3},{3,2},{4,5},{5,4},{6,7},{7,6},{8,9},{9,8},{10,11... | collective-permute-start | bytes 786440 | tf_op jit(solution)/shard_map/ppermute | solution.py:535
  126.0 9.5 %collective-permute-start.13 = (bf16[16,64,128]{2,1,0:T(8,128)(2,1)S(1)}, bf16[16,64,128]{2,1,0:T(8,128)(2,1)S(1)}, u32[]{:S(2)}, u32[]{:S(2)}) collective-permute-start(bf16[16,64,128]{2,1,0:T(8,128)(2,1)S(1)} %slice.8.refs_0_), channel_id=1, source_target_pairs={{0,2},{2,4},{4,6},{6,0},{1,3},{3,5},{5,7},{7,1},{8,10},{10,12},{12... | collective-permute-start | bytes 786440 | tf_op jit(solution)/shard_map/ppermute | solution.py:577
  126.3 9.3 %collective-permute-start.14 = (bf16[16,64,128]{2,1,0:T(8,128)(2,1)S(1)}, bf16[16,64,128]{2,1,0:T(8,128)(2,1)S(1)}, u32[]{:S(2)}, u32[]{:S(2)}) collective-permute-start(bf16[16,64,128]{2,1,0:T(8,128)(2,1)S(1)} %slice.8.refs_0_), channel_id=1, source_target_pairs={{0,6},{2,0},{4,2},{6,4},{1,7},{3,1},{5,3},{7,5},{8,14},{10,8},{12,... | collective-permute-start | bytes 786440 | tf_op jit(solution)/shard_map/ppermute | solution.py:577
  128.7 11.4 %collective-permute-start.15 = (bf16[16,64,128]{2,1,0:T(8,128)(2,1)S(1)}, bf16[16,64,128]{2,1,0:T(8,128)(2,1)S(1)}, u32[]{:S(2)}, u32[]{:S(2)}) collective-permute-start(bf16[16,64,128]{2,1,0:T(8,128)(2,1)S(1)} %slice.8.refs_0_), channel_id=1, source_target_pairs={{0,4},{2,6},{4,0},{6,2},{1,5},{3,7},{5,1},{7,3},{8,12},{10,14},{12... | collective-permute-start | bytes 786440 | tf_op jit(solution)/shard_map/ppermute | solution.py:577
  140.1 5.7 %collective-permute-start.16 = (bf16[16,64,128]{2,1,0:T(8,128)(2,1)S(1)}, bf16[16,64,128]{2,1,0:T(8,128)(2,1)S(1)}, u32[]{:S(2)}, u32[]{:S(2)}) collective-permute-start(bf16[16,64,128]{2,1,0:T(8,128)(2,1)S(1)} %collective-permute-done.13.refs_0_), channel_id=1, source_target_pairs={{0,1},{1,0},{2,3},{3,2},{4,5},{5,4},{6,7},{7,6},{8,9},{9,8},{10,11... | collective-permute-start | bytes 786440 | tf_op jit(solution)/shard_map/ppermute | solution.py:535
  141.6 4.2 %collective-permute-start.17 = (bf16[16,64,128]{2,1,0:T(8,128)(2,1)S(1)}, bf16[16,64,128]{2,1,0:T(8,128)(2,1)S(1)}, u32[]{:S(2)}, u32[]{:S(2)}) collective-permute-start(bf16[16,64,128]{2,1,0:T(8,128)(2,1)S(1)} %collective-permute-done.14.refs_1_), channel_id=1, source_target_pairs={{0,1},{1,0},{2,3},{3,2},{4,5},{5,4},{6,7},{7,6},{8,9},{9,8},{10,11... | collective-permute-start | bytes 786440 | tf_op jit(solution)/shard_map/ppermute | solution.py:535
  141.7 4.2 %collective-permute-start.18 = (bf16[16,64,128]{2,1,0:T(8,128)(2,1)S(1)}, bf16[16,64,128]{2,1,0:T(8,128)(2,1)S(1)}, u32[]{:S(2)}, u32[]{:S(2)}) collective-permute-start(bf16[16,64,128]{2,1,0:T(8,128)(2,1)S(1)} %collective-permute-done.15.refs_2_), channel_id=1, source_target_pairs={{0,1},{1,0},{2,3},{3,2},{4,5},{5,4},{6,7},{7,6},{8,9},{9,8},{10,11... | collective-permute-start | bytes 786440 | tf_op jit(solution)/shard_map/ppermute | solution.py:535
  (10 other events, 30.2 us)

commit v9 on v8

--- a/solution.py
+++ b/solution.py
@@ -105,32 +105,54 @@
     )(core.reshape(1), *[rows, *weights])
 
 
-def out_project_kernel(
-    core_ref, tokens_ref, mine_ref, theirs_ref, my_ref, their_ref, natural_ref, grouped_ref, tail_ref
-):
+def tail_project_kernel(core_ref, tokens_ref, mine_ref, theirs_ref, my_ref, their_ref, tail_ref):
+    groups = QB // SHORT
+    total = dot(moves(16, lambda r: r + QB - SHORT), tokens_ref[...], ((1,), (0,)))
+    take = moves(16, lambda r: r * groups + groups - 1)
+    mine = dot(take, mine_ref[0], ((1,), (0,))).astype(jnp.bfloat16)
+    theirs = dot(take, theirs_ref[...], ((1,), (0,))).astype(jnp.bfloat16)
+    total = total + dot(mine, my_ref[...], ((1,), (0,))) + dot(theirs, their_ref[...], ((1,), (0,)))
+    tail_ref[...] = total.astype(jnp.bfloat16)
+
+
+def tail_project(core, tokens, mixed, theirs, weight):
+    count, width = tokens.shape
+    half = width // 2
+    last = count // QB - 1
+    tile = width // 2
+    return pl.pallas_call(
+        tail_project_kernel,
+        name="tail_project",
+        grid_spec=pltpu.PrefetchScalarGridSpec(
+            num_scalar_prefetch=1,
+            grid=(2,),
+            in_specs=[
+                pl.BlockSpec((QB, tile), lambda i, c: (last, i)),
+                pl.BlockSpec((1, QB, half), lambda i, c: (0, last, 0)),
+                pl.BlockSpec((QB, half), lambda i, c: (last, 0)),
+                pl.BlockSpec((half, tile), lambda i, c: (c[0], i)),
+                pl.BlockSpec((half, tile), lambda i, c: (1 - c[0], i)),
+            ],
+            out_specs=pl.BlockSpec((16, tile), lambda i, c: (0, i)),
+        ),
+        out_shape=jax.ShapeDtypeStruct((16, width), jnp.bfloat16),
+        compiler_params=params(20),
+    )(core.reshape(1), tokens, mixed, theirs, weight, weight)
+
+
+def out_project_kernel(core_ref, tokens_ref, mine_ref, theirs_ref, my_ref, their_ref, hidden_ref, natural_ref):
     total = reorder(moves(QB, spots), tokens_ref[...])
     total = total + dot(mine_ref[0], my_ref[...], ((1,), (0,)))
     total = total + dot(theirs_ref[...], their_ref[...], ((1,), (0,)))
     hidden = total.astype(jnp.bfloat16)
+    hidden_ref[...] = hidden
     groups = QB // SHORT
     natural_ref[...] = reorder(moves(QB, lambda r: (r % SHORT) * groups + r // SHORT), hidden).astype(jnp.bfloat16)
-    tail = dot(moves(16, lambda r: r * groups + groups - 1), hidden[-QB:], ((1,), (0,)))
-    tail_ref[...] = tail.astype(jnp.bfloat16)
-    count, tile = hidden.shape
-    rows = count // SHORT
-    blocks = hidden.reshape(count // QB, SHORT, groups, tile)
-    for j in range(SHORT):
-        p = (j + 1) % SHORT
-        part = blocks[:, p].reshape(rows, tile)
-        if p > 0:
-            part = pltpu.roll(part.astype(jnp.float32), 1, 0).astype(jnp.bfloat16)
-        grouped_ref[j % 2, 0, j // 2] = part
 
 
 def out_project(core, tokens, mixed, theirs, weight):
     count, width = tokens.shape
     half = width // 2
-    rows = count // SHORT
     by_column = pl.BlockSpec((count, half), lambda i, c: (0, i))
     return pl.pallas_call(
         out_project_kernel,
@@ -145,46 +167,40 @@
                 pl.BlockSpec((half, half), lambda i, c: (c[0], i)),
                 pl.BlockSpec((half, half), lambda i, c: (1 - c[0], i)),
             ],
-            out_specs=[
-                by_column,
-                pl.BlockSpec((2, 1, 4, rows, half), lambda i, c: (0, i, 0, 0, 0)),
-                pl.BlockSpec((16, half), lambda i, c: (0, i)),
-            ],
+            out_specs=[by_column, by_column],
         ),
-        out_shape=[
-            jax.ShapeDtypeStruct((count, width), jnp.bfloat16),
-            jax.ShapeDtypeStruct((2, 2, 4, rows, half), jnp.bfloat16),
-            jax.ShapeDtypeStruct((16, width), jnp.bfloat16),
-        ],
+        out_shape=[jax.ShapeDtypeStruct((count, width), jnp.bfloat16)] * 2,
         compiler_params=params(20),
     )(core.reshape(1), tokens, mixed, theirs, weight, weight)
 
 
-def fix_first_kernel(grouped_ref, tail_ref, out_ref):
-    half = grouped_ref.shape[-1]
+def pack_kernel(hidden_ref, tail_ref, out_ref):
+    blocks, places, groups, width = hidden_ref.shape
+    rows = blocks * groups
+    half = width // 2
     for j in range(SHORT):
+        p = (j + 1) % SHORT
+        part = hidden_ref[:, p].reshape(rows, width)
+        if p > 0:
+            wide = part.astype(jnp.float32)
+            tail = tail_ref[p : p + 1, :].astype(jnp.float32)
+            first = lax.broadcasted_iota(jnp.int32, wide.shape, 0) == 0
+            wide = jnp.where(first, tail, pltpu.roll(wide, 1, 0))
+            part = wide.astype(jnp.bfloat16)
         for f in range(2):
-            old = grouped_ref[j % 2, f, j // 2].astype(jnp.float32)
-            if j < SHORT - 1:
-                row = tail_ref[j + 1 : j + 2, f * half : (f + 1) * half].astype(jnp.float32)
-                first = lax.broadcasted_iota(jnp.int32, old.shape, 0) == 0
-                old = jnp.where(first, row, old)
-            out_ref[j % 2, f, j // 2] = old.astype(jnp.bfloat16)
-
-
-def fix_first(grouped, tail):
-    block = (*grouped.shape[:3], 16, grouped.shape[4])
-    spec = pl.BlockSpec(block, lambda i: (0, 0, 0, 0, 0))
-    return pl.pallas_call(
-        fix_first_kernel,
-        name="fix_first",
-        grid=(1,),
-        in_specs=[spec, pl.BlockSpec(tail.shape, lambda i: (0, 0))],
-        out_specs=spec,
-        out_shape=jax.ShapeDtypeStruct(grouped.shape, jnp.bfloat16),
-        input_output_aliases={0: 0},
-        compiler_params=params(20),
-    )(grouped, tail)
+            out_ref[(j % 2) * 2 + f, j // 2] = part[:, f * half : (f + 1) * half]
+
+
+def pack(hidden, tail):
+    count, width = hidden.shape
+    groups = QB // SHORT
+    blocks = count // QB
+    return pl.pallas_call(
+        pack_kernel,
+        name="pack",
+        out_shape=jax.ShapeDtypeStruct((4, 4, count // SHORT, width // 2), jnp.bfloat16),
+        compiler_params=params(),
+    )(hidden.reshape(blocks, SHORT, groups, width), tail)
 
 
 def fine_own_kernel(q_ref, k_ref, v_ref, top_ref, acc_ref, s_ref, p_ref):
@@ -541,30 +557,29 @@
         [jnp.where(core == 0, tokens, mate), jnp.where(core == 0, mate, tokens)], axis=0
     )
 
-    def from_ahead(block):
-        return lax.ppermute(block, "x", [(i, (i + 3) % 4) for i in range(4)])
+    def along_x(block, distance):
+        return lax.ppermute(block, "x", [(i, (i + distance) % 4) for i in range(4)])
 
     together = lax.optimization_barrier
-    pieces = [short_weight, from_ahead(short_weight)]
     keys, values, query = project(core, chip, [*weights, fine_query])
-    keys, pieces[1] = together((keys, pieces[1]))
-    pieces.append(from_ahead(pieces[1]))
     state = fine_own(query, keys, values)
-    far, state, query, pieces[2] = together((far, state, query, pieces[2]))
-    pieces.append(from_ahead(pieces[2]))
+    far, state, query, short_weight = together((far, state, query, short_weight))
     near = across(far)
+    behind, ahead = along_x(short_weight, 1), along_x(short_weight, 3)
     far_keys, far_values = project(core, far, weights)
     near_keys, near_values = project(core, near, weights)
     where = jnp.stack([core, (place > 1).astype(jnp.int32)])
     fine_mixed = fine_before(where, query, (far_keys, near_keys), (far_values, near_values), state)
-    fine_mixed, pieces[3] = together((fine_mixed, pieces[3]))
+    fine_mixed, behind, ahead = together((fine_mixed, behind, ahead))
+    two_away = along_x(ahead, 3)
     theirs = across(fine_mixed[1])
-    natural, grouped, tail = out_project(core, tokens, fine_mixed, theirs, fine_out)
-    tail = from_behind(tail, 1)
-    grouped = fix_first(grouped, tail).reshape(4, 4, count // SHORT, width // 2)
+    tail = from_behind(tail_project(core, tokens, fine_mixed, theirs, fine_out), 1)
+    hidden, natural = out_project(core, tokens, fine_mixed, theirs, fine_out)
+    grouped, two_away = together((pack(hidden, tail), two_away))
     grouped = lax.all_to_all(grouped, "y", 0, 0)
+    pieces = [short_weight, behind, two_away, ahead]
     pieces = pieces + [across(piece) for piece in pieces]
-    spots_of = [(-d % 4, other, 0) for other in (0, 1) for d in range(4)]
+    spots_of = [(distance, other, 0) for other in (0, 1) for distance in range(4)]
     where = jnp.stack([lax.axis_index("x").astype(jnp.int32), core])
     partial = lax.all_to_all(shorten(where, grouped, pieces, spots_of), "y", 0, 0)
     shortened, qkv = coarse_project(partial, coarse_query, coarse_key, coarse_value)

time: 166 us -> 166 us (level)
  blocking collectives: 39.6 us -> 41.4 us
    ppermute x3, starting transfers between devices: 3.85 us -> 10.1 us  [along_x(): return lax.ppermute(block, 'x', [(i, (i + distance) % 4) for i in range(4)])]
    ppermute x2, starting transfers between devices: 10 us -> 6.19 us  [from_behind(): return lax.ppermute(block, ALL, route)]
    all_to_all x1, starting transfers between devices: 5.73 us -> 3.52 us  [body(): grouped = lax.all_to_all(grouped, 'y', 0, 0)]
    unnamed x29 -> x31, local copies, waits for them, and re-layouts: 10 us -> 11 us
  transfers between devices with their start and end apart: 20 -> 20, of which waited for: 11 -> 10; matrix products, arithmetic and copies ran while one was open for 3% -> 3% of each run, Pallas kernels for 15% -> 18%
where the time goes in v9:
time: 166 us
  Pallas kernels  47.8 us (29%)
  blocking collectives  41.4 us (25%)
  starting transfers between devices  33.5 us (20%)
  waiting for transfers between devices  29.2 us (18%)
  local copies, waits for them, and re-layouts  11.1 us (7%)
  other arithmetic  2.37 us (1%)
    all_to_all x1, blocking collectives, body(): qkv = lax.all_to_all(qkv, ('z', 'x'), 0, 0)  19.4 us
    all_to_all x1, blocking collectives, body(): lax.all_to_all(shorten(where, grouped, pieces, spots_of), 'y', 0, 0)  11.4 us
    unnamed x31, local copies, waits for them, and re-layouts  11 us
    ppermute x11, starting transfers between devices, across(): return lax.ppermute(block, 'c', [(0, 1), (1, 0)])  10.9 us
    all_to_all x1, blocking collectives, body(): mixed = lax.all_to_all(mixed, ('z', 'x'), 0, 0)  10.6 us
    pallas_call x3, Pallas kernels, coarse_attend(): pl.pallas_call(functools.partial(coarse_kernel, len(parts), first, final)...  10.2 us
    ppermute x3, starting transfers between devices, along_x(): return lax.ppermute(block, 'x', [(i, (i + distance) % 4) for i in range(4)])  10.1 us
    pallas_call x3, Pallas kernels, project(): pl.pallas_call(functools.partial(project_kernel, number), name='project',...  10.1 us
  transfers between devices with their start and end apart: 20, of which 10 were waited for; matrix products, arithmetic and copies ran while one was open for 3% of the time, Pallas kernels for 18%

profile of v9, /device:TPU:1, one launch (start us, length us, event | category | flops | bytes accessed | tf_op | source)
XLA Modules:
  0.0 165.7 jit_solution(14736151166255983994)
XLA Ops:
  1.4 4.3 %collective-permute-start = (bf16[512,1024]{1,0:T(8,128)(2,1)}, bf16[512,1024]{1,0:T(8,128)(2,1)}, u32[]{:S(2)}, u32[]{:S(2)}) collective-permute-start(bf16[512,1024]{1,0:T(8,128)(2,1)} %tokens_ref.3), channel_id=1, source_target_pairs={{0,2},{1,3},{2,4},{3,5},{4,6},{5,7},{6,8},{7,9},{8,10},{9,11},{10,... | collective-permute-start | bytes 3145736 | tf_op jit(solution)/shard_map/ppermute | solution.py:25
  5.7 2.9 %copy.11 = bf16[1024,1024]{0,1:T(8,128)(2,1)S(1)} copy(bf16[1024,1024]{1,0:T(8,128)(2,1)} %param.13) | data formatting | bytes 4194304 | tf_op args[3]
  12.3 4.7 %project.3 = (bf16[1024,512]{1,0:T(8,128)(2,1)S(1)}, bf16[512,1024]{1,0:T(8,128)(2,1)S(1)}, bf16[1024,512]{1,0:T(8,128)(2,1)S(1)}) custom-call(s32[1]{0:T(128)} %bitcast.5.core_ref, bf16[1024,1024]{1,0:T(8,128)(2,1)S(1)} %pad_maximum_fusion.rows_ref, bf16[1024,1024]{1,0:T(8,128)(2,1)S(1)} %copy-done.1, bf16[1024,1024]{1,0:T(8,128)(2,1)S(1)} %bitcast.15, ...), custom_call_target="tpu_custom_call" | custom-call | flops 1 | bytes 1 | tf_op jit(solution)/shard_map/project/pallas_call | solution.py:88
  17.0 6.5 %fine_own.1 = (f32[4,8,8,256]{3,2,1,0:T(8,128)S(1)}, f32[4,8,80,256]{3,2,1,0:T(8,128)S(1)}) custom-call(bf16[1024,512]{1,0:T(8,128)(2,1)S(1)} %get-tuple-element.47.q_ref, bf16[1024,512]{1,0:T(8,128)(2,1)S(1)} %get-tuple-element.43.k_ref, bf16[512,1024]{1,0:T(8,128)(2,1)S(1)} %get-tuple-element.44.v_ref), custom_call_target="tpu_custom_call" | custom-call | flops 1 | bytes 1 | tf_op jit(solution)/shard_map/fine_own/pallas_call | solution.py:294
  28.4 4.2 %collective-permute-start.3 = (bf16[256,1024]{1,0:T(8,128)(2,1)}, bf16[256,1024]{1,0:T(8,128)(2,1)}, u32[]{:S(2)}, u32[]{:S(2)}) collective-permute-start(bf16[256,1024]{1,0:T(8,128)(2,1)} %refs_0_.6), channel_id=1, source_target_pairs={{0,8},{8,16},{16,24},{24,0},{1,9},{9,17},{17,25},{25,1},{2,10},{10... | collective-permute-start | bytes 1572872 | tf_op jit(solution)/shard_map/ppermute | solution.py:561
  35.5 2.6 %project.4 = (bf16[512,512]{1,0:T(8,128)(2,1)S(1)}, bf16[512,512]{1,0:T(8,128)(2,1)S(1)}) custom-call(s32[1]{0:T(128)} %bitcast.5.core_ref, bf16[512,1024]{1,0:T(8,128)(2,1)} %collective-permute-done.rows_ref, bf16[1024,1024]{1,0:T(8,128)(2,1)S(1)} %copy-done.2, bf16[1024,1024]{1,0:T(8,128)(2,1)S(1)} %bitcast.16), custom_call_target="tpu_custom_call" | custom-call | flops 1 | bytes 1 | tf_op jit(solution)/shard_map/project/pallas_call | solution.py:88
  38.2 2.8 %project.5 = (bf16[512,512]{1,0:T(8,128)(2,1)S(1)}, bf16[512,512]{1,0:T(8,128)(2,1)S(1)}) custom-call(s32[1]{0:T(128)} %bitcast.5.core_ref, bf16[512,1024]{1,0:T(8,128)(2,1)} %collective-permute-done.2.rows_ref, bf16[1024,1024]{1,0:T(8,128)(2,1)S(1)} %copy-done.2, bf16[1024,1024]{1,0:T(8,128)(2,1)S(1)} %bitcast.17), custom_call_target="tpu_custom_call" | custom-call | flops 1 | bytes 1 | tf_op jit(solution)/shard_map/project/pallas_call | solution.py:88
  42.9 3.6 %collective-permute-done.3.refs_1_ = bf16[256,1024]{1,0:T(8,128)(2,1)} collective-permute-done((bf16[256,1024]{1,0:T(8,128)(2,1)}, bf16[256,1024]{1,0:T(8,128)(2,1)}, u32[]{:S(2)}, u32[]{:S(2)}) %collective-permute-start.3) | collective-permute-done | bytes 524320 | tf_op jit(solution)/shard_map/ppermute | solution.py:561
  47.4 4.7 %collective-permute-start.7 = (bf16[256,1024]{1,0:T(8,128)(2,1)}, bf16[256,1024]{1,0:T(8,128)(2,1)}, u32[]{:S(2)}, u32[]{:S(2)}) collective-permute-start(bf16[256,1024]{1,0:T(8,128)(2,1)} %collective-permute-done.4.refs_3_), channel_id=1, source_target_pairs={{0,24},{8,0},{16,8},{24,16},{1,25},{9,1},{17,9},{25,17},{2,26},{10... | collective-permute-start | bytes 1572872 | tf_op jit(solution)/shard_map/ppermute | solution.py:561
  59.5 3.9 %collective-permute-done.7.refs_2_ = bf16[256,1024]{1,0:T(8,128)(2,1)} collective-permute-done((bf16[256,1024]{1,0:T(8,128)(2,1)}, bf16[256,1024]{1,0:T(8,128)(2,1)}, u32[]{:S(2)}, u32[]{:S(2)}) %collective-permute-start.7) | collective-permute-done | bytes 524320 | tf_op jit(solution)/shard_map/ppermute | solution.py:561
  63.4 3.5 %all-to-all-start = ((bf16[4,4,64,512]{3,2,1,0:T(8,128)(2,1)}), bf16[4,4,64,512]{3,2,1,0:T(8,128)(2,1)S(1)}, u32[]{:S(2)}, u32[]{:S(2)}) async-start(bf16[4,4,64,512]{3,2,1,0:T(8,128)(2,1)} %pack.1), calls=%async_computation | async-start | bytes 2097152 | tf_op jit(solution)/shard_map/all_to_all | solution.py:579
  72.1 8.9 %all-to-all-done.grouped_ref = bf16[4,4,64,512]{3,2,1,0:T(8,128)(2,1)S(1)} async-done(((bf16[4,4,64,512]{3,2,1,0:T(8,128)(2,1)}), bf16[4,4,64,512]{3,2,1,0:T(8,128)(2,1)S(1)}, u32[]{:S(2)}, u32[]{:S(2)}) %all-to-all-start) | async-done | bytes 1048608 | tf_op jit(solution)/shard_map/all_to_all | solution.py:579
  81.9 4.4 %shorten.1 = bf16[4,64,1024]{2,1,0:T(8,128)(2,1)} custom-call(s32[2]{0:T(128)} %pad_add_fusion.1.where_ref, bf16[4,4,64,512]{3,2,1,0:T(8,128)(2,1)} %copy-done.10, bf16[256,1024]{1,0:T(8,128)(2,1)} %refs_0_.6, bf16[256,1024]{1,0:T(8,128)(2,1)} %collective-permute-done.3.refs_1_, bf16[256,1024]{1,0:T(8,128)(2,1)} %collective-permute-done.7.refs_2_, ...), custom_call_target="tpu_custom_call" | custom-call | tf_op jit(solution)/shard_map/shorten/pallas_call | solution.py:365
  86.4 11.4 %all_to_all.20.part_ref = bf16[4,64,1024]{2,1,0:T(8,128)(2,1)} all-to-all(bf16[4,64,1024]{2,1,0:T(8,128)(2,1)} %shorten.1), channel_id=1, replica_groups=mesh['z'=4,'x'=4,'y'=4,'c'=2] {'y'}, dimensions={0} | all-to-all | bytes 1048576 | tf_op jit(solution)/shard_map/all_to_all | solution.py:584
  97.8 5.6 %coarse_project.1 = (bf16[64,1024]{1,0:T(8,128)(2,1)}, bf16[16,64,192]{2,1,0:T(8,128)(2,1)}) custom-call(bf16[4,64,1024]{2,1,0:T(8,128)(2,1)} %all_to_all.20.part_ref, bf16[1024,1024]{1,0:T(8,128)(2,1)} %q_ref.1, bf16[1024,1024]{1,0:T(8,128)(2,1)} %k_ref.1, bf16[1024,1024]{1,0:T(8,128)(2,1)} %v_ref.1), custom_call_target="tpu_custom_call" | custom-call | tf_op jit(solution)/shard_map/coarse_project/pallas_call | solution.py:401
  103.4 19.4 %all_to_all.21.q_ref = bf16[16,64,192]{2,1,0:T(8,128)(2,1)S(1)} all-to-all(bf16[16,64,192]{2,1,0:T(8,128)(2,1)} %get-tuple-element.62), channel_id=1, replica_groups=mesh['z'=4,'x'=4,'y'=4,'c'=2] {'z','x'}, dimensions={0} | all-to-all | bytes 786432 | tf_op jit(solution)/shard_map/all_to_all | solution.py:586
  122.8 4.1 %collective-permute-start.12 = (bf16[16,64,128]{2,1,0:T(8,128)(2,1)S(1)}, bf16[16,64,128]{2,1,0:T(8,128)(2,1)S(1)}, u32[]{:S(2)}, u32[]{:S(2)}) collective-permute-start(bf16[16,64,128]{2,1,0:T(8,128)(2,1)S(1)} %slice.8.refs_0_), channel_id=1, source_target_pairs={{0,1},{1,0},{2,3},{3,2},{4,5},{5,4},{6,7},{7,6},{8,9},{9,8},{10,11... | collective-permute-start | bytes 786440 | tf_op jit(solution)/shard_map/ppermute | solution.py:551
  129.7 2.8 %coarse_attend.3 = (f32[4,8,256]{2,1,0:T(8,128)S(1)}, f32[4,80,256]{2,1,0:T(8,128)S(1)}) custom-call(s32[3]{0:T(128)S(1)} %pad_add_fusion.4.where_ref, bf16[16,64,192]{2,1,0:T(8,128)(2,1)S(1)} %all_to_all.21.q_ref, bf16[16,64,128]{2,1,0:T(8,128)(2,1)S(1)} %slice.8.refs_0_, bf16[16,64,128]{2,1,0:T(8,128)(2,1)S(1)} %collective-permute-done.12.refs_1_), custom_call_target="tpu_custom_call" | custom-call | flops 1610612736 | bytes 2097152 | tf_op jit(solution)/shard_map/coarse_attend/pallas_call | solution.py:520
  132.5 4.0 %collective-permute-done.13.refs_0_ = bf16[16,64,128]{2,1,0:T(8,128)(2,1)S(1)} collective-permute-done((bf16[16,64,128]{2,1,0:T(8,128)(2,1)S(1)}, bf16[16,64,128]{2,1,0:T(8,128)(2,1)S(1)}, u32[]{:S(2)}, u32[]{:S(2)}) %collective-permute-start.13) | collective-permute-done | bytes 262176 | tf_op jit(solution)/shard_map/ppermute | solution.py:592
  136.5 4.5 %collective-permute-done.15.refs_2_ = bf16[16,64,128]{2,1,0:T(8,128)(2,1)S(1)} collective-permute-done((bf16[16,64,128]{2,1,0:T(8,128)(2,1)S(1)}, bf16[16,64,128]{2,1,0:T(8,128)(2,1)S(1)}, u32[]{:S(2)}, u32[]{:S(2)}) %collective-permute-start.15) | collective-permute-done | bytes 262176 | tf_op jit(solution)/shard_map/ppermute | solution.py:592
  143.1 3.6 %coarse_attend.4 = (f32[4,8,256]{2,1,0:T(8,128)S(1)}, f32[4,80,256]{2,1,0:T(8,128)S(1)}) custom-call(s32[4]{0:T(128)S(1)} %get-tuple-element.82.where_ref, bf16[16,64,192]{2,1,0:T(8,128)(2,1)S(1)} %all_to_all.21.q_ref, bf16[16,64,128]{2,1,0:T(8,128)(2,1)S(1)} %collective-permute-done.13.refs_0_, bf16[16,64,128]{2,1,0:T(8,128)(2,1)S(1)} %collective-permute-done.14.refs_1_, ...), custom_call_target="tpu_custom_call" | custom-call | flops 2415919104 | bytes 2097152 | tf_op jit(solution)/shard_map/coarse_attend/pallas_call | solution.py:520
  146.7 3.8 %coarse_attend.5 = bf16[16,32,128]{2,1,0:T(8,128)(2,1)S(1)} custom-call(s32[4]{0:T(128)S(1)} %get-tuple-element.81.where_ref, bf16[16,64,192]{2,1,0:T(8,128)(2,1)S(1)} %all_to_all.21.q_ref, bf16[16,64,128]{2,1,0:T(8,128)(2,1)S(1)} %collective-permute-done.16.refs_0_, bf16[16,64,128]{2,1,0:T(8,128)(2,1)S(1)} %collective-permute-done.17.refs_1_, ...), custom_call_target="tpu_custom_call" | custom-call | flops 2415919104 | bytes 2097152 | tf_op jit(solution)/shard_map/coarse_attend/pallas_call | solution.py:520
  150.5 10.6 %all_to_all.22.mixed_ref = bf16[16,32,128]{2,1,0:T(8,128)(2,1)} all-to-all(bf16[16,32,128]{2,1,0:T(8,128)(2,1)S(1)} %coarse_attend.5), channel_id=1, replica_groups=mesh['z'=4,'x'=4,'y'=4,'c'=2] {'z','x'}, dimensions={0} | all-to-all | bytes 262144 | tf_op jit(solution)/shard_map/all_to_all | solution.py:606
  161.2 4.5 %finish.1 = bf16[512,1024]{1,0:T(8,128)(2,1)} custom-call(bf16[16,32,128]{2,1,0:T(8,128)(2,1)} %all_to_all.22.mixed_ref, bf16[1024,1024]{1,0:T(8,128)(2,1)} %out_weight_ref.1, bf16[64,1024]{1,0:T(8,128)(2,1)} %get-tuple-element.77.short_ref, bf16[512,1024]{1,0:T(8,128)(2,1)} %copy-done.9), custom_call_target="tpu_custom_call" | custom-call | tf_op jit(solution)/shard_map/finish/pallas_call | solution.py:441
  (72 shorter events, 34.1 us)
Async XLA Ops:
  0.0 8.7 %collective-permute-start.1 = (bf16[512,1024]{1,0:T(8,128)(2,1)}, bf16[512,1024]{1,0:T(8,128)(2,1)}, u32[]{:S(2)}, u32[]{:S(2)}) collective-permute-start(bf16[512,1024]{1,0:T(8,128)(2,1)} %tokens_ref.3), channel_id=1, source_target_pairs={{0,1},{1,0},{2,3},{3,2},{4,5},{5,4},{6,7},{7,6},{8,9},{9,8},{10,11... | collective-permute-start | bytes 3145736 | tf_op jit(solution)/shard_map/ppermute | solution.py:551
  1.4 26.2 %collective-permute-start = (bf16[512,1024]{1,0:T(8,128)(2,1)}, bf16[512,1024]{1,0:T(8,128)(2,1)}, u32[]{:S(2)}, u32[]{:S(2)}) collective-permute-start(bf16[512,1024]{1,0:T(8,128)(2,1)} %tokens_ref.3), channel_id=1, source_target_pairs={{0,2},{1,3},{2,4},{3,5},{4,6},{5,7},{6,8},{7,9},{8,10},{9,11},{10,... | collective-permute-start | bytes 3145736 | tf_op jit(solution)/shard_map/ppermute | solution.py:25
  27.6 10.6 %collective-permute-start.2 = (bf16[512,1024]{1,0:T(8,128)(2,1)}, bf16[512,1024]{1,0:T(8,128)(2,1)}, u32[]{:S(2)}, u32[]{:S(2)}) collective-permute-start(bf16[512,1024]{1,0:T(8,128)(2,1)} %collective-permute-done.rows_ref), channel_id=1, source_target_pairs={{0,1},{1,0},{2,3},{3,2},{4,5},{5,4},{6,7},{7,6},{8,9},{9,8},{10,11... | collective-permute-start | bytes 3145736 | tf_op jit(solution)/shard_map/ppermute | solution.py:551
  28.4 18.1 %collective-permute-start.3 = (bf16[256,1024]{1,0:T(8,128)(2,1)}, bf16[256,1024]{1,0:T(8,128)(2,1)}, u32[]{:S(2)}, u32[]{:S(2)}) collective-permute-start(bf16[256,1024]{1,0:T(8,128)(2,1)} %refs_0_.6), channel_id=1, source_target_pairs={{0,8},{8,16},{16,24},{24,0},{1,9},{9,17},{17,25},{25,1},{2,10},{10... | collective-permute-start | bytes 1572872 | tf_op jit(solution)/shard_map/ppermute | solution.py:561
  32.6 13.9 %collective-permute-start.4 = (bf16[256,1024]{1,0:T(8,128)(2,1)}, bf16[256,1024]{1,0:T(8,128)(2,1)}, u32[]{:S(2)}, u32[]{:S(2)}) collective-permute-start(bf16[256,1024]{1,0:T(8,128)(2,1)} %refs_0_.6), channel_id=1, source_target_pairs={{0,24},{8,0},{16,8},{24,16},{1,25},{9,1},{17,9},{25,17},{2,26},{10... | collective-permute-start | bytes 1572872 | tf_op jit(solution)/shard_map/ppermute | solution.py:561
  41.0 11.0 %copy-start = (bf16[1024,1024]{1,0:T(8,128)(2,1)S(1)}, bf16[1024,1024]{1,0:T(8,128)(2,1)}, u32[]{:S(2)}) copy-start(bf16[1024,1024]{1,0:T(8,128)(2,1)} %their_ref.3) | copy-start | bytes 6291460
  46.5 5.5 %collective-permute-start.5 = (bf16[512,512]{1,0:T(8,128)(2,1)S(1)}, bf16[512,512]{1,0:T(8,128)(2,1)S(1)}, u32[]{:S(2)}, u32[]{:S(2)}) collective-permute-start(bf16[512,512]{1,0:T(8,128)(2,1)S(1)} %slice_bitcast_fusion), channel_id=1, source_target_pairs={{0,1},{1,0},{2,3},{3,2},{4,5},{5,4},{6,7},{7,6},{8,9},{9,8},{10,11... | collective-permute-start | bytes 1572872 | tf_op jit(solution)/shard_map/ppermute | solution.py:551
  47.4 16.0 %collective-permute-start.7 = (bf16[256,1024]{1,0:T(8,128)(2,1)}, bf16[256,1024]{1,0:T(8,128)(2,1)}, u32[]{:S(2)}, u32[]{:S(2)}) collective-permute-start(bf16[256,1024]{1,0:T(8,128)(2,1)} %collective-permute-done.4.refs_3_), channel_id=1, source_target_pairs={{0,24},{8,0},{16,8},{24,16},{1,25},{9,1},{17,9},{25,17},{2,26},{10... | collective-permute-start | bytes 1572872 | tf_op jit(solution)/shard_map/ppermute | solution.py:561
  53.0 5.4 %collective-permute-start.6 = (bf16[16,1024]{1,0:T(8,128)(2,1)S(1)}, bf16[16,1024]{1,0:T(8,128)(2,1)S(1)}, u32[]{:S(2)}, u32[]{:S(2)}) collective-permute-start(bf16[16,1024]{1,0:T(8,128)(2,1)S(1)} %tail_project.1), channel_id=1, source_target_pairs={{0,1},{1,2},{2,3},{3,4},{4,5},{5,6},{6,7},{7,8},{8,9},{9,10},{10,1... | collective-permute-start | bytes 98312 | tf_op jit(solution)/shard_map/ppermute | solution.py:25
  63.4 17.5 %all-to-all-start = ((bf16[4,4,64,512]{3,2,1,0:T(8,128)(2,1)}), bf16[4,4,64,512]{3,2,1,0:T(8,128)(2,1)S(1)}, u32[]{:S(2)}, u32[]{:S(2)}) async-start(bf16[4,4,64,512]{3,2,1,0:T(8,128)(2,1)} %pack.1), calls=%async_computation | async-start | bytes 2097152 | tf_op jit(solution)/shard_map/all_to_all | solution.py:579
  66.9 2.9 %collective-permute-start.8 = (bf16[256,1024]{1,0:T(8,128)(2,1)}, bf16[256,1024]{1,0:T(8,128)(2,1)S(1)}, u32[]{:S(2)}, u32[]{:S(2)}) collective-permute-start(bf16[256,1024]{1,0:T(8,128)(2,1)} %refs_0_.6), channel_id=1, source_target_pairs={{0,1},{1,0},{2,3},{3,2},{4,5},{5,4},{6,7},{7,6},{8,9},{9,8},{10,11... | collective-permute-start | bytes 1572872 | tf_op jit(solution)/shard_map/ppermute | solution.py:551
  68.1 2.5 %collective-permute-start.11 = (bf16[256,1024]{1,0:T(8,128)(2,1)}, bf16[256,1024]{1,0:T(8,128)(2,1)S(1)}, u32[]{:S(2)}, u32[]{:S(2)}) collective-permute-start(bf16[256,1024]{1,0:T(8,128)(2,1)} %collective-permute-done.4.refs_3_), channel_id=1, source_target_pairs={{0,1},{1,0},{2,3},{3,2},{4,5},{5,4},{6,7},{7,6},{8,9},{9,8},{10,11... | collective-permute-start | bytes 1572872 | tf_op jit(solution)/shard_map/ppermute | solution.py:551
  68.2 3.2 %collective-permute-start.9 = (bf16[256,1024]{1,0:T(8,128)(2,1)}, bf16[256,1024]{1,0:T(8,128)(2,1)S(1)}, u32[]{:S(2)}, u32[]{:S(2)}) collective-permute-start(bf16[256,1024]{1,0:T(8,128)(2,1)} %collective-permute-done.3.refs_1_), channel_id=1, source_target_pairs={{0,1},{1,0},{2,3},{3,2},{4,5},{5,4},{6,7},{7,6},{8,9},{9,8},{10,11... | collective-permute-start | bytes 1572872 | tf_op jit(solution)/shard_map/ppermute | solution.py:551
  68.6 3.5 %collective-permute-start.10 = (bf16[256,1024]{1,0:T(8,128)(2,1)}, bf16[256,1024]{1,0:T(8,128)(2,1)S(1)}, u32[]{:S(2)}, u32[]{:S(2)}) collective-permute-start(bf16[256,1024]{1,0:T(8,128)(2,1)} %collective-permute-done.7.refs_2_), channel_id=1, source_target_pairs={{0,1},{1,0},{2,3},{3,2},{4,5},{5,4},{6,7},{7,6},{8,9},{9,8},{10,11... | collective-permute-start | bytes 1572872 | tf_op jit(solution)/shard_map/ppermute | solution.py:551
  69.8 11.1 %copy-start.11 = (bf16[256,1024]{1,0:T(8,128)(2,1)}, bf16[256,1024]{1,0:T(8,128)(2,1)S(1)}, u32[]{:S(2)}) copy-start(bf16[256,1024]{1,0:T(8,128)(2,1)S(1)} %collective-permute-done.8.refs_4_) | copy-start | bytes 1572868
  70.6 10.4 %copy-start.12 = (bf16[256,1024]{1,0:T(8,128)(2,1)}, bf16[256,1024]{1,0:T(8,128)(2,1)S(1)}, u32[]{:S(2)}) copy-start(bf16[256,1024]{1,0:T(8,128)(2,1)S(1)} %collective-permute-done.11.refs_7_) | copy-start | bytes 1572868
  71.3 9.6 %copy-start.13 = (bf16[256,1024]{1,0:T(8,128)(2,1)}, bf16[256,1024]{1,0:T(8,128)(2,1)S(1)}, u32[]{:S(2)}) copy-start(bf16[256,1024]{1,0:T(8,128)(2,1)S(1)} %collective-permute-done.9.refs_5_) | copy-start | bytes 1572868
  122.8 6.8 %collective-permute-start.12 = (bf16[16,64,128]{2,1,0:T(8,128)(2,1)S(1)}, bf16[16,64,128]{2,1,0:T(8,128)(2,1)S(1)}, u32[]{:S(2)}, u32[]{:S(2)}) collective-permute-start(bf16[16,64,128]{2,1,0:T(8,128)(2,1)S(1)} %slice.8.refs_0_), channel_id=1, source_target_pairs={{0,1},{1,0},{2,3},{3,2},{4,5},{5,4},{6,7},{7,6},{8,9},{9,8},{10,11... | collective-permute-start | bytes 786440 | tf_op jit(solution)/shard_map/ppermute | solution.py:551
  126.9 9.5 %collective-permute-start.13 = (bf16[16,64,128]{2,1,0:T(8,128)(2,1)S(1)}, bf16[16,64,128]{2,1,0:T(8,128)(2,1)S(1)}, u32[]{:S(2)}, u32[]{:S(2)}) collective-permute-start(bf16[16,64,128]{2,1,0:T(8,128)(2,1)S(1)} %slice.8.refs_0_), channel_id=1, source_target_pairs={{0,2},{2,4},{4,6},{6,0},{1,3},{3,5},{5,7},{7,1},{8,10},{10,12},{12... | collective-permute-start | bytes 786440 | tf_op jit(solution)/shard_map/ppermute | solution.py:592
  127.2 9.3 %collective-permute-start.14 = (bf16[16,64,128]{2,1,0:T(8,128)(2,1)S(1)}, bf16[16,64,128]{2,1,0:T(8,128)(2,1)S(1)}, u32[]{:S(2)}, u32[]{:S(2)}) collective-permute-start(bf16[16,64,128]{2,1,0:T(8,128)(2,1)S(1)} %slice.8.refs_0_), channel_id=1, source_target_pairs={{0,6},{2,0},{4,2},{6,4},{1,7},{3,1},{5,3},{7,5},{8,14},{10,8},{12,... | collective-permute-start | bytes 786440 | tf_op jit(solution)/shard_map/ppermute | solution.py:592
  129.6 11.4 %collective-permute-start.15 = (bf16[16,64,128]{2,1,0:T(8,128)(2,1)S(1)}, bf16[16,64,128]{2,1,0:T(8,128)(2,1)S(1)}, u32[]{:S(2)}, u32[]{:S(2)}) collective-permute-start(bf16[16,64,128]{2,1,0:T(8,128)(2,1)S(1)} %slice.8.refs_0_), channel_id=1, source_target_pairs={{0,4},{2,6},{4,0},{6,2},{1,5},{3,7},{5,1},{7,3},{8,12},{10,14},{12... | collective-permute-start | bytes 786440 | tf_op jit(solution)/shard_map/ppermute | solution.py:592
  141.0 5.7 %collective-permute-start.16 = (bf16[16,64,128]{2,1,0:T(8,128)(2,1)S(1)}, bf16[16,64,128]{2,1,0:T(8,128)(2,1)S(1)}, u32[]{:S(2)}, u32[]{:S(2)}) collective-permute-start(bf16[16,64,128]{2,1,0:T(8,128)(2,1)S(1)} %collective-permute-done.13.refs_0_), channel_id=1, source_target_pairs={{0,1},{1,0},{2,3},{3,2},{4,5},{5,4},{6,7},{7,6},{8,9},{9,8},{10,11... | collective-permute-start | bytes 786440 | tf_op jit(solution)/shard_map/ppermute | solution.py:551
  142.5 4.2 %collective-permute-start.17 = (bf16[16,64,128]{2,1,0:T(8,128)(2,1)S(1)}, bf16[16,64,128]{2,1,0:T(8,128)(2,1)S(1)}, u32[]{:S(2)}, u32[]{:S(2)}) collective-permute-start(bf16[16,64,128]{2,1,0:T(8,128)(2,1)S(1)} %collective-permute-done.14.refs_1_), channel_id=1, source_target_pairs={{0,1},{1,0},{2,3},{3,2},{4,5},{5,4},{6,7},{7,6},{8,9},{9,8},{10,11... | collective-permute-start | bytes 786440 | tf_op jit(solution)/shard_map/ppermute | solution.py:551
  142.6 4.2 %collective-permute-start.18 = (bf16[16,64,128]{2,1,0:T(8,128)(2,1)S(1)}, bf16[16,64,128]{2,1,0:T(8,128)(2,1)S(1)}, u32[]{:S(2)}, u32[]{:S(2)}) collective-permute-start(bf16[16,64,128]{2,1,0:T(8,128)(2,1)S(1)} %collective-permute-done.15.refs_2_), channel_id=1, source_target_pairs={{0,1},{1,0},{2,3},{3,2},{4,5},{5,4},{6,7},{7,6},{8,9},{9,8},{10,11... | collective-permute-start | bytes 786440 | tf_op jit(solution)/shard_map/ppermute | solution.py:551
  (11 other events, 27.3 us)

commit v10 on v9

--- a/solution.py
+++ b/solution.py
@@ -174,7 +174,8 @@
     )(core.reshape(1), tokens, mixed, theirs, weight, weight)
 
 
-def pack_kernel(hidden_ref, tail_ref, out_ref):
+def pack_kernel(y_ref, hidden_ref, tail_ref, *refs):
+    outs, all_ref = refs[:4], refs[4]
     blocks, places, groups, width = hidden_ref.shape
     rows = blocks * groups
     half = width // 2
@@ -188,19 +189,24 @@
             wide = jnp.where(first, tail, pltpu.roll(wide, 1, 0))
             part = wide.astype(jnp.bfloat16)
         for f in range(2):
-            out_ref[(j % 2) * 2 + f, j // 2] = part[:, f * half : (f + 1) * half]
-
-
-def pack(hidden, tail):
+            all_ref[(j % 2) * 2 + f, j // 2] = part[:, f * half : (f + 1) * half]
+    for r in range(4):
+        outs[r][...] = all_ref[(y_ref[0] + r) % 4]
+
+
+def pack(y, hidden, tail):
     count, width = hidden.shape
     groups = QB // SHORT
     blocks = count // QB
+    shape = (4, count // SHORT, width // 2)
     return pl.pallas_call(
         pack_kernel,
         name="pack",
-        out_shape=jax.ShapeDtypeStruct((4, 4, count // SHORT, width // 2), jnp.bfloat16),
+        in_specs=[pl.BlockSpec(memory_space=pltpu.SMEM)] + [pl.BlockSpec(memory_space=pltpu.VMEM)] * 2,
+        out_shape=[jax.ShapeDtypeStruct(shape, jnp.bfloat16)] * 4,
+        scratch_shapes=[pltpu.VMEM((4, *shape), jnp.bfloat16)],
         compiler_params=params(),
-    )(hidden.reshape(blocks, SHORT, groups, width), tail)
+    )(y.reshape(1), hidden.reshape(blocks, SHORT, groups, width), tail)
 
 
 def fine_own_kernel(q_ref, k_ref, v_ref, top_ref, acc_ref, s_ref, p_ref):
@@ -343,44 +349,45 @@
     )(where, q, *keys, *values, *state)
 
 
-def shorten_kernel(spots_of, where_ref, grouped_ref, *refs):
-    pieces, out_ref = refs[:-1], refs[-1]
-    owners, parts, rows, depth = grouped_ref.shape
+def shorten_kernel(spots_of, where_ref, *refs):
+    grouped, pieces, outs = refs[:4], refs[4:-4], refs[-4:]
+    parts, rows, depth = grouped[0].shape
     total = None
-    for (distance, other, first), piece in zip(spots_of, pieces):
+    for (distance, other), piece in zip(spots_of, pieces):
         size = piece.shape[0]
         x = (where_ref[0] + parts - distance) % parts
         core = 1 - where_ref[1] if other else where_ref[1]
-        columns = pl.ds(pl.multiple_of(core * (depth // 2) + first, 128), size)
-        part = grouped_ref[:, x, :, columns].reshape(owners * rows, size)
+        columns = pl.ds(pl.multiple_of(core * size, size), size)
+        part = jnp.concatenate([ref[x, :, columns] for ref in grouped], axis=0)
         term = dot(part, piece[...], ((1,), (0,)))
         total = term if total is None else total + term
-    out_ref[...] = total.reshape(owners, rows, -1).astype(jnp.bfloat16)
+    for r in range(4):
+        outs[r][...] = total[r * rows : (r + 1) * rows].astype(jnp.bfloat16)
 
 
 def shorten(where, grouped, pieces, spots_of):
-    owners, parts, rows, depth = grouped.shape
+    parts, rows, depth = grouped[0].shape
     width = pieces[0].shape[1]
     tile = width // 2
     return pl.pallas_call(
         functools.partial(shorten_kernel, spots_of),
         name="shorten",
         grid=(2,),
-        in_specs=[
-            pl.BlockSpec(memory_space=pltpu.SMEM),
-            pl.BlockSpec(grouped.shape, lambda i: (0, 0, 0, 0)),
-        ]
+        in_specs=[pl.BlockSpec(memory_space=pltpu.SMEM)]
+        + [pl.BlockSpec(grouped[0].shape, lambda i: (0, 0, 0))] * 4
         + [pl.BlockSpec((piece.shape[0], tile), lambda i: (0, i)) for piece in pieces],
-        out_specs=pl.BlockSpec((owners, rows, tile), lambda i: (0, 0, i)),
-        out_shape=jax.ShapeDtypeStruct((owners, rows, width), jnp.bfloat16),
+        out_specs=[pl.BlockSpec((rows, tile), lambda i: (0, i))] * 4,
+        out_shape=[jax.ShapeDtypeStruct((rows, width), jnp.bfloat16)] * 4,
         compiler_params=params(60),
-    )(where, grouped, *pieces)
-
-
-def coarse_project_kernel(part_ref, q_ref, k_ref, v_ref, short_ref, qkv_ref, norm_ref):
+    )(where, *grouped, *pieces)
+
+
+def coarse_project_kernel(*refs):
+    parts, (q_ref, k_ref, v_ref, short_ref, qkv_ref, norm_ref) = refs[:4], refs[4:]
+
     @pl.when(pl.program_id(0) == 0)
     def _():
-        short = jnp.sum(part_ref[...].astype(jnp.float32), axis=0).astype(jnp.bfloat16)
+        short = sum(ref[...].astype(jnp.float32) for ref in parts).astype(jnp.bfloat16)
         short_ref[...] = short
         norm_ref[...] = normed(short)
 
@@ -395,14 +402,14 @@
 
 
 def coarse_project(partial, query, key, value):
-    owners, rows, width = partial.shape
+    rows, width = partial[0].shape
     tile = 4 * HEAD_DIM
     spec = pl.BlockSpec((width, tile), lambda i: (0, i))
     return pl.pallas_call(
         coarse_project_kernel,
         name="coarse_project",
         grid=(width // tile,),
-        in_specs=[pl.BlockSpec(partial.shape, lambda i: (0, 0, 0)), spec, spec, spec],
+        in_specs=[pl.BlockSpec((rows, width), lambda i: (0, 0))] * 4 + [spec, spec, spec],
         out_specs=[
             pl.BlockSpec((rows, width), lambda i: (0, 0)),
             pl.BlockSpec((4, rows, 3 * HEAD_DIM), lambda i: (i, 0, 0)),
@@ -413,7 +420,7 @@
         ],
         scratch_shapes=[pltpu.VMEM((rows, width), jnp.bfloat16)],
         compiler_params=params(60),
-    )(partial, query, key, value)
+    )(*partial, query, key, value)
 
 
 def finish_kernel(mixed_ref, out_weight_ref, short_ref, hidden_ref, out_ref, rows_ref):
@@ -563,7 +570,8 @@
     together = lax.optimization_barrier
     keys, values, query = project(core, chip, [*weights, fine_query])
     state = fine_own(query, keys, values)
-    far, state, query, short_weight = together((far, state, query, short_weight))
+    mate_weight = across(short_weight)
+    far, state, query, short_weight, mate_weight = together((far, state, query, short_weight, mate_weight))
     near = across(far)
     behind, ahead = along_x(short_weight, 1), along_x(short_weight, 3)
     far_keys, far_values = project(core, far, weights)
@@ -575,27 +583,33 @@
     theirs = across(fine_mixed[1])
     tail = from_behind(tail_project(core, tokens, fine_mixed, theirs, fine_out), 1)
     hidden, natural = out_project(core, tokens, fine_mixed, theirs, fine_out)
-    grouped, two_away = together((pack(hidden, tail), two_away))
-    grouped = lax.all_to_all(grouped, "y", 0, 0)
-    pieces = [short_weight, behind, two_away, ahead]
-    pieces = pieces + [across(piece) for piece in pieces]
-    spots_of = [(distance, other, 0) for other in (0, 1) for distance in range(4)]
+    mate_behind, mate_ahead = across(behind), across(ahead)
+    hidden, mate_behind, mate_ahead = together((hidden, mate_behind, mate_ahead))
+    y = lax.axis_index("y").astype(jnp.int32)
+
+    def along_y(block, distance):
+        return lax.ppermute(block, "y", [(i, (i + distance) % 4) for i in range(4)])
+
+    def exchange(blocks, sign):
+        return [along_y(block, sign * r) if r > 0 else block for r, block in enumerate(blocks)]
+
+    grouped = exchange(pack(y, hidden, tail), 1)
+    *grouped, two_away = together((*grouped, two_away))
+    pieces = [short_weight, behind, two_away, ahead, mate_weight, mate_behind, across(two_away), mate_ahead]
+    spots_of = [(distance, other) for other in (0, 1) for distance in range(4)]
     where = jnp.stack([lax.axis_index("x").astype(jnp.int32), core])
-    partial = lax.all_to_all(shorten(where, grouped, pieces, spots_of), "y", 0, 0)
+    partial = exchange(shorten(where, grouped, pieces, spots_of), -1)
     shortened, qkv = coarse_project(partial, coarse_query, coarse_key, coarse_value)
     qkv = lax.all_to_all(qkv, ("z", "x"), 0, 0)
     kv = qkv[:, :, : 2 * HEAD_DIM]
-    y, c = lax.axis_index("y"), lax.axis_index("c")
+    c = core
     mine = y * 2 + c
-
-    def around(block, distance):
-        return lax.ppermute(block, "y", [(i, (i + distance) % 4) for i in range(4)])
 
     def spot(distance, other=0):
         return ((y + distance) % 4) * 2 + (1 - c if other else c)
 
     mate_kv = across(kv)
-    below, above, beyond = around(kv, 1), around(kv, 3), around(kv, 2)
+    below, above, beyond = along_y(kv, 1), along_y(kv, 3), along_y(kv, 2)
     state = coarse_attend((mine, mine, spot(0, 1)), qkv, (kv, mate_kv), None, False)
     others = (below, above, beyond)
     state, *others = lax.optimization_barrier((state, *others))

time: 166 us -> 162 us (0.976)
  blocking collectives: 41.4 us -> 28.5 us
  waiting for transfers between devices: 29.2 us -> 35 us
  local copies, waits for them, and re-layouts: 11.1 us -> 13 us
    ppermute x3 -> x9, waiting for transfers between devices: 8.5 us -> 29.1 us  [along_y(): return lax.ppermute(block, 'y', [(i, (i + distance) % 4) for i in range(4)])]
    all_to_all x1 -> x0, blocking collectives: 11.4 us -> none  [body(): lax.all_to_all(shorten(where, grouped, pieces, spots_of), 'y', 0, 0)]
    all_to_all x1 -> x0, waiting for transfers between devices: 8.86 us -> none  [body(): grouped = lax.all_to_all(grouped, 'y', 0, 0)]
    ppermute x3 -> x9, starting transfers between devices: 2.68 us -> 10 us  [along_y(): return lax.ppermute(block, 'y', [(i, (i + distance) % 4) for i in range(4)])]
    ppermute x3, waiting for transfers between devices: 7.42 us -> 3.56 us  [along_x(): return lax.ppermute(block, 'x', [(i, (i + distance) % 4) for i in range(4)])]
    all_to_all x1 -> x0, starting transfers between devices: 3.52 us -> none  [body(): grouped = lax.all_to_all(grouped, 'y', 0, 0)]
    ppermute x11, starting transfers between devices: 10.9 us -> 8.65 us  [across(): return lax.ppermute(block, 'c', [(0, 1), (1, 0)])]
    unnamed x31 -> x43, local copies, waits for them, and re-layouts: 11 us -> 13 us
  transfers between devices with their start and end apart: 20 -> 25, of which waited for: 10 -> 9; matrix products, arithmetic and copies ran while one was open for 3% -> 3% of each run, Pallas kernels for 18% -> 18%
where the time goes in v10:
time: 162 us; the launch traced here: 161 us
  Pallas kernels  46.8 us (29%)
  starting transfers between devices  35 us (22%)
  waiting for transfers between devices  35 us (22%)
  blocking collectives  28.5 us (18%)
  local copies, waits for them, and re-layouts  13 us (8%)
  other arithmetic  2.41 us (1%)
    ppermute x9, waiting for transfers between devices, along_y(): return lax.ppermute(block, 'y', [(i, (i + distance) % 4) for i in range(4)])  29.1 us
    all_to_all x1, blocking collectives, body(): qkv = lax.all_to_all(qkv, ('z', 'x'), 0, 0)  17.9 us
    unnamed x43, local copies, waits for them, and re-layouts  13 us
    all_to_all x1, blocking collectives, body(): mixed = lax.all_to_all(mixed, ('z', 'x'), 0, 0)  10.6 us
    pallas_call x3, Pallas kernels, coarse_attend(): pl.pallas_call(functools.partial(coarse_kernel, len(parts), first, final)...  10.2 us
    ppermute x3, starting transfers between devices, along_x(): return lax.ppermute(block, 'x', [(i, (i + distance) % 4) for i in range(4)])  10.2 us
    pallas_call x3, Pallas kernels, project(): pl.pallas_call(functools.partial(project_kernel, number), name='project',...  10.1 us
    ppermute x9, starting transfers between devices, along_y(): return lax.ppermute(block, 'y', [(i, (i + distance) % 4) for i in range(4)])  10 us
  transfers between devices with their start and end apart: 25, of which 9 were waited for; matrix products, arithmetic and copies ran while one was open for 3% of the time, Pallas kernels for 18%

profile of v10, /device:TPU:1, one launch (start us, length us, event | category | flops | bytes accessed | tf_op | source)
XLA Modules:
  0.0 161.0 jit_solution(16149043725430123119)
XLA Ops:
  1.4 4.2 %collective-permute-start = (bf16[512,1024]{1,0:T(8,128)(2,1)}, bf16[512,1024]{1,0:T(8,128)(2,1)}, u32[]{:S(2)}, u32[]{:S(2)}) collective-permute-start(bf16[512,1024]{1,0:T(8,128)(2,1)} %tokens_ref.3), channel_id=1, source_target_pairs={{0,2},{1,3},{2,4},{3,5},{4,6},{5,7},{6,8},{7,9},{8,10},{9,11},{10,... | collective-permute-start | bytes 3145736 | tf_op jit(solution)/shard_map/ppermute | solution.py:25
  6.0 2.9 %copy.11 = bf16[1024,1024]{0,1:T(8,128)(2,1)S(1)} copy(bf16[1024,1024]{1,0:T(8,128)(2,1)} %param.13) | data formatting | bytes 4194304 | tf_op args[3]
  12.5 4.7 %project.3 = (bf16[1024,512]{1,0:T(8,128)(2,1)S(1)}, bf16[512,1024]{1,0:T(8,128)(2,1)S(1)}, bf16[1024,512]{1,0:T(8,128)(2,1)S(1)}) custom-call(s32[1]{0:T(128)} %bitcast.5.core_ref, bf16[1024,1024]{1,0:T(8,128)(2,1)S(1)} %pad_maximum_fusion.rows_ref, bf16[1024,1024]{1,0:T(8,128)(2,1)S(1)} %copy-done.1, bf16[1024,1024]{1,0:T(8,128)(2,1)S(1)} %bitcast.16, ...), custom_call_target="tpu_custom_call" | custom-call | flops 1 | bytes 1 | tf_op jit(solution)/shard_map/project/pallas_call | solution.py:88
  17.2 6.5 %fine_own.1 = (f32[4,8,8,256]{3,2,1,0:T(8,128)S(1)}, f32[4,8,80,256]{3,2,1,0:T(8,128)S(1)}) custom-call(bf16[1024,512]{1,0:T(8,128)(2,1)S(1)} %get-tuple-element.62.q_ref, bf16[1024,512]{1,0:T(8,128)(2,1)S(1)} %get-tuple-element.58.k_ref, bf16[512,1024]{1,0:T(8,128)(2,1)S(1)} %get-tuple-element.59.v_ref), custom_call_target="tpu_custom_call" | custom-call | flops 1 | bytes 1 | tf_op jit(solution)/shard_map/fine_own/pallas_call | solution.py:300
  28.4 4.2 %collective-permute-start.4 = (bf16[256,1024]{1,0:T(8,128)(2,1)}, bf16[256,1024]{1,0:T(8,128)(2,1)}, u32[]{:S(2)}, u32[]{:S(2)}) collective-permute-start(bf16[256,1024]{1,0:T(8,128)(2,1)} %refs_4_.1), channel_id=1, source_target_pairs={{0,8},{8,16},{16,24},{24,0},{1,9},{9,17},{17,25},{25,1},{2,10},{10... | collective-permute-start | bytes 1572872 | tf_op jit(solution)/shard_map/ppermute | solution.py:568
  35.5 2.6 %project.4 = (bf16[512,512]{1,0:T(8,128)(2,1)S(1)}, bf16[512,512]{1,0:T(8,128)(2,1)S(1)}) custom-call(s32[1]{0:T(128)} %bitcast.5.core_ref, bf16[512,1024]{1,0:T(8,128)(2,1)} %collective-permute-done.rows_ref, bf16[1024,1024]{1,0:T(8,128)(2,1)S(1)} %copy-done.2, bf16[1024,1024]{1,0:T(8,128)(2,1)S(1)} %bitcast.17), custom_call_target="tpu_custom_call" | custom-call | flops 1 | bytes 1 | tf_op jit(solution)/shard_map/project/pallas_call | solution.py:88
  38.2 2.8 %project.5 = (bf16[512,512]{1,0:T(8,128)(2,1)S(1)}, bf16[512,512]{1,0:T(8,128)(2,1)S(1)}) custom-call(s32[1]{0:T(128)} %bitcast.5.core_ref, bf16[512,1024]{1,0:T(8,128)(2,1)} %collective-permute-done.3.rows_ref, bf16[1024,1024]{1,0:T(8,128)(2,1)S(1)} %copy-done.2, bf16[1024,1024]{1,0:T(8,128)(2,1)S(1)} %bitcast.18), custom_call_target="tpu_custom_call" | custom-call | flops 1 | bytes 1 | tf_op jit(solution)/shard_map/project/pallas_call | solution.py:88
  42.9 3.6 %collective-permute-done.4.refs_5_ = bf16[256,1024]{1,0:T(8,128)(2,1)} collective-permute-done((bf16[256,1024]{1,0:T(8,128)(2,1)}, bf16[256,1024]{1,0:T(8,128)(2,1)}, u32[]{:S(2)}, u32[]{:S(2)}) %collective-permute-start.4) | collective-permute-done | bytes 524320 | tf_op jit(solution)/shard_map/ppermute | solution.py:568
  48.1 4.7 %collective-permute-start.13 = (bf16[256,1024]{1,0:T(8,128)(2,1)}, bf16[256,1024]{1,0:T(8,128)(2,1)S(1)}, u32[]{:S(2)}, u32[]{:S(2)}) collective-permute-start(bf16[256,1024]{1,0:T(8,128)(2,1)} %collective-permute-done.5.refs_7_), channel_id=1, source_target_pairs={{0,24},{8,0},{16,8},{24,16},{1,25},{9,1},{17,9},{25,17},{2,26},{10... | collective-permute-start | bytes 1572872 | tf_op jit(solution)/shard_map/ppermute | solution.py:568
  61.6 2.9 %collective-permute-start.11 = (bf16[4,64,512]{2,1,0:T(8,128)(2,1)S(1)}, bf16[4,64,512]{2,1,0:T(8,128)(2,1)S(1)}, u32[]{:S(2)}, u32[]{:S(2)}) collective-permute-start(bf16[4,64,512]{2,1,0:T(8,128)(2,1)S(1)} %get-tuple-element.78), channel_id=1, source_target_pairs={{0,4},{2,6},{4,0},{6,2},{1,5},{3,7},{5,1},{7,3},{8,12},{10,14},{12... | collective-permute-start | bytes 786440 | tf_op jit(solution)/shard_map/ppermute | solution.py:591
  65.0 5.7 %collective-permute-done.10.refs_1_ = bf16[4,64,512]{2,1,0:T(8,128)(2,1)S(1)} collective-permute-done((bf16[4,64,512]{2,1,0:T(8,128)(2,1)S(1)}, bf16[4,64,512]{2,1,0:T(8,128)(2,1)S(1)}, u32[]{:S(2)}, u32[]{:S(2)}) %collective-permute-start.10) | collective-permute-done | bytes 262176 | tf_op jit(solution)/shard_map/ppermute | solution.py:591
  70.7 5.3 %collective-permute-done.11.refs_2_ = bf16[4,64,512]{2,1,0:T(8,128)(2,1)S(1)} collective-permute-done((bf16[4,64,512]{2,1,0:T(8,128)(2,1)S(1)}, bf16[4,64,512]{2,1,0:T(8,128)(2,1)S(1)}, u32[]{:S(2)}, u32[]{:S(2)}) %collective-permute-start.11) | collective-permute-done | bytes 262176 | tf_op jit(solution)/shard_map/ppermute | solution.py:591
  79.4 4.3 %shorten.1 = (bf16[64,1024]{1,0:T(8,128)(2,1)}, bf16[64,1024]{1,0:T(8,128)(2,1)}, bf16[64,1024]{1,0:T(8,128)(2,1)}, bf16[64,1024]{1,0:T(8,128)(2,1)}) custom-call(s32[2]{0:T(128)} %pad_add_fusion.1.where_ref, bf16[4,64,512]{2,1,0:T(8,128)(2,1)} %copy-done.10, bf16[4,64,512]{2,1,0:T(8,128)(2,1)} %copy-done.15, bf16[4,64,512]{2,1,0:T(8,128)(2,1)} %copy-done.16, ...), custom_call_target="tpu_custom_call" | custom-call | tf_op jit(solution)/shard_map/shorten/pallas_call | solution.py:372
  86.9 2.7 %collective-permute-done.15.refs_1_ = bf16[64,1024]{1,0:T(8,128)(2,1)S(1)} collective-permute-done((bf16[64,1024]{1,0:T(8,128)(2,1)}, bf16[64,1024]{1,0:T(8,128)(2,1)S(1)}, u32[]{:S(2)}, u32[]{:S(2)}) %collective-permute-start.15) | collective-permute-done | bytes 131104 | tf_op jit(solution)/shard_map/ppermute | solution.py:591
  92.2 3.8 %collective-permute-done.17.refs_3_ = bf16[64,1024]{1,0:T(8,128)(2,1)S(1)} collective-permute-done((bf16[64,1024]{1,0:T(8,128)(2,1)}, bf16[64,1024]{1,0:T(8,128)(2,1)S(1)}, u32[]{:S(2)}, u32[]{:S(2)}) %collective-permute-start.17) | collective-permute-done | bytes 131104 | tf_op jit(solution)/shard_map/ppermute | solution.py:591
  96.7 5.6 %coarse_project.1 = (bf16[64,1024]{1,0:T(8,128)(2,1)}, bf16[16,64,192]{2,1,0:T(8,128)(2,1)}) custom-call(bf16[64,1024]{1,0:T(8,128)(2,1)} %get-tuple-element.88.refs_0_, bf16[64,1024]{1,0:T(8,128)(2,1)} %copy-done.18, bf16[64,1024]{1,0:T(8,128)(2,1)} %copy-done.19, bf16[64,1024]{1,0:T(8,128)(2,1)} %copy-done.20, bf16[1024,1024]{1,0:T(8,128)(2,1)} %refs_4_.2, ...), custom_call_target="tpu_custom_call" | custom-call | tf_op jit(solution)/shard_map/coarse_project/pallas_call | solution.py:408
  102.3 17.9 %all_to_all.10.q_ref = bf16[16,64,192]{2,1,0:T(8,128)(2,1)S(1)} all-to-all(bf16[16,64,192]{2,1,0:T(8,128)(2,1)} %get-tuple-element.92), channel_id=1, replica_groups=mesh['z'=4,'x'=4,'y'=4,'c'=2] {'z','x'}, dimensions={0} | all-to-all | bytes 786432 | tf_op jit(solution)/shard_map/all_to_all | solution.py:603
  122.3 2.7 %collective-permute-start.20 = (bf16[16,64,128]{2,1,0:T(8,128)(2,1)S(1)}, bf16[16,64,128]{2,1,0:T(8,128)(2,1)S(1)}, u32[]{:S(2)}, u32[]{:S(2)}) collective-permute-start(bf16[16,64,128]{2,1,0:T(8,128)(2,1)S(1)} %slice.8.refs_0_), channel_id=1, source_target_pairs={{0,6},{2,0},{4,2},{6,4},{1,7},{3,1},{5,3},{7,5},{8,14},{10,8},{12,... | collective-permute-start | bytes 786440 | tf_op jit(solution)/shard_map/ppermute | solution.py:591
  125.0 2.8 %coarse_attend.3 = (f32[4,8,256]{2,1,0:T(8,128)S(1)}, f32[4,80,256]{2,1,0:T(8,128)S(1)}) custom-call(s32[3]{0:T(128)S(1)} %pad_add_fusion.4.where_ref, bf16[16,64,192]{2,1,0:T(8,128)(2,1)S(1)} %all_to_all.10.q_ref, bf16[16,64,128]{2,1,0:T(8,128)(2,1)S(1)} %slice.8.refs_0_, bf16[16,64,128]{2,1,0:T(8,128)(2,1)S(1)} %collective-permute-done.18.refs_1_), custom_call_target="tpu_custom_call" | custom-call | flops 1610612736 | bytes 2097152 | tf_op jit(solution)/shard_map/coarse_attend/pallas_call | solution.py:527
  127.8 9.1 %collective-permute-done.19.refs_0_ = bf16[16,64,128]{2,1,0:T(8,128)(2,1)S(1)} collective-permute-done((bf16[16,64,128]{2,1,0:T(8,128)(2,1)S(1)}, bf16[16,64,128]{2,1,0:T(8,128)(2,1)S(1)}, u32[]{:S(2)}, u32[]{:S(2)}) %collective-permute-start.19) | collective-permute-done | bytes 262176 | tf_op jit(solution)/shard_map/ppermute | solution.py:591
  138.4 3.6 %coarse_attend.4 = (f32[4,8,256]{2,1,0:T(8,128)S(1)}, f32[4,80,256]{2,1,0:T(8,128)S(1)}) custom-call(s32[4]{0:T(128)S(1)} %get-tuple-element.112.where_ref, bf16[16,64,192]{2,1,0:T(8,128)(2,1)S(1)} %all_to_all.10.q_ref, bf16[16,64,128]{2,1,0:T(8,128)(2,1)S(1)} %collective-permute-done.19.refs_0_, bf16[16,64,128]{2,1,0:T(8,128)(2,1)S(1)} %collective-permute-done.20.refs_1_, ...), custom_call_target="tpu_custom_call" | custom-call | flops 2415919104 | bytes 2097152 | tf_op jit(solution)/shard_map/coarse_attend/pallas_call | solution.py:527
  142.1 3.8 %coarse_attend.5 = bf16[16,32,128]{2,1,0:T(8,128)(2,1)S(1)} custom-call(s32[4]{0:T(128)S(1)} %get-tuple-element.111.where_ref, bf16[16,64,192]{2,1,0:T(8,128)(2,1)S(1)} %all_to_all.10.q_ref, bf16[16,64,128]{2,1,0:T(8,128)(2,1)S(1)} %collective-permute-done.22.refs_0_, bf16[16,64,128]{2,1,0:T(8,128)(2,1)S(1)} %collective-permute-done.23.refs_1_, ...), custom_call_target="tpu_custom_call" | custom-call | flops 2415919104 | bytes 2097152 | tf_op jit(solution)/shard_map/coarse_attend/pallas_call | solution.py:527
  145.9 10.6 %all_to_all.11.mixed_ref = bf16[16,32,128]{2,1,0:T(8,128)(2,1)} all-to-all(bf16[16,32,128]{2,1,0:T(8,128)(2,1)S(1)} %coarse_attend.5), channel_id=1, replica_groups=mesh['z'=4,'x'=4,'y'=4,'c'=2] {'z','x'}, dimensions={0} | all-to-all | bytes 262144 | tf_op jit(solution)/shard_map/all_to_all | solution.py:620
  156.5 4.5 %finish.1 = bf16[512,1024]{1,0:T(8,128)(2,1)} custom-call(bf16[16,32,128]{2,1,0:T(8,128)(2,1)} %all_to_all.11.mixed_ref, bf16[1024,1024]{1,0:T(8,128)(2,1)} %out_weight_ref.1, bf16[64,1024]{1,0:T(8,128)(2,1)} %get-tuple-element.107.short_ref, bf16[512,1024]{1,0:T(8,128)(2,1)} %copy-done.9), custom_call_target="tpu_custom_call" | custom-call | tf_op jit(solution)/shard_map/finish/pallas_call | solution.py:448
  (93 shorter events, 39.3 us)
Async XLA Ops:
  0.0 8.9 %collective-permute-start.1 = (bf16[512,1024]{1,0:T(8,128)(2,1)}, bf16[512,1024]{1,0:T(8,128)(2,1)}, u32[]{:S(2)}, u32[]{:S(2)}) collective-permute-start(bf16[512,1024]{1,0:T(8,128)(2,1)} %tokens_ref.3), channel_id=1, source_target_pairs={{0,1},{1,0},{2,3},{3,2},{4,5},{5,4},{6,7},{7,6},{8,9},{9,8},{10,11... | collective-permute-start | bytes 3145736 | tf_op jit(solution)/shard_map/ppermute | solution.py:558
  1.4 26.2 %collective-permute-start = (bf16[512,1024]{1,0:T(8,128)(2,1)}, bf16[512,1024]{1,0:T(8,128)(2,1)}, u32[]{:S(2)}, u32[]{:S(2)}) collective-permute-start(bf16[512,1024]{1,0:T(8,128)(2,1)} %tokens_ref.3), channel_id=1, source_target_pairs={{0,2},{1,3},{2,4},{3,5},{4,6},{5,7},{6,8},{7,9},{8,10},{9,11},{10,... | collective-permute-start | bytes 3145736 | tf_op jit(solution)/shard_map/ppermute | solution.py:25
  5.7 20.5 %collective-permute-start.2 = (bf16[256,1024]{1,0:T(8,128)(2,1)}, bf16[256,1024]{1,0:T(8,128)(2,1)}, u32[]{:S(2)}, u32[]{:S(2)}) collective-permute-start(bf16[256,1024]{1,0:T(8,128)(2,1)} %refs_4_.1), channel_id=1, source_target_pairs={{0,1},{1,0},{2,3},{3,2},{4,5},{5,4},{6,7},{7,6},{8,9},{9,8},{10,11... | collective-permute-start | bytes 1572872 | tf_op jit(solution)/shard_map/ppermute | solution.py:558
  27.6 10.6 %collective-permute-start.3 = (bf16[512,1024]{1,0:T(8,128)(2,1)}, bf16[512,1024]{1,0:T(8,128)(2,1)}, u32[]{:S(2)}, u32[]{:S(2)}) collective-permute-start(bf16[512,1024]{1,0:T(8,128)(2,1)} %collective-permute-done.rows_ref), channel_id=1, source_target_pairs={{0,1},{1,0},{2,3},{3,2},{4,5},{5,4},{6,7},{7,6},{8,9},{9,8},{10,11... | collective-permute-start | bytes 3145736 | tf_op jit(solution)/shard_map/ppermute | solution.py:558
  28.4 18.1 %collective-permute-start.4 = (bf16[256,1024]{1,0:T(8,128)(2,1)}, bf16[256,1024]{1,0:T(8,128)(2,1)}, u32[]{:S(2)}, u32[]{:S(2)}) collective-permute-start(bf16[256,1024]{1,0:T(8,128)(2,1)} %refs_4_.1), channel_id=1, source_target_pairs={{0,8},{8,16},{16,24},{24,0},{1,9},{9,17},{17,25},{25,1},{2,10},{10... | collective-permute-start | bytes 1572872 | tf_op jit(solution)/shard_map/ppermute | solution.py:568
  32.6 13.9 %collective-permute-start.5 = (bf16[256,1024]{1,0:T(8,128)(2,1)}, bf16[256,1024]{1,0:T(8,128)(2,1)}, u32[]{:S(2)}, u32[]{:S(2)}) collective-permute-start(bf16[256,1024]{1,0:T(8,128)(2,1)} %refs_4_.1), channel_id=1, source_target_pairs={{0,24},{8,0},{16,8},{24,16},{1,25},{9,1},{17,9},{25,17},{2,26},{10... | collective-permute-start | bytes 1572872 | tf_op jit(solution)/shard_map/ppermute | solution.py:568
  46.5 6.2 %collective-permute-start.6 = (bf16[512,512]{1,0:T(8,128)(2,1)S(1)}, bf16[512,512]{1,0:T(8,128)(2,1)S(1)}, u32[]{:S(2)}, u32[]{:S(2)}) collective-permute-start(bf16[512,512]{1,0:T(8,128)(2,1)S(1)} %slice_bitcast_fusion), channel_id=1, source_target_pairs={{0,1},{1,0},{2,3},{3,2},{4,5},{5,4},{6,7},{7,6},{8,9},{9,8},{10,11... | collective-permute-start | bytes 1572872 | tf_op jit(solution)/shard_map/ppermute | solution.py:558
  47.6 11.5 %collective-permute-start.7 = (bf16[256,1024]{1,0:T(8,128)(2,1)}, bf16[256,1024]{1,0:T(8,128)(2,1)S(1)}, u32[]{:S(2)}, u32[]{:S(2)}) collective-permute-start(bf16[256,1024]{1,0:T(8,128)(2,1)} %collective-permute-done.4.refs_5_), channel_id=1, source_target_pairs={{0,1},{1,0},{2,3},{3,2},{4,5},{5,4},{6,7},{7,6},{8,9},{9,8},{10,11... | collective-permute-start | bytes 1572872 | tf_op jit(solution)/shard_map/ppermute | solution.py:558
  47.6 11.4 %collective-permute-start.8 = (bf16[256,1024]{1,0:T(8,128)(2,1)}, bf16[256,1024]{1,0:T(8,128)(2,1)S(1)}, u32[]{:S(2)}, u32[]{:S(2)}) collective-permute-start(bf16[256,1024]{1,0:T(8,128)(2,1)} %collective-permute-done.5.refs_7_), channel_id=1, source_target_pairs={{0,1},{1,0},{2,3},{3,2},{4,5},{5,4},{6,7},{7,6},{8,9},{9,8},{10,11... | collective-permute-start | bytes 1572872 | tf_op jit(solution)/shard_map/ppermute | solution.py:558
  48.1 16.9 %collective-permute-start.13 = (bf16[256,1024]{1,0:T(8,128)(2,1)}, bf16[256,1024]{1,0:T(8,128)(2,1)S(1)}, u32[]{:S(2)}, u32[]{:S(2)}) collective-permute-start(bf16[256,1024]{1,0:T(8,128)(2,1)} %collective-permute-done.5.refs_7_), channel_id=1, source_target_pairs={{0,24},{8,0},{16,8},{24,16},{1,25},{9,1},{17,9},{25,17},{2,26},{10... | collective-permute-start | bytes 1572872 | tf_op jit(solution)/shard_map/ppermute | solution.py:568
  53.7 5.4 %collective-permute-start.9 = (bf16[16,1024]{1,0:T(8,128)(2,1)S(1)}, bf16[16,1024]{1,0:T(8,128)(2,1)S(1)}, u32[]{:S(2)}, u32[]{:S(2)}) collective-permute-start(bf16[16,1024]{1,0:T(8,128)(2,1)S(1)} %tail_project.1), channel_id=1, source_target_pairs={{0,1},{1,2},{2,3},{3,4},{4,5},{5,6},{6,7},{7,8},{8,9},{9,10},{10,1... | collective-permute-start | bytes 98312 | tf_op jit(solution)/shard_map/ppermute | solution.py:25
  60.9 9.8 %collective-permute-start.10 = (bf16[4,64,512]{2,1,0:T(8,128)(2,1)S(1)}, bf16[4,64,512]{2,1,0:T(8,128)(2,1)S(1)}, u32[]{:S(2)}, u32[]{:S(2)}) collective-permute-start(bf16[4,64,512]{2,1,0:T(8,128)(2,1)S(1)} %get-tuple-element.77), channel_id=1, source_target_pairs={{0,2},{2,4},{4,6},{6,0},{1,3},{3,5},{5,7},{7,1},{8,10},{10,12},{12... | collective-permute-start | bytes 786440 | tf_op jit(solution)/shard_map/ppermute | solution.py:591
  61.6 14.3 %collective-permute-start.11 = (bf16[4,64,512]{2,1,0:T(8,128)(2,1)S(1)}, bf16[4,64,512]{2,1,0:T(8,128)(2,1)S(1)}, u32[]{:S(2)}, u32[]{:S(2)}) collective-permute-start(bf16[4,64,512]{2,1,0:T(8,128)(2,1)S(1)} %get-tuple-element.78), channel_id=1, source_target_pairs={{0,4},{2,6},{4,0},{6,2},{1,5},{3,7},{5,1},{7,3},{8,12},{10,14},{12... | collective-permute-start | bytes 786440 | tf_op jit(solution)/shard_map/ppermute | solution.py:591
  64.4 11.5 %collective-permute-start.12 = (bf16[4,64,512]{2,1,0:T(8,128)(2,1)S(1)}, bf16[4,64,512]{2,1,0:T(8,128)(2,1)S(1)}, u32[]{:S(2)}, u32[]{:S(2)}) collective-permute-start(bf16[4,64,512]{2,1,0:T(8,128)(2,1)S(1)} %get-tuple-element.79), channel_id=1, source_target_pairs={{0,6},{2,0},{4,2},{6,4},{1,7},{3,1},{5,3},{7,5},{8,14},{10,8},{12,... | collective-permute-start | bytes 786440 | tf_op jit(solution)/shard_map/ppermute | solution.py:591
  83.7 5.9 %collective-permute-start.15 = (bf16[64,1024]{1,0:T(8,128)(2,1)}, bf16[64,1024]{1,0:T(8,128)(2,1)S(1)}, u32[]{:S(2)}, u32[]{:S(2)}) collective-permute-start(bf16[64,1024]{1,0:T(8,128)(2,1)} %get-tuple-element.89), channel_id=1, source_target_pairs={{0,6},{2,0},{4,2},{6,4},{1,7},{3,1},{5,3},{7,5},{8,14},{10,8},{12,... | collective-permute-start | bytes 393224 | tf_op jit(solution)/shard_map/ppermute | solution.py:591
  86.1 6.1 %collective-permute-start.16 = (bf16[64,1024]{1,0:T(8,128)(2,1)}, bf16[64,1024]{1,0:T(8,128)(2,1)S(1)}, u32[]{:S(2)}, u32[]{:S(2)}) collective-permute-start(bf16[64,1024]{1,0:T(8,128)(2,1)} %get-tuple-element.90), channel_id=1, source_target_pairs={{0,4},{2,6},{4,0},{6,2},{1,5},{3,7},{5,1},{7,3},{8,12},{10,14},{12... | collective-permute-start | bytes 393224 | tf_op jit(solution)/shard_map/ppermute | solution.py:591
  86.9 9.1 %collective-permute-start.17 = (bf16[64,1024]{1,0:T(8,128)(2,1)}, bf16[64,1024]{1,0:T(8,128)(2,1)S(1)}, u32[]{:S(2)}, u32[]{:S(2)}) collective-permute-start(bf16[64,1024]{1,0:T(8,128)(2,1)} %get-tuple-element.91), channel_id=1, source_target_pairs={{0,2},{2,4},{4,6},{6,0},{1,3},{3,5},{5,7},{7,1},{8,10},{10,12},{12... | collective-permute-start | bytes 393224 | tf_op jit(solution)/shard_map/ppermute | solution.py:591
  120.2 4.8 %collective-permute-start.18 = (bf16[16,64,128]{2,1,0:T(8,128)(2,1)S(1)}, bf16[16,64,128]{2,1,0:T(8,128)(2,1)S(1)}, u32[]{:S(2)}, u32[]{:S(2)}) collective-permute-start(bf16[16,64,128]{2,1,0:T(8,128)(2,1)S(1)} %slice.8.refs_0_), channel_id=1, source_target_pairs={{0,1},{1,0},{2,3},{3,2},{4,5},{5,4},{6,7},{7,6},{8,9},{9,8},{10,11... | collective-permute-start | bytes 786440 | tf_op jit(solution)/shard_map/ppermute | solution.py:558
  122.3 14.6 %collective-permute-start.19 = (bf16[16,64,128]{2,1,0:T(8,128)(2,1)S(1)}, bf16[16,64,128]{2,1,0:T(8,128)(2,1)S(1)}, u32[]{:S(2)}, u32[]{:S(2)}) collective-permute-start(bf16[16,64,128]{2,1,0:T(8,128)(2,1)S(1)} %slice.8.refs_0_), channel_id=1, source_target_pairs={{0,2},{2,4},{4,6},{6,0},{1,3},{3,5},{5,7},{7,1},{8,10},{10,12},{12... | collective-permute-start | bytes 786440 | tf_op jit(solution)/shard_map/ppermute | solution.py:591
  122.3 14.6 %collective-permute-start.20 = (bf16[16,64,128]{2,1,0:T(8,128)(2,1)S(1)}, bf16[16,64,128]{2,1,0:T(8,128)(2,1)S(1)}, u32[]{:S(2)}, u32[]{:S(2)}) collective-permute-start(bf16[16,64,128]{2,1,0:T(8,128)(2,1)S(1)} %slice.8.refs_0_), channel_id=1, source_target_pairs={{0,6},{2,0},{4,2},{6,4},{1,7},{3,1},{5,3},{7,5},{8,14},{10,8},{12,... | collective-permute-start | bytes 786440 | tf_op jit(solution)/shard_map/ppermute | solution.py:591
  124.9 11.9 %collective-permute-start.21 = (bf16[16,64,128]{2,1,0:T(8,128)(2,1)S(1)}, bf16[16,64,128]{2,1,0:T(8,128)(2,1)S(1)}, u32[]{:S(2)}, u32[]{:S(2)}) collective-permute-start(bf16[16,64,128]{2,1,0:T(8,128)(2,1)S(1)} %slice.8.refs_0_), channel_id=1, source_target_pairs={{0,4},{2,6},{4,0},{6,2},{1,5},{3,7},{5,1},{7,3},{8,12},{10,14},{12... | collective-permute-start | bytes 786440 | tf_op jit(solution)/shard_map/ppermute | solution.py:591
  136.9 5.2 %collective-permute-start.22 = (bf16[16,64,128]{2,1,0:T(8,128)(2,1)S(1)}, bf16[16,64,128]{2,1,0:T(8,128)(2,1)S(1)}, u32[]{:S(2)}, u32[]{:S(2)}) collective-permute-start(bf16[16,64,128]{2,1,0:T(8,128)(2,1)S(1)} %collective-permute-done.19.refs_0_), channel_id=1, source_target_pairs={{0,1},{1,0},{2,3},{3,2},{4,5},{5,4},{6,7},{7,6},{8,9},{9,8},{10,11... | collective-permute-start | bytes 786440 | tf_op jit(solution)/shard_map/ppermute | solution.py:558
  137.8 4.2 %collective-permute-start.23 = (bf16[16,64,128]{2,1,0:T(8,128)(2,1)S(1)}, bf16[16,64,128]{2,1,0:T(8,128)(2,1)S(1)}, u32[]{:S(2)}, u32[]{:S(2)}) collective-permute-start(bf16[16,64,128]{2,1,0:T(8,128)(2,1)S(1)} %collective-permute-done.20.refs_1_), channel_id=1, source_target_pairs={{0,1},{1,0},{2,3},{3,2},{4,5},{5,4},{6,7},{7,6},{8,9},{9,8},{10,11... | collective-permute-start | bytes 786440 | tf_op jit(solution)/shard_map/ppermute | solution.py:558
  137.9 4.2 %collective-permute-start.24 = (bf16[16,64,128]{2,1,0:T(8,128)(2,1)S(1)}, bf16[16,64,128]{2,1,0:T(8,128)(2,1)S(1)}, u32[]{:S(2)}, u32[]{:S(2)}) collective-permute-start(bf16[16,64,128]{2,1,0:T(8,128)(2,1)S(1)} %collective-permute-done.21.refs_2_), channel_id=1, source_target_pairs={{0,1},{1,0},{2,3},{3,2},{4,5},{5,4},{6,7},{7,6},{8,9},{9,8},{10,11... | collective-permute-start | bytes 786440 | tf_op jit(solution)/shard_map/ppermute | solution.py:558
  (22 other events, 88.9 us)

commit v11 on v10

--- a/solution.py
+++ b/solution.py
@@ -383,44 +383,44 @@
 
 
 def coarse_project_kernel(*refs):
-    parts, (q_ref, k_ref, v_ref, short_ref, qkv_ref, norm_ref) = refs[:4], refs[4:]
-
-    @pl.when(pl.program_id(0) == 0)
-    def _():
-        short = sum(ref[...].astype(jnp.float32) for ref in parts).astype(jnp.bfloat16)
-        short_ref[...] = short
-        norm_ref[...] = normed(short)
-
-    rows = norm_ref[...]
-    for i, (ref, scale) in enumerate(((k_ref, None), (v_ref, None), (q_ref, SCALE))):
-        out = dot(rows, ref[...], ((1,), (0,)))
-        if scale is not None:
-            out = out * scale
+    parts, (k_ref, v_ref, q_ref, short_ref, qkv_ref, weight_ref, sems) = refs[:4], refs[4:]
+    copies = [
+        pltpu.make_async_copy(ref, weight_ref.at[i], sems.at[i])
+        for i, ref in enumerate((k_ref, v_ref, q_ref))
+    ]
+    for copy in copies:
+        copy.start()
+    short = sum(ref[...].astype(jnp.float32) for ref in parts).astype(jnp.bfloat16)
+    short_ref[...] = short
+    rows = normed(short)
+    for i, copy in enumerate(copies):
+        copy.wait()
+        out = dot(rows, weight_ref[i], ((1,), (0,)))
+        if i == 2:
+            out = out * SCALE
         out = out.astype(jnp.bfloat16)
-        for h in range(qkv_ref.shape[0]):
+        for h in range(HEADS):
             qkv_ref[h, :, i * HEAD_DIM : (i + 1) * HEAD_DIM] = out[:, h * HEAD_DIM : (h + 1) * HEAD_DIM]
 
 
 def coarse_project(partial, query, key, value):
     rows, width = partial[0].shape
-    tile = 4 * HEAD_DIM
-    spec = pl.BlockSpec((width, tile), lambda i: (0, i))
+    vmem = pl.BlockSpec(memory_space=pltpu.VMEM)
     return pl.pallas_call(
         coarse_project_kernel,
         name="coarse_project",
-        grid=(width // tile,),
-        in_specs=[pl.BlockSpec((rows, width), lambda i: (0, 0))] * 4 + [spec, spec, spec],
-        out_specs=[
-            pl.BlockSpec((rows, width), lambda i: (0, 0)),
-            pl.BlockSpec((4, rows, 3 * HEAD_DIM), lambda i: (i, 0, 0)),
-        ],
+        in_specs=[vmem] * 4 + [pl.BlockSpec(memory_space=pl.ANY)] * 3,
+        out_specs=[vmem] * 2,
         out_shape=[
             jax.ShapeDtypeStruct((rows, width), jnp.bfloat16),
             jax.ShapeDtypeStruct((HEADS, rows, 3 * HEAD_DIM), jnp.bfloat16),
         ],
-        scratch_shapes=[pltpu.VMEM((rows, width), jnp.bfloat16)],
+        scratch_shapes=[
+            pltpu.VMEM((3, width, width), jnp.bfloat16),
+            pltpu.SemaphoreType.DMA((3,)),
+        ],
         compiler_params=params(60),
-    )(*partial, query, key, value)
+    )(*partial, key, value, query)
 
 
 def finish_kernel(mixed_ref, out_weight_ref, short_ref, hidden_ref, out_ref, rows_ref):
@@ -444,11 +444,11 @@
 def finish(mixed, out_weight, short, hidden):
     count, width = hidden.shape
     rows = count // SHORT
-    tile = width // 4
+    tile = width // 2
     return pl.pallas_call(
         finish_kernel,
         name="finish",
-        grid=(4,),
+        grid=(2,),
         in_specs=[
             pl.BlockSpec(mixed.shape, lambda i: (0, 0, 0)),
             pl.BlockSpec((width, tile), lambda i: (0, i)),

time: 162 us -> 160 us (0.988)
  no operation moved by 1% of the time
where the time goes in v11:
time: 160 us
  Pallas kernels  45.3 us (28%)
  starting transfers between devices  35 us (22%)
  waiting for transfers between devices  35 us (22%)
  blocking collectives  28.5 us (18%)
  local copies, waits for them, and re-layouts  13 us (8%)
  other arithmetic  2.41 us (2%)
    ppermute x9, waiting for transfers between devices, along_y(): return lax.ppermute(block, 'y', [(i, (i + distance) % 4) for i in range(4)])  29.1 us
    all_to_all x1, blocking collectives, body(): qkv = lax.all_to_all(qkv, ('z', 'x'), 0, 0)  17.9 us
    unnamed x43, local copies, waits for them, and re-layouts  13 us
    all_to_all x1, blocking collectives, body(): mixed = lax.all_to_all(mixed, ('z', 'x'), 0, 0)  10.6 us
    pallas_call x3, Pallas kernels, coarse_attend(): pl.pallas_call(functools.partial(coarse_kernel, len(parts), first, final)...  10.2 us
    ppermute x3, starting transfers between devices, along_x(): return lax.ppermute(block, 'x', [(i, (i + distance) % 4) for i in range(4)])  10.2 us
    pallas_call x3, Pallas kernels, project(): pl.pallas_call(functools.partial(project_kernel, number), name='project',...  10.1 us
    ppermute x9, starting transfers between devices, along_y(): return lax.ppermute(block, 'y', [(i, (i + distance) % 4) for i in range(4)])  10 us
  transfers between devices with their start and end apart: 25, of which 9 were waited for; matrix products, arithmetic and copies ran while one was open for 3% of the time, Pallas kernels for 18%

profile of v11, /device:TPU:1, one launch (start us, length us, event | category | flops | bytes accessed | tf_op | source)
XLA Modules:
  0.0 159.6 jit_solution(6189231378711148396)
XLA Ops:
  1.4 4.2 %collective-permute-start = (bf16[512,1024]{1,0:T(8,128)(2,1)}, bf16[512,1024]{1,0:T(8,128)(2,1)}, u32[]{:S(2)}, u32[]{:S(2)}) collective-permute-start(bf16[512,1024]{1,0:T(8,128)(2,1)} %tokens_ref.3), channel_id=1, source_target_pairs={{0,2},{1,3},{2,4},{3,5},{4,6},{5,7},{6,8},{7,9},{8,10},{9,11},{10,... | collective-permute-start | bytes 3145736 | tf_op jit(solution)/shard_map/ppermute | solution.py:25
  6.0 2.9 %copy.11 = bf16[1024,1024]{0,1:T(8,128)(2,1)S(1)} copy(bf16[1024,1024]{1,0:T(8,128)(2,1)} %param.13) | data formatting | bytes 4194304 | tf_op args[3]
  12.5 4.7 %project.3 = (bf16[1024,512]{1,0:T(8,128)(2,1)S(1)}, bf16[512,1024]{1,0:T(8,128)(2,1)S(1)}, bf16[1024,512]{1,0:T(8,128)(2,1)S(1)}) custom-call(s32[1]{0:T(128)} %bitcast.5.core_ref, bf16[1024,1024]{1,0:T(8,128)(2,1)S(1)} %pad_maximum_fusion.rows_ref, bf16[1024,1024]{1,0:T(8,128)(2,1)S(1)} %copy-done.1, bf16[1024,1024]{1,0:T(8,128)(2,1)S(1)} %bitcast.16, ...), custom_call_target="tpu_custom_call" | custom-call | flops 1 | bytes 1 | tf_op jit(solution)/shard_map/project/pallas_call | solution.py:88
  17.2 6.5 %fine_own.1 = (f32[4,8,8,256]{3,2,1,0:T(8,128)S(1)}, f32[4,8,80,256]{3,2,1,0:T(8,128)S(1)}) custom-call(bf16[1024,512]{1,0:T(8,128)(2,1)S(1)} %get-tuple-element.62.q_ref, bf16[1024,512]{1,0:T(8,128)(2,1)S(1)} %get-tuple-element.58.k_ref, bf16[512,1024]{1,0:T(8,128)(2,1)S(1)} %get-tuple-element.59.v_ref), custom_call_target="tpu_custom_call" | custom-call | flops 1 | bytes 1 | tf_op jit(solution)/shard_map/fine_own/pallas_call | solution.py:300
  28.4 4.2 %collective-permute-start.4 = (bf16[256,1024]{1,0:T(8,128)(2,1)}, bf16[256,1024]{1,0:T(8,128)(2,1)}, u32[]{:S(2)}, u32[]{:S(2)}) collective-permute-start(bf16[256,1024]{1,0:T(8,128)(2,1)} %refs_4_.1), channel_id=1, source_target_pairs={{0,8},{8,16},{16,24},{24,0},{1,9},{9,17},{17,25},{25,1},{2,10},{10... | collective-permute-start | bytes 1572872 | tf_op jit(solution)/shard_map/ppermute | solution.py:568
  35.5 2.6 %project.4 = (bf16[512,512]{1,0:T(8,128)(2,1)S(1)}, bf16[512,512]{1,0:T(8,128)(2,1)S(1)}) custom-call(s32[1]{0:T(128)} %bitcast.5.core_ref, bf16[512,1024]{1,0:T(8,128)(2,1)} %collective-permute-done.rows_ref, bf16[1024,1024]{1,0:T(8,128)(2,1)S(1)} %copy-done.2, bf16[1024,1024]{1,0:T(8,128)(2,1)S(1)} %bitcast.17), custom_call_target="tpu_custom_call" | custom-call | flops 1 | bytes 1 | tf_op jit(solution)/shard_map/project/pallas_call | solution.py:88
  38.2 2.8 %project.5 = (bf16[512,512]{1,0:T(8,128)(2,1)S(1)}, bf16[512,512]{1,0:T(8,128)(2,1)S(1)}) custom-call(s32[1]{0:T(128)} %bitcast.5.core_ref, bf16[512,1024]{1,0:T(8,128)(2,1)} %collective-permute-done.3.rows_ref, bf16[1024,1024]{1,0:T(8,128)(2,1)S(1)} %copy-done.2, bf16[1024,1024]{1,0:T(8,128)(2,1)S(1)} %bitcast.18), custom_call_target="tpu_custom_call" | custom-call | flops 1 | bytes 1 | tf_op jit(solution)/shard_map/project/pallas_call | solution.py:88
  42.9 3.6 %collective-permute-done.4.refs_5_ = bf16[256,1024]{1,0:T(8,128)(2,1)} collective-permute-done((bf16[256,1024]{1,0:T(8,128)(2,1)}, bf16[256,1024]{1,0:T(8,128)(2,1)}, u32[]{:S(2)}, u32[]{:S(2)}) %collective-permute-start.4) | collective-permute-done | bytes 524320 | tf_op jit(solution)/shard_map/ppermute | solution.py:568
  48.1 4.7 %collective-permute-start.13 = (bf16[256,1024]{1,0:T(8,128)(2,1)}, bf16[256,1024]{1,0:T(8,128)(2,1)S(1)}, u32[]{:S(2)}, u32[]{:S(2)}) collective-permute-start(bf16[256,1024]{1,0:T(8,128)(2,1)} %collective-permute-done.5.refs_7_), channel_id=1, source_target_pairs={{0,24},{8,0},{16,8},{24,16},{1,25},{9,1},{17,9},{25,17},{2,26},{10... | collective-permute-start | bytes 1572872 | tf_op jit(solution)/shard_map/ppermute | solution.py:568
  61.6 2.9 %collective-permute-start.11 = (bf16[4,64,512]{2,1,0:T(8,128)(2,1)S(1)}, bf16[4,64,512]{2,1,0:T(8,128)(2,1)S(1)}, u32[]{:S(2)}, u32[]{:S(2)}) collective-permute-start(bf16[4,64,512]{2,1,0:T(8,128)(2,1)S(1)} %get-tuple-element.78), channel_id=1, source_target_pairs={{0,4},{2,6},{4,0},{6,2},{1,5},{3,7},{5,1},{7,3},{8,12},{10,14},{12... | collective-permute-start | bytes 786440 | tf_op jit(solution)/shard_map/ppermute | solution.py:591
  65.0 5.7 %collective-permute-done.10.refs_1_ = bf16[4,64,512]{2,1,0:T(8,128)(2,1)S(1)} collective-permute-done((bf16[4,64,512]{2,1,0:T(8,128)(2,1)S(1)}, bf16[4,64,512]{2,1,0:T(8,128)(2,1)S(1)}, u32[]{:S(2)}, u32[]{:S(2)}) %collective-permute-start.10) | collective-permute-done | bytes 262176 | tf_op jit(solution)/shard_map/ppermute | solution.py:591
  70.7 5.3 %collective-permute-done.11.refs_2_ = bf16[4,64,512]{2,1,0:T(8,128)(2,1)S(1)} collective-permute-done((bf16[4,64,512]{2,1,0:T(8,128)(2,1)S(1)}, bf16[4,64,512]{2,1,0:T(8,128)(2,1)S(1)}, u32[]{:S(2)}, u32[]{:S(2)}) %collective-permute-start.11) | collective-permute-done | bytes 262176 | tf_op jit(solution)/shard_map/ppermute | solution.py:591
  79.4 4.3 %shorten.1 = (bf16[64,1024]{1,0:T(8,128)(2,1)}, bf16[64,1024]{1,0:T(8,128)(2,1)}, bf16[64,1024]{1,0:T(8,128)(2,1)}, bf16[64,1024]{1,0:T(8,128)(2,1)}) custom-call(s32[2]{0:T(128)} %pad_add_fusion.1.where_ref, bf16[4,64,512]{2,1,0:T(8,128)(2,1)} %copy-done.10, bf16[4,64,512]{2,1,0:T(8,128)(2,1)} %copy-done.15, bf16[4,64,512]{2,1,0:T(8,128)(2,1)} %copy-done.16, ...), custom_call_target="tpu_custom_call" | custom-call | tf_op jit(solution)/shard_map/shorten/pallas_call | solution.py:372
  86.9 2.7 %collective-permute-done.15.refs_1_ = bf16[64,1024]{1,0:T(8,128)(2,1)S(1)} collective-permute-done((bf16[64,1024]{1,0:T(8,128)(2,1)}, bf16[64,1024]{1,0:T(8,128)(2,1)S(1)}, u32[]{:S(2)}, u32[]{:S(2)}) %collective-permute-start.15) | collective-permute-done | bytes 131104 | tf_op jit(solution)/shard_map/ppermute | solution.py:591
  92.2 3.8 %collective-permute-done.17.refs_3_ = bf16[64,1024]{1,0:T(8,128)(2,1)S(1)} collective-permute-done((bf16[64,1024]{1,0:T(8,128)(2,1)}, bf16[64,1024]{1,0:T(8,128)(2,1)S(1)}, u32[]{:S(2)}, u32[]{:S(2)}) %collective-permute-start.17) | collective-permute-done | bytes 131104 | tf_op jit(solution)/shard_map/ppermute | solution.py:591
  96.7 5.3 %coarse_project.1 = (bf16[64,1024]{1,0:T(8,128)(2,1)}, bf16[16,64,192]{2,1,0:T(8,128)(2,1)}) custom-call(bf16[64,1024]{1,0:T(8,128)(2,1)} %get-tuple-element.88.refs_0_, bf16[64,1024]{1,0:T(8,128)(2,1)} %copy-done.18, bf16[64,1024]{1,0:T(8,128)(2,1)} %copy-done.19, bf16[64,1024]{1,0:T(8,128)(2,1)} %copy-done.20, bf16[1024,1024]{1,0:T(8,128)(2,1)} %refs_4_.2, ...), custom_call_target="tpu_custom_call" | custom-call | tf_op jit(solution)/shard_map/coarse_project/pallas_call | solution.py:409
  102.0 17.9 %all_to_all.10.q_ref = bf16[16,64,192]{2,1,0:T(8,128)(2,1)S(1)} all-to-all(bf16[16,64,192]{2,1,0:T(8,128)(2,1)} %get-tuple-element.92), channel_id=1, replica_groups=mesh['z'=4,'x'=4,'y'=4,'c'=2] {'z','x'}, dimensions={0} | all-to-all | bytes 786432 | tf_op jit(solution)/shard_map/all_to_all | solution.py:603
  122.0 2.7 %collective-permute-start.20 = (bf16[16,64,128]{2,1,0:T(8,128)(2,1)S(1)}, bf16[16,64,128]{2,1,0:T(8,128)(2,1)S(1)}, u32[]{:S(2)}, u32[]{:S(2)}) collective-permute-start(bf16[16,64,128]{2,1,0:T(8,128)(2,1)S(1)} %slice.8.refs_0_), channel_id=1, source_target_pairs={{0,6},{2,0},{4,2},{6,4},{1,7},{3,1},{5,3},{7,5},{8,14},{10,8},{12,... | collective-permute-start | bytes 786440 | tf_op jit(solution)/shard_map/ppermute | solution.py:591
  124.8 2.8 %coarse_attend.3 = (f32[4,8,256]{2,1,0:T(8,128)S(1)}, f32[4,80,256]{2,1,0:T(8,128)S(1)}) custom-call(s32[3]{0:T(128)S(1)} %pad_add_fusion.4.where_ref, bf16[16,64,192]{2,1,0:T(8,128)(2,1)S(1)} %all_to_all.10.q_ref, bf16[16,64,128]{2,1,0:T(8,128)(2,1)S(1)} %slice.8.refs_0_, bf16[16,64,128]{2,1,0:T(8,128)(2,1)S(1)} %collective-permute-done.18.refs_1_), custom_call_target="tpu_custom_call" | custom-call | flops 1610612736 | bytes 2097152 | tf_op jit(solution)/shard_map/coarse_attend/pallas_call | solution.py:527
  127.6 9.1 %collective-permute-done.19.refs_0_ = bf16[16,64,128]{2,1,0:T(8,128)(2,1)S(1)} collective-permute-done((bf16[16,64,128]{2,1,0:T(8,128)(2,1)S(1)}, bf16[16,64,128]{2,1,0:T(8,128)(2,1)S(1)}, u32[]{:S(2)}, u32[]{:S(2)}) %collective-permute-start.19) | collective-permute-done | bytes 262176 | tf_op jit(solution)/shard_map/ppermute | solution.py:591
  138.2 3.6 %coarse_attend.4 = (f32[4,8,256]{2,1,0:T(8,128)S(1)}, f32[4,80,256]{2,1,0:T(8,128)S(1)}) custom-call(s32[4]{0:T(128)S(1)} %get-tuple-element.112.where_ref, bf16[16,64,192]{2,1,0:T(8,128)(2,1)S(1)} %all_to_all.10.q_ref, bf16[16,64,128]{2,1,0:T(8,128)(2,1)S(1)} %collective-permute-done.19.refs_0_, bf16[16,64,128]{2,1,0:T(8,128)(2,1)S(1)} %collective-permute-done.20.refs_1_, ...), custom_call_target="tpu_custom_call" | custom-call | flops 2415919104 | bytes 2097152 | tf_op jit(solution)/shard_map/coarse_attend/pallas_call | solution.py:527
  141.8 3.8 %coarse_attend.5 = bf16[16,32,128]{2,1,0:T(8,128)(2,1)S(1)} custom-call(s32[4]{0:T(128)S(1)} %get-tuple-element.111.where_ref, bf16[16,64,192]{2,1,0:T(8,128)(2,1)S(1)} %all_to_all.10.q_ref, bf16[16,64,128]{2,1,0:T(8,128)(2,1)S(1)} %collective-permute-done.22.refs_0_, bf16[16,64,128]{2,1,0:T(8,128)(2,1)S(1)} %collective-permute-done.23.refs_1_, ...), custom_call_target="tpu_custom_call" | custom-call | flops 2415919104 | bytes 2097152 | tf_op jit(solution)/shard_map/coarse_attend/pallas_call | solution.py:527
  145.6 10.6 %all_to_all.11.mixed_ref = bf16[16,32,128]{2,1,0:T(8,128)(2,1)} all-to-all(bf16[16,32,128]{2,1,0:T(8,128)(2,1)S(1)} %coarse_attend.5), channel_id=1, replica_groups=mesh['z'=4,'x'=4,'y'=4,'c'=2] {'z','x'}, dimensions={0} | all-to-all | bytes 262144 | tf_op jit(solution)/shard_map/all_to_all | solution.py:620
  156.2 3.3 %finish.1 = bf16[512,1024]{1,0:T(8,128)(2,1)} custom-call(bf16[16,32,128]{2,1,0:T(8,128)(2,1)} %all_to_all.11.mixed_ref, bf16[1024,1024]{1,0:T(8,128)(2,1)} %out_weight_ref.1, bf16[64,1024]{1,0:T(8,128)(2,1)} %get-tuple-element.107.short_ref, bf16[512,1024]{1,0:T(8,128)(2,1)} %copy-done.9), custom_call_target="tpu_custom_call" | custom-call | tf_op jit(solution)/shard_map/finish/pallas_call | solution.py:448
  (93 shorter events, 39.3 us)
Async XLA Ops:
  0.0 8.9 %collective-permute-start.1 = (bf16[512,1024]{1,0:T(8,128)(2,1)}, bf16[512,1024]{1,0:T(8,128)(2,1)}, u32[]{:S(2)}, u32[]{:S(2)}) collective-permute-start(bf16[512,1024]{1,0:T(8,128)(2,1)} %tokens_ref.3), channel_id=1, source_target_pairs={{0,1},{1,0},{2,3},{3,2},{4,5},{5,4},{6,7},{7,6},{8,9},{9,8},{10,11... | collective-permute-start | bytes 3145736 | tf_op jit(solution)/shard_map/ppermute | solution.py:558
  1.4 26.2 %collective-permute-start = (bf16[512,1024]{1,0:T(8,128)(2,1)}, bf16[512,1024]{1,0:T(8,128)(2,1)}, u32[]{:S(2)}, u32[]{:S(2)}) collective-permute-start(bf16[512,1024]{1,0:T(8,128)(2,1)} %tokens_ref.3), channel_id=1, source_target_pairs={{0,2},{1,3},{2,4},{3,5},{4,6},{5,7},{6,8},{7,9},{8,10},{9,11},{10,... | collective-permute-start | bytes 3145736 | tf_op jit(solution)/shard_map/ppermute | solution.py:25
  5.7 20.5 %collective-permute-start.2 = (bf16[256,1024]{1,0:T(8,128)(2,1)}, bf16[256,1024]{1,0:T(8,128)(2,1)}, u32[]{:S(2)}, u32[]{:S(2)}) collective-permute-start(bf16[256,1024]{1,0:T(8,128)(2,1)} %refs_4_.1), channel_id=1, source_target_pairs={{0,1},{1,0},{2,3},{3,2},{4,5},{5,4},{6,7},{7,6},{8,9},{9,8},{10,11... | collective-permute-start | bytes 1572872 | tf_op jit(solution)/shard_map/ppermute | solution.py:558
  27.6 10.6 %collective-permute-start.3 = (bf16[512,1024]{1,0:T(8,128)(2,1)}, bf16[512,1024]{1,0:T(8,128)(2,1)}, u32[]{:S(2)}, u32[]{:S(2)}) collective-permute-start(bf16[512,1024]{1,0:T(8,128)(2,1)} %collective-permute-done.rows_ref), channel_id=1, source_target_pairs={{0,1},{1,0},{2,3},{3,2},{4,5},{5,4},{6,7},{7,6},{8,9},{9,8},{10,11... | collective-permute-start | bytes 3145736 | tf_op jit(solution)/shard_map/ppermute | solution.py:558
  28.4 18.1 %collective-permute-start.4 = (bf16[256,1024]{1,0:T(8,128)(2,1)}, bf16[256,1024]{1,0:T(8,128)(2,1)}, u32[]{:S(2)}, u32[]{:S(2)}) collective-permute-start(bf16[256,1024]{1,0:T(8,128)(2,1)} %refs_4_.1), channel_id=1, source_target_pairs={{0,8},{8,16},{16,24},{24,0},{1,9},{9,17},{17,25},{25,1},{2,10},{10... | collective-permute-start | bytes 1572872 | tf_op jit(solution)/shard_map/ppermute | solution.py:568
  32.6 13.9 %collective-permute-start.5 = (bf16[256,1024]{1,0:T(8,128)(2,1)}, bf16[256,1024]{1,0:T(8,128)(2,1)}, u32[]{:S(2)}, u32[]{:S(2)}) collective-permute-start(bf16[256,1024]{1,0:T(8,128)(2,1)} %refs_4_.1), channel_id=1, source_target_pairs={{0,24},{8,0},{16,8},{24,16},{1,25},{9,1},{17,9},{25,17},{2,26},{10... | collective-permute-start | bytes 1572872 | tf_op jit(solution)/shard_map/ppermute | solution.py:568
  46.5 6.2 %collective-permute-start.6 = (bf16[512,512]{1,0:T(8,128)(2,1)S(1)}, bf16[512,512]{1,0:T(8,128)(2,1)S(1)}, u32[]{:S(2)}, u32[]{:S(2)}) collective-permute-start(bf16[512,512]{1,0:T(8,128)(2,1)S(1)} %slice_bitcast_fusion), channel_id=1, source_target_pairs={{0,1},{1,0},{2,3},{3,2},{4,5},{5,4},{6,7},{7,6},{8,9},{9,8},{10,11... | collective-permute-start | bytes 1572872 | tf_op jit(solution)/shard_map/ppermute | solution.py:558
  47.6 11.5 %collective-permute-start.7 = (bf16[256,1024]{1,0:T(8,128)(2,1)}, bf16[256,1024]{1,0:T(8,128)(2,1)S(1)}, u32[]{:S(2)}, u32[]{:S(2)}) collective-permute-start(bf16[256,1024]{1,0:T(8,128)(2,1)} %collective-permute-done.4.refs_5_), channel_id=1, source_target_pairs={{0,1},{1,0},{2,3},{3,2},{4,5},{5,4},{6,7},{7,6},{8,9},{9,8},{10,11... | collective-permute-start | bytes 1572872 | tf_op jit(solution)/shard_map/ppermute | solution.py:558
  47.6 11.4 %collective-permute-start.8 = (bf16[256,1024]{1,0:T(8,128)(2,1)}, bf16[256,1024]{1,0:T(8,128)(2,1)S(1)}, u32[]{:S(2)}, u32[]{:S(2)}) collective-permute-start(bf16[256,1024]{1,0:T(8,128)(2,1)} %collective-permute-done.5.refs_7_), channel_id=1, source_target_pairs={{0,1},{1,0},{2,3},{3,2},{4,5},{5,4},{6,7},{7,6},{8,9},{9,8},{10,11... | collective-permute-start | bytes 1572872 | tf_op jit(solution)/shard_map/ppermute | solution.py:558
  48.1 16.9 %collective-permute-start.13 = (bf16[256,1024]{1,0:T(8,128)(2,1)}, bf16[256,1024]{1,0:T(8,128)(2,1)S(1)}, u32[]{:S(2)}, u32[]{:S(2)}) collective-permute-start(bf16[256,1024]{1,0:T(8,128)(2,1)} %collective-permute-done.5.refs_7_), channel_id=1, source_target_pairs={{0,24},{8,0},{16,8},{24,16},{1,25},{9,1},{17,9},{25,17},{2,26},{10... | collective-permute-start | bytes 1572872 | tf_op jit(solution)/shard_map/ppermute | solution.py:568
  53.7 5.4 %collective-permute-start.9 = (bf16[16,1024]{1,0:T(8,128)(2,1)S(1)}, bf16[16,1024]{1,0:T(8,128)(2,1)S(1)}, u32[]{:S(2)}, u32[]{:S(2)}) collective-permute-start(bf16[16,1024]{1,0:T(8,128)(2,1)S(1)} %tail_project.1), channel_id=1, source_target_pairs={{0,1},{1,2},{2,3},{3,4},{4,5},{5,6},{6,7},{7,8},{8,9},{9,10},{10,1... | collective-permute-start | bytes 98312 | tf_op jit(solution)/shard_map/ppermute | solution.py:25
  60.9 9.8 %collective-permute-start.10 = (bf16[4,64,512]{2,1,0:T(8,128)(2,1)S(1)}, bf16[4,64,512]{2,1,0:T(8,128)(2,1)S(1)}, u32[]{:S(2)}, u32[]{:S(2)}) collective-permute-start(bf16[4,64,512]{2,1,0:T(8,128)(2,1)S(1)} %get-tuple-element.77), channel_id=1, source_target_pairs={{0,2},{2,4},{4,6},{6,0},{1,3},{3,5},{5,7},{7,1},{8,10},{10,12},{12... | collective-permute-start | bytes 786440 | tf_op jit(solution)/shard_map/ppermute | solution.py:591
  61.6 14.3 %collective-permute-start.11 = (bf16[4,64,512]{2,1,0:T(8,128)(2,1)S(1)}, bf16[4,64,512]{2,1,0:T(8,128)(2,1)S(1)}, u32[]{:S(2)}, u32[]{:S(2)}) collective-permute-start(bf16[4,64,512]{2,1,0:T(8,128)(2,1)S(1)} %get-tuple-element.78), channel_id=1, source_target_pairs={{0,4},{2,6},{4,0},{6,2},{1,5},{3,7},{5,1},{7,3},{8,12},{10,14},{12... | collective-permute-start | bytes 786440 | tf_op jit(solution)/shard_map/ppermute | solution.py:591
  64.4 11.5 %collective-permute-start.12 = (bf16[4,64,512]{2,1,0:T(8,128)(2,1)S(1)}, bf16[4,64,512]{2,1,0:T(8,128)(2,1)S(1)}, u32[]{:S(2)}, u32[]{:S(2)}) collective-permute-start(bf16[4,64,512]{2,1,0:T(8,128)(2,1)S(1)} %get-tuple-element.79), channel_id=1, source_target_pairs={{0,6},{2,0},{4,2},{6,4},{1,7},{3,1},{5,3},{7,5},{8,14},{10,8},{12,... | collective-permute-start | bytes 786440 | tf_op jit(solution)/shard_map/ppermute | solution.py:591
  83.7 5.9 %collective-permute-start.15 = (bf16[64,1024]{1,0:T(8,128)(2,1)}, bf16[64,1024]{1,0:T(8,128)(2,1)S(1)}, u32[]{:S(2)}, u32[]{:S(2)}) collective-permute-start(bf16[64,1024]{1,0:T(8,128)(2,1)} %get-tuple-element.89), channel_id=1, source_target_pairs={{0,6},{2,0},{4,2},{6,4},{1,7},{3,1},{5,3},{7,5},{8,14},{10,8},{12,... | collective-permute-start | bytes 393224 | tf_op jit(solution)/shard_map/ppermute | solution.py:591
  86.1 6.1 %collective-permute-start.16 = (bf16[64,1024]{1,0:T(8,128)(2,1)}, bf16[64,1024]{1,0:T(8,128)(2,1)S(1)}, u32[]{:S(2)}, u32[]{:S(2)}) collective-permute-start(bf16[64,1024]{1,0:T(8,128)(2,1)} %get-tuple-element.90), channel_id=1, source_target_pairs={{0,4},{2,6},{4,0},{6,2},{1,5},{3,7},{5,1},{7,3},{8,12},{10,14},{12... | collective-permute-start | bytes 393224 | tf_op jit(solution)/shard_map/ppermute | solution.py:591
  86.9 9.1 %collective-permute-start.17 = (bf16[64,1024]{1,0:T(8,128)(2,1)}, bf16[64,1024]{1,0:T(8,128)(2,1)S(1)}, u32[]{:S(2)}, u32[]{:S(2)}) collective-permute-start(bf16[64,1024]{1,0:T(8,128)(2,1)} %get-tuple-element.91), channel_id=1, source_target_pairs={{0,2},{2,4},{4,6},{6,0},{1,3},{3,5},{5,7},{7,1},{8,10},{10,12},{12... | collective-permute-start | bytes 393224 | tf_op jit(solution)/shard_map/ppermute | solution.py:591
  120.0 4.8 %collective-permute-start.18 = (bf16[16,64,128]{2,1,0:T(8,128)(2,1)S(1)}, bf16[16,64,128]{2,1,0:T(8,128)(2,1)S(1)}, u32[]{:S(2)}, u32[]{:S(2)}) collective-permute-start(bf16[16,64,128]{2,1,0:T(8,128)(2,1)S(1)} %slice.8.refs_0_), channel_id=1, source_target_pairs={{0,1},{1,0},{2,3},{3,2},{4,5},{5,4},{6,7},{7,6},{8,9},{9,8},{10,11... | collective-permute-start | bytes 786440 | tf_op jit(solution)/shard_map/ppermute | solution.py:558
  122.0 14.6 %collective-permute-start.19 = (bf16[16,64,128]{2,1,0:T(8,128)(2,1)S(1)}, bf16[16,64,128]{2,1,0:T(8,128)(2,1)S(1)}, u32[]{:S(2)}, u32[]{:S(2)}) collective-permute-start(bf16[16,64,128]{2,1,0:T(8,128)(2,1)S(1)} %slice.8.refs_0_), channel_id=1, source_target_pairs={{0,2},{2,4},{4,6},{6,0},{1,3},{3,5},{5,7},{7,1},{8,10},{10,12},{12... | collective-permute-start | bytes 786440 | tf_op jit(solution)/shard_map/ppermute | solution.py:591
  122.0 14.6 %collective-permute-start.20 = (bf16[16,64,128]{2,1,0:T(8,128)(2,1)S(1)}, bf16[16,64,128]{2,1,0:T(8,128)(2,1)S(1)}, u32[]{:S(2)}, u32[]{:S(2)}) collective-permute-start(bf16[16,64,128]{2,1,0:T(8,128)(2,1)S(1)} %slice.8.refs_0_), channel_id=1, source_target_pairs={{0,6},{2,0},{4,2},{6,4},{1,7},{3,1},{5,3},{7,5},{8,14},{10,8},{12,... | collective-permute-start | bytes 786440 | tf_op jit(solution)/shard_map/ppermute | solution.py:591
  124.7 11.9 %collective-permute-start.21 = (bf16[16,64,128]{2,1,0:T(8,128)(2,1)S(1)}, bf16[16,64,128]{2,1,0:T(8,128)(2,1)S(1)}, u32[]{:S(2)}, u32[]{:S(2)}) collective-permute-start(bf16[16,64,128]{2,1,0:T(8,128)(2,1)S(1)} %slice.8.refs_0_), channel_id=1, source_target_pairs={{0,4},{2,6},{4,0},{6,2},{1,5},{3,7},{5,1},{7,3},{8,12},{10,14},{12... | collective-permute-start | bytes 786440 | tf_op jit(solution)/shard_map/ppermute | solution.py:591
  136.6 5.2 %collective-permute-start.22 = (bf16[16,64,128]{2,1,0:T(8,128)(2,1)S(1)}, bf16[16,64,128]{2,1,0:T(8,128)(2,1)S(1)}, u32[]{:S(2)}, u32[]{:S(2)}) collective-permute-start(bf16[16,64,128]{2,1,0:T(8,128)(2,1)S(1)} %collective-permute-done.19.refs_0_), channel_id=1, source_target_pairs={{0,1},{1,0},{2,3},{3,2},{4,5},{5,4},{6,7},{7,6},{8,9},{9,8},{10,11... | collective-permute-start | bytes 786440 | tf_op jit(solution)/shard_map/ppermute | solution.py:558
  137.6 4.2 %collective-permute-start.23 = (bf16[16,64,128]{2,1,0:T(8,128)(2,1)S(1)}, bf16[16,64,128]{2,1,0:T(8,128)(2,1)S(1)}, u32[]{:S(2)}, u32[]{:S(2)}) collective-permute-start(bf16[16,64,128]{2,1,0:T(8,128)(2,1)S(1)} %collective-permute-done.20.refs_1_), channel_id=1, source_target_pairs={{0,1},{1,0},{2,3},{3,2},{4,5},{5,4},{6,7},{7,6},{8,9},{9,8},{10,11... | collective-permute-start | bytes 786440 | tf_op jit(solution)/shard_map/ppermute | solution.py:558
  137.7 4.2 %collective-permute-start.24 = (bf16[16,64,128]{2,1,0:T(8,128)(2,1)S(1)}, bf16[16,64,128]{2,1,0:T(8,128)(2,1)S(1)}, u32[]{:S(2)}, u32[]{:S(2)}) collective-permute-start(bf16[16,64,128]{2,1,0:T(8,128)(2,1)S(1)} %collective-permute-done.21.refs_2_), channel_id=1, source_target_pairs={{0,1},{1,0},{2,3},{3,2},{4,5},{5,4},{6,7},{7,6},{8,9},{9,8},{10,11... | collective-permute-start | bytes 786440 | tf_op jit(solution)/shard_map/ppermute | solution.py:558
  (22 other events, 88.9 us)

commit v12 on v11

--- a/solution.py
+++ b/solution.py
@@ -523,7 +523,6 @@
         ]
     first = state is None
     arrays = [q, *parts] + ([] if first else list(state))
-    share = len(parts) / 8
     return pl.pallas_call(
         functools.partial(coarse_kernel, len(parts), first, final),
         in_specs=[pl.BlockSpec(memory_space=pltpu.SMEM)]
@@ -531,9 +530,7 @@
         out_shape=out_shape,
         name="coarse_attend",
         compiler_params=params(),
-        cost_estimate=pl.CostEstimate(
-            flops=int(share * 6 * 2**30), bytes_accessed=2 * 2**20, transcendentals=int(share * 5 * 2**20)
-        ),
+        cost_estimate=pl.CostEstimate(flops=1, bytes_accessed=1, transcendentals=0),
     )(jnp.stack(places).astype(jnp.int32), *arrays)
 
 
@@ -611,12 +608,13 @@
     mate_kv = across(kv)
     below, above, beyond = along_y(kv, 1), along_y(kv, 3), along_y(kv, 2)
     state = coarse_attend((mine, mine, spot(0, 1)), qkv, (kv, mate_kv), None, False)
-    others = (below, above, beyond)
-    state, *others = lax.optimization_barrier((state, *others))
-    swapped = [across(block) for block in others]
-    state = coarse_attend((mine, spot(3), spot(1), spot(2)), qkv, others, state, False)
-    state, *swapped = lax.optimization_barrier((state, *swapped))
-    mixed = coarse_attend((mine, spot(3, 1), spot(1, 1), spot(2, 1)), qkv, swapped, state, True)
+    state, below, above = together((state, below, above))
+    state = coarse_attend((mine, spot(3), spot(1)), qkv, (below, above), state, False)
+    mate_below, mate_above = across(below), across(above)
+    state, beyond, mate_below, mate_above = together((state, beyond, mate_below, mate_above))
+    places = (mine, spot(3, 1), spot(1, 1), spot(2), spot(2, 1))
+    parts = (mate_below, mate_above, beyond, across(beyond))
+    mixed = coarse_attend(places, qkv, parts, state, True)
     mixed = lax.all_to_all(mixed, ("z", "x"), 0, 0)
     return finish(mixed, coarse_out, shortened, natural)
 

time: 160 us -> 161 us (level)
  transfers between devices with their start and end apart: 25 -> 25, of which waited for: 9 -> 10; matrix products, arithmetic and copies ran while one was open for 3% -> 3% of each run, Pallas kernels for 18% -> 17%
where the time goes in v12:
time: 161 us; the launch traced here: 160 us
  Pallas kernels  45.4 us (28%)
  waiting for transfers between devices  36.1 us (22%)
  starting transfers between devices  35 us (22%)
  blocking collectives  28 us (17%)
  local copies, waits for them, and re-layouts  13.2 us (8%)
  other arithmetic  2.41 us (1%)
    ppermute x9, waiting for transfers between devices, along_y(): return lax.ppermute(block, 'y', [(i, (i + distance) % 4) for i in range(4)])  29.2 us
    all_to_all x1, blocking collectives, body(): qkv = lax.all_to_all(qkv, ('z', 'x'), 0, 0)  17.9 us
    unnamed x43, local copies, waits for them, and re-layouts  13 us
    pallas_call x3, Pallas kernels, coarse_attend(): pl.pallas_call(functools.partial(coarse_kernel, len(parts), first, final)...  10.3 us
    ppermute x3, starting transfers between devices, along_x(): return lax.ppermute(block, 'x', [(i, (i + distance) % 4) for i in range(4)])  10.2 us
    pallas_call x3, Pallas kernels, project(): pl.pallas_call(functools.partial(project_kernel, number), name='project',...  10.1 us
    all_to_all x1, blocking collectives, body(): mixed = lax.all_to_all(mixed, ('z', 'x'), 0, 0)  10.1 us
    ppermute x9, starting transfers between devices, along_y(): return lax.ppermute(block, 'y', [(i, (i + distance) % 4) for i in range(4)])  10 us
  transfers between devices with their start and end apart: 25, of which 10 were waited for; matrix products, arithmetic and copies ran while one was open for 3% of the time, Pallas kernels for 17%

profile of v12, /device:TPU:1, one launch (start us, length us, event | category | flops | bytes accessed | tf_op | source)
XLA Modules:
  0.0 160.4 jit_solution(6827265702245556756)
XLA Ops:
  1.4 4.3 %collective-permute-start = (bf16[512,1024]{1,0:T(8,128)(2,1)}, bf16[512,1024]{1,0:T(8,128)(2,1)}, u32[]{:S(2)}, u32[]{:S(2)}) collective-permute-start(bf16[512,1024]{1,0:T(8,128)(2,1)} %tokens_ref.3), channel_id=1, source_target_pairs={{0,2},{1,3},{2,4},{3,5},{4,6},{5,7},{6,8},{7,9},{8,10},{9,11},{10,... | collective-permute-start | bytes 3145736 | tf_op jit(solution)/shard_map/ppermute | solution.py:25
  6.0 2.9 %copy.11 = bf16[1024,1024]{0,1:T(8,128)(2,1)S(1)} copy(bf16[1024,1024]{1,0:T(8,128)(2,1)} %param.13) | data formatting | bytes 4194304 | tf_op args[3]
  12.5 4.7 %project.3 = (bf16[1024,512]{1,0:T(8,128)(2,1)S(1)}, bf16[512,1024]{1,0:T(8,128)(2,1)S(1)}, bf16[1024,512]{1,0:T(8,128)(2,1)S(1)}) custom-call(s32[1]{0:T(128)} %bitcast.6.core_ref, bf16[1024,1024]{1,0:T(8,128)(2,1)S(1)} %pad_maximum_fusion.rows_ref, bf16[1024,1024]{1,0:T(8,128)(2,1)S(1)} %copy-done.1, bf16[1024,1024]{1,0:T(8,128)(2,1)S(1)} %bitcast.16, ...), custom_call_target="tpu_custom_call" | custom-call | flops 1 | bytes 1 | tf_op jit(solution)/shard_map/project/pallas_call | solution.py:88
  17.2 6.5 %fine_own.1 = (f32[4,8,8,256]{3,2,1,0:T(8,128)S(1)}, f32[4,8,80,256]{3,2,1,0:T(8,128)S(1)}) custom-call(bf16[1024,512]{1,0:T(8,128)(2,1)S(1)} %get-tuple-element.61.q_ref, bf16[1024,512]{1,0:T(8,128)(2,1)S(1)} %get-tuple-element.57.k_ref, bf16[512,1024]{1,0:T(8,128)(2,1)S(1)} %get-tuple-element.58.v_ref), custom_call_target="tpu_custom_call" | custom-call | flops 1 | bytes 1 | tf_op jit(solution)/shard_map/fine_own/pallas_call | solution.py:300
  28.4 4.2 %collective-permute-start.4 = (bf16[256,1024]{1,0:T(8,128)(2,1)}, bf16[256,1024]{1,0:T(8,128)(2,1)}, u32[]{:S(2)}, u32[]{:S(2)}) collective-permute-start(bf16[256,1024]{1,0:T(8,128)(2,1)} %refs_4_.1), channel_id=1, source_target_pairs={{0,8},{8,16},{16,24},{24,0},{1,9},{9,17},{17,25},{25,1},{2,10},{10... | collective-permute-start | bytes 1572872 | tf_op jit(solution)/shard_map/ppermute | solution.py:565
  35.5 2.6 %project.4 = (bf16[512,512]{1,0:T(8,128)(2,1)S(1)}, bf16[512,512]{1,0:T(8,128)(2,1)S(1)}) custom-call(s32[1]{0:T(128)} %bitcast.6.core_ref, bf16[512,1024]{1,0:T(8,128)(2,1)} %collective-permute-done.rows_ref, bf16[1024,1024]{1,0:T(8,128)(2,1)S(1)} %copy-done.2, bf16[1024,1024]{1,0:T(8,128)(2,1)S(1)} %bitcast.17), custom_call_target="tpu_custom_call" | custom-call | flops 1 | bytes 1 | tf_op jit(solution)/shard_map/project/pallas_call | solution.py:88
  38.2 2.8 %project.5 = (bf16[512,512]{1,0:T(8,128)(2,1)S(1)}, bf16[512,512]{1,0:T(8,128)(2,1)S(1)}) custom-call(s32[1]{0:T(128)} %bitcast.6.core_ref, bf16[512,1024]{1,0:T(8,128)(2,1)} %collective-permute-done.3.rows_ref, bf16[1024,1024]{1,0:T(8,128)(2,1)S(1)} %copy-done.2, bf16[1024,1024]{1,0:T(8,128)(2,1)S(1)} %bitcast.18), custom_call_target="tpu_custom_call" | custom-call | flops 1 | bytes 1 | tf_op jit(solution)/shard_map/project/pallas_call | solution.py:88
  42.9 3.6 %collective-permute-done.4.refs_5_ = bf16[256,1024]{1,0:T(8,128)(2,1)} collective-permute-done((bf16[256,1024]{1,0:T(8,128)(2,1)}, bf16[256,1024]{1,0:T(8,128)(2,1)}, u32[]{:S(2)}, u32[]{:S(2)}) %collective-permute-start.4) | collective-permute-done | bytes 524320 | tf_op jit(solution)/shard_map/ppermute | solution.py:565
  48.1 4.7 %collective-permute-start.13 = (bf16[256,1024]{1,0:T(8,128)(2,1)}, bf16[256,1024]{1,0:T(8,128)(2,1)S(1)}, u32[]{:S(2)}, u32[]{:S(2)}) collective-permute-start(bf16[256,1024]{1,0:T(8,128)(2,1)} %collective-permute-done.5.refs_7_), channel_id=1, source_target_pairs={{0,24},{8,0},{16,8},{24,16},{1,25},{9,1},{17,9},{25,17},{2,26},{10... | collective-permute-start | bytes 1572872 | tf_op jit(solution)/shard_map/ppermute | solution.py:565
  61.6 2.9 %collective-permute-start.11 = (bf16[4,64,512]{2,1,0:T(8,128)(2,1)S(1)}, bf16[4,64,512]{2,1,0:T(8,128)(2,1)S(1)}, u32[]{:S(2)}, u32[]{:S(2)}) collective-permute-start(bf16[4,64,512]{2,1,0:T(8,128)(2,1)S(1)} %get-tuple-element.77), channel_id=1, source_target_pairs={{0,4},{2,6},{4,0},{6,2},{1,5},{3,7},{5,1},{7,3},{8,12},{10,14},{12... | collective-permute-start | bytes 786440 | tf_op jit(solution)/shard_map/ppermute | solution.py:588
  65.0 5.7 %collective-permute-done.10.refs_1_ = bf16[4,64,512]{2,1,0:T(8,128)(2,1)S(1)} collective-permute-done((bf16[4,64,512]{2,1,0:T(8,128)(2,1)S(1)}, bf16[4,64,512]{2,1,0:T(8,128)(2,1)S(1)}, u32[]{:S(2)}, u32[]{:S(2)}) %collective-permute-start.10) | collective-permute-done | bytes 262176 | tf_op jit(solution)/shard_map/ppermute | solution.py:588
  70.7 5.3 %collective-permute-done.11.refs_2_ = bf16[4,64,512]{2,1,0:T(8,128)(2,1)S(1)} collective-permute-done((bf16[4,64,512]{2,1,0:T(8,128)(2,1)S(1)}, bf16[4,64,512]{2,1,0:T(8,128)(2,1)S(1)}, u32[]{:S(2)}, u32[]{:S(2)}) %collective-permute-start.11) | collective-permute-done | bytes 262176 | tf_op jit(solution)/shard_map/ppermute | solution.py:588
  79.4 4.3 %shorten.1 = (bf16[64,1024]{1,0:T(8,128)(2,1)}, bf16[64,1024]{1,0:T(8,128)(2,1)}, bf16[64,1024]{1,0:T(8,128)(2,1)}, bf16[64,1024]{1,0:T(8,128)(2,1)}) custom-call(s32[2]{0:T(128)} %pad_add_fusion.where_ref, bf16[4,64,512]{2,1,0:T(8,128)(2,1)} %copy-done.10, bf16[4,64,512]{2,1,0:T(8,128)(2,1)} %copy-done.15, bf16[4,64,512]{2,1,0:T(8,128)(2,1)} %copy-done.16, ...), custom_call_target="tpu_custom_call" | custom-call | tf_op jit(solution)/shard_map/shorten/pallas_call | solution.py:372
  86.9 2.7 %collective-permute-done.15.refs_1_ = bf16[64,1024]{1,0:T(8,128)(2,1)S(1)} collective-permute-done((bf16[64,1024]{1,0:T(8,128)(2,1)}, bf16[64,1024]{1,0:T(8,128)(2,1)S(1)}, u32[]{:S(2)}, u32[]{:S(2)}) %collective-permute-start.15) | collective-permute-done | bytes 131104 | tf_op jit(solution)/shard_map/ppermute | solution.py:588
  92.2 3.8 %collective-permute-done.17.refs_3_ = bf16[64,1024]{1,0:T(8,128)(2,1)S(1)} collective-permute-done((bf16[64,1024]{1,0:T(8,128)(2,1)}, bf16[64,1024]{1,0:T(8,128)(2,1)S(1)}, u32[]{:S(2)}, u32[]{:S(2)}) %collective-permute-start.17) | collective-permute-done | bytes 131104 | tf_op jit(solution)/shard_map/ppermute | solution.py:588
  96.7 5.3 %coarse_project.1 = (bf16[64,1024]{1,0:T(8,128)(2,1)}, bf16[16,64,192]{2,1,0:T(8,128)(2,1)}) custom-call(bf16[64,1024]{1,0:T(8,128)(2,1)} %get-tuple-element.87.refs_0_, bf16[64,1024]{1,0:T(8,128)(2,1)} %copy-done.18, bf16[64,1024]{1,0:T(8,128)(2,1)} %copy-done.19, bf16[64,1024]{1,0:T(8,128)(2,1)} %copy-done.20, bf16[1024,1024]{1,0:T(8,128)(2,1)} %refs_4_.2, ...), custom_call_target="tpu_custom_call" | custom-call | tf_op jit(solution)/shard_map/coarse_project/pallas_call | solution.py:409
  102.0 17.9 %all_to_all.10.q_ref = bf16[16,64,192]{2,1,0:T(8,128)(2,1)S(1)} all-to-all(bf16[16,64,192]{2,1,0:T(8,128)(2,1)} %get-tuple-element.91), channel_id=1, replica_groups=mesh['z'=4,'x'=4,'y'=4,'c'=2] {'z','x'}, dimensions={0} | all-to-all | bytes 786432 | tf_op jit(solution)/shard_map/all_to_all | solution.py:600
  122.0 2.7 %collective-permute-start.20 = (bf16[16,64,128]{2,1,0:T(8,128)(2,1)S(1)}, bf16[16,64,128]{2,1,0:T(8,128)(2,1)S(1)}, u32[]{:S(2)}, u32[]{:S(2)}) collective-permute-start(bf16[16,64,128]{2,1,0:T(8,128)(2,1)S(1)} %slice.8.refs_0_), channel_id=1, source_target_pairs={{0,6},{2,0},{4,2},{6,4},{1,7},{3,1},{5,3},{7,5},{8,14},{10,8},{12,... | collective-permute-start | bytes 786440 | tf_op jit(solution)/shard_map/ppermute | solution.py:588
  124.8 2.8 %coarse_attend.3 = (f32[4,8,256]{2,1,0:T(8,128)S(1)}, f32[4,80,256]{2,1,0:T(8,128)S(1)}) custom-call(s32[3]{0:T(128)S(1)} %pad_add_fusion.3.where_ref, bf16[16,64,192]{2,1,0:T(8,128)(2,1)S(1)} %all_to_all.10.q_ref, bf16[16,64,128]{2,1,0:T(8,128)(2,1)S(1)} %slice.8.refs_0_, bf16[16,64,128]{2,1,0:T(8,128)(2,1)S(1)} %collective-permute-done.18.refs_1_), custom_call_target="tpu_custom_call" | custom-call | flops 1 | bytes 1 | tf_op jit(solution)/shard_map/coarse_attend/pallas_call | solution.py:526
  127.6 9.1 %collective-permute-done.19.refs_0_ = bf16[16,64,128]{2,1,0:T(8,128)(2,1)S(1)} collective-permute-done((bf16[16,64,128]{2,1,0:T(8,128)(2,1)S(1)}, bf16[16,64,128]{2,1,0:T(8,128)(2,1)S(1)}, u32[]{:S(2)}, u32[]{:S(2)}) %collective-permute-start.19) | collective-permute-done | bytes 262176 | tf_op jit(solution)/shard_map/ppermute | solution.py:588
  137.7 2.8 %coarse_attend.4 = (f32[4,8,256]{2,1,0:T(8,128)S(1)}, f32[4,80,256]{2,1,0:T(8,128)S(1)}) custom-call(s32[3]{0:T(128)S(1)} %pad_add_fusion.2.where_ref, bf16[16,64,192]{2,1,0:T(8,128)(2,1)S(1)} %all_to_all.10.q_ref, bf16[16,64,128]{2,1,0:T(8,128)(2,1)S(1)} %collective-permute-done.19.refs_0_, bf16[16,64,128]{2,1,0:T(8,128)(2,1)S(1)} %collective-permute-done.20.refs_1_, ...), custom_call_target="tpu_custom_call" | custom-call | flops 1 | bytes 1 | tf_op jit(solution)/shard_map/coarse_attend/pallas_call | solution.py:526
  142.3 4.7 %coarse_attend.5 = bf16[16,32,128]{2,1,0:T(8,128)(2,1)S(1)} custom-call(s32[5]{0:T(128)S(1)} %stack.60.where_ref, bf16[16,64,192]{2,1,0:T(8,128)(2,1)S(1)} %all_to_all.10.q_ref, bf16[16,64,128]{2,1,0:T(8,128)(2,1)S(1)} %collective-permute-done.22.refs_0_, bf16[16,64,128]{2,1,0:T(8,128)(2,1)S(1)} %collective-permute-done.23.refs_1_, ...), custom_call_target="tpu_custom_call" | custom-call | flops 1 | bytes 1 | tf_op jit(solution)/shard_map/coarse_attend/pallas_call | solution.py:526
  147.0 10.1 %all_to_all.11.mixed_ref = bf16[16,32,128]{2,1,0:T(8,128)(2,1)} all-to-all(bf16[16,32,128]{2,1,0:T(8,128)(2,1)S(1)} %coarse_attend.5), channel_id=1, replica_groups=mesh['z'=4,'x'=4,'y'=4,'c'=2] {'z','x'}, dimensions={0} | all-to-all | bytes 262144 | tf_op jit(solution)/shard_map/all_to_all | solution.py:618
  157.1 3.3 %finish.1 = bf16[512,1024]{1,0:T(8,128)(2,1)} custom-call(bf16[16,32,128]{2,1,0:T(8,128)(2,1)} %all_to_all.11.mixed_ref, bf16[1024,1024]{1,0:T(8,128)(2,1)} %out_weight_ref.1, bf16[64,1024]{1,0:T(8,128)(2,1)} %get-tuple-element.105.short_ref, bf16[512,1024]{1,0:T(8,128)(2,1)} %copy-done.9), custom_call_target="tpu_custom_call" | custom-call | tf_op jit(solution)/shard_map/finish/pallas_call | solution.py:448
  (94 shorter events, 40.5 us)
Async XLA Ops:
  0.0 8.9 %collective-permute-start.1 = (bf16[512,1024]{1,0:T(8,128)(2,1)}, bf16[512,1024]{1,0:T(8,128)(2,1)}, u32[]{:S(2)}, u32[]{:S(2)}) collective-permute-start(bf16[512,1024]{1,0:T(8,128)(2,1)} %tokens_ref.3), channel_id=1, source_target_pairs={{0,1},{1,0},{2,3},{3,2},{4,5},{5,4},{6,7},{7,6},{8,9},{9,8},{10,11... | collective-permute-start | bytes 3145736 | tf_op jit(solution)/shard_map/ppermute | solution.py:555
  1.4 26.2 %collective-permute-start = (bf16[512,1024]{1,0:T(8,128)(2,1)}, bf16[512,1024]{1,0:T(8,128)(2,1)}, u32[]{:S(2)}, u32[]{:S(2)}) collective-permute-start(bf16[512,1024]{1,0:T(8,128)(2,1)} %tokens_ref.3), channel_id=1, source_target_pairs={{0,2},{1,3},{2,4},{3,5},{4,6},{5,7},{6,8},{7,9},{8,10},{9,11},{10,... | collective-permute-start | bytes 3145736 | tf_op jit(solution)/shard_map/ppermute | solution.py:25
  5.7 20.5 %collective-permute-start.2 = (bf16[256,1024]{1,0:T(8,128)(2,1)}, bf16[256,1024]{1,0:T(8,128)(2,1)}, u32[]{:S(2)}, u32[]{:S(2)}) collective-permute-start(bf16[256,1024]{1,0:T(8,128)(2,1)} %refs_4_.1), channel_id=1, source_target_pairs={{0,1},{1,0},{2,3},{3,2},{4,5},{5,4},{6,7},{7,6},{8,9},{9,8},{10,11... | collective-permute-start | bytes 1572872 | tf_op jit(solution)/shard_map/ppermute | solution.py:555
  27.6 10.6 %collective-permute-start.3 = (bf16[512,1024]{1,0:T(8,128)(2,1)}, bf16[512,1024]{1,0:T(8,128)(2,1)}, u32[]{:S(2)}, u32[]{:S(2)}) collective-permute-start(bf16[512,1024]{1,0:T(8,128)(2,1)} %collective-permute-done.rows_ref), channel_id=1, source_target_pairs={{0,1},{1,0},{2,3},{3,2},{4,5},{5,4},{6,7},{7,6},{8,9},{9,8},{10,11... | collective-permute-start | bytes 3145736 | tf_op jit(solution)/shard_map/ppermute | solution.py:555
  28.4 18.1 %collective-permute-start.4 = (bf16[256,1024]{1,0:T(8,128)(2,1)}, bf16[256,1024]{1,0:T(8,128)(2,1)}, u32[]{:S(2)}, u32[]{:S(2)}) collective-permute-start(bf16[256,1024]{1,0:T(8,128)(2,1)} %refs_4_.1), channel_id=1, source_target_pairs={{0,8},{8,16},{16,24},{24,0},{1,9},{9,17},{17,25},{25,1},{2,10},{10... | collective-permute-start | bytes 1572872 | tf_op jit(solution)/shard_map/ppermute | solution.py:565
  32.6 13.9 %collective-permute-start.5 = (bf16[256,1024]{1,0:T(8,128)(2,1)}, bf16[256,1024]{1,0:T(8,128)(2,1)}, u32[]{:S(2)}, u32[]{:S(2)}) collective-permute-start(bf16[256,1024]{1,0:T(8,128)(2,1)} %refs_4_.1), channel_id=1, source_target_pairs={{0,24},{8,0},{16,8},{24,16},{1,25},{9,1},{17,9},{25,17},{2,26},{10... | collective-permute-start | bytes 1572872 | tf_op jit(solution)/shard_map/ppermute | solution.py:565
  46.5 6.2 %collective-permute-start.6 = (bf16[512,512]{1,0:T(8,128)(2,1)S(1)}, bf16[512,512]{1,0:T(8,128)(2,1)S(1)}, u32[]{:S(2)}, u32[]{:S(2)}) collective-permute-start(bf16[512,512]{1,0:T(8,128)(2,1)S(1)} %slice_bitcast_fusion), channel_id=1, source_target_pairs={{0,1},{1,0},{2,3},{3,2},{4,5},{5,4},{6,7},{7,6},{8,9},{9,8},{10,11... | collective-permute-start | bytes 1572872 | tf_op jit(solution)/shard_map/ppermute | solution.py:555
  47.6 11.5 %collective-permute-start.7 = (bf16[256,1024]{1,0:T(8,128)(2,1)}, bf16[256,1024]{1,0:T(8,128)(2,1)S(1)}, u32[]{:S(2)}, u32[]{:S(2)}) collective-permute-start(bf16[256,1024]{1,0:T(8,128)(2,1)} %collective-permute-done.4.refs_5_), channel_id=1, source_target_pairs={{0,1},{1,0},{2,3},{3,2},{4,5},{5,4},{6,7},{7,6},{8,9},{9,8},{10,11... | collective-permute-start | bytes 1572872 | tf_op jit(solution)/shard_map/ppermute | solution.py:555
  47.6 11.4 %collective-permute-start.8 = (bf16[256,1024]{1,0:T(8,128)(2,1)}, bf16[256,1024]{1,0:T(8,128)(2,1)S(1)}, u32[]{:S(2)}, u32[]{:S(2)}) collective-permute-start(bf16[256,1024]{1,0:T(8,128)(2,1)} %collective-permute-done.5.refs_7_), channel_id=1, source_target_pairs={{0,1},{1,0},{2,3},{3,2},{4,5},{5,4},{6,7},{7,6},{8,9},{9,8},{10,11... | collective-permute-start | bytes 1572872 | tf_op jit(solution)/shard_map/ppermute | solution.py:555
  48.1 16.9 %collective-permute-start.13 = (bf16[256,1024]{1,0:T(8,128)(2,1)}, bf16[256,1024]{1,0:T(8,128)(2,1)S(1)}, u32[]{:S(2)}, u32[]{:S(2)}) collective-permute-start(bf16[256,1024]{1,0:T(8,128)(2,1)} %collective-permute-done.5.refs_7_), channel_id=1, source_target_pairs={{0,24},{8,0},{16,8},{24,16},{1,25},{9,1},{17,9},{25,17},{2,26},{10... | collective-permute-start | bytes 1572872 | tf_op jit(solution)/shard_map/ppermute | solution.py:565
  53.7 5.4 %collective-permute-start.9 = (bf16[16,1024]{1,0:T(8,128)(2,1)S(1)}, bf16[16,1024]{1,0:T(8,128)(2,1)S(1)}, u32[]{:S(2)}, u32[]{:S(2)}) collective-permute-start(bf16[16,1024]{1,0:T(8,128)(2,1)S(1)} %tail_project.1), channel_id=1, source_target_pairs={{0,1},{1,2},{2,3},{3,4},{4,5},{5,6},{6,7},{7,8},{8,9},{9,10},{10,1... | collective-permute-start | bytes 98312 | tf_op jit(solution)/shard_map/ppermute | solution.py:25
  60.9 9.8 %collective-permute-start.10 = (bf16[4,64,512]{2,1,0:T(8,128)(2,1)S(1)}, bf16[4,64,512]{2,1,0:T(8,128)(2,1)S(1)}, u32[]{:S(2)}, u32[]{:S(2)}) collective-permute-start(bf16[4,64,512]{2,1,0:T(8,128)(2,1)S(1)} %get-tuple-element.76), channel_id=1, source_target_pairs={{0,2},{2,4},{4,6},{6,0},{1,3},{3,5},{5,7},{7,1},{8,10},{10,12},{12... | collective-permute-start | bytes 786440 | tf_op jit(solution)/shard_map/ppermute | solution.py:588
  61.6 14.3 %collective-permute-start.11 = (bf16[4,64,512]{2,1,0:T(8,128)(2,1)S(1)}, bf16[4,64,512]{2,1,0:T(8,128)(2,1)S(1)}, u32[]{:S(2)}, u32[]{:S(2)}) collective-permute-start(bf16[4,64,512]{2,1,0:T(8,128)(2,1)S(1)} %get-tuple-element.77), channel_id=1, source_target_pairs={{0,4},{2,6},{4,0},{6,2},{1,5},{3,7},{5,1},{7,3},{8,12},{10,14},{12... | collective-permute-start | bytes 786440 | tf_op jit(solution)/shard_map/ppermute | solution.py:588
  64.5 11.5 %collective-permute-start.12 = (bf16[4,64,512]{2,1,0:T(8,128)(2,1)S(1)}, bf16[4,64,512]{2,1,0:T(8,128)(2,1)S(1)}, u32[]{:S(2)}, u32[]{:S(2)}) collective-permute-start(bf16[4,64,512]{2,1,0:T(8,128)(2,1)S(1)} %get-tuple-element.78), channel_id=1, source_target_pairs={{0,6},{2,0},{4,2},{6,4},{1,7},{3,1},{5,3},{7,5},{8,14},{10,8},{12,... | collective-permute-start | bytes 786440 | tf_op jit(solution)/shard_map/ppermute | solution.py:588
  76.0 2.7 %collective-permute-start.14 = (bf16[256,1024]{1,0:T(8,128)(2,1)S(1)}, bf16[256,1024]{1,0:T(8,128)(2,1)S(1)}, u32[]{:S(2)}, u32[]{:S(2)}) collective-permute-start(bf16[256,1024]{1,0:T(8,128)(2,1)S(1)} %collective-permute-done.13.refs_6_), channel_id=1, source_target_pairs={{0,1},{1,0},{2,3},{3,2},{4,5},{5,4},{6,7},{7,6},{8,9},{9,8},{10,11... | collective-permute-start | bytes 1572872 | tf_op jit(solution)/shard_map/ppermute | solution.py:555
  83.7 5.9 %collective-permute-start.15 = (bf16[64,1024]{1,0:T(8,128)(2,1)}, bf16[64,1024]{1,0:T(8,128)(2,1)S(1)}, u32[]{:S(2)}, u32[]{:S(2)}) collective-permute-start(bf16[64,1024]{1,0:T(8,128)(2,1)} %get-tuple-element.88), channel_id=1, source_target_pairs={{0,6},{2,0},{4,2},{6,4},{1,7},{3,1},{5,3},{7,5},{8,14},{10,8},{12,... | collective-permute-start | bytes 393224 | tf_op jit(solution)/shard_map/ppermute | solution.py:588
  86.1 6.1 %collective-permute-start.16 = (bf16[64,1024]{1,0:T(8,128)(2,1)}, bf16[64,1024]{1,0:T(8,128)(2,1)S(1)}, u32[]{:S(2)}, u32[]{:S(2)}) collective-permute-start(bf16[64,1024]{1,0:T(8,128)(2,1)} %get-tuple-element.89), channel_id=1, source_target_pairs={{0,4},{2,6},{4,0},{6,2},{1,5},{3,7},{5,1},{7,3},{8,12},{10,14},{12... | collective-permute-start | bytes 393224 | tf_op jit(solution)/shard_map/ppermute | solution.py:588
  86.9 9.1 %collective-permute-start.17 = (bf16[64,1024]{1,0:T(8,128)(2,1)}, bf16[64,1024]{1,0:T(8,128)(2,1)S(1)}, u32[]{:S(2)}, u32[]{:S(2)}) collective-permute-start(bf16[64,1024]{1,0:T(8,128)(2,1)} %get-tuple-element.90), channel_id=1, source_target_pairs={{0,2},{2,4},{4,6},{6,0},{1,3},{3,5},{5,7},{7,1},{8,10},{10,12},{12... | collective-permute-start | bytes 393224 | tf_op jit(solution)/shard_map/ppermute | solution.py:588
  120.0 4.8 %collective-permute-start.18 = (bf16[16,64,128]{2,1,0:T(8,128)(2,1)S(1)}, bf16[16,64,128]{2,1,0:T(8,128)(2,1)S(1)}, u32[]{:S(2)}, u32[]{:S(2)}) collective-permute-start(bf16[16,64,128]{2,1,0:T(8,128)(2,1)S(1)} %slice.8.refs_0_), channel_id=1, source_target_pairs={{0,1},{1,0},{2,3},{3,2},{4,5},{5,4},{6,7},{7,6},{8,9},{9,8},{10,11... | collective-permute-start | bytes 786440 | tf_op jit(solution)/shard_map/ppermute | solution.py:555
  122.0 14.7 %collective-permute-start.19 = (bf16[16,64,128]{2,1,0:T(8,128)(2,1)S(1)}, bf16[16,64,128]{2,1,0:T(8,128)(2,1)S(1)}, u32[]{:S(2)}, u32[]{:S(2)}) collective-permute-start(bf16[16,64,128]{2,1,0:T(8,128)(2,1)S(1)} %slice.8.refs_0_), channel_id=1, source_target_pairs={{0,2},{2,4},{4,6},{6,0},{1,3},{3,5},{5,7},{7,1},{8,10},{10,12},{12... | collective-permute-start | bytes 786440 | tf_op jit(solution)/shard_map/ppermute | solution.py:588
  122.0 14.7 %collective-permute-start.20 = (bf16[16,64,128]{2,1,0:T(8,128)(2,1)S(1)}, bf16[16,64,128]{2,1,0:T(8,128)(2,1)S(1)}, u32[]{:S(2)}, u32[]{:S(2)}) collective-permute-start(bf16[16,64,128]{2,1,0:T(8,128)(2,1)S(1)} %slice.8.refs_0_), channel_id=1, source_target_pairs={{0,6},{2,0},{4,2},{6,4},{1,7},{3,1},{5,3},{7,5},{8,14},{10,8},{12,... | collective-permute-start | bytes 786440 | tf_op jit(solution)/shard_map/ppermute | solution.py:588
  124.8 15.7 %collective-permute-start.21 = (bf16[16,64,128]{2,1,0:T(8,128)(2,1)S(1)}, bf16[16,64,128]{2,1,0:T(8,128)(2,1)S(1)}, u32[]{:S(2)}, u32[]{:S(2)}) collective-permute-start(bf16[16,64,128]{2,1,0:T(8,128)(2,1)S(1)} %slice.8.refs_0_), channel_id=1, source_target_pairs={{0,4},{2,6},{4,0},{6,2},{1,5},{3,7},{5,1},{7,3},{8,12},{10,14},{12... | collective-permute-start | bytes 786440 | tf_op jit(solution)/shard_map/ppermute | solution.py:588
  136.7 3.8 %collective-permute-start.22 = (bf16[16,64,128]{2,1,0:T(8,128)(2,1)S(1)}, bf16[16,64,128]{2,1,0:T(8,128)(2,1)S(1)}, u32[]{:S(2)}, u32[]{:S(2)}) collective-permute-start(bf16[16,64,128]{2,1,0:T(8,128)(2,1)S(1)} %collective-permute-done.19.refs_0_), channel_id=1, source_target_pairs={{0,1},{1,0},{2,3},{3,2},{4,5},{5,4},{6,7},{7,6},{8,9},{9,8},{10,11... | collective-permute-start | bytes 786440 | tf_op jit(solution)/shard_map/ppermute | solution.py:555
  137.6 2.9 %collective-permute-start.23 = (bf16[16,64,128]{2,1,0:T(8,128)(2,1)S(1)}, bf16[16,64,128]{2,1,0:T(8,128)(2,1)S(1)}, u32[]{:S(2)}, u32[]{:S(2)}) collective-permute-start(bf16[16,64,128]{2,1,0:T(8,128)(2,1)S(1)} %collective-permute-done.20.refs_1_), channel_id=1, source_target_pairs={{0,1},{1,0},{2,3},{3,2},{4,5},{5,4},{6,7},{7,6},{8,9},{9,8},{10,11... | collective-permute-start | bytes 786440 | tf_op jit(solution)/shard_map/ppermute | solution.py:555
  (22 other events, 88.1 us)

commit v13 on v11

--- a/solution.py
+++ b/solution.py
@@ -247,7 +247,7 @@
         o = o * (1.0 / total)
         mixed = jnp.concatenate([o[:, :QB], o[:, QB:]], axis=0)
         at = b * QB // half
-        out_ref[(at + core) % 2, b * QB - at * half : (b + 1) * QB - at * half, :] = mixed.T.astype(jnp.bfloat16)
+        out_ref[(at + core) % 2, b * QB - at * half : (b + 1) * QB - at * half, :] = mixed.astype(jnp.bfloat16).T
 
     @pl.when(where_ref[1] == 0)
     def _():
@@ -399,8 +399,14 @@
         if i == 2:
             out = out * SCALE
         out = out.astype(jnp.bfloat16)
+        count = out.shape[0]
         for h in range(HEADS):
-            qkv_ref[h, :, i * HEAD_DIM : (i + 1) * HEAD_DIM] = out[:, h * HEAD_DIM : (h + 1) * HEAD_DIM]
+            head = out[:, h * HEAD_DIM : (h + 1) * HEAD_DIM]
+            if i < 2:
+                qkv_ref[h, :count, i * HEAD_DIM : (i + 1) * HEAD_DIM] = head
+            else:
+                qkv_ref[h, count:, :HEAD_DIM] = head[: count // 2]
+                qkv_ref[h, count:, HEAD_DIM:] = head[count // 2 :]
 
 
 def coarse_project(partial, query, key, value):
@@ -413,7 +419,7 @@
         out_specs=[vmem] * 2,
         out_shape=[
             jax.ShapeDtypeStruct((rows, width), jnp.bfloat16),
-            jax.ShapeDtypeStruct((HEADS, rows, 3 * HEAD_DIM), jnp.bfloat16),
+            jax.ShapeDtypeStruct((HEADS, rows + rows // 2, PAIR), jnp.bfloat16),
         ],
         scratch_shapes=[
             pltpu.VMEM((3, width, width), jnp.bfloat16),
@@ -477,7 +483,8 @@
     ones = jnp.ones((16, number * tile), jnp.bfloat16)
     queries = []
     for t in range(tiles):
-        q = q_ref[4 * t : 4 * t + 4, :, 2 * HEAD_DIM :].reshape(tile, HEAD_DIM)
+        halves = [q_ref[4 * t + i, rows:, :] for i in range(4)]
+        q = jnp.concatenate([half[:, at : at + HEAD_DIM] for half in halves for at in (0, HEAD_DIM)], axis=0)
         queries.append(jnp.concatenate([q, jnp.zeros_like(q)], axis=1))
     if first:
         tops = [jnp.full((1, tile), NEG, jnp.float32)] * tiles
@@ -502,7 +509,7 @@
     for t in range(tiles):
         if final:
             o = accs[t][16:] * (1.0 / accs[t][0:1])
-            o = o.T.astype(jnp.bfloat16)
+            o = o.astype(jnp.bfloat16).T
             for i in range(0, tile, rows):
                 low, high = o[i : i + rows // 2], o[i + rows // 2 : i + rows]
                 outs[0][4 * t + i // rows] = jnp.concatenate([low, high], axis=1)
@@ -512,7 +519,7 @@
 
 
 def coarse_attend(places, q, parts, state, final):
-    heads, rows, _ = q.shape
+    heads, rows, _ = parts[0].shape
     tile = 4 * rows
     if final:
         out_shape = jax.ShapeDtypeStruct((heads, rows // 2, PAIR), jnp.bfloat16)
@@ -601,7 +608,7 @@
     partial = exchange(shorten(where, grouped, pieces, spots_of), -1)
     shortened, qkv = coarse_project(partial, coarse_query, coarse_key, coarse_value)
     qkv = lax.all_to_all(qkv, ("z", "x"), 0, 0)
-    kv = qkv[:, :, : 2 * HEAD_DIM]
+    kv = qkv[:, : count // SHORT]
     c = core
     mine = y * 2 + c
 

time: 160 us -> 158 us (0.988)
  no operation moved by 1% of the time
where the time goes in v13:
time: 158 us
  Pallas kernels  45.3 us (29%)
  waiting for transfers between devices  35 us (22%)
  starting transfers between devices  34.8 us (22%)
  blocking collectives  27 us (17%)
  local copies, waits for them, and re-layouts  13 us (8%)
  other arithmetic  2.41 us (2%)
    ppermute x9, waiting for transfers between devices, along_y(): return lax.ppermute(block, 'y', [(i, (i + distance) % 4) for i in range(4)])  29.1 us
    all_to_all x1, blocking collectives, body(): qkv = lax.all_to_all(qkv, ('z', 'x'), 0, 0)  16.4 us
    unnamed x43, local copies, waits for them, and re-layouts  13 us
    all_to_all x1, blocking collectives, body(): mixed = lax.all_to_all(mixed, ('z', 'x'), 0, 0)  10.6 us
    pallas_call x3, Pallas kernels, coarse_attend(): pl.pallas_call(functools.partial(coarse_kernel, len(parts), first, final)...  10.3 us
    pallas_call x3, Pallas kernels, project(): pl.pallas_call(functools.partial(project_kernel, number), name='project',...  10.1 us
    ppermute x9, starting transfers between devices, along_y(): return lax.ppermute(block, 'y', [(i, (i + distance) % 4) for i in range(4)])  10 us
    ppermute x3, starting transfers between devices, along_x(): return lax.ppermute(block, 'x', [(i, (i + distance) % 4) for i in range(4)])  9.96 us
  transfers between devices with their start and end apart: 25, of which 9 were waited for; matrix products, arithmetic and copies ran while one was open for 3% of the time, Pallas kernels for 18%

profile of v13, /device:TPU:1, one launch (start us, length us, event | category | flops | bytes accessed | tf_op | source)
XLA Modules:
  0.0 157.9 jit_solution(8412580579388453664)
XLA Ops:
  1.4 4.2 %collective-permute-start = (bf16[512,1024]{1,0:T(8,128)(2,1)}, bf16[512,1024]{1,0:T(8,128)(2,1)}, u32[]{:S(2)}, u32[]{:S(2)}) collective-permute-start(bf16[512,1024]{1,0:T(8,128)(2,1)} %tokens_ref.3), channel_id=1, source_target_pairs={{0,2},{1,3},{2,4},{3,5},{4,6},{5,7},{6,8},{7,9},{8,10},{9,11},{10,... | collective-permute-start | bytes 3145736 | tf_op jit(solution)/shard_map/ppermute | solution.py:25
  6.0 2.9 %copy.11 = bf16[1024,1024]{0,1:T(8,128)(2,1)S(1)} copy(bf16[1024,1024]{1,0:T(8,128)(2,1)} %param.13) | data formatting | bytes 4194304 | tf_op args[3]
  12.5 4.7 %project.3 = (bf16[1024,512]{1,0:T(8,128)(2,1)S(1)}, bf16[512,1024]{1,0:T(8,128)(2,1)S(1)}, bf16[1024,512]{1,0:T(8,128)(2,1)S(1)}) custom-call(s32[1]{0:T(128)} %bitcast.5.core_ref, bf16[1024,1024]{1,0:T(8,128)(2,1)S(1)} %pad_maximum_fusion.rows_ref, bf16[1024,1024]{1,0:T(8,128)(2,1)S(1)} %copy-done.1, bf16[1024,1024]{1,0:T(8,128)(2,1)S(1)} %bitcast.16, ...), custom_call_target="tpu_custom_call" | custom-call | flops 1 | bytes 1 | tf_op jit(solution)/shard_map/project/pallas_call | solution.py:88
  17.2 6.5 %fine_own.1 = (f32[4,8,8,256]{3,2,1,0:T(8,128)S(1)}, f32[4,8,80,256]{3,2,1,0:T(8,128)S(1)}) custom-call(bf16[1024,512]{1,0:T(8,128)(2,1)S(1)} %get-tuple-element.62.q_ref, bf16[1024,512]{1,0:T(8,128)(2,1)S(1)} %get-tuple-element.58.k_ref, bf16[512,1024]{1,0:T(8,128)(2,1)S(1)} %get-tuple-element.59.v_ref), custom_call_target="tpu_custom_call" | custom-call | flops 1 | bytes 1 | tf_op jit(solution)/shard_map/fine_own/pallas_call | solution.py:300
  28.4 4.2 %collective-permute-start.4 = (bf16[256,1024]{1,0:T(8,128)(2,1)}, bf16[256,1024]{1,0:T(8,128)(2,1)}, u32[]{:S(2)}, u32[]{:S(2)}) collective-permute-start(bf16[256,1024]{1,0:T(8,128)(2,1)} %refs_4_.1), channel_id=1, source_target_pairs={{0,8},{8,16},{16,24},{24,0},{1,9},{9,17},{17,25},{25,1},{2,10},{10... | collective-permute-start | bytes 1572872 | tf_op jit(solution)/shard_map/ppermute | solution.py:575
  35.5 2.6 %project.4 = (bf16[512,512]{1,0:T(8,128)(2,1)S(1)}, bf16[512,512]{1,0:T(8,128)(2,1)S(1)}) custom-call(s32[1]{0:T(128)} %bitcast.5.core_ref, bf16[512,1024]{1,0:T(8,128)(2,1)} %collective-permute-done.rows_ref, bf16[1024,1024]{1,0:T(8,128)(2,1)S(1)} %copy-done.2, bf16[1024,1024]{1,0:T(8,128)(2,1)S(1)} %bitcast.17), custom_call_target="tpu_custom_call" | custom-call | flops 1 | bytes 1 | tf_op jit(solution)/shard_map/project/pallas_call | solution.py:88
  38.2 2.8 %project.5 = (bf16[512,512]{1,0:T(8,128)(2,1)S(1)}, bf16[512,512]{1,0:T(8,128)(2,1)S(1)}) custom-call(s32[1]{0:T(128)} %bitcast.5.core_ref, bf16[512,1024]{1,0:T(8,128)(2,1)} %collective-permute-done.3.rows_ref, bf16[1024,1024]{1,0:T(8,128)(2,1)S(1)} %copy-done.2, bf16[1024,1024]{1,0:T(8,128)(2,1)S(1)} %bitcast.18), custom_call_target="tpu_custom_call" | custom-call | flops 1 | bytes 1 | tf_op jit(solution)/shard_map/project/pallas_call | solution.py:88
  42.9 3.6 %collective-permute-done.4.refs_5_ = bf16[256,1024]{1,0:T(8,128)(2,1)} collective-permute-done((bf16[256,1024]{1,0:T(8,128)(2,1)}, bf16[256,1024]{1,0:T(8,128)(2,1)}, u32[]{:S(2)}, u32[]{:S(2)}) %collective-permute-start.4) | collective-permute-done | bytes 524320 | tf_op jit(solution)/shard_map/ppermute | solution.py:575
  48.1 4.5 %collective-permute-start.13 = (bf16[256,1024]{1,0:T(8,128)(2,1)}, bf16[256,1024]{1,0:T(8,128)(2,1)S(1)}, u32[]{:S(2)}, u32[]{:S(2)}) collective-permute-start(bf16[256,1024]{1,0:T(8,128)(2,1)} %collective-permute-done.5.refs_7_), channel_id=1, source_target_pairs={{0,24},{8,0},{16,8},{24,16},{1,25},{9,1},{17,9},{25,17},{2,26},{10... | collective-permute-start | bytes 1572872 | tf_op jit(solution)/shard_map/ppermute | solution.py:575
  61.4 2.9 %collective-permute-start.11 = (bf16[4,64,512]{2,1,0:T(8,128)(2,1)S(1)}, bf16[4,64,512]{2,1,0:T(8,128)(2,1)S(1)}, u32[]{:S(2)}, u32[]{:S(2)}) collective-permute-start(bf16[4,64,512]{2,1,0:T(8,128)(2,1)S(1)} %get-tuple-element.78), channel_id=1, source_target_pairs={{0,4},{2,6},{4,0},{6,2},{1,5},{3,7},{5,1},{7,3},{8,12},{10,14},{12... | collective-permute-start | bytes 786440 | tf_op jit(solution)/shard_map/ppermute | solution.py:598
  64.8 5.6 %collective-permute-done.10.refs_1_ = bf16[4,64,512]{2,1,0:T(8,128)(2,1)S(1)} collective-permute-done((bf16[4,64,512]{2,1,0:T(8,128)(2,1)S(1)}, bf16[4,64,512]{2,1,0:T(8,128)(2,1)S(1)}, u32[]{:S(2)}, u32[]{:S(2)}) %collective-permute-start.10) | collective-permute-done | bytes 262176 | tf_op jit(solution)/shard_map/ppermute | solution.py:598
  70.4 5.3 %collective-permute-done.11.refs_2_ = bf16[4,64,512]{2,1,0:T(8,128)(2,1)S(1)} collective-permute-done((bf16[4,64,512]{2,1,0:T(8,128)(2,1)S(1)}, bf16[4,64,512]{2,1,0:T(8,128)(2,1)S(1)}, u32[]{:S(2)}, u32[]{:S(2)}) %collective-permute-start.11) | collective-permute-done | bytes 262176 | tf_op jit(solution)/shard_map/ppermute | solution.py:598
  79.2 4.3 %shorten.1 = (bf16[64,1024]{1,0:T(8,128)(2,1)}, bf16[64,1024]{1,0:T(8,128)(2,1)}, bf16[64,1024]{1,0:T(8,128)(2,1)}, bf16[64,1024]{1,0:T(8,128)(2,1)}) custom-call(s32[2]{0:T(128)} %pad_add_fusion.1.where_ref, bf16[4,64,512]{2,1,0:T(8,128)(2,1)} %copy-done.10, bf16[4,64,512]{2,1,0:T(8,128)(2,1)} %copy-done.15, bf16[4,64,512]{2,1,0:T(8,128)(2,1)} %copy-done.16, ...), custom_call_target="tpu_custom_call" | custom-call | tf_op jit(solution)/shard_map/shorten/pallas_call | solution.py:372
  86.7 2.7 %collective-permute-done.15.refs_1_ = bf16[64,1024]{1,0:T(8,128)(2,1)S(1)} collective-permute-done((bf16[64,1024]{1,0:T(8,128)(2,1)}, bf16[64,1024]{1,0:T(8,128)(2,1)S(1)}, u32[]{:S(2)}, u32[]{:S(2)}) %collective-permute-start.15) | collective-permute-done | bytes 131104 | tf_op jit(solution)/shard_map/ppermute | solution.py:598
  92.0 3.8 %collective-permute-done.17.refs_3_ = bf16[64,1024]{1,0:T(8,128)(2,1)S(1)} collective-permute-done((bf16[64,1024]{1,0:T(8,128)(2,1)}, bf16[64,1024]{1,0:T(8,128)(2,1)S(1)}, u32[]{:S(2)}, u32[]{:S(2)}) %collective-permute-start.17) | collective-permute-done | bytes 131104 | tf_op jit(solution)/shard_map/ppermute | solution.py:598
  96.5 5.3 %coarse_project.1 = (bf16[64,1024]{1,0:T(8,128)(2,1)}, bf16[16,96,128]{2,1,0:T(8,128)(2,1)}) custom-call(bf16[64,1024]{1,0:T(8,128)(2,1)} %get-tuple-element.88.refs_0_, bf16[64,1024]{1,0:T(8,128)(2,1)} %copy-done.18, bf16[64,1024]{1,0:T(8,128)(2,1)} %copy-done.19, bf16[64,1024]{1,0:T(8,128)(2,1)} %copy-done.20, bf16[1024,1024]{1,0:T(8,128)(2,1)} %refs_4_.2, ...), custom_call_target="tpu_custom_call" | custom-call | tf_op jit(solution)/shard_map/coarse_project/pallas_call | solution.py:415
  101.8 16.4 %all_to_all.10.q_ref = bf16[16,96,128]{2,1,0:T(8,128)(2,1)S(1)} all-to-all(bf16[16,96,128]{2,1,0:T(8,128)(2,1)} %get-tuple-element.92), channel_id=1, replica_groups=mesh['z'=4,'x'=4,'y'=4,'c'=2] {'z','x'}, dimensions={0} | all-to-all | bytes 786432 | tf_op jit(solution)/shard_map/all_to_all | solution.py:610
  120.3 2.7 %collective-permute-start.20 = (bf16[16,64,128]{2,1,0:T(8,128)(2,1)S(1)}, bf16[16,64,128]{2,1,0:T(8,128)(2,1)S(1)}, u32[]{:S(2)}, u32[]{:S(2)}) collective-permute-start(bf16[16,64,128]{2,1,0:T(8,128)(2,1)S(1)} %slice.8.refs_0_), channel_id=1, source_target_pairs={{0,6},{2,0},{4,2},{6,4},{1,7},{3,1},{5,3},{7,5},{8,14},{10,8},{12,... | collective-permute-start | bytes 786440 | tf_op jit(solution)/shard_map/ppermute | solution.py:598
  123.1 2.8 %coarse_attend.3 = (f32[4,8,256]{2,1,0:T(8,128)S(1)}, f32[4,80,256]{2,1,0:T(8,128)S(1)}) custom-call(s32[3]{0:T(128)S(1)} %pad_add_fusion.4.where_ref, bf16[16,96,128]{2,1,0:T(8,128)(2,1)S(1)} %all_to_all.10.q_ref, bf16[16,64,128]{2,1,0:T(8,128)(2,1)S(1)} %slice.8.refs_0_, bf16[16,64,128]{2,1,0:T(8,128)(2,1)S(1)} %collective-permute-done.18.refs_1_), custom_call_target="tpu_custom_call" | custom-call | flops 1610612736 | bytes 2097152 | tf_op jit(solution)/shard_map/coarse_attend/pallas_call | solution.py:534
  125.9 9.0 %collective-permute-done.19.refs_0_ = bf16[16,64,128]{2,1,0:T(8,128)(2,1)S(1)} collective-permute-done((bf16[16,64,128]{2,1,0:T(8,128)(2,1)S(1)}, bf16[16,64,128]{2,1,0:T(8,128)(2,1)S(1)}, u32[]{:S(2)}, u32[]{:S(2)}) %collective-permute-start.19) | collective-permute-done | bytes 262176 | tf_op jit(solution)/shard_map/ppermute | solution.py:598
  136.4 3.7 %coarse_attend.4 = (f32[4,8,256]{2,1,0:T(8,128)S(1)}, f32[4,80,256]{2,1,0:T(8,128)S(1)}) custom-call(s32[4]{0:T(128)S(1)} %get-tuple-element.112.where_ref, bf16[16,96,128]{2,1,0:T(8,128)(2,1)S(1)} %all_to_all.10.q_ref, bf16[16,64,128]{2,1,0:T(8,128)(2,1)S(1)} %collective-permute-done.19.refs_0_, bf16[16,64,128]{2,1,0:T(8,128)(2,1)S(1)} %collective-permute-done.20.refs_1_, ...), custom_call_target="tpu_custom_call" | custom-call | flops 2415919104 | bytes 2097152 | tf_op jit(solution)/shard_map/coarse_attend/pallas_call | solution.py:534
  140.2 3.8 %coarse_attend.5 = bf16[16,32,128]{2,1,0:T(8,128)(2,1)S(1)} custom-call(s32[4]{0:T(128)S(1)} %get-tuple-element.111.where_ref, bf16[16,96,128]{2,1,0:T(8,128)(2,1)S(1)} %all_to_all.10.q_ref, bf16[16,64,128]{2,1,0:T(8,128)(2,1)S(1)} %collective-permute-done.22.refs_0_, bf16[16,64,128]{2,1,0:T(8,128)(2,1)S(1)} %collective-permute-done.23.refs_1_, ...), custom_call_target="tpu_custom_call" | custom-call | flops 2415919104 | bytes 2097152 | tf_op jit(solution)/shard_map/coarse_attend/pallas_call | solution.py:534
  144.0 10.6 %all_to_all.11.mixed_ref = bf16[16,32,128]{2,1,0:T(8,128)(2,1)} all-to-all(bf16[16,32,128]{2,1,0:T(8,128)(2,1)S(1)} %coarse_attend.5), channel_id=1, replica_groups=mesh['z'=4,'x'=4,'y'=4,'c'=2] {'z','x'}, dimensions={0} | all-to-all | bytes 262144 | tf_op jit(solution)/shard_map/all_to_all | solution.py:627
  154.6 3.3 %finish.1 = bf16[512,1024]{1,0:T(8,128)(2,1)} custom-call(bf16[16,32,128]{2,1,0:T(8,128)(2,1)} %all_to_all.11.mixed_ref, bf16[1024,1024]{1,0:T(8,128)(2,1)} %out_weight_ref.1, bf16[64,1024]{1,0:T(8,128)(2,1)} %get-tuple-element.107.short_ref, bf16[512,1024]{1,0:T(8,128)(2,1)} %copy-done.9), custom_call_target="tpu_custom_call" | custom-call | tf_op jit(solution)/shard_map/finish/pallas_call | solution.py:454
  (93 shorter events, 39.3 us)
Async XLA Ops:
  0.0 8.9 %collective-permute-start.1 = (bf16[512,1024]{1,0:T(8,128)(2,1)}, bf16[512,1024]{1,0:T(8,128)(2,1)}, u32[]{:S(2)}, u32[]{:S(2)}) collective-permute-start(bf16[512,1024]{1,0:T(8,128)(2,1)} %tokens_ref.3), channel_id=1, source_target_pairs={{0,1},{1,0},{2,3},{3,2},{4,5},{5,4},{6,7},{7,6},{8,9},{9,8},{10,11... | collective-permute-start | bytes 3145736 | tf_op jit(solution)/shard_map/ppermute | solution.py:565
  1.4 26.2 %collective-permute-start = (bf16[512,1024]{1,0:T(8,128)(2,1)}, bf16[512,1024]{1,0:T(8,128)(2,1)}, u32[]{:S(2)}, u32[]{:S(2)}) collective-permute-start(bf16[512,1024]{1,0:T(8,128)(2,1)} %tokens_ref.3), channel_id=1, source_target_pairs={{0,2},{1,3},{2,4},{3,5},{4,6},{5,7},{6,8},{7,9},{8,10},{9,11},{10,... | collective-permute-start | bytes 3145736 | tf_op jit(solution)/shard_map/ppermute | solution.py:25
  5.7 20.5 %collective-permute-start.2 = (bf16[256,1024]{1,0:T(8,128)(2,1)}, bf16[256,1024]{1,0:T(8,128)(2,1)}, u32[]{:S(2)}, u32[]{:S(2)}) collective-permute-start(bf16[256,1024]{1,0:T(8,128)(2,1)} %refs_4_.1), channel_id=1, source_target_pairs={{0,1},{1,0},{2,3},{3,2},{4,5},{5,4},{6,7},{7,6},{8,9},{9,8},{10,11... | collective-permute-start | bytes 1572872 | tf_op jit(solution)/shard_map/ppermute | solution.py:565
  27.6 10.6 %collective-permute-start.3 = (bf16[512,1024]{1,0:T(8,128)(2,1)}, bf16[512,1024]{1,0:T(8,128)(2,1)}, u32[]{:S(2)}, u32[]{:S(2)}) collective-permute-start(bf16[512,1024]{1,0:T(8,128)(2,1)} %collective-permute-done.rows_ref), channel_id=1, source_target_pairs={{0,1},{1,0},{2,3},{3,2},{4,5},{5,4},{6,7},{7,6},{8,9},{9,8},{10,11... | collective-permute-start | bytes 3145736 | tf_op jit(solution)/shard_map/ppermute | solution.py:565
  28.4 18.1 %collective-permute-start.4 = (bf16[256,1024]{1,0:T(8,128)(2,1)}, bf16[256,1024]{1,0:T(8,128)(2,1)}, u32[]{:S(2)}, u32[]{:S(2)}) collective-permute-start(bf16[256,1024]{1,0:T(8,128)(2,1)} %refs_4_.1), channel_id=1, source_target_pairs={{0,8},{8,16},{16,24},{24,0},{1,9},{9,17},{17,25},{25,1},{2,10},{10... | collective-permute-start | bytes 1572872 | tf_op jit(solution)/shard_map/ppermute | solution.py:575
  32.6 13.9 %collective-permute-start.5 = (bf16[256,1024]{1,0:T(8,128)(2,1)}, bf16[256,1024]{1,0:T(8,128)(2,1)}, u32[]{:S(2)}, u32[]{:S(2)}) collective-permute-start(bf16[256,1024]{1,0:T(8,128)(2,1)} %refs_4_.1), channel_id=1, source_target_pairs={{0,24},{8,0},{16,8},{24,16},{1,25},{9,1},{17,9},{25,17},{2,26},{10... | collective-permute-start | bytes 1572872 | tf_op jit(solution)/shard_map/ppermute | solution.py:575
  46.5 6.0 %collective-permute-start.6 = (bf16[512,512]{1,0:T(8,128)(2,1)S(1)}, bf16[512,512]{1,0:T(8,128)(2,1)S(1)}, u32[]{:S(2)}, u32[]{:S(2)}) collective-permute-start(bf16[512,512]{1,0:T(8,128)(2,1)S(1)} %slice_bitcast_fusion), channel_id=1, source_target_pairs={{0,1},{1,0},{2,3},{3,2},{4,5},{5,4},{6,7},{7,6},{8,9},{9,8},{10,11... | collective-permute-start | bytes 1572872 | tf_op jit(solution)/shard_map/ppermute | solution.py:565
  47.6 11.3 %collective-permute-start.7 = (bf16[256,1024]{1,0:T(8,128)(2,1)}, bf16[256,1024]{1,0:T(8,128)(2,1)S(1)}, u32[]{:S(2)}, u32[]{:S(2)}) collective-permute-start(bf16[256,1024]{1,0:T(8,128)(2,1)} %collective-permute-done.4.refs_5_), channel_id=1, source_target_pairs={{0,1},{1,0},{2,3},{3,2},{4,5},{5,4},{6,7},{7,6},{8,9},{9,8},{10,11... | collective-permute-start | bytes 1572872 | tf_op jit(solution)/shard_map/ppermute | solution.py:565
  47.6 11.2 %collective-permute-start.8 = (bf16[256,1024]{1,0:T(8,128)(2,1)}, bf16[256,1024]{1,0:T(8,128)(2,1)S(1)}, u32[]{:S(2)}, u32[]{:S(2)}) collective-permute-start(bf16[256,1024]{1,0:T(8,128)(2,1)} %collective-permute-done.5.refs_7_), channel_id=1, source_target_pairs={{0,1},{1,0},{2,3},{3,2},{4,5},{5,4},{6,7},{7,6},{8,9},{9,8},{10,11... | collective-permute-start | bytes 1572872 | tf_op jit(solution)/shard_map/ppermute | solution.py:565
  48.1 16.7 %collective-permute-start.13 = (bf16[256,1024]{1,0:T(8,128)(2,1)}, bf16[256,1024]{1,0:T(8,128)(2,1)S(1)}, u32[]{:S(2)}, u32[]{:S(2)}) collective-permute-start(bf16[256,1024]{1,0:T(8,128)(2,1)} %collective-permute-done.5.refs_7_), channel_id=1, source_target_pairs={{0,24},{8,0},{16,8},{24,16},{1,25},{9,1},{17,9},{25,17},{2,26},{10... | collective-permute-start | bytes 1572872 | tf_op jit(solution)/shard_map/ppermute | solution.py:575
  53.5 5.4 %collective-permute-start.9 = (bf16[16,1024]{1,0:T(8,128)(2,1)S(1)}, bf16[16,1024]{1,0:T(8,128)(2,1)S(1)}, u32[]{:S(2)}, u32[]{:S(2)}) collective-permute-start(bf16[16,1024]{1,0:T(8,128)(2,1)S(1)} %tail_project.1), channel_id=1, source_target_pairs={{0,1},{1,2},{2,3},{3,4},{4,5},{5,6},{6,7},{7,8},{8,9},{9,10},{10,1... | collective-permute-start | bytes 98312 | tf_op jit(solution)/shard_map/ppermute | solution.py:25
  60.7 9.7 %collective-permute-start.10 = (bf16[4,64,512]{2,1,0:T(8,128)(2,1)S(1)}, bf16[4,64,512]{2,1,0:T(8,128)(2,1)S(1)}, u32[]{:S(2)}, u32[]{:S(2)}) collective-permute-start(bf16[4,64,512]{2,1,0:T(8,128)(2,1)S(1)} %get-tuple-element.77), channel_id=1, source_target_pairs={{0,2},{2,4},{4,6},{6,0},{1,3},{3,5},{5,7},{7,1},{8,10},{10,12},{12... | collective-permute-start | bytes 786440 | tf_op jit(solution)/shard_map/ppermute | solution.py:598
  61.4 14.3 %collective-permute-start.11 = (bf16[4,64,512]{2,1,0:T(8,128)(2,1)S(1)}, bf16[4,64,512]{2,1,0:T(8,128)(2,1)S(1)}, u32[]{:S(2)}, u32[]{:S(2)}) collective-permute-start(bf16[4,64,512]{2,1,0:T(8,128)(2,1)S(1)} %get-tuple-element.78), channel_id=1, source_target_pairs={{0,4},{2,6},{4,0},{6,2},{1,5},{3,7},{5,1},{7,3},{8,12},{10,14},{12... | collective-permute-start | bytes 786440 | tf_op jit(solution)/shard_map/ppermute | solution.py:598
  64.3 11.5 %collective-permute-start.12 = (bf16[4,64,512]{2,1,0:T(8,128)(2,1)S(1)}, bf16[4,64,512]{2,1,0:T(8,128)(2,1)S(1)}, u32[]{:S(2)}, u32[]{:S(2)}) collective-permute-start(bf16[4,64,512]{2,1,0:T(8,128)(2,1)S(1)} %get-tuple-element.79), channel_id=1, source_target_pairs={{0,6},{2,0},{4,2},{6,4},{1,7},{3,1},{5,3},{7,5},{8,14},{10,8},{12,... | collective-permute-start | bytes 786440 | tf_op jit(solution)/shard_map/ppermute | solution.py:598
  83.5 5.9 %collective-permute-start.15 = (bf16[64,1024]{1,0:T(8,128)(2,1)}, bf16[64,1024]{1,0:T(8,128)(2,1)S(1)}, u32[]{:S(2)}, u32[]{:S(2)}) collective-permute-start(bf16[64,1024]{1,0:T(8,128)(2,1)} %get-tuple-element.89), channel_id=1, source_target_pairs={{0,6},{2,0},{4,2},{6,4},{1,7},{3,1},{5,3},{7,5},{8,14},{10,8},{12,... | collective-permute-start | bytes 393224 | tf_op jit(solution)/shard_map/ppermute | solution.py:598
  85.9 6.1 %collective-permute-start.16 = (bf16[64,1024]{1,0:T(8,128)(2,1)}, bf16[64,1024]{1,0:T(8,128)(2,1)S(1)}, u32[]{:S(2)}, u32[]{:S(2)}) collective-permute-start(bf16[64,1024]{1,0:T(8,128)(2,1)} %get-tuple-element.90), channel_id=1, source_target_pairs={{0,4},{2,6},{4,0},{6,2},{1,5},{3,7},{5,1},{7,3},{8,12},{10,14},{12... | collective-permute-start | bytes 393224 | tf_op jit(solution)/shard_map/ppermute | solution.py:598
  86.7 9.1 %collective-permute-start.17 = (bf16[64,1024]{1,0:T(8,128)(2,1)}, bf16[64,1024]{1,0:T(8,128)(2,1)S(1)}, u32[]{:S(2)}, u32[]{:S(2)}) collective-permute-start(bf16[64,1024]{1,0:T(8,128)(2,1)} %get-tuple-element.91), channel_id=1, source_target_pairs={{0,2},{2,4},{4,6},{6,0},{1,3},{3,5},{5,7},{7,1},{8,10},{10,12},{12... | collective-permute-start | bytes 393224 | tf_op jit(solution)/shard_map/ppermute | solution.py:598
  118.2 4.8 %collective-permute-start.18 = (bf16[16,64,128]{2,1,0:T(8,128)(2,1)S(1)}, bf16[16,64,128]{2,1,0:T(8,128)(2,1)S(1)}, u32[]{:S(2)}, u32[]{:S(2)}) collective-permute-start(bf16[16,64,128]{2,1,0:T(8,128)(2,1)S(1)} %slice.8.refs_0_), channel_id=1, source_target_pairs={{0,1},{1,0},{2,3},{3,2},{4,5},{5,4},{6,7},{7,6},{8,9},{9,8},{10,11... | collective-permute-start | bytes 786440 | tf_op jit(solution)/shard_map/ppermute | solution.py:565
  120.3 14.6 %collective-permute-start.19 = (bf16[16,64,128]{2,1,0:T(8,128)(2,1)S(1)}, bf16[16,64,128]{2,1,0:T(8,128)(2,1)S(1)}, u32[]{:S(2)}, u32[]{:S(2)}) collective-permute-start(bf16[16,64,128]{2,1,0:T(8,128)(2,1)S(1)} %slice.8.refs_0_), channel_id=1, source_target_pairs={{0,2},{2,4},{4,6},{6,0},{1,3},{3,5},{5,7},{7,1},{8,10},{10,12},{12... | collective-permute-start | bytes 786440 | tf_op jit(solution)/shard_map/ppermute | solution.py:598
  120.3 14.6 %collective-permute-start.20 = (bf16[16,64,128]{2,1,0:T(8,128)(2,1)S(1)}, bf16[16,64,128]{2,1,0:T(8,128)(2,1)S(1)}, u32[]{:S(2)}, u32[]{:S(2)}) collective-permute-start(bf16[16,64,128]{2,1,0:T(8,128)(2,1)S(1)} %slice.8.refs_0_), channel_id=1, source_target_pairs={{0,6},{2,0},{4,2},{6,4},{1,7},{3,1},{5,3},{7,5},{8,14},{10,8},{12,... | collective-permute-start | bytes 786440 | tf_op jit(solution)/shard_map/ppermute | solution.py:598
  123.0 11.9 %collective-permute-start.21 = (bf16[16,64,128]{2,1,0:T(8,128)(2,1)S(1)}, bf16[16,64,128]{2,1,0:T(8,128)(2,1)S(1)}, u32[]{:S(2)}, u32[]{:S(2)}) collective-permute-start(bf16[16,64,128]{2,1,0:T(8,128)(2,1)S(1)} %slice.8.refs_0_), channel_id=1, source_target_pairs={{0,4},{2,6},{4,0},{6,2},{1,5},{3,7},{5,1},{7,3},{8,12},{10,14},{12... | collective-permute-start | bytes 786440 | tf_op jit(solution)/shard_map/ppermute | solution.py:598
  134.9 5.2 %collective-permute-start.22 = (bf16[16,64,128]{2,1,0:T(8,128)(2,1)S(1)}, bf16[16,64,128]{2,1,0:T(8,128)(2,1)S(1)}, u32[]{:S(2)}, u32[]{:S(2)}) collective-permute-start(bf16[16,64,128]{2,1,0:T(8,128)(2,1)S(1)} %collective-permute-done.19.refs_0_), channel_id=1, source_target_pairs={{0,1},{1,0},{2,3},{3,2},{4,5},{5,4},{6,7},{7,6},{8,9},{9,8},{10,11... | collective-permute-start | bytes 786440 | tf_op jit(solution)/shard_map/ppermute | solution.py:565
  135.9 4.3 %collective-permute-start.23 = (bf16[16,64,128]{2,1,0:T(8,128)(2,1)S(1)}, bf16[16,64,128]{2,1,0:T(8,128)(2,1)S(1)}, u32[]{:S(2)}, u32[]{:S(2)}) collective-permute-start(bf16[16,64,128]{2,1,0:T(8,128)(2,1)S(1)} %collective-permute-done.20.refs_1_), channel_id=1, source_target_pairs={{0,1},{1,0},{2,3},{3,2},{4,5},{5,4},{6,7},{7,6},{8,9},{9,8},{10,11... | collective-permute-start | bytes 786440 | tf_op jit(solution)/shard_map/ppermute | solution.py:565
  135.9 4.2 %collective-permute-start.24 = (bf16[16,64,128]{2,1,0:T(8,128)(2,1)S(1)}, bf16[16,64,128]{2,1,0:T(8,128)(2,1)S(1)}, u32[]{:S(2)}, u32[]{:S(2)}) collective-permute-start(bf16[16,64,128]{2,1,0:T(8,128)(2,1)S(1)} %collective-permute-done.21.refs_2_), channel_id=1, source_target_pairs={{0,1},{1,0},{2,3},{3,2},{4,5},{5,4},{6,7},{7,6},{8,9},{9,8},{10,11... | collective-permute-start | bytes 786440 | tf_op jit(solution)/shard_map/ppermute | solution.py:565
  (22 other events, 88.7 us)

commit v14 on v13

--- a/solution.py
+++ b/solution.py
@@ -378,7 +378,7 @@
         + [pl.BlockSpec((piece.shape[0], tile), lambda i: (0, i)) for piece in pieces],
         out_specs=[pl.BlockSpec((rows, tile), lambda i: (0, i))] * 4,
         out_shape=[jax.ShapeDtypeStruct((rows, width), jnp.bfloat16)] * 4,
-        compiler_params=params(60),
+        compiler_params=params(24),
     )(where, *grouped, *pieces)
 
 

time: 158 us -> 156 us (0.987)
  local copies, waits for them, and re-layouts: 13 us -> 11.4 us
    unnamed x43 -> x29, local copies, waits for them, and re-layouts: 13 us -> 11.3 us
  transfers between devices with their start and end apart: 25 -> 25, of which waited for: 9 -> 10; matrix products, arithmetic and copies ran while one was open for 3% -> 3% of each run, Pallas kernels for 18% -> 18%
where the time goes in v14:
time: 156 us; the launch traced here: 155 us
  Pallas kernels  43.8 us (28%)
  waiting for transfers between devices  35.3 us (23%)
  starting transfers between devices  34.6 us (22%)
  blocking collectives  27.8 us (18%)
  local copies, waits for them, and re-layouts  11.4 us (7%)
  other arithmetic  1.84 us (1%)
    ppermute x9, waiting for transfers between devices, along_y(): return lax.ppermute(block, 'y', [(i, (i + distance) % 4) for i in range(4)])  28.1 us
    all_to_all x1, blocking collectives, body(): qkv = lax.all_to_all(qkv, ('z', 'x'), 0, 0)  17.2 us
    unnamed x29, local copies, waits for them, and re-layouts  11.3 us
    all_to_all x1, blocking collectives, body(): mixed = lax.all_to_all(mixed, ('z', 'x'), 0, 0)  10.6 us
    pallas_call x3, Pallas kernels, coarse_attend(): pl.pallas_call(functools.partial(coarse_kernel, len(parts), first, final)...  10.3 us
    pallas_call x3, Pallas kernels, project(): pl.pallas_call(functools.partial(project_kernel, number), name='project',...  10.1 us
    ppermute x9, starting transfers between devices, along_y(): return lax.ppermute(block, 'y', [(i, (i + distance) % 4) for i in range(4)])  9.99 us
    ppermute x3, starting transfers between devices, along_x(): return lax.ppermute(block, 'x', [(i, (i + distance) % 4) for i in range(4)])  9.74 us
  transfers between devices with their start and end apart: 25, of which 10 were waited for; matrix products, arithmetic and copies ran while one was open for 3% of the time, Pallas kernels for 18%

profile of v14, /device:TPU:1, one launch (start us, length us, event | category | flops | bytes accessed | tf_op | source)
XLA Modules:
  0.0 155.1 jit_solution(9463740149156392880)
XLA Ops:
  1.4 4.3 %collective-permute-start = (bf16[512,1024]{1,0:T(8,128)(2,1)}, bf16[512,1024]{1,0:T(8,128)(2,1)}, u32[]{:S(2)}, u32[]{:S(2)}) collective-permute-start(bf16[512,1024]{1,0:T(8,128)(2,1)} %tokens_ref.3), channel_id=1, source_target_pairs={{0,2},{1,3},{2,4},{3,5},{4,6},{5,7},{6,8},{7,9},{8,10},{9,11},{10,... | collective-permute-start | bytes 3145736 | tf_op jit(solution)/shard_map/ppermute | solution.py:25
  6.0 2.9 %copy.11 = bf16[1024,1024]{0,1:T(8,128)(2,1)S(1)} copy(bf16[1024,1024]{1,0:T(8,128)(2,1)} %param.13) | data formatting | bytes 4194304 | tf_op args[3]
  12.6 4.7 %project.3 = (bf16[1024,512]{1,0:T(8,128)(2,1)S(1)}, bf16[512,1024]{1,0:T(8,128)(2,1)S(1)}, bf16[1024,512]{1,0:T(8,128)(2,1)S(1)}) custom-call(s32[1]{0:T(128)} %bitcast.5.core_ref, bf16[1024,1024]{1,0:T(8,128)(2,1)S(1)} %pad_maximum_fusion.rows_ref, bf16[1024,1024]{1,0:T(8,128)(2,1)S(1)} %copy-done.1, bf16[1024,1024]{1,0:T(8,128)(2,1)S(1)} %bitcast.16, ...), custom_call_target="tpu_custom_call" | custom-call | flops 1 | bytes 1 | tf_op jit(solution)/shard_map/project/pallas_call | solution.py:88
  17.3 6.5 %fine_own.1 = (f32[4,8,8,256]{3,2,1,0:T(8,128)S(1)}, f32[4,8,80,256]{3,2,1,0:T(8,128)S(1)}) custom-call(bf16[1024,512]{1,0:T(8,128)(2,1)S(1)} %get-tuple-element.62.q_ref, bf16[1024,512]{1,0:T(8,128)(2,1)S(1)} %get-tuple-element.58.k_ref, bf16[512,1024]{1,0:T(8,128)(2,1)S(1)} %get-tuple-element.59.v_ref), custom_call_target="tpu_custom_call" | custom-call | flops 1 | bytes 1 | tf_op jit(solution)/shard_map/fine_own/pallas_call | solution.py:300
  28.4 4.2 %collective-permute-start.4 = (bf16[256,1024]{1,0:T(8,128)(2,1)}, bf16[256,1024]{1,0:T(8,128)(2,1)}, u32[]{:S(2)}, u32[]{:S(2)}) collective-permute-start(bf16[256,1024]{1,0:T(8,128)(2,1)} %refs_4_.1), channel_id=1, source_target_pairs={{0,8},{8,16},{16,24},{24,0},{1,9},{9,17},{17,25},{25,1},{2,10},{10... | collective-permute-start | bytes 1572872 | tf_op jit(solution)/shard_map/ppermute | solution.py:575
  35.5 2.6 %project.4 = (bf16[512,512]{1,0:T(8,128)(2,1)S(1)}, bf16[512,512]{1,0:T(8,128)(2,1)S(1)}) custom-call(s32[1]{0:T(128)} %bitcast.5.core_ref, bf16[512,1024]{1,0:T(8,128)(2,1)} %collective-permute-done.rows_ref, bf16[1024,1024]{1,0:T(8,128)(2,1)S(1)} %copy-done.2, bf16[1024,1024]{1,0:T(8,128)(2,1)S(1)} %bitcast.17), custom_call_target="tpu_custom_call" | custom-call | flops 1 | bytes 1 | tf_op jit(solution)/shard_map/project/pallas_call | solution.py:88
  38.2 2.8 %project.5 = (bf16[512,512]{1,0:T(8,128)(2,1)S(1)}, bf16[512,512]{1,0:T(8,128)(2,1)S(1)}) custom-call(s32[1]{0:T(128)} %bitcast.5.core_ref, bf16[512,1024]{1,0:T(8,128)(2,1)} %collective-permute-done.3.rows_ref, bf16[1024,1024]{1,0:T(8,128)(2,1)S(1)} %copy-done.2, bf16[1024,1024]{1,0:T(8,128)(2,1)S(1)} %bitcast.18), custom_call_target="tpu_custom_call" | custom-call | flops 1 | bytes 1 | tf_op jit(solution)/shard_map/project/pallas_call | solution.py:88
  42.9 3.6 %collective-permute-done.4.refs_5_ = bf16[256,1024]{1,0:T(8,128)(2,1)} collective-permute-done((bf16[256,1024]{1,0:T(8,128)(2,1)}, bf16[256,1024]{1,0:T(8,128)(2,1)}, u32[]{:S(2)}, u32[]{:S(2)}) %collective-permute-start.4) | collective-permute-done | bytes 524320 | tf_op jit(solution)/shard_map/ppermute | solution.py:575
  48.1 4.2 %collective-permute-start.13 = (bf16[256,1024]{1,0:T(8,128)(2,1)}, bf16[256,1024]{1,0:T(8,128)(2,1)S(1)}, u32[]{:S(2)}, u32[]{:S(2)}) collective-permute-start(bf16[256,1024]{1,0:T(8,128)(2,1)} %collective-permute-done.5.refs_7_), channel_id=1, source_target_pairs={{0,24},{8,0},{16,8},{24,16},{1,25},{9,1},{17,9},{25,17},{2,26},{10... | collective-permute-start | bytes 1572872 | tf_op jit(solution)/shard_map/ppermute | solution.py:575
  59.7 2.9 %collective-permute-start.11 = (bf16[4,64,512]{2,1,0:T(8,128)(2,1)S(1)}, bf16[4,64,512]{2,1,0:T(8,128)(2,1)S(1)}, u32[]{:S(2)}, u32[]{:S(2)}) collective-permute-start(bf16[4,64,512]{2,1,0:T(8,128)(2,1)S(1)} %get-tuple-element.78), channel_id=1, source_target_pairs={{0,4},{2,6},{4,0},{6,2},{1,5},{3,7},{5,1},{7,3},{8,12},{10,14},{12... | collective-permute-start | bytes 786440 | tf_op jit(solution)/shard_map/ppermute | solution.py:598
  63.9 4.2 %collective-permute-done.10.refs_1_ = bf16[4,64,512]{2,1,0:T(8,128)(2,1)S(1)} collective-permute-done((bf16[4,64,512]{2,1,0:T(8,128)(2,1)S(1)}, bf16[4,64,512]{2,1,0:T(8,128)(2,1)S(1)}, u32[]{:S(2)}, u32[]{:S(2)}) %collective-permute-start.10) | collective-permute-done | bytes 262176 | tf_op jit(solution)/shard_map/ppermute | solution.py:598
  68.1 6.0 %collective-permute-done.11.refs_2_ = bf16[4,64,512]{2,1,0:T(8,128)(2,1)S(1)} collective-permute-done((bf16[4,64,512]{2,1,0:T(8,128)(2,1)S(1)}, bf16[4,64,512]{2,1,0:T(8,128)(2,1)S(1)}, u32[]{:S(2)}, u32[]{:S(2)}) %collective-permute-start.11) | collective-permute-done | bytes 262176 | tf_op jit(solution)/shard_map/ppermute | solution.py:598
  76.7 2.7 %shorten.1 = (bf16[64,1024]{1,0:T(8,128)(2,1)S(1)}, bf16[64,1024]{1,0:T(8,128)(2,1)S(1)}, bf16[64,1024]{1,0:T(8,128)(2,1)S(1)}, bf16[64,1024]{1,0:T(8,128)(2,1)S(1)}) custom-call(s32[2]{0:T(128)S(1)} %pad_add_fusion.1.where_ref, bf16[4,64,512]{2,1,0:T(8,128)(2,1)S(1)} %get-tuple-element.80.refs_0_, bf16[4,64,512]{2,1,0:T(8,128)(2,1)S(1)} %collective-permute-done.10.refs_1_, ...), custom_call_target="tpu_custom_call" | custom-call | tf_op jit(solution)/shard_map/shorten/pallas_call | solution.py:372
  85.6 2.7 %collective-permute-done.16.refs_2_ = bf16[64,1024]{1,0:T(8,128)(2,1)S(1)} collective-permute-done((bf16[64,1024]{1,0:T(8,128)(2,1)S(1)}, bf16[64,1024]{1,0:T(8,128)(2,1)S(1)}, u32[]{:S(2)}, u32[]{:S(2)}) %collective-permute-start.16) | collective-permute-done | bytes 131104 | tf_op jit(solution)/shard_map/ppermute | solution.py:598
  88.4 3.8 %collective-permute-done.17.refs_3_ = bf16[64,1024]{1,0:T(8,128)(2,1)S(1)} collective-permute-done((bf16[64,1024]{1,0:T(8,128)(2,1)S(1)}, bf16[64,1024]{1,0:T(8,128)(2,1)S(1)}, u32[]{:S(2)}, u32[]{:S(2)}) %collective-permute-start.17) | collective-permute-done | bytes 131104 | tf_op jit(solution)/shard_map/ppermute | solution.py:598
  92.8 5.3 %coarse_project.1 = (bf16[64,1024]{1,0:T(8,128)(2,1)}, bf16[16,96,128]{2,1,0:T(8,128)(2,1)}) custom-call(bf16[64,1024]{1,0:T(8,128)(2,1)} %copy-done.10, bf16[64,1024]{1,0:T(8,128)(2,1)} %copy-done.11, bf16[64,1024]{1,0:T(8,128)(2,1)} %copy-done.12, bf16[64,1024]{1,0:T(8,128)(2,1)} %copy-done.13, bf16[1024,1024]{1,0:T(8,128)(2,1)} %refs_4_.2, ...), custom_call_target="tpu_custom_call" | custom-call | tf_op jit(solution)/shard_map/coarse_project/pallas_call | solution.py:415
  98.1 17.2 %all_to_all.10.q_ref = bf16[16,96,128]{2,1,0:T(8,128)(2,1)S(1)} all-to-all(bf16[16,96,128]{2,1,0:T(8,128)(2,1)} %get-tuple-element.92), channel_id=1, replica_groups=mesh['z'=4,'x'=4,'y'=4,'c'=2] {'z','x'}, dimensions={0} | all-to-all | bytes 786432 | tf_op jit(solution)/shard_map/all_to_all | solution.py:610
  117.4 2.7 %collective-permute-start.20 = (bf16[16,64,128]{2,1,0:T(8,128)(2,1)S(1)}, bf16[16,64,128]{2,1,0:T(8,128)(2,1)S(1)}, u32[]{:S(2)}, u32[]{:S(2)}) collective-permute-start(bf16[16,64,128]{2,1,0:T(8,128)(2,1)S(1)} %slice.8.refs_0_), channel_id=1, source_target_pairs={{0,6},{2,0},{4,2},{6,4},{1,7},{3,1},{5,3},{7,5},{8,14},{10,8},{12,... | collective-permute-start | bytes 786440 | tf_op jit(solution)/shard_map/ppermute | solution.py:598
  120.2 2.8 %coarse_attend.3 = (f32[4,8,256]{2,1,0:T(8,128)S(1)}, f32[4,80,256]{2,1,0:T(8,128)S(1)}) custom-call(s32[3]{0:T(128)S(1)} %pad_add_fusion.4.where_ref, bf16[16,96,128]{2,1,0:T(8,128)(2,1)S(1)} %all_to_all.10.q_ref, bf16[16,64,128]{2,1,0:T(8,128)(2,1)S(1)} %slice.8.refs_0_, bf16[16,64,128]{2,1,0:T(8,128)(2,1)S(1)} %collective-permute-done.18.refs_1_), custom_call_target="tpu_custom_call" | custom-call | flops 1610612736 | bytes 2097152 | tf_op jit(solution)/shard_map/coarse_attend/pallas_call | solution.py:534
  123.0 9.0 %collective-permute-done.19.refs_0_ = bf16[16,64,128]{2,1,0:T(8,128)(2,1)S(1)} collective-permute-done((bf16[16,64,128]{2,1,0:T(8,128)(2,1)S(1)}, bf16[16,64,128]{2,1,0:T(8,128)(2,1)S(1)}, u32[]{:S(2)}, u32[]{:S(2)}) %collective-permute-start.19) | collective-permute-done | bytes 262176 | tf_op jit(solution)/shard_map/ppermute | solution.py:598
  133.6 3.7 %coarse_attend.4 = (f32[4,8,256]{2,1,0:T(8,128)S(1)}, f32[4,80,256]{2,1,0:T(8,128)S(1)}) custom-call(s32[4]{0:T(128)S(1)} %get-tuple-element.112.where_ref, bf16[16,96,128]{2,1,0:T(8,128)(2,1)S(1)} %all_to_all.10.q_ref, bf16[16,64,128]{2,1,0:T(8,128)(2,1)S(1)} %collective-permute-done.19.refs_0_, bf16[16,64,128]{2,1,0:T(8,128)(2,1)S(1)} %collective-permute-done.20.refs_1_, ...), custom_call_target="tpu_custom_call" | custom-call | flops 2415919104 | bytes 2097152 | tf_op jit(solution)/shard_map/coarse_attend/pallas_call | solution.py:534
  137.3 3.8 %coarse_attend.5 = bf16[16,32,128]{2,1,0:T(8,128)(2,1)S(1)} custom-call(s32[4]{0:T(128)S(1)} %get-tuple-element.111.where_ref, bf16[16,96,128]{2,1,0:T(8,128)(2,1)S(1)} %all_to_all.10.q_ref, bf16[16,64,128]{2,1,0:T(8,128)(2,1)S(1)} %collective-permute-done.22.refs_0_, bf16[16,64,128]{2,1,0:T(8,128)(2,1)S(1)} %collective-permute-done.23.refs_1_, ...), custom_call_target="tpu_custom_call" | custom-call | flops 2415919104 | bytes 2097152 | tf_op jit(solution)/shard_map/coarse_attend/pallas_call | solution.py:534
  141.1 10.6 %all_to_all.11.mixed_ref = bf16[16,32,128]{2,1,0:T(8,128)(2,1)} all-to-all(bf16[16,32,128]{2,1,0:T(8,128)(2,1)S(1)} %coarse_attend.5), channel_id=1, replica_groups=mesh['z'=4,'x'=4,'y'=4,'c'=2] {'z','x'}, dimensions={0} | all-to-all | bytes 262144 | tf_op jit(solution)/shard_map/all_to_all | solution.py:627
  151.7 3.3 %finish.1 = bf16[512,1024]{1,0:T(8,128)(2,1)} custom-call(bf16[16,32,128]{2,1,0:T(8,128)(2,1)} %all_to_all.11.mixed_ref, bf16[1024,1024]{1,0:T(8,128)(2,1)} %out_weight_ref.1, bf16[64,1024]{1,0:T(8,128)(2,1)} %get-tuple-element.107.short_ref, bf16[512,1024]{1,0:T(8,128)(2,1)} %copy-done.9), custom_call_target="tpu_custom_call" | custom-call | tf_op jit(solution)/shard_map/finish/pallas_call | solution.py:454
  (79 shorter events, 38.1 us)
Async XLA Ops:
  0.0 8.9 %collective-permute-start.1 = (bf16[512,1024]{1,0:T(8,128)(2,1)}, bf16[512,1024]{1,0:T(8,128)(2,1)}, u32[]{:S(2)}, u32[]{:S(2)}) collective-permute-start(bf16[512,1024]{1,0:T(8,128)(2,1)} %tokens_ref.3), channel_id=1, source_target_pairs={{0,1},{1,0},{2,3},{3,2},{4,5},{5,4},{6,7},{7,6},{8,9},{9,8},{10,11... | collective-permute-start | bytes 3145736 | tf_op jit(solution)/shard_map/ppermute | solution.py:565
  1.4 26.2 %collective-permute-start = (bf16[512,1024]{1,0:T(8,128)(2,1)}, bf16[512,1024]{1,0:T(8,128)(2,1)}, u32[]{:S(2)}, u32[]{:S(2)}) collective-permute-start(bf16[512,1024]{1,0:T(8,128)(2,1)} %tokens_ref.3), channel_id=1, source_target_pairs={{0,2},{1,3},{2,4},{3,5},{4,6},{5,7},{6,8},{7,9},{8,10},{9,11},{10,... | collective-permute-start | bytes 3145736 | tf_op jit(solution)/shard_map/ppermute | solution.py:25
  5.7 20.5 %collective-permute-start.2 = (bf16[256,1024]{1,0:T(8,128)(2,1)}, bf16[256,1024]{1,0:T(8,128)(2,1)}, u32[]{:S(2)}, u32[]{:S(2)}) collective-permute-start(bf16[256,1024]{1,0:T(8,128)(2,1)} %refs_4_.1), channel_id=1, source_target_pairs={{0,1},{1,0},{2,3},{3,2},{4,5},{5,4},{6,7},{7,6},{8,9},{9,8},{10,11... | collective-permute-start | bytes 1572872 | tf_op jit(solution)/shard_map/ppermute | solution.py:565
  27.6 10.6 %collective-permute-start.3 = (bf16[512,1024]{1,0:T(8,128)(2,1)}, bf16[512,1024]{1,0:T(8,128)(2,1)}, u32[]{:S(2)}, u32[]{:S(2)}) collective-permute-start(bf16[512,1024]{1,0:T(8,128)(2,1)} %collective-permute-done.rows_ref), channel_id=1, source_target_pairs={{0,1},{1,0},{2,3},{3,2},{4,5},{5,4},{6,7},{7,6},{8,9},{9,8},{10,11... | collective-permute-start | bytes 3145736 | tf_op jit(solution)/shard_map/ppermute | solution.py:565
  28.4 18.1 %collective-permute-start.4 = (bf16[256,1024]{1,0:T(8,128)(2,1)}, bf16[256,1024]{1,0:T(8,128)(2,1)}, u32[]{:S(2)}, u32[]{:S(2)}) collective-permute-start(bf16[256,1024]{1,0:T(8,128)(2,1)} %refs_4_.1), channel_id=1, source_target_pairs={{0,8},{8,16},{16,24},{24,0},{1,9},{9,17},{17,25},{25,1},{2,10},{10... | collective-permute-start | bytes 1572872 | tf_op jit(solution)/shard_map/ppermute | solution.py:575
  32.6 13.9 %collective-permute-start.5 = (bf16[256,1024]{1,0:T(8,128)(2,1)}, bf16[256,1024]{1,0:T(8,128)(2,1)}, u32[]{:S(2)}, u32[]{:S(2)}) collective-permute-start(bf16[256,1024]{1,0:T(8,128)(2,1)} %refs_4_.1), channel_id=1, source_target_pairs={{0,24},{8,0},{16,8},{24,16},{1,25},{9,1},{17,9},{25,17},{2,26},{10... | collective-permute-start | bytes 1572872 | tf_op jit(solution)/shard_map/ppermute | solution.py:575
  46.5 5.8 %collective-permute-start.6 = (bf16[512,512]{1,0:T(8,128)(2,1)S(1)}, bf16[512,512]{1,0:T(8,128)(2,1)S(1)}, u32[]{:S(2)}, u32[]{:S(2)}) collective-permute-start(bf16[512,512]{1,0:T(8,128)(2,1)S(1)} %slice_bitcast_fusion), channel_id=1, source_target_pairs={{0,1},{1,0},{2,3},{3,2},{4,5},{5,4},{6,7},{7,6},{8,9},{9,8},{10,11... | collective-permute-start | bytes 1572872 | tf_op jit(solution)/shard_map/ppermute | solution.py:565
  47.6 11.1 %collective-permute-start.7 = (bf16[256,1024]{1,0:T(8,128)(2,1)}, bf16[256,1024]{1,0:T(8,128)(2,1)S(1)}, u32[]{:S(2)}, u32[]{:S(2)}) collective-permute-start(bf16[256,1024]{1,0:T(8,128)(2,1)} %collective-permute-done.4.refs_5_), channel_id=1, source_target_pairs={{0,1},{1,0},{2,3},{3,2},{4,5},{5,4},{6,7},{7,6},{8,9},{9,8},{10,11... | collective-permute-start | bytes 1572872 | tf_op jit(solution)/shard_map/ppermute | solution.py:565
  47.6 11.0 %collective-permute-start.8 = (bf16[256,1024]{1,0:T(8,128)(2,1)}, bf16[256,1024]{1,0:T(8,128)(2,1)S(1)}, u32[]{:S(2)}, u32[]{:S(2)}) collective-permute-start(bf16[256,1024]{1,0:T(8,128)(2,1)} %collective-permute-done.5.refs_7_), channel_id=1, source_target_pairs={{0,1},{1,0},{2,3},{3,2},{4,5},{5,4},{6,7},{7,6},{8,9},{9,8},{10,11... | collective-permute-start | bytes 1572872 | tf_op jit(solution)/shard_map/ppermute | solution.py:565
  48.1 15.8 %collective-permute-start.13 = (bf16[256,1024]{1,0:T(8,128)(2,1)}, bf16[256,1024]{1,0:T(8,128)(2,1)S(1)}, u32[]{:S(2)}, u32[]{:S(2)}) collective-permute-start(bf16[256,1024]{1,0:T(8,128)(2,1)} %collective-permute-done.5.refs_7_), channel_id=1, source_target_pairs={{0,24},{8,0},{16,8},{24,16},{1,25},{9,1},{17,9},{25,17},{2,26},{10... | collective-permute-start | bytes 1572872 | tf_op jit(solution)/shard_map/ppermute | solution.py:575
  53.3 5.4 %collective-permute-start.9 = (bf16[16,1024]{1,0:T(8,128)(2,1)S(1)}, bf16[16,1024]{1,0:T(8,128)(2,1)S(1)}, u32[]{:S(2)}, u32[]{:S(2)}) collective-permute-start(bf16[16,1024]{1,0:T(8,128)(2,1)S(1)} %tail_project.1), channel_id=1, source_target_pairs={{0,1},{1,2},{2,3},{3,4},{4,5},{5,6},{6,7},{7,8},{8,9},{9,10},{10,1... | collective-permute-start | bytes 98312 | tf_op jit(solution)/shard_map/ppermute | solution.py:25
  59.0 9.1 %collective-permute-start.10 = (bf16[4,64,512]{2,1,0:T(8,128)(2,1)S(1)}, bf16[4,64,512]{2,1,0:T(8,128)(2,1)S(1)}, u32[]{:S(2)}, u32[]{:S(2)}) collective-permute-start(bf16[4,64,512]{2,1,0:T(8,128)(2,1)S(1)} %get-tuple-element.77), channel_id=1, source_target_pairs={{0,2},{2,4},{4,6},{6,0},{1,3},{3,5},{5,7},{7,1},{8,10},{10,12},{12... | collective-permute-start | bytes 786440 | tf_op jit(solution)/shard_map/ppermute | solution.py:598
  59.7 14.3 %collective-permute-start.11 = (bf16[4,64,512]{2,1,0:T(8,128)(2,1)S(1)}, bf16[4,64,512]{2,1,0:T(8,128)(2,1)S(1)}, u32[]{:S(2)}, u32[]{:S(2)}) collective-permute-start(bf16[4,64,512]{2,1,0:T(8,128)(2,1)S(1)} %get-tuple-element.78), channel_id=1, source_target_pairs={{0,4},{2,6},{4,0},{6,2},{1,5},{3,7},{5,1},{7,3},{8,12},{10,14},{12... | collective-permute-start | bytes 786440 | tf_op jit(solution)/shard_map/ppermute | solution.py:598
  62.6 11.5 %collective-permute-start.12 = (bf16[4,64,512]{2,1,0:T(8,128)(2,1)S(1)}, bf16[4,64,512]{2,1,0:T(8,128)(2,1)S(1)}, u32[]{:S(2)}, u32[]{:S(2)}) collective-permute-start(bf16[4,64,512]{2,1,0:T(8,128)(2,1)S(1)} %get-tuple-element.79), channel_id=1, source_target_pairs={{0,6},{2,0},{4,2},{6,4},{1,7},{3,1},{5,3},{7,5},{8,14},{10,8},{12,... | collective-permute-start | bytes 786440 | tf_op jit(solution)/shard_map/ppermute | solution.py:598
  80.1 5.5 %collective-permute-start.15 = (bf16[64,1024]{1,0:T(8,128)(2,1)S(1)}, bf16[64,1024]{1,0:T(8,128)(2,1)S(1)}, u32[]{:S(2)}, u32[]{:S(2)}) collective-permute-start(bf16[64,1024]{1,0:T(8,128)(2,1)S(1)} %get-tuple-element.89), channel_id=1, source_target_pairs={{0,6},{2,0},{4,2},{6,4},{1,7},{3,1},{5,3},{7,5},{8,14},{10,8},{12,... | collective-permute-start | bytes 393224 | tf_op jit(solution)/shard_map/ppermute | solution.py:598
  82.5 5.9 %collective-permute-start.16 = (bf16[64,1024]{1,0:T(8,128)(2,1)S(1)}, bf16[64,1024]{1,0:T(8,128)(2,1)S(1)}, u32[]{:S(2)}, u32[]{:S(2)}) collective-permute-start(bf16[64,1024]{1,0:T(8,128)(2,1)S(1)} %get-tuple-element.90), channel_id=1, source_target_pairs={{0,4},{2,6},{4,0},{6,2},{1,5},{3,7},{5,1},{7,3},{8,12},{10,14},{12... | collective-permute-start | bytes 393224 | tf_op jit(solution)/shard_map/ppermute | solution.py:598
  83.3 8.9 %collective-permute-start.17 = (bf16[64,1024]{1,0:T(8,128)(2,1)S(1)}, bf16[64,1024]{1,0:T(8,128)(2,1)S(1)}, u32[]{:S(2)}, u32[]{:S(2)}) collective-permute-start(bf16[64,1024]{1,0:T(8,128)(2,1)S(1)} %get-tuple-element.91), channel_id=1, source_target_pairs={{0,2},{2,4},{4,6},{6,0},{1,3},{3,5},{5,7},{7,1},{8,10},{10,12},{12... | collective-permute-start | bytes 393224 | tf_op jit(solution)/shard_map/ppermute | solution.py:598
  115.4 4.8 %collective-permute-start.18 = (bf16[16,64,128]{2,1,0:T(8,128)(2,1)S(1)}, bf16[16,64,128]{2,1,0:T(8,128)(2,1)S(1)}, u32[]{:S(2)}, u32[]{:S(2)}) collective-permute-start(bf16[16,64,128]{2,1,0:T(8,128)(2,1)S(1)} %slice.8.refs_0_), channel_id=1, source_target_pairs={{0,1},{1,0},{2,3},{3,2},{4,5},{5,4},{6,7},{7,6},{8,9},{9,8},{10,11... | collective-permute-start | bytes 786440 | tf_op jit(solution)/shard_map/ppermute | solution.py:565
  117.4 14.6 %collective-permute-start.19 = (bf16[16,64,128]{2,1,0:T(8,128)(2,1)S(1)}, bf16[16,64,128]{2,1,0:T(8,128)(2,1)S(1)}, u32[]{:S(2)}, u32[]{:S(2)}) collective-permute-start(bf16[16,64,128]{2,1,0:T(8,128)(2,1)S(1)} %slice.8.refs_0_), channel_id=1, source_target_pairs={{0,2},{2,4},{4,6},{6,0},{1,3},{3,5},{5,7},{7,1},{8,10},{10,12},{12... | collective-permute-start | bytes 786440 | tf_op jit(solution)/shard_map/ppermute | solution.py:598
  117.4 14.6 %collective-permute-start.20 = (bf16[16,64,128]{2,1,0:T(8,128)(2,1)S(1)}, bf16[16,64,128]{2,1,0:T(8,128)(2,1)S(1)}, u32[]{:S(2)}, u32[]{:S(2)}) collective-permute-start(bf16[16,64,128]{2,1,0:T(8,128)(2,1)S(1)} %slice.8.refs_0_), channel_id=1, source_target_pairs={{0,6},{2,0},{4,2},{6,4},{1,7},{3,1},{5,3},{7,5},{8,14},{10,8},{12,... | collective-permute-start | bytes 786440 | tf_op jit(solution)/shard_map/ppermute | solution.py:598
  120.1 11.9 %collective-permute-start.21 = (bf16[16,64,128]{2,1,0:T(8,128)(2,1)S(1)}, bf16[16,64,128]{2,1,0:T(8,128)(2,1)S(1)}, u32[]{:S(2)}, u32[]{:S(2)}) collective-permute-start(bf16[16,64,128]{2,1,0:T(8,128)(2,1)S(1)} %slice.8.refs_0_), channel_id=1, source_target_pairs={{0,4},{2,6},{4,0},{6,2},{1,5},{3,7},{5,1},{7,3},{8,12},{10,14},{12... | collective-permute-start | bytes 786440 | tf_op jit(solution)/shard_map/ppermute | solution.py:598
  132.0 5.2 %collective-permute-start.22 = (bf16[16,64,128]{2,1,0:T(8,128)(2,1)S(1)}, bf16[16,64,128]{2,1,0:T(8,128)(2,1)S(1)}, u32[]{:S(2)}, u32[]{:S(2)}) collective-permute-start(bf16[16,64,128]{2,1,0:T(8,128)(2,1)S(1)} %collective-permute-done.19.refs_0_), channel_id=1, source_target_pairs={{0,1},{1,0},{2,3},{3,2},{4,5},{5,4},{6,7},{7,6},{8,9},{9,8},{10,11... | collective-permute-start | bytes 786440 | tf_op jit(solution)/shard_map/ppermute | solution.py:565
  133.0 4.3 %collective-permute-start.23 = (bf16[16,64,128]{2,1,0:T(8,128)(2,1)S(1)}, bf16[16,64,128]{2,1,0:T(8,128)(2,1)S(1)}, u32[]{:S(2)}, u32[]{:S(2)}) collective-permute-start(bf16[16,64,128]{2,1,0:T(8,128)(2,1)S(1)} %collective-permute-done.20.refs_1_), channel_id=1, source_target_pairs={{0,1},{1,0},{2,3},{3,2},{4,5},{5,4},{6,7},{7,6},{8,9},{9,8},{10,11... | collective-permute-start | bytes 786440 | tf_op jit(solution)/shard_map/ppermute | solution.py:565
  133.1 4.2 %collective-permute-start.24 = (bf16[16,64,128]{2,1,0:T(8,128)(2,1)S(1)}, bf16[16,64,128]{2,1,0:T(8,128)(2,1)S(1)}, u32[]{:S(2)}, u32[]{:S(2)}) collective-permute-start(bf16[16,64,128]{2,1,0:T(8,128)(2,1)S(1)} %collective-permute-done.21.refs_2_), channel_id=1, source_target_pairs={{0,1},{1,0},{2,3},{3,2},{4,5},{5,4},{6,7},{7,6},{8,9},{9,8},{10,11... | collective-permute-start | bytes 786440 | tf_op jit(solution)/shard_map/ppermute | solution.py:565
  (15 other events, 43.1 us)
